TPU v7x, 32 devices: a whole 2x2x4 slice. The times are simulated.
32 devices in a mesh: depth: 8 (over z, core), wave: 4 (over y, x).
Axes of the slice: x: 2, y: 2, z: 4, core: 2. Of those that a mesh axis runs over, the one named last changes fastest.
Arguments:
- rhs: float32 [2, 64, 32, 4096], P(None, 'depth', None, 'wave'), may hold values from -0.8 to 0.8
- cotangent: float32 [2, 64, 32, 4096], P(None, 'depth', None, 'wave'), may hold values from -0.8 to 0.8
- thickness: float32 [64], replicated, may hold values from 0.5 to 2
- ky_shift: float32 [32], replicated, may hold values from 1e-05 to 0.001
Outputs:
- pressure: float32 [2, 64, 32, 4096], P(None, 'depth', None, 'wave')
- adjoint_field: float32 [2, 64, 32, 4096], P(None, 'depth', None, 'wave')
All inputs are finite; a program needn't handle non-finite values.
Results may differ from a plain program's by a relative error of at most 0.0003.
Values sent between devices are 32-bit elements; how exact they have to be, the bound alone decides.
No kernel may reach another device: no remote copies, remote signals or barrier semaphores. Data moves between devices by JAX's collectives and lax.ppermute only.
A program may use at most 192 MiB of HBM per device.

v0:
```python
import math

import jax
import jax.numpy as jnp
from jax import lax
from jax.sharding import PartitionSpec as P

aspect_ratio = 1.0
highest = lax.Precision.HIGHEST


def entering(part, axis, combine, identity, reverse):
    count = lax.axis_size(axis)
    place = lax.axis_index(axis)
    ahead = count - 1 - place if reverse else place
    gathered = jax.tree.map(lambda a: lax.all_gather(a, axis), part)
    state = jax.tree.map(lambda a, e: jnp.zeros_like(a) + jnp.asarray(e, a.dtype), part, identity)

    def one(turn, state):
        source = count - 1 - turn if reverse else turn
        return combine(
            state, jax.tree.map(lambda a: lax.dynamic_index_in_dim(a, source, 0, False), gathered)
        )

    return lax.fori_loop(0, ahead, one, state)


def level_terms(thickness):
    inner_face = 2.0 / (thickness[:-1] + thickness[1:])
    nothing = jnp.zeros((1,), jnp.float32)
    top_face = 2.0 / thickness[:1]
    below_face = jnp.concatenate([inner_face, nothing])
    above_face = jnp.concatenate([top_face, inner_face])
    lower_band = -jnp.concatenate([nothing, inner_face]) / thickness
    upper_band = -below_face / thickness
    centre = (above_face + below_face) / thickness
    return (lower_band, centre, upper_band)


def phase_table(row_count, col_count, length, orient):
    row_index = lax.broadcasted_iota(jnp.int32, (row_count, col_count), 0)
    col_index = lax.broadcasted_iota(jnp.int32, (row_count, col_count), 1)
    phases = (row_index * col_index % length).astype(jnp.float32) * (
        orient * 2.0 * math.pi / length
    )
    return (jnp.cos(phases), jnp.sin(phases))


def contract(pattern, first_operand, second_operand):
    return jnp.einsum(
        pattern,
        first_operand,
        second_operand,
        precision=highest,
        preferred_element_type=jnp.float32,
    )


def transform(values, orient, factor):
    full_width = values.shape[-1]
    inner_size = min(64, full_width)
    outer_size = full_width // inner_size
    lead_shape = values.shape[1:-1]
    real_part = values[0].reshape(lead_shape + (outer_size, inner_size))
    imag_part = values[1].reshape(lead_shape + (outer_size, inner_size))
    first_cos, first_sin = phase_table(outer_size, outer_size, outer_size, orient)
    pattern = "...st,sk->...tk"
    section_real = contract(pattern, real_part, first_cos) - contract(pattern, imag_part, first_sin)
    section_imag = contract(pattern, real_part, first_sin) + contract(pattern, imag_part, first_cos)
    twist_cos, twist_sin = phase_table(inner_size, outer_size, full_width, orient)
    turned_real = section_real * twist_cos - section_imag * twist_sin
    turned_imag = section_real * twist_sin + section_imag * twist_cos
    last_cos, last_sin = phase_table(inner_size, inner_size, inner_size, orient)
    pattern = "...tk,tm->...mk"
    final_real = contract(pattern, turned_real, last_cos) - contract(pattern, turned_imag, last_sin)
    final_imag = contract(pattern, turned_real, last_sin) + contract(pattern, turned_imag, last_cos)
    final_shape = lead_shape + (full_width,)
    return jnp.stack([final_real.reshape(final_shape), final_imag.reshape(final_shape)]) * factor


def spectra(fields):
    return (transform(fields[0], -1.0, 1.0), transform(fields[1], -1.0, 1.0))


def block_solve(lower_part, diagonal, upper_part, right_side):
    levels = diagonal.shape[0]
    level_index = lax.broadcasted_iota(jnp.int32, diagonal.shape, 0)
    first_unit = jnp.where(level_index == 0, 1.0, 0.0).astype(jnp.float32)
    last_unit = jnp.where(level_index == levels - 1, 1.0, 0.0).astype(jnp.float32)
    augmented = jnp.concatenate([right_side, first_unit[None], last_unit[None]], 0)
    pivot = diagonal[0]
    ratio = upper_part[0] / pivot
    reduced = augmented[:, 0] / pivot
    ratios = [ratio]
    reduced_rows = [reduced]
    for level in range(1, levels):
        pivot = diagonal[level] - lower_part[level] * ratio
        ratio = upper_part[level] / pivot
        reduced = (augmented[:, level] - lower_part[level] * reduced) / pivot
        ratios.append(ratio)
        reduced_rows.append(reduced)
    current = reduced_rows[levels - 1]
    solved_rows = [current]
    for level in range(levels - 2, -1, -1):
        current = reduced_rows[level] - ratios[level] * current
        solved_rows.append(current)
    ordered_rows = solved_rows[::-1]
    return jnp.stack(ordered_rows, 1)


def summarize(answer, couple_above, couple_below):
    count = answer.shape[0] - 2
    first_unit = answer[count]
    last_unit = answer[count + 1]
    return (
        answer[:count, 0],
        answer[:count, -1],
        -couple_above * first_unit[0],
        -couple_below * last_unit[0],
        -couple_above * first_unit[-1],
        -couple_below * last_unit[-1],
    )


def expand(coefficient):
    return coefficient[..., None, :]


def merge_blocks(upper_block, lower_block):
    top_first, top_last, top_first_up, top_first_down, top_last_up, top_last_down = upper_block
    deep_first, deep_last, deep_first_up, deep_first_down, deep_last_up, deep_last_down = (
        lower_block
    )
    denominator = 1.0 - top_last_down * deep_first_up
    joint_base = (top_last + expand(top_last_down) * deep_first) / expand(denominator)
    joint_up = top_last_up / denominator
    joint_down = top_last_down * deep_first_down / denominator
    inner_base = deep_first + expand(deep_first_up) * joint_base
    inner_up = deep_first_up * joint_up
    inner_down = deep_first_down + deep_first_up * joint_down
    return (
        top_first + expand(top_first_down) * inner_base,
        deep_last + expand(deep_last_up) * joint_base,
        top_first_up + top_first_down * inner_up,
        top_first_down * inner_down,
        deep_last_up * joint_up,
        deep_last_down + deep_last_up * joint_down,
    )


def merge_reversed(earlier, later):
    return merge_blocks(later, earlier)


def shards(rhs, cotangent, thickness, ky_shift):
    forward_hat, adjoint_hat = spectra(
        (
            lax.all_to_all(rhs, "wave", split_axis=2, concat_axis=3, tiled=True),
            lax.all_to_all(cotangent, "wave", split_axis=2, concat_axis=3, tiled=True),
        )
    )
    levels = forward_hat.shape[1]
    ky_local = forward_hat.shape[2]
    full_width = forward_hat.shape[3]
    batch = ky_local * full_width
    depth_pos = lax.axis_index("depth")
    wave_pos = lax.axis_index("wave")
    lower_band, centre, upper_band = level_terms(thickness)
    nothing = jnp.zeros((1,), jnp.float32)
    lower_padded = jnp.concatenate([nothing, lower_band, nothing])
    upper_padded = jnp.concatenate([nothing, upper_band, nothing])
    lower_full_t = jnp.concatenate([nothing, upper_band[:-1]])
    upper_full_t = jnp.concatenate([lower_band[1:], nothing])
    first_row = depth_pos * levels
    lower_here = lax.dynamic_slice_in_dim(lower_padded, first_row + 1, levels)
    upper_here = lax.dynamic_slice_in_dim(upper_padded, first_row + 1, levels)
    centre_here = lax.dynamic_slice_in_dim(centre, first_row, levels)
    shifts = lax.dynamic_slice_in_dim(ky_shift, wave_pos * ky_local, ky_local)
    wavenumber = jnp.arange(full_width, dtype=jnp.float32)
    horizontal = aspect_ratio * 4.0 * jnp.sin(math.pi * wavenumber / full_width) ** 2
    eigen_shift = (shifts[:, None] + horizontal[None, :]).reshape(batch)
    forward_flat = forward_hat.reshape(2, levels, batch)
    adjoint_flat = adjoint_hat.reshape(2, levels, batch)
    lower_transposed = lax.dynamic_slice_in_dim(upper_padded, first_row, levels)
    upper_transposed = lax.dynamic_slice_in_dim(lower_padded, first_row + 2, levels)
    systems = [
        (lower_here, upper_here, lower_band, upper_band, forward_flat),
        (lower_transposed, upper_transposed, lower_full_t, upper_full_t, adjoint_flat),
    ]
    diagonal = centre_here[:, None] + eigen_shift[None, :]
    solved = []
    coupling = []
    pieces = []
    for lower_part, upper_part, lower_full, upper_full, right_side in systems:
        answer = block_solve(lower_part, diagonal, upper_part, right_side)
        couple_above = lower_part[0]
        couple_below = upper_part[levels - 1]
        solved.append(answer)
        coupling.append((couple_above, couple_below))
        pieces.append(summarize(answer, couple_above, couple_below))
    summary = tuple((jnp.stack([piece[member] for piece in pieces]) for member in range(6)))
    blank_values = jnp.zeros_like(summary[0])
    blank_coef = jnp.zeros_like(summary[2])
    unit_coef = jnp.ones_like(summary[2])
    identity = (blank_values, blank_values, blank_coef, unit_coef, unit_coef, blank_coef)
    before = entering(summary, "depth", merge_blocks, identity, False)
    after = entering(summary, "depth", merge_reversed, identity, True)
    pull_first_up = expand(summary[2])
    pull_first_down = expand(summary[3])
    pull_last_up = expand(summary[4])
    pull_last_down = expand(summary[5])
    above_slope = expand(before[5])
    below_slope = expand(after[2])
    entry_one = 1.0 - pull_first_up * above_slope
    entry_two = -pull_first_down * below_slope
    entry_three = -pull_last_up * above_slope
    entry_four = 1.0 - pull_last_down * below_slope
    source_first = summary[0] + pull_first_up * before[1] + pull_first_down * after[0]
    source_last = summary[1] + pull_last_up * before[1] + pull_last_down * after[0]
    determinant = entry_one * entry_four - entry_two * entry_three
    value_first = (source_first * entry_four - entry_two * source_last) / determinant
    value_last = (entry_one * source_last - entry_three * source_first) / determinant
    neighbour_above = before[1] + above_slope * value_first
    neighbour_below = after[0] + below_slope * value_last
    results = []
    for position in range(len(solved)):
        answer = solved[position]
        count = answer.shape[0] - 2
        couple_above, couple_below = coupling[position]
        fixed = (
            answer[:count]
            - couple_above * neighbour_above[position][:, None, :] * answer[count][None]
            - couple_below * neighbour_below[position][:, None, :] * answer[count + 1][None]
        )
        results.append(fixed)
    pressure_flat = results[0]
    adjoint_solved = results[1]
    shape_modes = (2, levels, ky_local, full_width)
    pressure_back = transform(pressure_flat.reshape(shape_modes), 1.0, 1.0 / full_width)
    adjoint_back = transform(adjoint_solved.reshape(shape_modes), 1.0, 1.0 / full_width)
    return (
        lax.all_to_all(pressure_back, "wave", split_axis=3, concat_axis=2, tiled=True),
        lax.all_to_all(adjoint_back, "wave", split_axis=3, concat_axis=2, tiled=True),
    )


def solution(mesh):
    in_specs = (P(None, "depth", None, "wave"), P(None, "depth", None, "wave"), P(), P())
    out_specs = (P(None, "depth", None, "wave"), P(None, "depth", None, "wave"))
    return jax.shard_map(shards, mesh=mesh, in_specs=in_specs, out_specs=out_specs, check_vma=False)
```

profile of v0, /device:TPU:0, one launch (start us, length us, event | category | flops | bytes accessed | tf_op | source)
XLA Modules:
  0.0 833.0 jit_solution(3932457750181570921)
XLA Ops:
  7.2 4.1 copy.142
  11.3 5.3 all-to-all-start
  20.3 11.4 %multiply_subtract_fusion.26 = (f32[1,32768]{1,0:T(1,128)}, f32[1,32768]{1,0:T(1,128)S(1)}, f32[1,32768]{1,0:T(1,128)}, f32[1,32768]{1,0:T(1,128)}, f32[1,32768]...) fusion(f32[8,32768]{1,0:T(8,128)S(1)} %broadcast_add_fusion, ...), kind=kLoop, calls=%fused_computation.197 | loop fusion | flops 688128 | bytes 2883640 | tf_op jit(solution)/shard_map/sub | solution.py:97
  31.6 11.8 %multiply_subtract_fusion.33 = (f32[1,32768]{1,0:T(1,128)}, f32[1,32768]{1,0:T(1,128)}, f32[1,32768]{1,0:T(1,128)}, f32[1,32768]{1,0:T(1,128)}, f32[1,32768]{1,0...) fusion(f32[8,32768]{1,0:T(8,128)S(1)} %broadcast_add_fusion, ...), kind=kLoop, calls=%fused_computation.204 | loop fusion | flops 688128 | bytes 2883640 | tf_op jit(solution)/shard_map/sub | solution.py:97
  46.4 4.1 copy.150
  50.7 4.5 all-to-all-start.1
  60.0 3.4 fusion.95
  63.4 3.4 fusion.106
  68.9 4.4 convolution_add_fusion.3
  75.5 8.1 fusion.18
  83.5 7.6 fusion.20
  98.4 5.1 fusion.90
  103.4 3.4 fusion.101
  109.0 4.6 convolution_add_fusion.2
  115.7 7.8 fusion.24
  123.5 7.6 fusion.26
  131.0 7.6 add_bitcast_fusion.3
  141.6 9.8 %subtract_bitcast_fusion.3 = f32[8,8,64,64]{3,2,1,0:T(8,128)} fusion(f32[64,8,8,64]{3,0,2,1:T(8,128)} %fusion.20, f32[64,8,8,64]{3,0,2,1:T(8,128)S(1)} %convolution_add_fusion.3, f32[64,8,8,64]{3,0,2,1:T(8,128)} %copy-done, f32[64,64]{0,1:T(8,128)S(1)} %get-tuple-element.507, f32[64,64]{0,1:T(8,128)S(1)} %get-tuple-element.508), kind=kOutput, calls=%fused_computation.54 | convolution fusion | flops 202432512 | bytes 4227072 | tf_op jit(solution)/shard_map/...tk,tm->...mk/dot_general | solution.py:50
  151.4 3.5 stack.78
  154.9 9.8 %add_bitcast_fusion.2 = f32[8,8,64,64]{3,2,1,0:T(8,128)} fusion(f32[64,8,8,64]{3,0,2,1:T(8,128)} %fusion.24, f32[64,8,8,64]{3,0,2,1:T(8,128)S(1)} %copy-done.5, f32[64,8,8,64]{3,0,2,1:T(8,128)} %copy-done.6, f32[64,64]{0,1:T(8,128)S(1)} %get-tuple-element.507, f32[64,64]{0,1:T(8,128)S(1)} %get-tuple-element.508), kind=kOutput, calls=%fused_computation.51 | convolution fusion | flops 202432512 | bytes 4227072 | tf_op jit(solution)/shard_map/...tk,tm->...mk/dot_general | solution.py:50
  164.7 3.5 stack.81
  168.2 9.8 %subtract_bitcast_fusion.2 = f32[8,8,64,64]{3,2,1,0:T(8,128)} fusion(f32[64,8,8,64]{3,0,2,1:T(8,128)} %fusion.26, f32[64,8,8,64]{3,0,2,1:T(8,128)S(1)} %copy-done.5, f32[64,8,8,64]{3,0,2,1:T(8,128)} %copy-done.6, f32[64,64]{0,1:T(8,128)S(1)} %get-tuple-element.507, f32[64,64]{0,1:T(8,128)S(1)} %get-tuple-element.508), kind=kOutput, calls=%fused_computation.52 | convolution fusion | flops 202432512 | bytes 4227072 | tf_op jit(solution)/shard_map/...tk,tm->...mk/dot_general | solution.py:50
  177.9 3.5 stack.80
  182.8 6.3 pad_maximum_fusion
  189.2 6.8 multiply_subtract_fusion.15
  197.9 9.2 %constant_dynamic-update-slice_fusion.4 = (f32[4,8,32768]{2,0,1:T(4,128)S(1)}, f32[4,1,32768]{2,0,1:T(4,128)S(1)}, f32[4,1,32768]{2,0,1:T(4,128)S(1)}, f32[4,1,3...) fusion(f32[32768]{0:T(1024)S(1)} %bitcast.576, ...), kind=kLoop, calls=%fused_computation.241 | loop fusion | flops 4325375 | bytes 10747928
  210.2 6.8 multiply_subtract_fusion.14
  217.2 6.7 constant_dynamic-update-slice_fusion.9
  248.5 7.1 fusion.256
  266.1 21.9 %all-gather.25.cloned.1.call-done = f32[8,2,32768]{2,1,0:T(2,128)} async-done(((f32[1,2,32768]{2,1,0:T(2,128)}), f32[8,2,32768]{2,1,0:T(2,128)}) %all-gather.25.cloned.1.call-update) | async-done | bytes 2097168 | tf_op jit(solution)/shard_map/all_gather | solution.py:16
  287.9 30.2 %all-gather.23.cloned.1.call-done = f32[8,2,32768]{2,1,0:T(2,128)} async-done(((f32[1,2,32768]{2,1,0:T(2,128)}), f32[8,2,32768]{2,1,0:T(2,128)}) %all-gather.23.cloned.1.call-update) | async-done | bytes 2097168 | tf_op jit(solution)/shard_map/all_gather | solution.py:16
  318.2 30.1 %all-gather.27.cloned.1.call-done = f32[8,2,32768]{2,1,0:T(2,128)} async-done(((f32[1,2,32768]{2,1,0:T(2,128)}), f32[8,2,32768]{2,1,0:T(2,128)}) %all-gather.27.cloned.1.call-update) | async-done | bytes 2097168 | tf_op jit(solution)/shard_map/all_gather | solution.py:16
  348.3 48.1 %all-gather.17.cloned.1.call-done = f32[16,2,32768]{2,1,0:T(2,128)} async-done(((f32[2,2,32768]{2,1,0:T(2,128)}), f32[16,2,32768]{2,1,0:T(2,128)}) %all-gather.17.cloned.1.call-update) | async-done | bytes 4194320 | tf_op jit(solution)/shard_map/all_gather | solution.py:16
  396.4 47.4 %all-gather.19.cloned.1.call-done = f32[16,2,32768]{2,1,0:T(2,128)} async-done(((f32[2,2,32768]{2,1,0:T(2,128)}), f32[16,2,32768]{2,1,0:T(2,128)}) %all-gather.19.cloned.1.call-update) | async-done | bytes 4194320 | tf_op jit(solution)/shard_map/all_gather | solution.py:16
  444.2 33.6 %while.39 = (s32[]{:T(128)}, f32[2,2,32768]{2,1,0:T(2,128)S(1)}, f32[2,32768]{1,0:T(2,128)S(1)}, s32[]{:T(128)}, f32[8,2,2,32768]{3,2,1,0:T(2,128)}, /*index=5*/...) while((s32[]{:T(128)}, f32[2,2,32768]{2,1,0:T(2,128)S(1)}, ...), condition=%wide.region_3.4_spmd, body=%wide.region_2.3_spmd.sunk | while | flops 1441798 | bytes 6815943 | solution.py:25
  489.8 6.4 slice_reduce_fusion.2
  498.3 4.8 fusion.85
  503.1 4.7 fusion.72
  509.4 6.8 slice_reduce_fusion
  518.3 4.8 fusion.78
  523.1 4.8 fusion.69
  529.9 5.8 convolution_add_fusion
  535.7 3.5 convolution_subtract_fusion
  542.6 3.4 fusion.15
  548.2 6.0 convolution_add_fusion.1
  554.3 4.9 convolution_subtract_fusion.1
  559.2 3.5 add_bitcast_fusion
  564.8 6.2 subtract_bitcast_fusion
  576.7 17.6 %copy.178 = f32[2,8,8,4096]{2,1,0,3:T(8,128)} copy(f32[2,8,8,4096]{3,2,1,0:T(8,128)} %maximum_multiply_fusion.1) | data formatting | bytes 4194304 | tf_op jit(solution)/shard_map/mul | solution.py:78
  594.3 34.4 %reshape.1424 = f32[4,1,131072]{2,1,0:T(1,128)} reshape(f32[4096,2,8,8]{3,2,1,0:T(8,128)} %bitcast.500) | data formatting | bytes 4194304
  628.7 4.9 all-to-all-start.3
  633.6 3.8 fusion.12
  637.4 3.5 add_bitcast_fusion.1
  643.1 3.8 fusion.13
  646.9 3.5 subtract_bitcast_fusion.1
  654.7 16.7 %copy.168 = f32[2,8,8,4096]{2,1,0,3:T(8,128)} copy(f32[2,8,8,4096]{3,2,1,0:T(8,128)S(1)} %maximum_multiply_fusion) | data formatting | bytes 4194304 | tf_op jit(solution)/shard_map/mul | solution.py:78
  671.4 34.6 %reshape.1422 = f32[4,1,131072]{2,1,0:T(1,128)} reshape(f32[4096,2,8,8]{3,2,1,0:T(8,128)} %bitcast.501) | data formatting | bytes 4194304
  705.9 4.5 all-to-all-start.2
  711.0 7.7 reduce.9
  718.7 29.7 %reshape.1425 = f32[4096,2,8,8]{3,2,1,0:T(8,128)} reshape(f32[4,131072]{1,0:T(4,128)S(1)} %reduce.9) | data formatting | bytes 4194304
  748.5 20.1 %copy.179 = f32[2,8,4,8,1024]{4,3,2,1,0:T(8,128)} copy(f32[2,8,4,8,1024]{3,1,0,4,2:T(8,128)} %bitcast.502) | data formatting | bytes 4194304 | tf_op jit(solution)/shard_map/all_to_all | solution.py:243
  768.6 7.7 reduce.8
  776.3 29.5 %reshape.1423 = f32[4096,2,8,8]{3,2,1,0:T(8,128)} reshape(f32[4,131072]{1,0:T(4,128)S(1)} %reduce.8) | data formatting | bytes 4194304
  805.8 20.1 %copy.169 = f32[2,8,4,8,1024]{4,3,2,1,0:T(8,128)} copy(f32[2,8,4,8,1024]{3,1,0,4,2:T(8,128)} %bitcast.503) | data formatting | bytes 4194304 | tf_op jit(solution)/shard_map/all_to_all | solution.py:242
  (312 shorter events, 141.8 us)
Async XLA Ops:
  11.3 5.4 copy-start.81
  11.3 8.6 %copy-start.82 = (f32[32]{0:T(128)S(1)}, f32[32]{0:T(128)}, u32[]{:S(2)}) copy-start(f32[32]{0:T(128)} %param.11) | copy-start | bytes 388
  11.3 39.4 %all-to-all-start = ((f32[2,8,32,1024]{3,1,0,2:T(8,128)}), f32[2,8,32,1024]{3,1,0,2:T(8,128)S(1)}, u32[]{:S(2)}, u32[]{:S(2)}) async-start(f32[2,8,32,1024]{3,1,0,2:T(8,128)} %copy.142), calls=%async_computation | async-start | bytes 4194304 | tf_op jit(solution)/shard_map/all_to_all | solution.py:158
  50.7 40.5 %all-to-all-start.1 = ((f32[2,8,32,1024]{3,1,0,2:T(8,128)}), f32[2,8,32,1024]{3,1,0,2:T(8,128)}, u32[]{:S(2)}, u32[]{:S(2)}) async-start(f32[2,8,32,1024]{3,1,0,2:T(8,128)} %copy.150), calls=%async_computation.1 | async-start | bytes 4194304 | tf_op jit(solution)/shard_map/all_to_all | solution.py:159
  55.2 210.9 %all-gather.21.cloned.1.call-start = ((), (), s32[]{:S(2)}) async-start(), calls=%async_computation.6 | async-start | bytes 2359296 | tf_op jit(solution)/shard_map/all_gather | solution.py:16
  68.9 4.4 copy-start.11
  68.9 4.4 copy-start.16
  75.4 8.1 copy-start
  98.4 5.1 copy-start.14
  109.0 4.6 copy-start.12
  109.0 4.6 copy-start.17
  113.6 9.9 %copy-start.4 = (f32[64,8,8,64]{3,0,2,1:T(8,128)}, f32[64,8,8,64]{3,0,2,1:T(8,128)S(1)}, u32[]{:S(2)}) copy-start(f32[64,8,8,64]{3,0,2,1:T(8,128)S(1)} %convolution_add_fusion.2) | copy-start | bytes 3145732
  115.7 7.8 copy-start.6
  123.5 7.6 copy-start.1
  123.5 7.6 copy-start.19
  177.9 4.7 copy-start.25
  177.9 4.7 copy-start.26
  182.7 6.4 copy-start.38
  182.7 6.4 copy-start.40
  182.7 6.4 copy-start.55
  182.7 6.4 copy-start.56
  182.7 6.4 copy-start.57
  182.7 6.4 copy-start.58
  182.7 6.4 copy-start.59
  182.8 6.4 copy-start.60
  182.8 6.4 copy-start.61
  182.8 6.4 copy-start.62
  182.8 6.4 copy-start.72
  189.2 6.9 copy-start.71
  207.9 9.2 %copy-start.23 = (f32[4,8,32768]{2,0,1:T(4,128)}, f32[4,8,32768]{2,0,1:T(4,128)S(1)}, u32[]{:S(2)}) copy-start(f32[4,8,32768]{2,0,1:T(4,128)S(1)} %constant_dynamic-update-slice_fusion.1) | copy-start | bytes 12582916
  208.8 16.9 %copy-start.74 = (f32[1,32768]{1,0:T(1,128)}, f32[1,32768]{1,0:T(1,128)S(1)}, u32[]{:S(2)}) copy-start(f32[1,32768]{1,0:T(1,128)S(1)} %get-tuple-element.448) | copy-start | bytes 393220
  210.2 6.9 copy-start.41
  210.2 6.9 copy-start.63
  210.2 6.9 copy-start.65
  223.9 4.9 copy-start.76
  224.8 4.0 copy-start.78
  226.7 61.2 %all-gather.25.cloned.1.call-start = ((), (), s32[]{:S(2)}) async-start(), calls=%async_computation.8 | async-start | bytes 2359296 | tf_op jit(solution)/shard_map/all_gather | solution.py:16
  231.5 86.6 %all-gather.23.cloned.1.call-start = ((), (), s32[]{:S(2)}) async-start(), calls=%async_computation.7 | async-start | bytes 2359296 | tf_op jit(solution)/shard_map/all_gather | solution.py:16
  235.5 5.2 copy-start.37
  235.5 5.2 copy-start.46
  235.6 112.7 %all-gather.27.cloned.1.call-start = ((), (), s32[]{:S(2)}) async-start(), calls=%async_computation.9 | async-start | bytes 2359296 | tf_op jit(solution)/shard_map/all_gather | solution.py:16
  240.7 155.7 %all-gather.17.cloned.1.call-start = ((), (), s32[]{:S(2)}) async-start(), calls=%async_computation.4 | async-start | bytes 4718592 | tf_op jit(solution)/shard_map/all_gather | solution.py:16
  241.7 3.9 copy-start.42
  241.7 3.9 copy-start.64
  241.7 3.9 copy-start.66
  243.7 200.1 %all-gather.19.cloned.1.call-start = ((), (), s32[]{:S(2)}) async-start(), calls=%async_computation.5 | async-start | bytes 4718592 | tf_op jit(solution)/shard_map/all_gather | solution.py:16
  248.5 7.2 copy-start.45
  444.2 33.7 %copy-start.75 = (f32[1,32768]{1,0:T(1,128)S(1)}, f32[1,32768]{1,0:T(1,128)}, u32[]{:S(2)}) copy-start(f32[1,32768]{1,0:T(1,128)} %copy-done.74) | copy-start | bytes 393220
  444.2 33.7 %copy-start.77 = (f32[1,32768]{1,0:T(1,128)S(1)}, f32[1,32768]{1,0:T(1,128)}, u32[]{:S(2)}) copy-start(f32[1,32768]{1,0:T(1,128)} %get-tuple-element.449) | copy-start | bytes 393220
  482.2 6.0 copy-start.31
  498.3 9.6 %copy-start.28 = (f32[1,8,32768]{2,1,0:T(8,128)S(1)}, f32[1,8,32768]{2,1,0:T(8,128)}, u32[]{:S(2)}) copy-start(f32[1,8,32768]{2,1,0:T(8,128)} %copy.230) | copy-start | bytes 3145732
  498.3 9.6 %copy-start.29 = (f32[1,8,32768]{2,1,0:T(8,128)S(1)}, f32[1,8,32768]{2,1,0:T(8,128)}, u32[]{:S(2)}) copy-start(f32[1,8,32768]{2,1,0:T(8,128)} %copy.229) | copy-start | bytes 3145732
  498.3 9.5 %copy-start.79 = (f32[2,32768]{1,0:T(2,128)S(1)}, f32[2,32768]{1,0:T(2,128)}, u32[]{:S(2)}) copy-start(f32[2,32768]{1,0:T(2,128)} %get-tuple-element.446) | copy-start | bytes 786436
  498.3 9.5 %copy-start.80 = (f32[2,32768]{1,0:T(2,128)S(1)}, f32[2,32768]{1,0:T(2,128)}, u32[]{:S(2)}) copy-start(f32[2,32768]{1,0:T(2,128)} %get-tuple-element.444) | copy-start | bytes 786436
  503.1 4.8 copy-start.22
  529.9 5.8 copy-start.18
  535.7 6.9 copy-start.7
  548.2 6.0 copy-start.13
  548.2 6.0 copy-start.15
  554.3 4.9 copy-start.8
  554.3 4.9 copy-start.10
  554.3 4.9 copy-start.20
  628.7 77.2 %all-to-all-start.3 = ((f32[4,1,131072]{2,1,0:T(1,128)}), f32[4,1,131072]{2,1,0:T(1,128)}, u32[]{:S(2)}, u32[]{:S(2)}) async-start(f32[4,1,131072]{2,1,0:T(1,128)} %reshape.1424), calls=%async_computation.3 | async-start | bytes 4194304 | tf_op jit(solution)/shard_map/all_to_all | solution.py:243
  705.9 62.6 %all-to-all-start.2 = ((f32[4,1,131072]{2,1,0:T(1,128)}), f32[4,1,131072]{2,1,0:T(1,128)}, u32[]{:S(2)}, u32[]{:S(2)}) async-start(f32[4,1,131072]{2,1,0:T(1,128)} %reshape.1422), calls=%async_computation.2 | async-start | bytes 4194304 | tf_op jit(solution)/shard_map/all_to_all | solution.py:242
  (29 other events, 80.3 us)
Sparse Core Ops, SparseCore 0:
  226.9 30.8 all-gather.20
  259.3 28.5 all-gather.24
  289.6 28.5 all-gather.22
  319.6 28.5 all-gather.26
  349.7 46.6 all-gather.16
  397.8 45.8 all-gather.18
where the time goes:
time: 843 us; the launch traced here: 833 us
  local copies, waits for them, and re-layouts  306 us (36%)
  waiting for transfers between devices  178 us (21%)
  matrix products  167 us (20%)
  other arithmetic  144 us (17%)
  starting transfers between devices  19.4 us (2%)
  between operations  18.2 us (2%)
    all_gather x6, waiting for transfers between devices, entering(): gathered = jax.tree.map(lambda a: lax.all_gather(a, axis), part)  178 us
    dot_general x32, matrix products, contract(): jnp.einsum(pattern, first_operand, second_operand, precision=highest, pre...  167 us
    unnamed x183, local copies, waits for them, and re-layouts  147 us
    mul x2, local copies, waits for them, and re-layouts, transform(): jnp.stack([final_real.reshape(final_shape), final_imag.reshape(final_shap...  34.3 us
    another operation x8, local copies, waits for them, and re-layouts, transform(): jnp.stack([final_real.reshape(final_shape), final_imag.reshape(final_shap...  23.5 us
    sub x2, other arithmetic, block_solve(): pivot = diagonal[level] - lower_part[level] * ratio  23.1 us
    unnamed x9, other arithmetic  22.5 us
    all_to_all x2, local copies, waits for them, and re-layouts, shards(): lax.all_to_all(pressure_back, 'wave', split_axis=3, concat_axis=2, tiled=...  20.7 us
  transfers between devices with their start and end apart: 10, of which 5 were waited for; matrix products, arithmetic and copies ran while one was open for 28% of the time, Pallas kernels for 0%

commit v1 on v0

v1 whole, which is shorter than its diff:
```python
import functools
import math

import jax
import jax.numpy as jnp
import numpy as np
from jax import lax
from jax.experimental import pallas as pl
from jax.experimental.pallas import tpu as pltpu
from jax.sharding import PartitionSpec as P

aspect_ratio = 1.0
LANES = 128
ROWS = 8
VMEM_BYTES = 24 * 1024 * 1024
real_dot = functools.partial(jnp.dot, preferred_element_type=jnp.float32)


def butterflies(values, orient):
    size = len(values)
    if size == 1:
        return values
    even = butterflies(values[0::2], orient)
    odd = butterflies(values[1::2], orient)
    low, high = [], []
    half = size // 2
    for at in range(half):
        (er, ei), (re, im) = even[at], odd[at]
        if at == 0:
            tr, ti = re, im
        elif 4 * at == size:
            tr, ti = (-im, re) if orient > 0 else (im, -re)
        elif 8 * at == size:
            root = math.sqrt(0.5)
            tr, ti = root * (re - orient * im), root * (im + orient * re)
        elif 8 * at == 3 * size:
            root = math.sqrt(0.5)
            tr, ti = -root * (re + orient * im), root * (orient * re - im)
        else:
            angle = orient * 2.0 * math.pi * at / size
            c, s = math.cos(angle), math.sin(angle)
            tr, ti = c * re - s * im, s * re + c * im
        low.append((er + tr, ei + ti))
        high.append((er - tr, ei - ti))
    return low + high


def tables(outer, orient):
    full = outer * LANES
    angle = orient * 2.0 * np.pi * np.outer(np.arange(outer), np.arange(LANES)) / full
    wide = lambda a: np.broadcast_to(a[:, None, :], (outer, ROWS, LANES)).astype(np.float32)
    turn = orient * 2.0 * np.pi * (np.outer(np.arange(LANES), np.arange(LANES)) % LANES) / LANES
    c, s = np.cos(turn), np.sin(turn)
    matrix = np.block([[c, s], [-s, c]]).astype(np.float32)
    top = matrix.astype(jnp.bfloat16)
    rest = (matrix - top.astype(np.float32)).astype(jnp.bfloat16)
    return wide(np.cos(angle)), wide(np.sin(angle)), top, rest


def lane_dft(values, top, rest):
    high = values.astype(jnp.bfloat16)
    low = (values - high.astype(jnp.float32)).astype(jnp.bfloat16)
    return real_dot(high, top) + (real_dot(low, top) + real_dot(high, rest))


def coefficient_kernel(levels, total, group, place, thick, face, lam, q_out, p_out, r_out, m_out, end_out, down_out, up_out, r_all, m_all, n_all, u_all, f_all):
    rows = group * ROWS
    shift = lam[...].reshape(rows, LANES)
    zero = jnp.zeros((rows, LANES), jnp.float32)

    def step(j, state):
        f, r, phi, s = state
        m = face[j] * r
        f = shift * thick[j] + jnp.where(j == 0, face[0], m * f)
        r = 1.0 / (face[j + 1] + f)
        m_all[j] = jnp.where(j == 0, 0.0, m)
        r_all[j] = r
        f_all[j] = f
        i = total - 1 - j
        n = face[i + 1] * s
        u = n * phi
        phi = shift * thick[i] + u
        s = 1.0 / (face[i] + phi)
        n_all[i] = n
        u_all[i] = u
        return f, r, phi, s

    lax.fori_loop(0, total, step, (zero, zero, zero, zero))
    first = place[0] * levels
    wide = (group, ROWS, LANES)
    q = jnp.ones((rows, LANES), jnp.float32)
    p = q
    for i in range(levels):
        back = levels - 1 - i
        q_out[back] = q.reshape(wide)
        q = q * m_all[first + back]
        p_out[i] = p.reshape(wide)
        p = p * n_all[first + i]
        r_out[i] = r_all[first + i].reshape(wide)
        m_out[i] = m_all[first + i].reshape(wide)
    last = first + levels - 1
    end_out[0] = n_all[last].reshape(wide)
    end_out[1] = (1.0 / (f_all[last] + u_all[last])).reshape(wide)
    for block in range(total // levels):
        down = m_all[block * levels]
        up = n_all[block * levels]
        for i in range(1, levels):
            down = down * m_all[block * levels + i]
            up = up * n_all[block * levels + i]
        down_out[block] = down.reshape(wide)
        up_out[block] = up.reshape(wide)


def coefficients(place, thick, face, lam, levels):
    outer = lam.shape[0]
    total = thick.shape[0]
    count = total // levels
    group = min(8, outer)
    tall = lambda n: pl.BlockSpec((n, group, ROWS, LANES), lambda g: (0, g, 0, 0))
    shape = lambda n: jax.ShapeDtypeStruct((n, outer, ROWS, LANES), jnp.float32)
    smem = pl.BlockSpec(memory_space=pltpu.SMEM)
    sizes = (levels, levels, levels, levels, 2, count, count)
    return pl.pallas_call(
        functools.partial(coefficient_kernel, levels, total, group),
        grid=(outer // group,),
        in_specs=[smem, smem, smem, pl.BlockSpec((group, ROWS, LANES), lambda g: (g, 0, 0))],
        out_specs=[tall(n) for n in sizes],
        out_shape=[shape(n) for n in sizes],
        scratch_shapes=[pltpu.VMEM((total, group * ROWS, LANES), jnp.float32)] * 5,
        compiler_params=pltpu.CompilerParams(vmem_limit_bytes=2 * VMEM_BYTES),
        name="coefficients",
    )(place, thick, face, lam)


def forward_kernel(scale, x, tw_cos, tw_sin, top, rest, q, p, b_out, c_out, lhs):
    at = pl.program_id(0)
    waves, _, _, _, local = x.shape
    per = local // LANES
    outer = waves * per

    def piece(part, s):
        return x[s // per, part, 0, :, (s % per) * LANES:(s % per + 1) * LANES]

    turned = butterflies([(piece(0, s), piece(1, s)) for s in range(outer)], -1.0)
    for k, (re, im) in enumerate(turned):
        c, s = tw_cos[k], tw_sin[k]
        lhs[k * ROWS:(k + 1) * ROWS, :LANES] = re * c - im * s
        lhs[k * ROWS:(k + 1) * ROWS, LANES:] = re * s + im * c
    y = lane_dft(lhs[...], top[...], rest[...]) * scale[at]

    @pl.when(at == 0)
    def _():
        c_out[...] = jnp.zeros_like(c_out)

    for part in range(2):
        b = y[:, part * LANES:(part + 1) * LANES].reshape(outer, ROWS, LANES)
        b_out[part, 0] = b
        c_out[:, 0, part] += q[0] * b
        c_out[:, 1, part] += p[0] * b


def forward(x, scale, q, p):
    waves, _, levels, _, local = x.shape
    outer = waves * local // LANES
    consts = tables(outer, -1.0)
    whole = lambda a: pl.BlockSpec(a.shape, lambda l: (0,) * a.ndim)
    level = pl.BlockSpec((1, outer, ROWS, LANES), lambda l: (l, 0, 0, 0))
    return pl.pallas_call(
        forward_kernel,
        grid=(levels,),
        in_specs=[
            pl.BlockSpec(memory_space=pltpu.SMEM),
            pl.BlockSpec((waves, 2, 1, ROWS, local), lambda l: (0, 0, l, 0, 0)),
            *[whole(a) for a in consts],
            level,
            level,
        ],
        out_specs=[
            pl.BlockSpec((2, 1, outer, ROWS, LANES), lambda l: (0, l, 0, 0, 0)),
            pl.BlockSpec((outer, 2, 2, ROWS, LANES), lambda l: (0, 0, 0, 0, 0)),
        ],
        out_shape=[
            jax.ShapeDtypeStruct((2, levels, outer, ROWS, LANES), jnp.float32),
            jax.ShapeDtypeStruct((outer, 2, 2, ROWS, LANES), jnp.float32),
        ],
        scratch_shapes=[pltpu.VMEM((outer * ROWS, 2 * LANES), jnp.float32)],
        compiler_params=pltpu.CompilerParams(vmem_limit_bytes=VMEM_BYTES),
        name="forward",
    )(scale, x, *consts, q, p)


def join_kernel(c, down, up, out):
    count = c.shape[0]
    y = jnp.zeros(c.shape[1:2] + c.shape[3:], jnp.float32)
    z = y
    for block in range(count):
        out[block, :, 0] = y
        y = c[block, :, 0] + down[block][:, None] * y
        back = count - 1 - block
        out[back, :, 1] = z
        z = c[back, :, 1] + up[back][:, None] * z


def join(c, down, up):
    return pl.pallas_call(
        join_kernel,
        out_shape=jax.ShapeDtypeStruct(c.shape, jnp.float32),
        compiler_params=pltpu.CompilerParams(vmem_limit_bytes=VMEM_BYTES),
        name="join",
    )(c, down, up)


def backward_kernel(scale, b, ends, r, m, end, tw_cos, tw_sin, top, rest, out, y_all, now):
    at = pl.program_id(0)
    waves, _, _, _, local = out.shape
    per = local // LANES
    levels, outer = r.shape[:2]
    rows = outer * ROWS

    @pl.when(at == 0)
    def _():
        for part in range(2):
            y = ends[:, 0, part]
            for j in range(levels):
                y = b[part, j] + m[j] * y
                y_all[part, j] = y
            now[part] = (y + end[0] * ends[:, 1, part]) * end[1]

    level = levels - 1 - at

    @pl.when(at > 0)
    def _():
        for part in range(2):
            now[part] = r[level] * y_all[part, level] + m[level + 1] * now[part]

    spectrum = jnp.concatenate([now[0].reshape(rows, LANES), now[1].reshape(rows, LANES)], 1)
    z = lane_dft(spectrum, top[...], rest[...]) * scale[level]
    pairs = []
    for k in range(outer):
        re = z[k * ROWS:(k + 1) * ROWS, :LANES]
        im = z[k * ROWS:(k + 1) * ROWS, LANES:]
        c, s = tw_cos[k], tw_sin[k]
        pairs.append((re * c - im * s, re * s + im * c))
    for s, pair in enumerate(butterflies(pairs, 1.0)):
        for part in range(2):
            out[s // per, part, 0, :, (s % per) * LANES:(s % per + 1) * LANES] = pair[part]


def backward(b, ends, r, m, end, scale, waves):
    _, levels, outer, _, _ = b.shape
    local = outer * LANES // waves
    consts = tables(outer, 1.0)
    whole = lambda a: pl.BlockSpec(a.shape, lambda l: (0,) * a.ndim)
    return pl.pallas_call(
        backward_kernel,
        grid=(levels,),
        in_specs=[pl.BlockSpec(memory_space=pltpu.SMEM)] + [whole(a) for a in (b, ends, r, m, end, *consts)],
        out_specs=pl.BlockSpec((waves, 2, 1, ROWS, local), lambda l: (0, 0, levels - 1 - l, 0, 0)),
        out_shape=jax.ShapeDtypeStruct((waves, 2, levels, ROWS, local), jnp.float32),
        scratch_shapes=[
            pltpu.VMEM((2, levels, outer, ROWS, LANES), jnp.float32),
            pltpu.VMEM((2, outer, ROWS, LANES), jnp.float32),
        ],
        compiler_params=pltpu.CompilerParams(vmem_limit_bytes=VMEM_BYTES),
        name="backward",
    )(scale, b, ends, r, m, end, *consts)


def swap(a, axis):
    return lax.all_to_all(a, axis, split_axis=0, concat_axis=0, tiled=True)


def shards(rhs, cotangent, thickness, ky_shift):
    waves = lax.axis_size("wave")
    count = lax.axis_size("depth")
    depth_pos = lax.axis_index("depth")
    wave_pos = lax.axis_index("wave")
    _, levels, ky, local = rhs.shape
    full = waves * local
    ky_local = ky // waves
    spare = -ky_local % ROWS

    def pack(a):
        a = a.reshape(2, levels, waves, ky_local, local)
        return a.transpose(2, 0, 1, 3, 4)

    def unpack(a):
        return a.transpose(1, 2, 0, 3, 4).reshape(2, levels, ky, local)

    def pad(a):
        return jnp.pad(a, [(0, 0)] * 3 + [(0, spare), (0, 0)]) if spare else a

    def trim(a):
        return a[:, :, :, :ky_local] if spare else a

    rhs_in = swap(pack(rhs), "wave")
    rhs_in, cotangent = lax.optimization_barrier((rhs_in, cotangent))
    cotangent_in = swap(pack(cotangent), "wave")

    inner_face = 2.0 / (thickness[:-1] + thickness[1:])
    face = jnp.concatenate([2.0 / thickness[:1], inner_face, jnp.zeros((1,), jnp.float32)])
    outer = full // LANES
    wavenumber = np.arange(outer)[:, None] + outer * np.arange(LANES)[None, :]
    wavenumber = jnp.asarray(wavenumber, jnp.float32)
    horizontal = aspect_ratio * 4.0 * jnp.sin(math.pi * wavenumber / full) ** 2
    shifts = lax.dynamic_slice_in_dim(ky_shift, wave_pos * ky_local, ky_local)
    shifts = jnp.pad(shifts, (0, spare), constant_values=1.0)
    lam = shifts[None, :, None] + horizontal[:, None, :]
    place = depth_pos.astype(jnp.int32).reshape(1)
    q, p, r, m, end, down, up = coefficients(place, thickness, face, lam, levels)
    share = outer // count
    down = lax.dynamic_slice_in_dim(down, depth_pos * share, share, 1)
    up = lax.dynamic_slice_in_dim(up, depth_pos * share, share, 1)
    thick_here = lax.dynamic_slice_in_dim(thickness, depth_pos * levels, levels)
    even = jnp.ones_like(thick_here)

    def solve(field, before, after):
        b, c = forward(pad(field), before, q, p)
        c = swap(c.reshape((count, share) + c.shape[1:]), "depth")
        ends = swap(join(c, down, up), "depth").reshape((outer, 2, 2, ROWS, LANES))
        return trim(backward(b, ends, r, m, end, after / full, waves))

    pressure = swap(solve(rhs_in, thick_here, even), "wave")
    adjoint = solve(cotangent_in, even, thick_here)
    pressure, adjoint = lax.optimization_barrier((pressure, adjoint))
    adjoint = swap(adjoint, "wave")
    return unpack(pressure), unpack(adjoint)


def solution(mesh):
    spec = P(None, "depth", None, "wave")
    return jax.shard_map(shards, mesh=mesh, in_specs=(spec, spec, P(), P()), out_specs=(spec, spec), check_vma=False)
```

time: 843 us -> 205 us (0.24); the launches traced: 833 us -> 204 us
  local copies, waits for them, and re-layouts: 306 us -> 40.4 us
  matrix products: 167 us -> 0 us
  other arithmetic: 144 us -> 0.31 us
  waiting for transfers between devices: 178 us -> 68.7 us
  Pallas kernels: 0 us -> 32.1 us
  blocking collectives: 0 us -> 30.6 us
  between operations: 18.2 us -> 1.01 us
  starting transfers between devices: 19.4 us -> 30.9 us
    all_gather x6 -> x0, waiting for transfers between devices: 178 us -> none  [entering(): gathered = jax.tree.map(lambda a: lax.all_gather(a, axis), part)]
    dot_general x32 -> x0, matrix products: 167 us -> none  [contract(): jnp.einsum(pattern, first_operand, second_operand, precision=highest, pre...]
    unnamed x183 -> x76, local copies, waits for them, and re-layouts: 147 us -> 31.4 us
    all_to_all x4 -> x7, waiting for transfers between devices: 0.01 us -> 68.7 us  [swap(): return lax.all_to_all(a, axis, split_axis=0, concat_axis=0, tiled=True)]
    all_to_all x5 -> x0, local copies, waits for them, and re-layouts: 45.1 us -> none  [the longest x2 20.7 us: shards(): lax.all_to_all(pressure_back, 'wave', split_axis=3, concat_axis=2, tiled=...]
    sub x14 -> x0, other arithmetic: 43.5 us -> none  [the longest x2 23.1 us: block_solve(): pivot = diagonal[level] - lower_part[level] * ratio]
    another operation x20 -> x2, local copies, waits for them, and re-layouts: 43.3 us -> 0.01 us  [the longest x8 23.5 us: transform(): jnp.stack([final_real.reshape(final_shape), final_imag.reshape(final_shap...]
    mul x9 -> x0, local copies, waits for them, and re-layouts: 41.2 us -> none  [the longest x2 34.3 us: transform(): jnp.stack([final_real.reshape(final_shape), final_imag.reshape(final_shap...]
  transfers between devices with their start and end apart: 10 -> 7, of which waited for: 5 -> 6; matrix products, arithmetic and copies ran while one was open for 28% -> 2% of each run, Pallas kernels for 0% -> 16%
where the time goes in v1:
time: 205 us; the launch traced here: 204 us
  waiting for transfers between devices  68.7 us (34%)
  local copies, waits for them, and re-layouts  40.4 us (20%)
  Pallas kernels  32.1 us (16%)
  starting transfers between devices  30.9 us (15%)
  blocking collectives  30.6 us (15%)
    all_to_all x7, waiting for transfers between devices, swap(): return lax.all_to_all(a, axis, split_axis=0, concat_axis=0, tiled=True)  68.7 us
    unnamed x76, local copies, waits for them, and re-layouts  31.4 us
    all_to_all x7, starting transfers between devices, swap(): return lax.all_to_all(a, axis, split_axis=0, concat_axis=0, tiled=True)  30.9 us
    all_to_all x1, blocking collectives, swap(): return lax.all_to_all(a, axis, split_axis=0, concat_axis=0, tiled=True)  30.6 us
    pallas_call x2, Pallas kernels, forward(): pl.pallas_call(forward_kernel, grid=(levels,), in_specs=[pl.BlockSpec(mem...  10.6 us
    pallas_call x1, Pallas kernels, coefficients(): pl.pallas_call(functools.partial(coefficient_kernel, levels, total, group...  9.88 us
    pallas_call x2, Pallas kernels, backward(): pl.pallas_call(backward_kernel, grid=(levels,), in_specs=[pl.BlockSpec(me...  9.36 us
    reshape x2, local copies, waits for them, and re-layouts, unpack(): return a.transpose(1, 2, 0, 3, 4).reshape(2, levels, ky, local)  6.32 us
  transfers between devices with their start and end apart: 7, of which 6 were waited for; matrix products, arithmetic and copies ran while one was open for 2% of the time, Pallas kernels for 16%

profile of v1, /device:TPU:0, one launch (start us, length us, event | category | flops | bytes accessed | tf_op | source)
XLA Modules:
  0.0 203.9 jit_solution(165329212256951021)
XLA Ops:
  0.6 0.0 copy-start
  0.6 1.6 copy-done
  2.2 0.1 copy_bitcast_fusion.3
  2.4 0.0 copy-start.35
  2.4 30.6 %all_to_all.40.x = f32[4,2,8,8,1024]{4,3,2,1,0:T(8,128)} all-to-all(f32[4,2,8,8,1024]{4,3,2,1,0:T(8,128)S(1)} %copy_bitcast_fusion.3), channel_id=1, replica_groups=mesh['depth'=8,'wave'=4] {'wave'}, dimensions={0} | all-to-all | bytes 4194304 | tf_op jit(solution)/shard_map/all_to_all | solution.py:270
  33.0 1.5 copy_bitcast_fusion.2
  34.4 0.0 copy-start.27
  34.4 0.0 copy-start.28
  34.4 4.6 %all-to-all-start.4 = ((f32[4,2,8,8,1024]{4,3,2,1,0:T(8,128)}), f32[4,2,8,8,1024]{4,3,2,1,0:T(8,128)}, u32[]{:S(2)}, u32[]{:S(2)}) async-start(f32[4,2,8,8,1024]{4,3,2,1,0:T(8,128)} %copy_bitcast_fusion.2), calls=%async_computation.4 | async-start | bytes 4194304 | tf_op jit(solution)/shard_map/all_to_all | solution.py:270
  39.2 0.1 dynamic_slice.13
  39.2 0.1 add_divide_fusion
  39.3 0.1 pad_maximum_fusion.face
  39.4 0.1 broadcast_add_fusion.lam
  39.5 9.9 %coefficients.1 = (f32[8,32,8,128]{3,2,1,0:T(8,128)S(1)}, f32[8,32,8,128]{3,2,1,0:T(8,128)S(1)}, f32[8,32,8,128]{3,2,1,0:T(8,128)S(1)}, f32[8,32,8,128]{3,2,1,0:...) custom-call(s32[1]{0:T(128)} %bitcast.2.place, ...), custom_call_target="tpu_custom_call" | custom-call | tf_op jit(solution)/shard_map/coefficients/pallas_call | solution.py:123
  49.4 1.0 copy-done.6
  50.4 1.0 copy-done.8
  51.3 0.7 copy-done.18
  52.1 1.1 copy-done.33
  53.1 0.1 broadcast_multiply_fusion
  53.2 1.6 copy-done.1
  54.8 0.9 copy-done.29
  55.7 4.4 %forward.2 = (f32[2,8,32,8,128]{4,3,2,1,0:T(8,128)S(1)}, f32[32,2,2,8,128]{4,3,2,1,0:T(8,128)S(1)}) custom-call(f32[8]{0:T(128)S(1)} %get-tuple-element.33.scale, f32[4,2,8,8,1024]{4,3,2,1,0:T(8,128)S(1)} %copy-done.1, f32[32,8,128]{2,1,0:T(8,128)S(1)} %copy-done.11, f32[32,8,128]{2,1,0:T(8,128)S(1)} %copy-done.27, bf16[256,256]{1,0:T(8,128)(2,1)S(1)} %copy-done.28, ...), custom_call_target="tpu_custom_call" | custom-call | tf_op jit(solution)/shard_map/forward/pallas_call | solution.py:168
  60.1 1.0 copy-done.4
  61.1 1.3 copy-done.16
  62.4 0.8 copy-done.32
  63.2 4.9 %all-to-all-start.1 = ((f32[8,4,2,2,8,128]{5,4,3,2,1,0:T(8,128)}), f32[8,4,2,2,8,128]{5,4,3,2,1,0:T(8,128)}, u32[]{:S(2)}, u32[]{:S(2)}) async-start(f32[8,4,2,2,8,128]{5,4,3,2,1,0:T(8,128)} %bitcast.27), calls=%async_computation.1 | async-start | bytes 1048576 | tf_op jit(solution)/shard_map/all_to_all | solution.py:270
  68.1 1.2 copy-done.5
  69.3 0.9 copy-done.30
  70.2 6.2 %forward.3 = (f32[2,8,32,8,128]{4,3,2,1,0:T(8,128)S(1)}, f32[32,2,2,8,128]{4,3,2,1,0:T(8,128)S(1)}) custom-call(f32[8]{0:T(128)S(1)} %broadcast_5_scale.2.scale, f32[4,2,8,8,1024]{4,3,2,1,0:T(8,128)} %all-to-all-done.4.x, f32[32,8,128]{2,1,0:T(8,128)S(1)} %copy-done.11, f32[32,8,128]{2,1,0:T(8,128)S(1)} %copy-done.27, bf16[256,256]{1,0:T(8,128)(2,1)S(1)} %copy-done.28, ...), custom_call_target="tpu_custom_call" | custom-call | tf_op jit(solution)/shard_map/forward/pallas_call | solution.py:168
  76.4 1.3 copy-done.14
  77.7 0.8 copy-done.31
  78.5 5.0 %all-to-all-done.1.c = f32[8,4,2,2,8,128]{5,4,3,2,1,0:T(8,128)} async-done(((f32[8,4,2,2,8,128]{5,4,3,2,1,0:T(8,128)}), f32[8,4,2,2,8,128]{5,4,3,2,1,0:T(8,128)}, u32[]{:S(2)}, u32[]{:S(2)}) %all-to-all-start.1) | async-done | bytes 524320 | tf_op jit(solution)/shard_map/all_to_all | solution.py:270
  83.5 4.1 %all-to-all-start.5 = ((f32[8,4,2,2,8,128]{5,4,3,2,1,0:T(8,128)}), f32[8,4,2,2,8,128]{5,4,3,2,1,0:T(8,128)}, u32[]{:S(2)}, u32[]{:S(2)}) async-start(f32[8,4,2,2,8,128]{5,4,3,2,1,0:T(8,128)} %bitcast.26), calls=%async_computation.5 | async-start | bytes 1048576 | tf_op jit(solution)/shard_map/all_to_all | solution.py:270
  87.7 1.0 constant_dynamic-slice_fusion
  88.7 1.2 join.2
  89.9 0.8 copy-done.13
  90.7 12.4 %all-to-all-done.5.c = f32[8,4,2,2,8,128]{5,4,3,2,1,0:T(8,128)} async-done(((f32[8,4,2,2,8,128]{5,4,3,2,1,0:T(8,128)}), f32[8,4,2,2,8,128]{5,4,3,2,1,0:T(8,128)}, u32[]{:S(2)}, u32[]{:S(2)}) %all-to-all-start.5) | async-done | bytes 524320 | tf_op jit(solution)/shard_map/all_to_all | solution.py:270
  103.0 4.2 %all-to-all-start.2 = ((f32[8,4,2,2,8,128]{5,4,3,2,1,0:T(8,128)}), f32[8,4,2,2,8,128]{5,4,3,2,1,0:T(8,128)}, u32[]{:S(2)}, u32[]{:S(2)}) async-start(f32[8,4,2,2,8,128]{5,4,3,2,1,0:T(8,128)} %copy-done.13), calls=%async_computation.2 | async-start | bytes 1048576 | tf_op jit(solution)/shard_map/all_to_all | solution.py:270
  107.2 1.1 join.3
  108.3 0.8 copy-done.12
  109.1 13.5 %all-to-all-done.2 = f32[8,4,2,2,8,128]{5,4,3,2,1,0:T(8,128)} async-done(((f32[8,4,2,2,8,128]{5,4,3,2,1,0:T(8,128)}), f32[8,4,2,2,8,128]{5,4,3,2,1,0:T(8,128)}, u32[]{:S(2)}, u32[]{:S(2)}) %all-to-all-start.2) | async-done | bytes 524320 | tf_op jit(solution)/shard_map/all_to_all | solution.py:270
  122.6 4.2 %all-to-all-start.6 = ((f32[8,4,2,2,8,128]{5,4,3,2,1,0:T(8,128)}), f32[8,4,2,2,8,128]{5,4,3,2,1,0:T(8,128)}, u32[]{:S(2)}, u32[]{:S(2)}) async-start(f32[8,4,2,2,8,128]{5,4,3,2,1,0:T(8,128)} %copy-done.12), calls=%async_computation.6 | async-start | bytes 1048576 | tf_op jit(solution)/shard_map/all_to_all | solution.py:270
  126.8 1.2 copy-done.9
  128.0 1.6 copy-done.17
  129.6 0.9 copy-done.19
  130.5 0.9 copy-done.21
  131.4 0.9 copy-done.23
  132.3 0.9 copy-done.25
  133.2 4.7 %backward.2 = f32[4,2,8,8,1024]{4,3,2,1,0:T(8,128)S(1)} custom-call(f32[8]{0:T(128)S(1)} %broadcast_4_scale.2.scale, f32[2,8,32,8,128]{4,3,2,1,0:T(8,128)S(1)} %copy-done.17, f32[32,2,2,8,128]{4,3,2,1,0:T(8,128)} %bitcast.4.ends, f32[8,32,8,128]{3,2,1,0:T(8,128)S(1)} %copy-done.7, f32[8,32,8,128]{3,2,1,0:T(8,128)S(1)} %copy-done.9, ...), custom_call_target="tpu_custom_call" | custom-call | tf_op jit(solution)/shard_map/backward/pallas_call | solution.py:254
  137.9 1.3 copy-done.2
  139.2 2.8 %all-to-all-done.6 = f32[8,4,2,2,8,128]{5,4,3,2,1,0:T(8,128)} async-done(((f32[8,4,2,2,8,128]{5,4,3,2,1,0:T(8,128)}), f32[8,4,2,2,8,128]{5,4,3,2,1,0:T(8,128)}, u32[]{:S(2)}, u32[]{:S(2)}) %all-to-all-start.6) | async-done | bytes 524320 | tf_op jit(solution)/shard_map/all_to_all | solution.py:270
  142.1 4.5 %all-to-all-start.3 = ((f32[4,2,8,8,1024]{4,3,2,1,0:T(8,128)}), f32[4,2,8,8,1024]{4,3,2,1,0:T(8,128)}, u32[]{:S(2)}, u32[]{:S(2)}) async-start(f32[4,2,8,8,1024]{4,3,2,1,0:T(8,128)} %copy-done.2), calls=%async_computation.3 | async-start | bytes 4194304 | tf_op jit(solution)/shard_map/all_to_all | solution.py:270
  146.6 1.2 copy-done.10
  147.8 1.6 copy-done.15
  149.4 0.9 copy-done.22
  150.3 0.9 copy-done.24
  151.2 0.9 copy-done.26
  152.1 4.7 %backward.3 = f32[4,2,8,8,1024]{4,3,2,1,0:T(8,128)S(1)} custom-call(f32[8]{0:T(128)S(1)} %get-tuple-element.32.scale, f32[2,8,32,8,128]{4,3,2,1,0:T(8,128)S(1)} %copy-done.15, f32[32,2,2,8,128]{4,3,2,1,0:T(8,128)} %bitcast.8.ends, f32[8,32,8,128]{3,2,1,0:T(8,128)S(1)} %copy-done.7, f32[8,32,8,128]{3,2,1,0:T(8,128)S(1)} %copy-done.10, ...), custom_call_target="tpu_custom_call" | custom-call | tf_op jit(solution)/shard_map/backward/pallas_call | solution.py:254
  156.8 1.4 copy-done.3
  158.2 13.6 %all-to-all-done.3 = f32[4,2,8,8,1024]{4,3,2,1,0:T(8,128)} async-done(((f32[4,2,8,8,1024]{4,3,2,1,0:T(8,128)}), f32[4,2,8,8,1024]{4,3,2,1,0:T(8,128)}, u32[]{:S(2)}, u32[]{:S(2)}) %all-to-all-start.3) | async-done | bytes 2097184 | tf_op jit(solution)/shard_map/all_to_all | solution.py:270
  171.8 4.4 %all-to-all-start.7 = ((f32[4,2,8,8,1024]{4,3,2,1,0:T(8,128)}), f32[4,2,8,8,1024]{4,3,2,1,0:T(8,128)}, u32[]{:S(2)}, u32[]{:S(2)}) async-start(f32[4,2,8,8,1024]{4,3,2,1,0:T(8,128)} %copy-done.3), calls=%async_computation.7 | async-start | bytes 4194304 | tf_op jit(solution)/shard_map/all_to_all | solution.py:270
  176.2 3.2 %copy_bitcast_fusion.1 = f32[2,8,32,1024]{3,2,1,0:T(8,128)} fusion(f32[4,2,8,8,1024]{4,3,2,1,0:T(8,128)} %all-to-all-done.3), kind=kLoop, calls=%fused_computation.1 | loop fusion | bytes 4194304 | tf_op jit(solution)/shard_map/reshape | solution.py:288
  179.4 21.3 %all-to-all-done.7 = f32[4,2,8,8,1024]{4,3,2,1,0:T(8,128)} async-done(((f32[4,2,8,8,1024]{4,3,2,1,0:T(8,128)}), f32[4,2,8,8,1024]{4,3,2,1,0:T(8,128)}, u32[]{:S(2)}, u32[]{:S(2)}) %all-to-all-start.7) | async-done | bytes 2097184 | tf_op jit(solution)/shard_map/all_to_all | solution.py:270
  200.7 3.2 %copy_bitcast_fusion = f32[2,8,32,1024]{3,2,1,0:T(8,128)} fusion(f32[4,2,8,8,1024]{4,3,2,1,0:T(8,128)} %all-to-all-done.7), kind=kLoop, calls=%fused_computation | loop fusion | bytes 4194304 | tf_op jit(solution)/shard_map/reshape | solution.py:288
  (46 shorter events, 0.1 us)
Async XLA Ops:
  0.6 1.6 copy-start
  2.4 30.6 %copy-start.35 = (f32[2,8,32,1024]{3,2,1,0:T(8,128)S(1)}, f32[2,8,32,1024]{3,2,1,0:T(8,128)}, u32[]{:S(2)}) copy-start(f32[2,8,32,1024]{3,2,1,0:T(8,128)} %param.22) | copy-start | bytes 6291460
  34.4 4.7 %copy-start.34 = (f32[64]{0:T(128)S(1)}, f32[64]{0:T(128)}, u32[]{:S(2)}) copy-start(f32[64]{0:T(128)} %thick.1) | copy-start | bytes 772
  34.4 4.7 %copy-start.37 = (f32[32]{0:T(128)S(1)}, f32[32]{0:T(128)}, u32[]{:S(2)}) copy-start(f32[32]{0:T(128)} %param.24) | copy-start | bytes 388
  34.4 5.0 %copy-start.36 = (f32[32,128]{1,0:T(8,128)S(1)}, f32[32,128]{1,0:T(8,128)}, u32[]{:S(2)}) copy-start(f32[32,128]{1,0:T(8,128)} %constant.66) | copy-start | bytes 49156
  34.4 18.8 %copy-start.11 = (f32[32,8,128]{2,1,0:T(8,128)S(1)}, f32[32,8,128]{2,1,0:T(8,128)}, u32[]{:S(2)}) copy-start(f32[32,8,128]{2,1,0:T(8,128)} %constant.56.clone.tw_cos) | copy-start | bytes 393220
  34.4 18.8 %copy-start.27 = (f32[32,8,128]{2,1,0:T(8,128)S(1)}, f32[32,8,128]{2,1,0:T(8,128)}, u32[]{:S(2)}) copy-start(f32[32,8,128]{2,1,0:T(8,128)} %constant.57.clone.tw_sin) | copy-start | bytes 393220
  34.4 18.8 %copy-start.28 = (bf16[256,256]{1,0:T(8,128)(2,1)S(1)}, bf16[256,256]{1,0:T(8,128)(2,1)}, u32[]{:S(2)}) copy-start(bf16[256,256]{1,0:T(8,128)(2,1)} %constant.58.clone.top) | copy-start | bytes 393220
  34.4 28.7 %all-to-all-start.4 = ((f32[4,2,8,8,1024]{4,3,2,1,0:T(8,128)}), f32[4,2,8,8,1024]{4,3,2,1,0:T(8,128)}, u32[]{:S(2)}, u32[]{:S(2)}) async-start(f32[4,2,8,8,1024]{4,3,2,1,0:T(8,128)} %copy_bitcast_fusion.2), calls=%async_computation.4 | async-start | bytes 4194304 | tf_op jit(solution)/shard_map/all_to_all | solution.py:270
  49.4 1.0 copy-start.6
  50.3 1.0 copy-start.8
  51.3 0.7 copy-start.18
  52.1 1.1 copy-start.33
  53.2 1.6 copy-start.1
  54.8 0.9 copy-start.29
  60.1 1.0 copy-start.4
  61.1 1.3 copy-start.16
  62.4 0.8 copy-start.32
  63.2 20.3 %all-to-all-start.1 = ((f32[8,4,2,2,8,128]{5,4,3,2,1,0:T(8,128)}), f32[8,4,2,2,8,128]{5,4,3,2,1,0:T(8,128)}, u32[]{:S(2)}, u32[]{:S(2)}) async-start(f32[8,4,2,2,8,128]{5,4,3,2,1,0:T(8,128)} %bitcast.27), calls=%async_computation.1 | async-start | bytes 1048576 | tf_op jit(solution)/shard_map/all_to_all | solution.py:270
  68.1 1.2 copy-start.5
  69.3 0.9 copy-start.30
  76.4 1.3 copy-start.14
  77.7 0.8 copy-start.31
  83.5 19.5 %all-to-all-start.5 = ((f32[8,4,2,2,8,128]{5,4,3,2,1,0:T(8,128)}), f32[8,4,2,2,8,128]{5,4,3,2,1,0:T(8,128)}, u32[]{:S(2)}, u32[]{:S(2)}) async-start(f32[8,4,2,2,8,128]{5,4,3,2,1,0:T(8,128)} %bitcast.26), calls=%async_computation.5 | async-start | bytes 1048576 | tf_op jit(solution)/shard_map/all_to_all | solution.py:270
  88.7 38.1 %copy-start.7 = (f32[8,32,8,128]{3,2,1,0:T(8,128)S(1)}, f32[8,32,8,128]{3,2,1,0:T(8,128)}, u32[]{:S(2)}) copy-start(f32[8,32,8,128]{3,2,1,0:T(8,128)} %copy-done.6) | copy-start | bytes 3145732
  89.9 0.8 copy-start.13
  103.0 19.5 %all-to-all-start.2 = ((f32[8,4,2,2,8,128]{5,4,3,2,1,0:T(8,128)}), f32[8,4,2,2,8,128]{5,4,3,2,1,0:T(8,128)}, u32[]{:S(2)}, u32[]{:S(2)}) async-start(f32[8,4,2,2,8,128]{5,4,3,2,1,0:T(8,128)} %copy-done.13), calls=%async_computation.2 | async-start | bytes 1048576 | tf_op jit(solution)/shard_map/all_to_all | solution.py:270
  108.3 0.8 copy-start.12
  122.6 19.5 %all-to-all-start.6 = ((f32[8,4,2,2,8,128]{5,4,3,2,1,0:T(8,128)}), f32[8,4,2,2,8,128]{5,4,3,2,1,0:T(8,128)}, u32[]{:S(2)}, u32[]{:S(2)}) async-start(f32[8,4,2,2,8,128]{5,4,3,2,1,0:T(8,128)} %copy-done.12), calls=%async_computation.6 | async-start | bytes 1048576 | tf_op jit(solution)/shard_map/all_to_all | solution.py:270
  126.8 1.2 copy-start.9
  128.0 1.6 copy-start.17
  129.6 0.9 copy-start.19
  130.5 0.9 copy-start.21
  131.4 0.9 copy-start.23
  132.3 0.9 copy-start.25
  137.9 1.3 copy-start.2
  139.2 7.3 %copy-start.20 = (f32[2,32,8,128]{3,2,1,0:T(8,128)S(1)}, f32[2,32,8,128]{3,2,1,0:T(8,128)}, u32[]{:S(2)}) copy-start(f32[2,32,8,128]{3,2,1,0:T(8,128)} %copy-done.18) | copy-start | bytes 786436
  142.1 29.7 %all-to-all-start.3 = ((f32[4,2,8,8,1024]{4,3,2,1,0:T(8,128)}), f32[4,2,8,8,1024]{4,3,2,1,0:T(8,128)}, u32[]{:S(2)}, u32[]{:S(2)}) async-start(f32[4,2,8,8,1024]{4,3,2,1,0:T(8,128)} %copy-done.2), calls=%async_computation.3 | async-start | bytes 4194304 | tf_op jit(solution)/shard_map/all_to_all | solution.py:270
  146.6 1.2 copy-start.10
  147.8 1.6 copy-start.15
  149.4 0.9 copy-start.22
  150.3 0.9 copy-start.24
  151.2 0.9 copy-start.26
  156.8 1.4 copy-start.3
  171.8 29.0 %all-to-all-start.7 = ((f32[4,2,8,8,1024]{4,3,2,1,0:T(8,128)}), f32[4,2,8,8,1024]{4,3,2,1,0:T(8,128)}, u32[]{:S(2)}, u32[]{:S(2)}) async-start(f32[4,2,8,8,1024]{4,3,2,1,0:T(8,128)} %copy-done.3), calls=%async_computation.7 | async-start | bytes 4194304 | tf_op jit(solution)/shard_map/all_to_all | solution.py:270

commit v2 on v1

v2 whole, which is shorter than its diff:
```python
import functools
import math

import jax
import jax.numpy as jnp
import numpy as np
from jax import lax
from jax.experimental import pallas as pl
from jax.experimental.pallas import tpu as pltpu
from jax.sharding import PartitionSpec as P

aspect_ratio = 1.0
LANES = 128
ROWS = 8
VMEM_BYTES = 56 * 1024 * 1024
real_dot = functools.partial(jnp.dot, preferred_element_type=jnp.float32)


def butterflies(values, orient):
    size = len(values)
    if size == 1:
        return values
    even = butterflies(values[0::2], orient)
    odd = butterflies(values[1::2], orient)
    low, high = [], []
    half = size // 2
    for at in range(half):
        (er, ei), (re, im) = even[at], odd[at]
        if at == 0:
            tr, ti = re, im
        elif 4 * at == size:
            tr, ti = (-im, re) if orient > 0 else (im, -re)
        elif 8 * at == size:
            root = math.sqrt(0.5)
            tr, ti = root * (re - orient * im), root * (im + orient * re)
        elif 8 * at == 3 * size:
            root = math.sqrt(0.5)
            tr, ti = -root * (re + orient * im), root * (orient * re - im)
        else:
            angle = orient * 2.0 * math.pi * at / size
            c, s = math.cos(angle), math.sin(angle)
            tr, ti = c * re - s * im, s * re + c * im
        low.append((er + tr, ei + ti))
        high.append((er - tr, ei - ti))
    return low + high


def tables(outer, orient):
    full = outer * LANES
    angle = orient * 2.0 * np.pi * np.outer(np.arange(outer), np.arange(LANES)) / full
    wide = lambda a: np.broadcast_to(a[:, None, :], (outer, ROWS, LANES)).astype(np.float32)
    turn = orient * 2.0 * np.pi * (np.outer(np.arange(LANES), np.arange(LANES)) % LANES) / LANES
    c, s = np.cos(turn), np.sin(turn)
    matrix = np.block([[c, s], [-s, c]]).astype(np.float32)
    top = matrix.astype(jnp.bfloat16)
    rest = (matrix - top.astype(np.float32)).astype(jnp.bfloat16)
    return wide(np.cos(angle)), wide(np.sin(angle)), top, rest


def lane_dft(values, top, rest):
    high = values.astype(jnp.bfloat16)
    low = (values - high.astype(jnp.float32)).astype(jnp.bfloat16)
    return real_dot(high, top) + (real_dot(low, top) + real_dot(high, rest))


def coefficient_kernel(levels, total, group, place, thick, face, lam, q_out, p_out, r_out, m_out, end_out, pair_out, far_out, r_all, m_all, n_all, u_all, f_all, down_all, up_all):
    rows = group * ROWS
    shift = lam[...].reshape(rows, LANES)
    zero = jnp.zeros((rows, LANES), jnp.float32)

    def step(j, state):
        f, r, phi, s = state
        m = face[j] * r
        f = shift * thick[j] + jnp.where(j == 0, face[0], m * f)
        r = 1.0 / (face[j + 1] + f)
        m_all[j] = jnp.where(j == 0, 0.0, m)
        r_all[j] = r
        f_all[j] = f
        i = total - 1 - j
        n = face[i + 1] * s
        u = n * phi
        phi = shift * thick[i] + u
        s = 1.0 / (face[i] + phi)
        n_all[i] = n
        u_all[i] = u
        return f, r, phi, s

    lax.fori_loop(0, total, step, (zero, zero, zero, zero))
    first = place[0] * levels
    wide = (group, ROWS, LANES)
    q = jnp.ones((rows, LANES), jnp.float32)
    p = q
    for i in range(levels):
        back = levels - 1 - i
        q_out[back] = q.reshape(wide)
        q = q * m_all[first + back]
        p_out[i] = p.reshape(wide)
        p = p * n_all[first + i]
        r_out[i] = r_all[first + i].reshape(wide)
        m_out[i] = m_all[first + i].reshape(wide)
    last = first + levels - 1
    end_out[0] = n_all[last].reshape(wide)
    end_out[1] = (1.0 / (f_all[last] + u_all[last])).reshape(wide)

    blocks = total // levels
    for block in range(blocks):
        down = m_all[block * levels]
        up = n_all[block * levels]
        for i in range(1, levels):
            down = down * m_all[block * levels + i]
            up = up * n_all[block * levels + i]
        down_all[block] = down
        up_all[block] = up

    chips = blocks // 2
    chip = place[0] // 2
    for core in range(2):
        pair_out[core] = down_all[2 * chip + core].reshape(wide)
        pair_out[2 + core] = up_all[2 * chip + core].reshape(wide)
    above, below = [jnp.ones((rows, LANES), jnp.float32)], [jnp.ones((rows, LANES), jnp.float32)]
    for apart in range(1, chips - 1):
        one = jnp.maximum(chip - apart, 0)
        above.append(above[-1] * down_all[2 * one] * down_all[2 * one + 1])
        one = jnp.minimum(chip + apart, chips - 1)
        below.append(below[-1] * up_all[2 * one] * up_all[2 * one + 1])
    for apart in range(1, chips):
        far_out[apart - 1] = jnp.where(chip >= apart, above[apart - 1], below[chips - apart - 1]).reshape(wide)


def coefficients(place, thick, face, lam, levels):
    outer = lam.shape[0]
    total = thick.shape[0]
    count = total // levels
    group = min(8, outer)
    tall = lambda n: pl.BlockSpec((n, group, ROWS, LANES), lambda g: (0, g, 0, 0))
    shape = lambda n: jax.ShapeDtypeStruct((n, outer, ROWS, LANES), jnp.float32)
    smem = pl.BlockSpec(memory_space=pltpu.SMEM)
    sizes = (levels, levels, levels, levels, 2, 4, count // 2 - 1)
    return pl.pallas_call(
        functools.partial(coefficient_kernel, levels, total, group),
        grid=(outer // group,),
        in_specs=[smem, smem, smem, pl.BlockSpec((group, ROWS, LANES), lambda g: (g, 0, 0))],
        out_specs=[tall(n) for n in sizes],
        out_shape=[shape(n) for n in sizes],
        scratch_shapes=[pltpu.VMEM((total, group * ROWS, LANES), jnp.float32)] * 5
        + [pltpu.VMEM((count, group * ROWS, LANES), jnp.float32)] * 2,
        compiler_params=pltpu.CompilerParams(vmem_limit_bytes=VMEM_BYTES),
        name="coefficients",
    )(place, thick, face, lam)


def forward_kernel(waves, place, scale, *refs):
    at = pl.program_id(0)
    blocks = refs[:waves]
    tw_cos, tw_sin, top, rest, q, p, b_out, keep_out, give_out, x, lhs, c_all = refs[waves:]
    local = x.shape[-1]
    per = local // LANES
    outer = waves * per
    half = outer // 2
    for s in range(waves):
        x[place[1] ^ s] = blocks[s][:, 0]

    def piece(part, s):
        return x[s // per, part, :, (s % per) * LANES:(s % per + 1) * LANES]

    turned = butterflies([(piece(0, s), piece(1, s)) for s in range(outer)], -1.0)
    for k, (re, im) in enumerate(turned):
        c, s = tw_cos[k], tw_sin[k]
        lhs[k * ROWS:(k + 1) * ROWS, :LANES] = re * c - im * s
        lhs[k * ROWS:(k + 1) * ROWS, LANES:] = re * s + im * c
    y = lane_dft(lhs[...], top[...], rest[...]) * scale[at]

    @pl.when(at == 0)
    def _():
        c_all[...] = jnp.zeros_like(c_all)

    for part in range(2):
        b = y[:, part * LANES:(part + 1) * LANES].reshape(outer, ROWS, LANES)
        b_out[part, 0] = b
        c_all[:, 0, part] += q[0] * b
        c_all[:, 1, part] += p[0] * b

    @pl.when(at == pl.num_programs(0) - 1)
    def _():
        core = place[0] % 2
        keep_out[...] = c_all[pl.ds(core * half, half)]
        give_out[...] = c_all[pl.ds((1 - core) * half, half)]


def forward(place, blocks, scale, q, p):
    waves = len(blocks)
    _, levels, _, local = blocks[0].shape
    outer = waves * local // LANES
    consts = tables(outer, -1.0)
    whole = lambda a: pl.BlockSpec(a.shape, lambda l: (0,) * a.ndim)
    level = pl.BlockSpec((1, outer, ROWS, LANES), lambda l: (l, 0, 0, 0))
    smem = pl.BlockSpec(memory_space=pltpu.SMEM)
    half = (outer // 2, 2, 2, ROWS, LANES)
    return pl.pallas_call(
        functools.partial(forward_kernel, waves),
        grid=(levels,),
        in_specs=[
            smem,
            smem,
            *[pl.BlockSpec((2, 1, ROWS, local), lambda l: (0, l, 0, 0))] * waves,
            *[whole(a) for a in consts],
            level,
            level,
        ],
        out_specs=[
            pl.BlockSpec((2, 1, outer, ROWS, LANES), lambda l: (0, l, 0, 0, 0)),
            *[pl.BlockSpec(half, lambda l: (0, 0, 0, 0, 0))] * 2,
        ],
        out_shape=[
            jax.ShapeDtypeStruct((2, levels, outer, ROWS, LANES), jnp.float32),
            *[jax.ShapeDtypeStruct(half, jnp.float32)] * 2,
        ],
        scratch_shapes=[
            pltpu.VMEM((waves, 2, ROWS, local), jnp.float32),
            pltpu.VMEM((outer * ROWS, 2 * LANES), jnp.float32),
            pltpu.VMEM((outer, 2, 2, ROWS, LANES), jnp.float32),
        ],
        compiler_params=pltpu.CompilerParams(vmem_limit_bytes=VMEM_BYTES),
        name="forward",
    )(place, scale, *blocks, *consts, q, p)


def chip_kernel(chips, place, keep, got, pair, *outs):
    chip = place[0] // 2
    upper = place[0] % 2 == 0
    above, below = keep[...], got[...]
    first, second = jnp.where(upper, above, below), jnp.where(upper, below, above)
    down = second[:, 0] + pair[1][:, None] * first[:, 0]
    up = first[:, 1] + pair[2][:, None] * second[:, 1]
    for apart in range(1, chips):
        outs[apart - 1][...] = jnp.where(chip + apart < chips, down, up)


def chip_sums(place, keep, got, pair, chips):
    half = keep.shape[0]
    full = pl.BlockSpec(keep.shape, lambda i, place: (0,) * keep.ndim)
    shape = (half, 2, ROWS, LANES)
    return pl.pallas_call(
        functools.partial(chip_kernel, chips),
        grid_spec=pltpu.PrefetchScalarGridSpec(
            num_scalar_prefetch=1,
            grid=(1,),
            in_specs=[full, full, pl.BlockSpec((4, half, ROWS, LANES), lambda i, place: (0, place[0] % 2, 0, 0))],
            out_specs=[pl.BlockSpec(shape, lambda i, place: (0, 0, 0, 0))] * (chips - 1),
        ),
        out_shape=[jax.ShapeDtypeStruct(shape, jnp.float32)] * (chips - 1),
        compiler_params=pltpu.CompilerParams(vmem_limit_bytes=VMEM_BYTES),
        name="chip_sums",
    )(place, keep, got, pair)


def join_kernel(chips, place, keep, got, pair, far, *refs):
    news = refs[:chips - 1]
    mine, theirs = refs[chips - 1:]
    chip = place[0] // 2
    upper = place[0] % 2 == 0
    first, second = jnp.where(upper, keep[...], got[...]), jnp.where(upper, got[...], keep[...])
    down = jnp.zeros(first.shape[:1] + first.shape[2:], jnp.float32)
    up = down
    for apart in range(1, chips):
        term = far[apart - 1][:, None] * news[apart - 1][...]
        down = down + jnp.where(chip >= apart, term, 0.0)
        up = up + jnp.where(chip >= apart, 0.0, term)
    inner_up = second[:, 1] + pair[3][:, None] * up
    inner_down = first[:, 0] + pair[0][:, None] * down
    mine[:, 0] = jnp.where(upper, down, inner_down)
    mine[:, 1] = jnp.where(upper, inner_up, up)
    theirs[:, 0] = jnp.where(upper, inner_down, down)
    theirs[:, 1] = jnp.where(upper, up, inner_up)


def join(place, keep, got, pair, far, news):
    half = keep.shape[0]
    chips = len(news) + 1
    full = lambda a: pl.BlockSpec(a.shape, lambda i, place: (0,) * a.ndim)
    part = lambda n: pl.BlockSpec((n, half, ROWS, LANES), lambda i, place: (0, place[0] % 2, 0, 0))
    return pl.pallas_call(
        functools.partial(join_kernel, chips),
        grid_spec=pltpu.PrefetchScalarGridSpec(
            num_scalar_prefetch=1,
            grid=(1,),
            in_specs=[full(keep), full(got), part(4), part(chips - 1), *[full(a) for a in news]],
            out_specs=[full(keep)] * 2,
        ),
        out_shape=[jax.ShapeDtypeStruct(keep.shape, jnp.float32)] * 2,
        compiler_params=pltpu.CompilerParams(vmem_limit_bytes=VMEM_BYTES),
        name="join",
    )(place, keep, got, pair, far, *news)


def backward_kernel(waves, place, scale, b, mine, theirs, r, m, end, tw_cos, tw_sin, top, rest, *refs):
    at = pl.program_id(0)
    outs = refs[:waves]
    y_all, now, x = refs[waves:]
    local = x.shape[-1]
    per = local // LANES
    levels, outer = r.shape[:2]
    rows = outer * ROWS
    half = outer // 2

    @pl.when(at == 0)
    def _():
        core = place[0] % 2
        for source, start in ((mine, core * half), (theirs, (1 - core) * half)):
            here = pl.ds(start, half)
            for part in range(2):
                y = source[:, 0, part]
                for j in range(levels):
                    y = b[part, j, here] + m[j, here] * y
                    y_all[part, j, here] = y
                now[part, here] = (y + end[0, here] * source[:, 1, part]) * end[1, here]

    level = levels - 1 - at

    @pl.when(at > 0)
    def _():
        for part in range(2):
            now[part] = r[level] * y_all[part, level] + m[level + 1] * now[part]

    spectrum = jnp.concatenate([now[0].reshape(rows, LANES), now[1].reshape(rows, LANES)], 1)
    z = lane_dft(spectrum, top[...], rest[...]) * scale[level]
    pairs = []
    for k in range(outer):
        re = z[k * ROWS:(k + 1) * ROWS, :LANES]
        im = z[k * ROWS:(k + 1) * ROWS, LANES:]
        c, s = tw_cos[k], tw_sin[k]
        pairs.append((re * c - im * s, re * s + im * c))
    for s, pair in enumerate(butterflies(pairs, 1.0)):
        for part in range(2):
            x[s // per, part, :, (s % per) * LANES:(s % per + 1) * LANES] = pair[part]
    for s in range(waves):
        outs[s][:, 0] = x[place[1] ^ s]


def backward(place, b, mine, theirs, r, m, end, scale, waves):
    _, levels, outer, _, _ = b.shape
    local = outer * LANES // waves
    consts = tables(outer, 1.0)
    whole = lambda a: pl.BlockSpec(a.shape, lambda l: (0,) * a.ndim)
    smem = pl.BlockSpec(memory_space=pltpu.SMEM)
    return pl.pallas_call(
        functools.partial(backward_kernel, waves),
        grid=(levels,),
        in_specs=[smem, smem] + [whole(a) for a in (b, mine, theirs, r, m, end, *consts)],
        out_specs=[pl.BlockSpec((2, 1, ROWS, local), lambda l: (0, levels - 1 - l, 0, 0))] * waves,
        out_shape=[jax.ShapeDtypeStruct((2, levels, ROWS, local), jnp.float32)] * waves,
        scratch_shapes=[
            pltpu.VMEM((2, levels, outer, ROWS, LANES), jnp.float32),
            pltpu.VMEM((2, outer, ROWS, LANES), jnp.float32),
            pltpu.VMEM((waves, 2, ROWS, local), jnp.float32),
        ],
        compiler_params=pltpu.CompilerParams(vmem_limit_bytes=VMEM_BYTES),
        name="backward",
    )(place, scale, b, mine, theirs, r, m, end, *consts)


def shards(rhs, cotangent, thickness, ky_shift):
    waves = lax.axis_size("wave")
    count = lax.axis_size("depth")
    depth_pos = lax.axis_index("depth")
    wave_pos = lax.axis_index("wave")
    _, levels, ky, local = rhs.shape
    full = waves * local
    ky_local = ky // waves
    spare = -ky_local % ROWS
    chips = count // 2
    place = jnp.stack([depth_pos, wave_pos]).astype(jnp.int32)

    def exchange(blocks):
        turns = [[(w, w ^ s) for w in range(waves)] for s in range(waves)]
        return [blocks[0]] + [lax.ppermute(blocks[s], "wave", turns[s]) for s in range(1, waves)]

    def cut(a):
        return [lax.dynamic_slice_in_dim(a, (wave_pos ^ s) * ky_local, ky_local, 2) for s in range(waves)]

    def glue(blocks):
        out = jnp.zeros((2, levels, ky, local), jnp.float32)
        for s in range(waves):
            out = lax.dynamic_update_slice_in_dim(out, blocks[s], (wave_pos ^ s) * ky_local, 2)
        return out

    def pad(a):
        return jnp.pad(a, [(0, 0)] * 2 + [(0, spare), (0, 0)]) if spare else a

    def trim(a):
        return a[:, :, :ky_local] if spare else a

    def across(a):
        return lax.ppermute(a, "depth", [(d, d ^ 1) for d in range(count)])

    def along(a, apart):
        return lax.ppermute(a, "depth", [(d, (d + 2 * apart) % count) for d in range(count)])

    rhs_in = exchange(cut(rhs))
    cotangent_in = exchange(cut(cotangent))

    inner_face = 2.0 / (thickness[:-1] + thickness[1:])
    face = jnp.concatenate([2.0 / thickness[:1], inner_face, jnp.zeros((1,), jnp.float32)])
    outer = full // LANES
    wavenumber = np.arange(outer)[:, None] + outer * np.arange(LANES)[None, :]
    wavenumber = jnp.asarray(wavenumber, jnp.float32)
    horizontal = aspect_ratio * 4.0 * jnp.sin(math.pi * wavenumber / full) ** 2
    shifts = lax.dynamic_slice_in_dim(ky_shift, wave_pos * ky_local, ky_local)
    shifts = jnp.pad(shifts, (0, spare), constant_values=1.0)
    lam = shifts[None, :, None] + horizontal[:, None, :]
    q, p, r, m, end, pair, far = coefficients(place, thickness, face, lam, levels)
    thick_here = lax.dynamic_slice_in_dim(thickness, depth_pos * levels, levels)
    even = jnp.ones_like(thick_here)

    def solve(blocks, before, after):
        b, keep, give = forward(place, [pad(a) for a in blocks], before, q, p)
        got = across(give)
        sums = chip_sums(place, keep, got, pair, chips)
        news = [along(sums[apart - 1], apart) for apart in range(1, chips)]
        mine, theirs = join(place, keep, got, pair, far, news)
        theirs = across(theirs)
        return [trim(a) for a in backward(place, b, mine, theirs, r, m, end, after / full, waves)]

    pressure = exchange(solve(rhs_in, thick_here, even))
    adjoint = exchange(solve(cotangent_in, even, thick_here))
    return glue(pressure), glue(adjoint)


def solution(mesh):
    spec = P(None, "depth", None, "wave")
    return jax.shard_map(shards, mesh=mesh, in_specs=(spec, spec, P(), P()), out_specs=(spec, spec), check_vma=False)
```

time: 205 us -> 140 us (0.68)
  blocking collectives: 30.6 us -> 0 us
  waiting for transfers between devices: 68.7 us -> 39.3 us
  local copies, waits for them, and re-layouts: 40.4 us -> 14.2 us
  Pallas kernels: 32.1 us -> 53.2 us
  other arithmetic: 0.31 us -> 2.61 us
    all_to_all x7 -> x0, waiting for transfers between devices: 68.7 us -> none  [swap(): return lax.all_to_all(a, axis, split_axis=0, concat_axis=0, tiled=True)]
    ppermute x0 -> x22, waiting for transfers between devices: none -> 39.3 us  [the longest x12 37.6 us: exchange(): lax.ppermute(blocks[s], 'wave', turns[s])]
    all_to_all x7 -> x0, starting transfers between devices: 30.9 us -> none  [swap(): return lax.all_to_all(a, axis, split_axis=0, concat_axis=0, tiled=True)]
    all_to_all x1 -> x0, blocking collectives: 30.6 us -> none  [swap(): return lax.all_to_all(a, axis, split_axis=0, concat_axis=0, tiled=True)]
    ppermute x0 -> x22, starting transfers between devices: none -> 28.9 us  [the longest x12 18 us: exchange(): lax.ppermute(blocks[s], 'wave', turns[s])]
    unnamed x76 -> x52, local copies, waits for them, and re-layouts: 31.4 us -> 7.85 us
    pallas_call x6 -> x8, Pallas kernels: 22.2 us -> 42.7 us  [the longest x2 16.5 us: forward(): pl.pallas_call(functools.partial(forward_kernel, waves), grid=(levels,),...]
    reshape x2 -> x0, local copies, waits for them, and re-layouts: 6.32 us -> none  [unpack(): return a.transpose(1, 2, 0, 3, 4).reshape(2, levels, ky, local)]
  transfers between devices with their start and end apart: 7 -> 22, of which waited for: 6 -> 5; matrix products, arithmetic and copies ran while one was open for 2% -> 4% of each run, Pallas kernels for 16% -> 38%
where the time goes in v2:
time: 140 us; the launch traced here: 139 us
  Pallas kernels  53.2 us (38%)
  waiting for transfers between devices  39.3 us (28%)
  starting transfers between devices  28.9 us (21%)
  local copies, waits for them, and re-layouts  14.2 us (10%)
  other arithmetic  2.61 us (2%)
    ppermute x12, waiting for transfers between devices, exchange(): lax.ppermute(blocks[s], 'wave', turns[s])  37.6 us
    ppermute x12, starting transfers between devices, exchange(): lax.ppermute(blocks[s], 'wave', turns[s])  18 us
    pallas_call x2, Pallas kernels, forward(): pl.pallas_call(functools.partial(forward_kernel, waves), grid=(levels,),...  16.5 us
    pallas_call x2, Pallas kernels, backward(): pl.pallas_call(functools.partial(backward_kernel, waves), grid=(levels,),...  15.3 us
    pallas_call x1, Pallas kernels, coefficients(): pl.pallas_call(functools.partial(coefficient_kernel, levels, total, group...  10.5 us
    ppermute x6, starting transfers between devices, along(): lax.ppermute(a, 'depth', [(d, (d + 2 * apart) % count) for d in range(cou...  10.2 us
    unnamed x52, local copies, waits for them, and re-layouts  7.85 us
    pallas_call x2, Pallas kernels, join(): pl.pallas_call(functools.partial(join_kernel, chips), grid_spec=pltpu.Pre...  5.71 us
  transfers between devices with their start and end apart: 22, of which 5 were waited for; matrix products, arithmetic and copies ran while one was open for 4% of the time, Pallas kernels for 38%

profile of v2, /device:TPU:0, one launch (start us, length us, event | category | flops | bytes accessed | tf_op | source)
XLA Modules:
  0.0 139.3 jit_solution(13379444841884980347)
XLA Ops:
  0.7 2.9 %constant_dynamic-slice_fusion = (f32[2,8,8,1024]{3,2,1,0:T(8,128)}, f32[2,8,8,1024]{3,2,1,0:T(8,128)S(1)}, f32[2,8,8,1024]{3,2,1,0:T(8,128)}, f32[2,8,8,1024]{3,2,1,0:T(8,128)}) fusion(f32[2,8,32,1024]{3,2,1,0:T(8,128)} %param.22, s32[]{:T(128)S(6)} %select_n.14, s32[]{:T(128)S(6)} %select_n.12, s32[]{:T(128)S(6)} %select_n.11, s32[]{:T(128)S(6)} %select_n.13), kind=kLoop, calls=%fused_computation.5 | loop fusion | bytes 4194320 | tf_op jit(solution)/shard_map/dynamic_slice | solution.py:379
  3.5 2.9 %collective-permute-start.11 = (f32[2,8,8,1024]{3,2,1,0:T(8,128)S(1)}, f32[2,8,8,1024]{3,2,1,0:T(8,128)S(1)}, u32[]{:S(2)}, u32[]{:S(2)}) collective-permute-start(f32[2,8,8,1024]{3,2,1,0:T(8,128)S(1)} %get-tuple-element.67), channel_id=1, source_target_pairs={{0,1},{1,0},{2,3},{3,2},{4,5},{5,4},{6,7},{7,6},{8,9},{9,8},{10,11... | collective-permute-start | bytes 1572872 | tf_op jit(solution)/shard_map/ppermute | solution.py:376
  6.5 1.5 %collective-permute-start.12 = (f32[2,8,8,1024]{3,2,1,0:T(8,128)}, f32[2,8,8,1024]{3,2,1,0:T(8,128)S(1)}, u32[]{:S(2)}, u32[]{:S(2)}) collective-permute-start(f32[2,8,8,1024]{3,2,1,0:T(8,128)} %get-tuple-element.69), channel_id=1, source_target_pairs={{0,2},{1,3},{2,0},{3,1},{4,6},{5,7},{6,4},{7,5},{8,10},{9,11},{10,... | collective-permute-start | bytes 1572872 | tf_op jit(solution)/shard_map/ppermute | solution.py:376
  8.0 1.4 constant_dynamic-slice_fusion.4
  9.4 1.9 %collective-permute-start = (f32[2,8,8,1024]{3,2,1,0:T(8,128)}, f32[2,8,8,1024]{3,2,1,0:T(8,128)S(1)}, u32[]{:S(2)}, u32[]{:S(2)}) collective-permute-start(f32[2,8,8,1024]{3,2,1,0:T(8,128)} %get-tuple-element.71), channel_id=1, source_target_pairs={{0,1},{1,0},{2,3},{3,2},{4,5},{5,4},{6,7},{7,6},{8,9},{9,8},{10,11... | collective-permute-start | bytes 1572872 | tf_op jit(solution)/shard_map/ppermute | solution.py:376
  11.3 1.5 %collective-permute-start.1 = (f32[2,8,8,1024]{3,2,1,0:T(8,128)}, f32[2,8,8,1024]{3,2,1,0:T(8,128)S(1)}, u32[]{:S(2)}, u32[]{:S(2)}) collective-permute-start(f32[2,8,8,1024]{3,2,1,0:T(8,128)} %get-tuple-element.73), channel_id=1, source_target_pairs={{0,2},{1,3},{2,0},{3,1},{4,6},{5,7},{6,4},{7,5},{8,10},{9,11},{10,... | collective-permute-start | bytes 1572872 | tf_op jit(solution)/shard_map/ppermute | solution.py:376
  12.8 0.1 dynamic_slice.35
  12.9 0.7 broadcast_add_fusion.lam
  13.7 0.1 add_divide_fusion
  13.7 5.5 %collective-permute-done.11.refs_1_ = f32[2,8,8,1024]{3,2,1,0:T(8,128)S(1)} collective-permute-done((f32[2,8,8,1024]{3,2,1,0:T(8,128)S(1)}, f32[2,8,8,1024]{3,2,1,0:T(8,128)S(1)}, u32[]{:S(2)}, u32[]{:S(2)}) %collective-permute-start.11) | collective-permute-done | bytes 524320 | tf_op jit(solution)/shard_map/ppermute | solution.py:376
  19.2 3.0 %collective-permute-start.2 = (f32[2,8,8,1024]{3,2,1,0:T(8,128)}, f32[2,8,8,1024]{3,2,1,0:T(8,128)S(1)}, u32[]{:S(2)}, u32[]{:S(2)}) collective-permute-start(f32[2,8,8,1024]{3,2,1,0:T(8,128)} %get-tuple-element.70), channel_id=1, source_target_pairs={{0,3},{1,2},{2,1},{3,0},{4,7},{5,6},{6,5},{7,4},{8,11},{9,10},{10,... | collective-permute-start | bytes 1572872 | tf_op jit(solution)/shard_map/ppermute | solution.py:376
  22.2 0.6 pad_add_fusion.place
  22.9 0.6 pad_maximum_fusion.face
  23.5 10.5 %coefficients.1 = (f32[8,32,8,128]{3,2,1,0:T(8,128)}, f32[8,32,8,128]{3,2,1,0:T(8,128)}, f32[8,32,8,128]{3,2,1,0:T(8,128)}, f32[8,32,8,128]{3,2,1,0:T(8,128)}, f...) custom-call(s32[2]{0:T(128)} %pad_add_fusion.place, f32[64]{0:T(128)} %thick.1, ...), custom_call_target="tpu_custom_call" | custom-call | tf_op jit(solution)/shard_map/coefficients/pallas_call | solution.py:139
  34.1 0.6 broadcast_7_scale.2.scale
  34.7 0.2 copy-done.9
  34.9 0.2 copy-done.10
  35.1 8.3 %forward.3 = (f32[2,8,32,8,128]{4,3,2,1,0:T(8,128)}, f32[16,2,2,8,128]{4,3,2,1,0:T(8,128)}, f32[16,2,2,8,128]{4,3,2,1,0:T(8,128)}) custom-call(s32[2]{0:T(128)} %pad_add_fusion.place, f32[8]{0:T(128)} %broadcast_7_scale.2.scale, f32[2,8,8,1024]{3,2,1,0:T(8,128)} %get-tuple-element.68.refs_0_, f32[2,8,8,1024]{3,2,1,0:T(8,128)} %copy-done.8, ...), custom_call_target="tpu_custom_call" | custom-call | tf_op jit(solution)/shard_map/forward/pallas_call | solution.py:199
  43.4 0.1 collective-permute-start.14
  43.4 1.7 %collective-permute-done.14.got = f32[16,2,2,8,128]{4,3,2,1,0:T(8,128)S(1)} collective-permute-done((f32[16,2,2,8,128]{4,3,2,1,0:T(8,128)}, f32[16,2,2,8,128]{4,3,2,1,0:T(8,128)S(1)}, u32[]{:S(2)}, u32[]{:S(2)}) %collective-permute-start.14) | collective-permute-done | bytes 262176 | tf_op jit(solution)/shard_map/ppermute | solution.py:394
  45.2 0.7 copy-done.4
  45.9 2.6 %chip_sums.3 = (f32[16,2,8,128]{3,2,1,0:T(8,128)}, f32[16,2,8,128]{3,2,1,0:T(8,128)}, f32[16,2,8,128]{3,2,1,0:T(8,128)}) custom-call(s32[2]{0:T(128)} %pad_add_fusion.place, f32[16,2,2,8,128]{4,3,2,1,0:T(8,128)} %get-tuple-element.53.keep, f32[16,2,2,8,128]{4,3,2,1,0:T(8,128)} %copy-done.4, f32[4,32,8,128]{3,2,1,0:T(8,128)} %get-tuple-element.38.pair), custom_call_target="tpu_custom_call" | custom-call | tf_op jit(solution)/shard_map/chip_sums/pallas_call | solution.py:243
  48.4 1.6 %collective-permute-start.15 = (f32[16,2,8,128]{3,2,1,0:T(8,128)}, f32[16,2,8,128]{3,2,1,0:T(8,128)S(1)}, u32[]{:S(2)}, u32[]{:S(2)}) collective-permute-start(f32[16,2,8,128]{3,2,1,0:T(8,128)} %get-tuple-element.55), channel_id=1, source_target_pairs={{0,8},{4,12},{8,16},{12,20},{16,24},{20,28},{24,0},{28,4},{1,9},{5... | collective-permute-start | bytes 393224 | tf_op jit(solution)/shard_map/ppermute | solution.py:397
  50.0 2.6 %collective-permute-start.16 = (f32[16,2,8,128]{3,2,1,0:T(8,128)}, f32[16,2,8,128]{3,2,1,0:T(8,128)S(1)}, u32[]{:S(2)}, u32[]{:S(2)}) collective-permute-start(f32[16,2,8,128]{3,2,1,0:T(8,128)} %get-tuple-element.56), channel_id=1, source_target_pairs={{0,16},{4,20},{8,24},{12,28},{16,0},{20,4},{24,8},{28,12},{1,17},{... | collective-permute-start | bytes 393224 | tf_op jit(solution)/shard_map/ppermute | solution.py:397
  52.6 1.3 collective-permute-start.17
  54.0 0.6 broadcast_multiply_fusion
  54.6 0.8 copy-done.6
  55.4 0.2 copy-done.7
  55.5 8.3 %forward.2 = (f32[2,8,32,8,128]{4,3,2,1,0:T(8,128)}, f32[16,2,2,8,128]{4,3,2,1,0:T(8,128)}, f32[16,2,2,8,128]{4,3,2,1,0:T(8,128)}) custom-call(s32[2]{0:T(128)} %pad_add_fusion.place, f32[8]{0:T(128)} %get-tuple-element.65.scale, f32[2,8,8,1024]{3,2,1,0:T(8,128)} %get-tuple-element.72.refs_0_, f32[2,8,8,1024]{3,2,1,0:T(8,128)} %copy-done.5, ...), custom_call_target="tpu_custom_call" | custom-call | tf_op jit(solution)/shard_map/forward/pallas_call | solution.py:199
  63.8 0.1 collective-permute-start.3
  64.0 0.6 copy-done.15
  64.6 0.1 copy-done.16
  64.7 0.1 copy-done.17
  64.7 2.9 %join.3 = (f32[16,2,2,8,128]{4,3,2,1,0:T(8,128)}, f32[16,2,2,8,128]{4,3,2,1,0:T(8,128)}) custom-call(s32[2]{0:T(128)} %pad_add_fusion.place, f32[16,2,2,8,128]{4,3,2,1,0:T(8,128)} %get-tuple-element.53.keep, f32[16,2,2,8,128]{4,3,2,1,0:T(8,128)} %copy-done.4, f32[4,32,8,128]{3,2,1,0:T(8,128)} %get-tuple-element.38.pair, ...), custom_call_target="tpu_custom_call" | custom-call | tf_op jit(solution)/shard_map/join/pallas_call | solution.py:282
  67.6 0.5 collective-permute-start.18
  68.1 0.7 copy-done.3
  68.8 2.6 %chip_sums.2 = (f32[16,2,8,128]{3,2,1,0:T(8,128)}, f32[16,2,8,128]{3,2,1,0:T(8,128)}, f32[16,2,8,128]{3,2,1,0:T(8,128)}) custom-call(s32[2]{0:T(128)} %pad_add_fusion.place, f32[16,2,2,8,128]{4,3,2,1,0:T(8,128)} %get-tuple-element.36.keep, f32[16,2,2,8,128]{4,3,2,1,0:T(8,128)} %copy-done.3, f32[4,32,8,128]{3,2,1,0:T(8,128)} %get-tuple-element.38.pair), custom_call_target="tpu_custom_call" | custom-call | tf_op jit(solution)/shard_map/chip_sums/pallas_call | solution.py:243
  71.4 0.8 collective-permute-start.4
  72.1 2.6 %collective-permute-start.5 = (f32[16,2,8,128]{3,2,1,0:T(8,128)}, f32[16,2,8,128]{3,2,1,0:T(8,128)S(1)}, u32[]{:S(2)}, u32[]{:S(2)}) collective-permute-start(f32[16,2,8,128]{3,2,1,0:T(8,128)} %get-tuple-element.41), channel_id=1, source_target_pairs={{0,16},{4,20},{8,24},{12,28},{16,0},{20,4},{24,8},{28,12},{1,17},{... | collective-permute-start | bytes 393224 | tf_op jit(solution)/shard_map/ppermute | solution.py:397
  74.7 1.3 collective-permute-start.6
  76.1 0.7 copy-done.13
  76.8 7.7 %backward.3 = (f32[2,8,8,1024]{3,2,1,0:T(8,128)}, f32[2,8,8,1024]{3,2,1,0:T(8,128)}, f32[2,8,8,1024]{3,2,1,0:T(8,128)}, f32[2,8,8,1024]{3,2,1,0:T(8,128)}) custom-call(s32[2]{0:T(128)} %pad_add_fusion.place, f32[8]{0:T(128)} %get-tuple-element.64.scale, f32[2,8,32,8,128]{4,3,2,1,0:T(8,128)} %get-tuple-element.52.b, ...), custom_call_target="tpu_custom_call" | custom-call | tf_op jit(solution)/shard_map/backward/pallas_call | solution.py:346
  84.5 0.9 collective-permute-start.19
  85.4 0.6 copy-done.18
  86.0 0.1 copy-done.19
  86.1 0.6 copy-done.20
  86.8 2.8 %join.2 = (f32[16,2,2,8,128]{4,3,2,1,0:T(8,128)}, f32[16,2,2,8,128]{4,3,2,1,0:T(8,128)}) custom-call(s32[2]{0:T(128)} %pad_add_fusion.place, f32[16,2,2,8,128]{4,3,2,1,0:T(8,128)} %get-tuple-element.36.keep, f32[16,2,2,8,128]{4,3,2,1,0:T(8,128)} %copy-done.3, f32[4,32,8,128]{3,2,1,0:T(8,128)} %get-tuple-element.38.pair, ...), custom_call_target="tpu_custom_call" | custom-call | tf_op jit(solution)/shard_map/join/pallas_call | solution.py:282
  89.6 1.2 collective-permute-start.20
  90.8 1.4 %collective-permute-start.21 = (f32[2,8,8,1024]{3,2,1,0:T(8,128)}, f32[2,8,8,1024]{3,2,1,0:T(8,128)S(1)}, u32[]{:S(2)}, u32[]{:S(2)}) collective-permute-start(f32[2,8,8,1024]{3,2,1,0:T(8,128)} %get-tuple-element.63), channel_id=1, source_target_pairs={{0,3},{1,2},{2,1},{3,0},{4,7},{5,6},{6,5},{7,4},{8,11},{9,10},{10,... | collective-permute-start | bytes 1572872 | tf_op jit(solution)/shard_map/ppermute | solution.py:376
  92.2 0.6 broadcast_6_scale.2.scale
  92.8 0.1 copy-done.14
  92.9 7.6 %backward.2 = (f32[2,8,8,1024]{3,2,1,0:T(8,128)}, f32[2,8,8,1024]{3,2,1,0:T(8,128)}, f32[2,8,8,1024]{3,2,1,0:T(8,128)}, f32[2,8,8,1024]{3,2,1,0:T(8,128)}) custom-call(s32[2]{0:T(128)} %pad_add_fusion.place, f32[8]{0:T(128)} %broadcast_6_scale.2.scale, f32[2,8,32,8,128]{4,3,2,1,0:T(8,128)} %get-tuple-element.35.b, ...), custom_call_target="tpu_custom_call" | custom-call | tf_op jit(solution)/shard_map/backward/pallas_call | solution.py:346
  100.5 0.9 collective-permute-start.8
  101.5 1.2 collective-permute-start.9
  102.6 0.2 broadcast.11.clone.1
  103.0 0.2 broadcast.11.clone
  103.2 0.7 copy-done.12
  104.0 0.1 copy-done.24
  104.1 1.5 %collective-permute-start.10 = (f32[2,8,8,1024]{3,2,1,0:T(8,128)S(1)}, f32[2,8,8,1024]{3,2,1,0:T(8,128)S(1)}, u32[]{:S(2)}, u32[]{:S(2)}) collective-permute-start(f32[2,8,8,1024]{3,2,1,0:T(8,128)S(1)} %copy-done.24), channel_id=1, source_target_pairs={{0,3},{1,2},{2,1},{3,0},{4,7},{5,6},{6,5},{7,4},{8,11},{9,10},{10,... | collective-permute-start | bytes 1572872 | tf_op jit(solution)/shard_map/ppermute | solution.py:376
  105.6 10.2 %collective-permute-done.20 = f32[2,8,8,1024]{3,2,1,0:T(8,128)S(1)} collective-permute-done((f32[2,8,8,1024]{3,2,1,0:T(8,128)}, f32[2,8,8,1024]{3,2,1,0:T(8,128)S(1)}, u32[]{:S(2)}, u32[]{:S(2)}) %collective-permute-start.20) | collective-permute-done | bytes 524320 | tf_op jit(solution)/shard_map/ppermute | solution.py:376
  115.8 0.1 constant_dynamic-update-slice_fusion
  115.9 6.2 %collective-permute-done.8 = f32[2,8,8,1024]{3,2,1,0:T(8,128)S(1)} collective-permute-done((f32[2,8,8,1024]{3,2,1,0:T(8,128)}, f32[2,8,8,1024]{3,2,1,0:T(8,128)S(1)}, u32[]{:S(2)}, u32[]{:S(2)}) %collective-permute-start.8) | collective-permute-done | bytes 524320 | tf_op jit(solution)/shard_map/ppermute | solution.py:376
  122.2 15.7 %collective-permute-done.9 = f32[2,8,8,1024]{3,2,1,0:T(8,128)S(1)} collective-permute-done((f32[2,8,8,1024]{3,2,1,0:T(8,128)}, f32[2,8,8,1024]{3,2,1,0:T(8,128)S(1)}, u32[]{:S(2)}, u32[]{:S(2)}) %collective-permute-start.9) | collective-permute-done | bytes 524320 | tf_op jit(solution)/shard_map/ppermute | solution.py:376
  138.0 1.3 copy-done
  (61 shorter events, 0.5 us)
Async XLA Ops:
  0.7 7.4 %copy-start.2 = (f32[2,8,32,1024]{3,2,1,0:T(8,128)S(1)}, f32[2,8,32,1024]{3,2,1,0:T(8,128)}, u32[]{:S(2)}) copy-start(f32[2,8,32,1024]{3,2,1,0:T(8,128)} %param.21) | copy-start | bytes 6291460
  3.5 15.7 %collective-permute-start.11 = (f32[2,8,8,1024]{3,2,1,0:T(8,128)S(1)}, f32[2,8,8,1024]{3,2,1,0:T(8,128)S(1)}, u32[]{:S(2)}, u32[]{:S(2)}) collective-permute-start(f32[2,8,8,1024]{3,2,1,0:T(8,128)S(1)} %get-tuple-element.67), channel_id=1, source_target_pairs={{0,1},{1,0},{2,3},{3,2},{4,5},{5,4},{6,7},{7,6},{8,9},{9,8},{10,11... | collective-permute-start | bytes 1572872 | tf_op jit(solution)/shard_map/ppermute | solution.py:376
  6.5 27.6 %collective-permute-start.12 = (f32[2,8,8,1024]{3,2,1,0:T(8,128)}, f32[2,8,8,1024]{3,2,1,0:T(8,128)S(1)}, u32[]{:S(2)}, u32[]{:S(2)}) collective-permute-start(f32[2,8,8,1024]{3,2,1,0:T(8,128)} %get-tuple-element.69), channel_id=1, source_target_pairs={{0,2},{1,3},{2,0},{3,1},{4,6},{5,7},{6,4},{7,5},{8,10},{9,11},{10,... | collective-permute-start | bytes 1572872 | tf_op jit(solution)/shard_map/ppermute | solution.py:376
  8.0 4.9 %copy-start.25 = (f32[32]{0:T(128)S(1)}, f32[32]{0:T(128)}, u32[]{:S(2)}) copy-start(f32[32]{0:T(128)} %param.24) | copy-start | bytes 388
  8.0 4.9 %copy-start.21 = (f32[32,128]{1,0:T(8,128)S(1)}, f32[32,128]{1,0:T(8,128)}, u32[]{:S(2)}) copy-start(f32[32,128]{1,0:T(8,128)} %constant.72) | copy-start | bytes 49156
  8.0 5.7 %copy-start.22 = (f32[64]{0:T(128)S(1)}, f32[64]{0:T(128)}, u32[]{:S(2)}) copy-start(f32[64]{0:T(128)} %thick.1) | copy-start | bytes 772
  8.0 26.1 %collective-permute-start.13 = (f32[2,8,8,1024]{3,2,1,0:T(8,128)}, f32[2,8,8,1024]{3,2,1,0:T(8,128)S(1)}, u32[]{:S(2)}, u32[]{:S(2)}) collective-permute-start(f32[2,8,8,1024]{3,2,1,0:T(8,128)} %get-tuple-element.66), channel_id=1, source_target_pairs={{0,3},{1,2},{2,1},{3,0},{4,7},{5,6},{6,5},{7,4},{8,11},{9,10},{10,... | collective-permute-start | bytes 1572872 | tf_op jit(solution)/shard_map/ppermute | solution.py:376
  9.4 43.2 %collective-permute-start = (f32[2,8,8,1024]{3,2,1,0:T(8,128)}, f32[2,8,8,1024]{3,2,1,0:T(8,128)S(1)}, u32[]{:S(2)}, u32[]{:S(2)}) collective-permute-start(f32[2,8,8,1024]{3,2,1,0:T(8,128)} %get-tuple-element.71), channel_id=1, source_target_pairs={{0,1},{1,0},{2,3},{3,2},{4,5},{5,4},{6,7},{7,6},{8,9},{9,8},{10,11... | collective-permute-start | bytes 1572872 | tf_op jit(solution)/shard_map/ppermute | solution.py:376
  11.3 43.2 %collective-permute-start.1 = (f32[2,8,8,1024]{3,2,1,0:T(8,128)}, f32[2,8,8,1024]{3,2,1,0:T(8,128)S(1)}, u32[]{:S(2)}, u32[]{:S(2)}) collective-permute-start(f32[2,8,8,1024]{3,2,1,0:T(8,128)} %get-tuple-element.73), channel_id=1, source_target_pairs={{0,2},{1,3},{2,0},{3,1},{4,6},{5,7},{6,4},{7,5},{8,10},{9,11},{10,... | collective-permute-start | bytes 1572872 | tf_op jit(solution)/shard_map/ppermute | solution.py:376
  19.2 15.5 %copy-start.8 = (f32[2,8,8,1024]{3,2,1,0:T(8,128)}, f32[2,8,8,1024]{3,2,1,0:T(8,128)S(1)}, u32[]{:S(2)}) copy-start(f32[2,8,8,1024]{3,2,1,0:T(8,128)S(1)} %collective-permute-done.11.refs_1_) | copy-start | bytes 1572868
  19.2 35.3 %collective-permute-start.2 = (f32[2,8,8,1024]{3,2,1,0:T(8,128)}, f32[2,8,8,1024]{3,2,1,0:T(8,128)S(1)}, u32[]{:S(2)}, u32[]{:S(2)}) collective-permute-start(f32[2,8,8,1024]{3,2,1,0:T(8,128)} %get-tuple-element.70), channel_id=1, source_target_pairs={{0,3},{1,2},{2,1},{3,0},{4,7},{5,6},{6,5},{7,4},{8,11},{9,10},{10,... | collective-permute-start | bytes 1572872 | tf_op jit(solution)/shard_map/ppermute | solution.py:376
  34.1 0.8 copy-start.9
  34.1 1.0 copy-start.10
  35.1 18.9 %copy-start.23 = (f32[64]{0:T(128)S(1)}, f32[64]{0:T(128)}, u32[]{:S(2)}) copy-start(f32[64]{0:T(128)} %thick.1) | copy-start | bytes 772
  43.4 1.8 %collective-permute-start.14 = (f32[16,2,2,8,128]{4,3,2,1,0:T(8,128)}, f32[16,2,2,8,128]{4,3,2,1,0:T(8,128)S(1)}, u32[]{:S(2)}, u32[]{:S(2)}) collective-permute-start(f32[16,2,2,8,128]{4,3,2,1,0:T(8,128)} %get-tuple-element.54), channel_id=1, source_target_pairs={{0,4},{4,0},{8,12},{12,8},{16,20},{20,16},{24,28},{28,24},{1,5},{5... | collective-permute-start | bytes 786440 | tf_op jit(solution)/shard_map/ppermute | solution.py:394
  45.2 0.7 copy-start.4
  48.4 15.5 %collective-permute-start.15 = (f32[16,2,8,128]{3,2,1,0:T(8,128)}, f32[16,2,8,128]{3,2,1,0:T(8,128)S(1)}, u32[]{:S(2)}, u32[]{:S(2)}) collective-permute-start(f32[16,2,8,128]{3,2,1,0:T(8,128)} %get-tuple-element.55), channel_id=1, source_target_pairs={{0,8},{4,12},{8,16},{12,20},{16,24},{20,28},{24,0},{28,4},{1,9},{5... | collective-permute-start | bytes 393224 | tf_op jit(solution)/shard_map/ppermute | solution.py:397
  50.0 13.9 %collective-permute-start.16 = (f32[16,2,8,128]{3,2,1,0:T(8,128)}, f32[16,2,8,128]{3,2,1,0:T(8,128)S(1)}, u32[]{:S(2)}, u32[]{:S(2)}) collective-permute-start(f32[16,2,8,128]{3,2,1,0:T(8,128)} %get-tuple-element.56), channel_id=1, source_target_pairs={{0,16},{4,20},{8,24},{12,28},{16,0},{20,4},{24,8},{28,12},{1,17},{... | collective-permute-start | bytes 393224 | tf_op jit(solution)/shard_map/ppermute | solution.py:397
  52.6 2.0 %copy-start.5 = (f32[2,8,8,1024]{3,2,1,0:T(8,128)}, f32[2,8,8,1024]{3,2,1,0:T(8,128)S(1)}, u32[]{:S(2)}) copy-start(f32[2,8,8,1024]{3,2,1,0:T(8,128)S(1)} %collective-permute-done.refs_1_) | copy-start | bytes 1572868
  52.6 11.3 %collective-permute-start.17 = (f32[16,2,8,128]{3,2,1,0:T(8,128)}, f32[16,2,8,128]{3,2,1,0:T(8,128)S(1)}, u32[]{:S(2)}, u32[]{:S(2)}) collective-permute-start(f32[16,2,8,128]{3,2,1,0:T(8,128)} %get-tuple-element.57), channel_id=1, source_target_pairs={{0,24},{4,28},{8,0},{12,4},{16,8},{20,12},{24,16},{28,20},{1,25},{... | collective-permute-start | bytes 393224 | tf_op jit(solution)/shard_map/ppermute | solution.py:397
  54.6 0.8 copy-start.6
  54.6 1.0 copy-start.7
  63.8 4.2 %collective-permute-start.3 = (f32[16,2,2,8,128]{4,3,2,1,0:T(8,128)}, f32[16,2,2,8,128]{4,3,2,1,0:T(8,128)S(1)}, u32[]{:S(2)}, u32[]{:S(2)}) collective-permute-start(f32[16,2,2,8,128]{4,3,2,1,0:T(8,128)} %get-tuple-element.37), channel_id=1, source_target_pairs={{0,4},{4,0},{8,12},{12,8},{16,20},{20,16},{24,28},{28,24},{1,5},{5... | collective-permute-start | bytes 786440 | tf_op jit(solution)/shard_map/ppermute | solution.py:394
  63.9 0.7 copy-start.15
  64.0 0.7 copy-start.16
  64.0 0.7 copy-start.17
  67.6 8.5 %collective-permute-start.18 = (f32[16,2,2,8,128]{4,3,2,1,0:T(8,128)}, f32[16,2,2,8,128]{4,3,2,1,0:T(8,128)S(1)}, u32[]{:S(2)}, u32[]{:S(2)}) collective-permute-start(f32[16,2,2,8,128]{4,3,2,1,0:T(8,128)} %get-tuple-element.59), channel_id=1, source_target_pairs={{0,4},{4,0},{8,12},{12,8},{16,20},{20,16},{24,28},{28,24},{1,5},{5... | collective-permute-start | bytes 786440 | tf_op jit(solution)/shard_map/ppermute | solution.py:394
  68.1 0.7 copy-start.3
  71.4 14.1 %collective-permute-start.4 = (f32[16,2,8,128]{3,2,1,0:T(8,128)}, f32[16,2,8,128]{3,2,1,0:T(8,128)S(1)}, u32[]{:S(2)}, u32[]{:S(2)}) collective-permute-start(f32[16,2,8,128]{3,2,1,0:T(8,128)} %get-tuple-element.40), channel_id=1, source_target_pairs={{0,8},{4,12},{8,16},{12,20},{16,24},{20,28},{24,0},{28,4},{1,9},{5... | collective-permute-start | bytes 393224 | tf_op jit(solution)/shard_map/ppermute | solution.py:397
  72.1 13.3 %collective-permute-start.5 = (f32[16,2,8,128]{3,2,1,0:T(8,128)}, f32[16,2,8,128]{3,2,1,0:T(8,128)S(1)}, u32[]{:S(2)}, u32[]{:S(2)}) collective-permute-start(f32[16,2,8,128]{3,2,1,0:T(8,128)} %get-tuple-element.41), channel_id=1, source_target_pairs={{0,16},{4,20},{8,24},{12,28},{16,0},{20,4},{24,8},{28,12},{1,17},{... | collective-permute-start | bytes 393224 | tf_op jit(solution)/shard_map/ppermute | solution.py:397
  74.7 10.7 %collective-permute-start.6 = (f32[16,2,8,128]{3,2,1,0:T(8,128)}, f32[16,2,8,128]{3,2,1,0:T(8,128)S(1)}, u32[]{:S(2)}, u32[]{:S(2)}) collective-permute-start(f32[16,2,8,128]{3,2,1,0:T(8,128)} %get-tuple-element.42), channel_id=1, source_target_pairs={{0,24},{4,28},{8,0},{12,4},{16,8},{20,12},{24,16},{28,20},{1,25},{... | collective-permute-start | bytes 393224 | tf_op jit(solution)/shard_map/ppermute | solution.py:397
  76.1 0.7 copy-start.13
  84.5 19.5 %collective-permute-start.19 = (f32[2,8,8,1024]{3,2,1,0:T(8,128)}, f32[2,8,8,1024]{3,2,1,0:T(8,128)S(1)}, u32[]{:S(2)}, u32[]{:S(2)}) collective-permute-start(f32[2,8,8,1024]{3,2,1,0:T(8,128)} %get-tuple-element.61), channel_id=1, source_target_pairs={{0,1},{1,0},{2,3},{3,2},{4,5},{5,4},{6,7},{7,6},{8,9},{9,8},{10,11... | collective-permute-start | bytes 1572872 | tf_op jit(solution)/shard_map/ppermute | solution.py:376
  85.4 0.6 copy-start.18
  85.4 0.7 copy-start.19
  86.1 0.6 copy-start.20
  89.6 2.6 %collective-permute-start.7 = (f32[16,2,2,8,128]{4,3,2,1,0:T(8,128)}, f32[16,2,2,8,128]{4,3,2,1,0:T(8,128)S(1)}, u32[]{:S(2)}, u32[]{:S(2)}) collective-permute-start(f32[16,2,2,8,128]{4,3,2,1,0:T(8,128)} %get-tuple-element.44), channel_id=1, source_target_pairs={{0,4},{4,0},{8,12},{12,8},{16,20},{20,16},{24,28},{28,24},{1,5},{5... | collective-permute-start | bytes 786440 | tf_op jit(solution)/shard_map/ppermute | solution.py:394
  89.6 26.2 %collective-permute-start.20 = (f32[2,8,8,1024]{3,2,1,0:T(8,128)}, f32[2,8,8,1024]{3,2,1,0:T(8,128)S(1)}, u32[]{:S(2)}, u32[]{:S(2)}) collective-permute-start(f32[2,8,8,1024]{3,2,1,0:T(8,128)} %get-tuple-element.62), channel_id=1, source_target_pairs={{0,2},{1,3},{2,0},{3,1},{4,6},{5,7},{6,4},{7,5},{8,10},{9,11},{10,... | collective-permute-start | bytes 1572872 | tf_op jit(solution)/shard_map/ppermute | solution.py:376
  90.8 25.1 %collective-permute-start.21 = (f32[2,8,8,1024]{3,2,1,0:T(8,128)}, f32[2,8,8,1024]{3,2,1,0:T(8,128)S(1)}, u32[]{:S(2)}, u32[]{:S(2)}) collective-permute-start(f32[2,8,8,1024]{3,2,1,0:T(8,128)} %get-tuple-element.63), channel_id=1, source_target_pairs={{0,3},{1,2},{2,1},{3,0},{4,7},{5,6},{6,5},{7,4},{8,11},{9,10},{10,... | collective-permute-start | bytes 1572872 | tf_op jit(solution)/shard_map/ppermute | solution.py:376
  92.2 0.7 copy-start.14
  100.5 2.4 %copy-start.11 = (f32[2,8,8,1024]{3,2,1,0:T(8,128)S(1)}, f32[2,8,8,1024]{3,2,1,0:T(8,128)}, u32[]{:S(2)}) copy-start(f32[2,8,8,1024]{3,2,1,0:T(8,128)} %get-tuple-element.60) | copy-start | bytes 1572868
  100.5 21.6 %collective-permute-start.8 = (f32[2,8,8,1024]{3,2,1,0:T(8,128)}, f32[2,8,8,1024]{3,2,1,0:T(8,128)S(1)}, u32[]{:S(2)}, u32[]{:S(2)}) collective-permute-start(f32[2,8,8,1024]{3,2,1,0:T(8,128)} %get-tuple-element.49), channel_id=1, source_target_pairs={{0,1},{1,0},{2,3},{3,2},{4,5},{5,4},{6,7},{7,6},{8,9},{9,8},{10,11... | collective-permute-start | bytes 1572872 | tf_op jit(solution)/shard_map/ppermute | solution.py:376
  101.5 36.4 %collective-permute-start.9 = (f32[2,8,8,1024]{3,2,1,0:T(8,128)}, f32[2,8,8,1024]{3,2,1,0:T(8,128)S(1)}, u32[]{:S(2)}, u32[]{:S(2)}) collective-permute-start(f32[2,8,8,1024]{3,2,1,0:T(8,128)} %get-tuple-element.50), channel_id=1, source_target_pairs={{0,2},{1,3},{2,0},{3,1},{4,6},{5,7},{6,4},{7,5},{8,10},{9,11},{10,... | collective-permute-start | bytes 1572872 | tf_op jit(solution)/shard_map/ppermute | solution.py:376
  102.9 1.0 copy-start.12
  102.9 1.2 copy-start.24
  104.1 33.8 %collective-permute-start.10 = (f32[2,8,8,1024]{3,2,1,0:T(8,128)S(1)}, f32[2,8,8,1024]{3,2,1,0:T(8,128)S(1)}, u32[]{:S(2)}, u32[]{:S(2)}) collective-permute-start(f32[2,8,8,1024]{3,2,1,0:T(8,128)S(1)} %copy-done.24), channel_id=1, source_target_pairs={{0,3},{1,2},{2,1},{3,0},{4,7},{5,6},{6,5},{7,4},{8,11},{9,10},{10,... | collective-permute-start | bytes 1572872 | tf_op jit(solution)/shard_map/ppermute | solution.py:376
  115.9 22.1 %copy-start.1 = (f32[2,8,32,1024]{3,2,1,0:T(8,128)}, f32[2,8,32,1024]{3,2,1,0:T(8,128)S(1)}, u32[]{:S(2)}) copy-start(f32[2,8,32,1024]{3,2,1,0:T(8,128)S(1)} %constant_dynamic-update-slice_fusion) | copy-start | bytes 6291460
  138.0 1.3 copy-start

commit v3 on v2

v3 whole, which is shorter than its diff:
```python
import functools
import math

import jax
import jax.numpy as jnp
import numpy as np
from jax import lax
from jax.experimental import pallas as pl
from jax.experimental.pallas import tpu as pltpu
from jax.sharding import PartitionSpec as P

aspect_ratio = 1.0
LANES = 128
ROWS = 8
VMEM_BYTES = 40 * 1024 * 1024
real_dot = functools.partial(jnp.dot, preferred_element_type=jnp.float32)
exact_dot = functools.partial(lax.dot_general, precision=lax.Precision.HIGHEST, preferred_element_type=jnp.float32)
NN = (((1,), (0,)), ((), ()))
NT = (((1,), (1,)), ((), ()))
in_smem = pl.BlockSpec(memory_space=pltpu.SMEM)
in_vmem = pl.BlockSpec(memory_space=pltpu.VMEM)
params = pltpu.CompilerParams(vmem_limit_bytes=VMEM_BYTES)


def sine_matrix(size):
    turn = np.outer(np.arange(size), np.arange(size)) % (2 * size)
    matrix = np.sin(np.pi * turn / size)
    matrix[0] = 0.0
    matrix[:, 0] = 0.0
    matrix = matrix.astype(np.float32)
    top = matrix.astype(jnp.bfloat16)
    return top, (matrix - top.astype(np.float32)).astype(jnp.bfloat16)


def edge_signs(size):
    lane = np.arange(LANES)
    signs = np.zeros((ROWS, LANES), np.float32)
    signs[0] = 2.0 / size
    signs[1] = np.where(lane % 2 == 1, 2.0 / size, -2.0 / size)
    return signs


def spread_matrix(total):
    lane = np.arange(LANES)
    sign = np.where(lane % 2 == 1, 1.0, -1.0)
    matrix = np.zeros((2, total, total, LANES), np.float32)
    for j in range(total):
        matrix[0, j, j] = 1.0
        matrix[1, j, j] = sign
    return matrix.reshape(2 * total, total * LANES).astype(jnp.bfloat16)


def interface_matrix(waves, count, size):
    classes = waves // 2 + 1
    matrix = np.zeros((classes, waves, 2, 4, count, waves, 4, 2))
    for c in range(classes):
        weight = (1.0 if c in (0, waves // 2) else 2.0) / (size * waves)
        for w in range(waves):
            for e in range(2):
                for v in range(waves):
                    for g in range(2):
                        value = weight * math.cos(2.0 * math.pi * (c * (w + e - v - g) % waves) / waves)
                        for f in range(4):
                            matrix[c, w, e, f, :, v, f, g] = value
    return matrix.reshape(classes * waves * 8, count * waves * 8).astype(np.float32)


def three_parts(values):
    parts = []
    for _ in range(3):
        part = values.astype(jnp.bfloat16)
        values = values - part.astype(jnp.float32)
        parts.append(part)
    return parts


def sine_transform(values, top, rest):
    high = values.astype(jnp.bfloat16)
    low = (values - high.astype(jnp.float32)).astype(jnp.bfloat16)
    return real_dot(high, top) + (real_dot(low, top) + real_dot(high, rest))


def coefficient_kernel(levels, total, place, thick, face, lam, t_out, r_out, m_out, end_out, pair_out, far_out, m_chip, r_chip, f_chip, n_chip, u_chip, down_all, up_all):
    span = 2 * levels
    chips = total // span
    chip = place[0] // 2
    start = chip * span
    shift = lam[...]
    one = jnp.ones_like(shift)
    zero = jnp.zeros_like(shift)

    def down_step(j, f, r):
        m = face[j] * r
        f = shift * thick[j] + m * f
        return m, f, 1.0 / (face[j + 1] + f)

    def up_step(j, phi, s):
        n = face[j + 1] * s
        u = n * phi
        phi = shift * thick[j] + u
        return n, u, phi, 1.0 / (face[j] + phi)

    def down_chip(c, state):
        f, r = state
        product = one
        for i in range(span):
            m, f, r = down_step(c * span + i, f, r)
            t_out[c * span + i] = m
            product = product * m
        down_all[c] = product
        return f, r

    def up_chip(back, state):
        phi, s = state
        c = chips - 1 - back
        product = one
        for i in range(span - 1, -1, -1):
            n, _, phi, s = up_step(c * span + i, phi, s)
            t_out[c * span + i + 1] = n
            product = product * n
        up_all[c] = product
        return phi, s

    f, r = lax.fori_loop(0, chip, down_chip, (one, one))
    for i in range(span):
        m, f, r = down_step(start + i, f, r)
        m_chip[i], f_chip[i], r_chip[i] = m, f, r
    phi, s = lax.fori_loop(0, chips - 1 - chip, up_chip, (zero, zero))
    for i in range(span - 1, -1, -1):
        n, u, phi, s = up_step(start + i, phi, s)
        n_chip[i], u_chip[i] = n, u

    for i in range(levels):
        t_out[start + i] = m_chip[i]
        t_out[start + levels + 1 + i] = n_chip[levels + i]
    upper = place[0] % 2 == 0
    t_out[start + levels] = jnp.where(upper, n_chip[levels - 1], m_chip[levels])
    own = (place[0] % 2) * levels
    for i in range(levels):
        r_out[i] = r_chip[own + i]
        m_out[i] = m_chip[own + i]
    last = own + levels - 1
    end_out[0] = n_chip[last]
    end_out[1] = 1.0 / (f_chip[last] + u_chip[last])
    end_out[2] = f_chip[own] + u_chip[own]
    for core in range(2):
        down, up = m_chip[core * levels], n_chip[core * levels]
        for i in range(1, levels):
            down = down * m_chip[core * levels + i]
            up = up * n_chip[core * levels + i]
        pair_out[core] = down
        pair_out[2 + core] = up
    above, below = [one], [one]
    for apart in range(1, chips - 1):
        above.append(above[-1] * jnp.where(chip >= apart, down_all[jnp.maximum(chip - apart, 0)], one))
        below.append(below[-1] * jnp.where(chip + apart < chips, up_all[jnp.minimum(chip + apart, chips - 1)], one))
    for apart in range(1, chips):
        far_out[apart - 1] = jnp.where(chip >= apart, above[apart - 1], below[chips - apart - 1])


def coefficients(place, thick, face, lam, levels):
    ky, size = lam.shape
    total = thick.shape[0]
    chips = total // (2 * levels)
    group = min(2 * ROWS, ky)
    tall = lambda n: pl.BlockSpec((n, group, size), lambda g: (0, g, 0))
    sizes = (total + 1, levels, levels, 3, 4, chips - 1)
    scratch = lambda n: pltpu.VMEM((n, group, size), jnp.float32)
    return pl.pallas_call(
        functools.partial(coefficient_kernel, levels, total),
        grid=(ky // group,),
        in_specs=[in_smem, in_smem, in_smem, pl.BlockSpec((group, size), lambda g: (g, 0))],
        out_specs=[tall(n) for n in sizes],
        out_shape=[jax.ShapeDtypeStruct((n, ky, size), jnp.float32) for n in sizes],
        scratch_shapes=[scratch(2 * levels)] * 5 + [scratch(chips)] * 2,
        compiler_params=params,
        name="coefficients",
    )(place, thick, face, lam)


def lane_sum(values):
    tiles = [values[:, t * LANES:(t + 1) * LANES] for t in range(values.shape[1] // LANES)]
    while len(tiles) > 1:
        tiles = [a + b for a, b in zip(tiles[0::2], tiles[1::2])]
    return tiles[0]


def forward_kernel(total, place, before, share, x, top, rest, sines, signs, heights, t, r, m, end, b_out, keep_out, give_out, edge_out, c_all, z_all, sums):
    _, levels, ky, size = x.shape
    first = place[0] * levels
    half = ky // 2
    b = sine_transform(x[0].reshape(levels * ky, size), top[...], rest[...]).reshape(levels, ky, size)
    for j in range(levels):
        b_out[0, j] = b[j] * before[j]
    lane = lax.broadcasted_iota(jnp.int32, (ROWS, LANES), 1)
    spot = jnp.where((lane == 1) | (lane == 2), size / 4.0, 0.0)

    def tile(g, _):
        here = pl.ds(pl.multiple_of(g * ROWS, ROWS), ROWS)
        wave = sines[...]
        y = b_out[0, 0, here]
        ys = [y]
        for j in range(1, levels):
            y = b_out[0, j, here] + m[j, here] * y
            ys.append(y)
        c_all[0, here] = y
        value = y * end[1, here]
        z_all[1, here] = value * wave
        for j in range(levels - 1, -1, -1):
            if j < levels - 1:
                value = r[j, here] * ys[j] + m[j + 1, here] * value
            own = jnp.broadcast_to(x[0, j, here, 0:1], (ROWS, LANES)) * (spot * share[j])
            sums[pl.ds(g * ROWS * total + first + j, ROWS, stride=total), :] = lane_sum(value * wave) + own
        z_all[0, here] = value * wave
        c_all[1, here] = value * end[2, here]
        return 0

    lax.fori_loop(0, ky // ROWS, tile, 0)

    def reach_up(back, z):
        j = first - 1 - back
        z = t[j + 1] * z
        sums[pl.ds(j, ky, stride=total), :] = lane_sum(z)
        return z

    def reach_down(ahead, z):
        j = first + levels + ahead
        z = t[j] * z
        sums[pl.ds(j, ky, stride=total), :] = lane_sum(z)
        return z

    lax.fori_loop(0, first, reach_up, z_all[0])
    lax.fori_loop(0, total - levels - first, reach_down, z_all[1])
    edges = exact_dot(signs[...], sums[...], NT)
    edge_out[0] = (edges * heights[...])[:2]
    core = place[0] % 2
    keep_out[:, 0] = c_all[:, pl.ds(pl.multiple_of(core * half, ROWS), half)]
    give_out[:, 0] = c_all[:, pl.ds(pl.multiple_of((1 - core) * half, ROWS), half)]


def forward(place, x, before, share, heights, sines, t, r, m, end):
    _, levels, ky, size = x.shape
    total = t.shape[0] - 1
    top, rest = sine_matrix(size)
    half = (2, 2, ky // 2, size)
    half_spec = pl.BlockSpec((2, 1, ky // 2, size), lambda i: (0, i, 0, 0))
    field = pl.BlockSpec((1, levels, ky, size), lambda i: (i, 0, 0, 0))
    return pl.pallas_call(
        functools.partial(forward_kernel, total),
        grid=(2,),
        in_specs=[in_smem, in_smem, in_smem, field] + [in_vmem] * 9,
        out_specs=[field, half_spec, half_spec, pl.BlockSpec((1, 2, ky * total), lambda i: (i, 0, 0))],
        out_shape=[
            jax.ShapeDtypeStruct(x.shape, jnp.float32),
            jax.ShapeDtypeStruct(half, jnp.float32),
            jax.ShapeDtypeStruct(half, jnp.float32),
            jax.ShapeDtypeStruct((2, 2, ky * total), jnp.float32),
        ],
        scratch_shapes=[
            pltpu.VMEM((2, ky, size), jnp.float32),
            pltpu.VMEM((2, ky, size), jnp.float32),
            pltpu.VMEM((ky * total, LANES), jnp.float32),
        ],
        compiler_params=params,
        name="forward",
    )(place, before, share, x, top, rest, sines, edge_signs(size), heights, t, r, m, end)


def chip_kernel(chips, place, keep, got, pair, *outs):
    chip = place[0] // 2
    upper = place[0] % 2 == 0
    first, second = jnp.where(upper, keep[...], got[...]), jnp.where(upper, got[...], keep[...])
    down = second[0] + pair[1] * first[0]
    up = first[1] + pair[2] * second[1]
    for apart in range(1, chips):
        outs[apart - 1][...] = jnp.where(chip + apart < chips, down, up)


def chip_sums(place, keep, got, pair, chips):
    _, _, half, size = keep.shape
    full = pl.BlockSpec(keep.shape, lambda i, place: (0,) * keep.ndim)
    shape = (2, half, size)
    return pl.pallas_call(
        functools.partial(chip_kernel, chips),
        grid_spec=pltpu.PrefetchScalarGridSpec(
            num_scalar_prefetch=1,
            grid=(1,),
            in_specs=[full, full, pl.BlockSpec((4, half, size), lambda i, place: (0, place[0] % 2, 0))],
            out_specs=[pl.BlockSpec(shape, lambda i, place: (0, 0, 0))] * (chips - 1),
        ),
        out_shape=[jax.ShapeDtypeStruct(shape, jnp.float32)] * (chips - 1),
        compiler_params=params,
        name="chip_sums",
    )(place, keep, got, pair)


def join_kernel(chips, place, keep, got, pair, far, *refs):
    news = refs[:chips - 1]
    mine, theirs = refs[chips - 1:]
    chip = place[0] // 2
    upper = place[0] % 2 == 0
    first, second = jnp.where(upper, keep[...], got[...]), jnp.where(upper, got[...], keep[...])
    down = jnp.zeros(first.shape[1:], jnp.float32)
    up = down
    for apart in range(1, chips):
        term = far[apart - 1] * news[apart - 1][...]
        down = down + jnp.where(chip >= apart, term, 0.0)
        up = up + jnp.where(chip >= apart, 0.0, term)
    inner_up = second[1] + pair[3] * up
    inner_down = first[0] + pair[0] * down
    mine[0] = jnp.where(upper, down, inner_down)
    mine[1] = jnp.where(upper, inner_up, up)
    theirs[0] = jnp.where(upper, inner_down, down)
    theirs[1] = jnp.where(upper, up, inner_up)


def join(place, keep, got, pair, far, news):
    _, _, half, size = keep.shape
    chips = len(news) + 1
    full = lambda a: pl.BlockSpec(a.shape, lambda i, place: (0,) * a.ndim)
    part = lambda n: pl.BlockSpec((n, half, size), lambda i, place: (0, place[0] % 2, 0))
    return pl.pallas_call(
        functools.partial(join_kernel, chips),
        grid_spec=pltpu.PrefetchScalarGridSpec(
            num_scalar_prefetch=1,
            grid=(1,),
            in_specs=[full(keep), full(got), part(4), part(chips - 1), *[full(a) for a in news]],
            out_specs=[full(keep)] * 2,
        ),
        out_shape=[jax.ShapeDtypeStruct(keep.shape, jnp.float32)] * 2,
        compiler_params=params,
        name="join",
    )(place, keep, got, pair, far, *news)


def inverse_kernel(per, thick, face, lam, out, m_all, f_all, g_all):
    total = f_all.shape[0]
    rows = lam.shape[0]
    classes = out.shape[0]
    shift = lam[...]
    one = jnp.ones_like(shift)
    zero = jnp.zeros_like(shift)

    def step(j, state):
        f, r, phi, s = state
        m = face[j] * r
        f = shift * thick[j] + m * f
        r = 1.0 / (face[j + 1] + f)
        m_all[j] = m
        f_all[j] = f
        i = total - 1 - j
        u = face[i + 1] * s * phi
        phi = shift * thick[i] + u
        s = 1.0 / (face[i] + phi)
        g_all[i] = u
        return f, r, phi, s

    lax.fori_loop(0, total, step, (one, one, zero, zero))

    def centre(j, _):
        g_all[j] = 1.0 / (f_all[j] + g_all[j])
        return 0

    lax.fori_loop(0, total, centre, 0)
    wide = out.shape[2]
    sub = lax.broadcasted_iota(jnp.int32, (ROWS, LANES), 0)
    lane = lax.broadcasted_iota(jnp.int32, (ROWS, wide), 1)
    row = lax.broadcasted_iota(jnp.int32, (ROWS, wide), 0)
    line = lambda ref, j, t: jnp.broadcast_to(ref[j, t:t + 1, :], (ROWS, LANES))

    def put(j, z, sums):
        new = []
        for c in range(classes):
            tiles = z[c * per:(c + 1) * per]
            total_tile = tiles[0]
            for tile in tiles[1:]:
                total_tile = total_tile + tile
            value = jnp.sum(total_tile, axis=1, keepdims=True)
            new.append(jnp.where(lane == j, value, sums[c]))
        return new

    for base in range(0, total, ROWS):
        z = [jnp.zeros((ROWS, LANES), jnp.float32)] * (classes * per)
        sums = [jnp.zeros((ROWS, wide), jnp.float32)] * classes
        for i in range(ROWS - 1, -1, -1):
            j = base + i
            for t in range(classes * per):
                moved = z[t] * line(m_all, j + 1, t) if i < ROWS - 1 else z[t]
                z[t] = jnp.where(sub == i, line(g_all, j, t), moved)
            sums = put(j, z, sums)

        def above(back, state):
            z, sums = state
            j = base - 1 - back
            z = [z[t] * line(m_all, j + 1, t) for t in range(classes * per)]
            return z, put(j, z, sums)

        if base:
            z, sums = lax.fori_loop(0, base, above, (z, sums))
        for c in range(classes):
            out[c, base:base + ROWS, :] = sums[c] * jnp.where(lane == base + row, 0.5, 1.0)


def inverse_sums(thick, face, lam, per):
    total = thick.shape[0]
    classes = lam.shape[0] // per
    wide = -(-total // LANES) * LANES
    spare = -lam.shape[0] % ROWS
    lam = jnp.pad(lam, ((0, spare), (0, 0)), constant_values=1.0)
    return pl.pallas_call(
        functools.partial(inverse_kernel, per),
        in_specs=[in_smem, in_smem, in_vmem],
        out_shape=jax.ShapeDtypeStruct((classes, total, wide), jnp.float32),
        scratch_shapes=[pltpu.VMEM((total,) + lam.shape, jnp.float32)] * 3,
        compiler_params=params,
        name="inverse_sums",
    )(thick, face, lam)


def interface_kernel(matrix, edges, inverse, out):
    total = edges.shape[1]
    rows = out.shape[0]
    mixed = exact_dot(matrix[...], edges[...], NN)
    result = jnp.zeros((rows, total), jnp.float32)
    for c in range(inverse.shape[0]):
        part = mixed[c * rows:(c + 1) * rows]
        square = inverse[c][:, :total]
        result = result + (exact_dot(part, square, NN) + exact_dot(part, square, NT))
    out[...] = result


def interface(edges, inverse, waves, count, size):
    return pl.pallas_call(
        interface_kernel,
        in_specs=[in_vmem] * 3,
        out_shape=jax.ShapeDtypeStruct((waves * 8, edges.shape[1]), jnp.float32),
        compiler_params=params,
        name="interface",
    )(interface_matrix(waves, count, size), edges, inverse)


def backward_kernel(total, place, thick, after, b, edges, spread, mine, theirs, top, rest, sines, t, r, m, end, out, ends, u_all, q_all):
    _, levels, ky, size = b.shape
    first = place[0] * levels
    half = ky // 2
    core = place[0] % 2
    many = size // LANES
    ends[:, pl.ds(pl.multiple_of(core * half, ROWS), half)] = mine[:, 0]
    ends[:, pl.ds(pl.multiple_of((1 - core) * half, ROWS), half)] = theirs[:, 0]
    near = sum(real_dot(part, spread[...]) for part in three_parts(edges[0]))
    for j in range(total):
        u_all[j] = near[:, j * LANES:(j + 1) * LANES]

    def source(j):
        return jnp.concatenate([u_all[j] * thick[j]] * many, 1)

    def from_above(j, y):
        return t[j] * y + source(j)

    def from_below(back, y):
        j = total - 1 - back
        return t[j + 1] * y + source(j)

    zero = jnp.zeros((ky, size), jnp.float32)
    ends[0] += sines[...][:1] * lax.fori_loop(0, first, from_above, zero)
    ends[1] += sines[...][:1] * lax.fori_loop(0, total - levels - first, from_below, zero)

    def tile(g, _):
        here = pl.ds(pl.multiple_of(g * ROWS, ROWS), ROWS)
        wave = sines[...]
        y = ends[0, here]
        ys = []
        for j in range(levels):
            own = jnp.concatenate([u_all[first + j, here] * thick[first + j]] * many, 1)
            y = b[0, j, here] + wave * own + m[j, here] * y
            ys.append(y)
        value = (y + end[0, here] * ends[1, here]) * end[1, here]
        q_all[levels - 1, here] = value
        for j in range(levels - 2, -1, -1):
            value = r[j, here] * ys[j] + m[j + 1, here] * value
            q_all[j, here] = value
        return 0

    lax.fori_loop(0, ky // ROWS, tile, 0)
    field = sine_transform(q_all[...].reshape(levels * ky, size), top[...], rest[...]).reshape(levels, ky, size)
    lane = lax.broadcasted_iota(jnp.int32, (ky, LANES), 1)
    for j in range(levels):
        u = u_all[first + j]
        here = 0.5 * (u + pltpu.roll(u, 1, 1))
        value = field[j] * ((2.0 / size) * after[j])
        out[0, j] = value
        out[0, j, :, :LANES] = jnp.where(lane == 0, here * after[j], value[:, :LANES])


def backward(place, thick, after, b, edges, mine, theirs, sines, t, r, m, end):
    _, levels, ky, size = b.shape
    total = t.shape[0] - 1
    top, rest = sine_matrix(size)
    half_spec = pl.BlockSpec((2, 1, ky // 2, size), lambda i: (0, i, 0, 0))
    field = pl.BlockSpec((1, levels, ky, size), lambda i: (i, 0, 0, 0))
    return pl.pallas_call(
        functools.partial(backward_kernel, total),
        grid=(2,),
        in_specs=[in_smem, in_smem, in_smem, field, pl.BlockSpec((1, ky, 2 * total), lambda i: (i, 0, 0)), in_vmem, half_spec, half_spec]
        + [in_vmem] * 7,
        out_specs=field,
        out_shape=jax.ShapeDtypeStruct(b.shape, jnp.float32),
        scratch_shapes=[
            pltpu.VMEM((2, ky, size), jnp.float32),
            pltpu.VMEM((total, ky, LANES), jnp.float32),
            pltpu.VMEM((levels, ky, size), jnp.float32),
        ],
        compiler_params=params,
        name="backward",
    )(place, thick, after, b, edges, spread_matrix(total), mine, theirs, top, rest, sines, t, r, m, end)


def shards(rhs, cotangent, thickness, ky_shift):
    waves = lax.axis_size("wave")
    count = lax.axis_size("depth")
    depth_pos = lax.axis_index("depth")
    wave_pos = lax.axis_index("wave")
    _, levels, ky, size = rhs.shape
    total = thickness.shape[0]
    full = waves * size
    devices = waves * count
    chips = count // 2
    everyone = ("depth", "wave")
    place = depth_pos.astype(jnp.int32).reshape(1)

    def across(a):
        return lax.ppermute(a, "depth", [(d, d ^ 1) for d in range(count)])

    def along(a, apart):
        return lax.ppermute(a, "depth", [(d, (d + 2 * apart) % count) for d in range(count)])

    def everywhere(a):
        return lax.all_to_all(a, everyone, split_axis=0, concat_axis=0, tiled=True)

    def horizontal(wavenumber, length):
        return aspect_ratio * 4.0 * jnp.sin(math.pi * jnp.asarray(wavenumber, jnp.float32) / length) ** 2

    inner_face = 2.0 / (thickness[:-1] + thickness[1:])
    face = jnp.concatenate([2.0 / thickness[:1], inner_face, jnp.zeros((1,), jnp.float32)])
    lam = ky_shift[:, None] + horizontal(np.arange(size), 2 * size)[None, :]
    t, r, m, end, pair, far = coefficients(place, thickness, face, lam, levels)
    thick_here = lax.dynamic_slice_in_dim(thickness, depth_pos * levels, levels)
    even = jnp.ones_like(thick_here)
    sines = jnp.asarray(np.broadcast_to(np.sin(np.pi * np.arange(size) / size)[None, :], (ROWS, size)), jnp.float32)
    heights = jnp.tile(thickness, ky).reshape(1, ky * total)

    share = -(-ky // devices)
    padded = share * devices - ky
    classes = waves // 2 + 1
    wavenumber = (np.arange(classes)[:, None] + waves * np.arange(size)[None, :]).reshape(-1, LANES)
    my_shifts = lax.dynamic_slice_in_dim(
        jnp.pad(ky_shift, (0, padded), constant_values=1.0), (depth_pos * waves + wave_pos) * share, share
    )
    across_k = horizontal(wavenumber, full)

    def start(field, before, ratio):
        b, keep, give, edges = forward(place, field, before, ratio, heights, sines, t, r, m, end)
        return b, keep, across(give), edges

    def middle(keep, got):
        sums = chip_sums(place, keep, got, pair, chips)
        news = [along(sums[apart - 1], apart) for apart in range(1, chips)]
        mine, theirs = join(place, keep, got, pair, far, news)
        return mine, across(theirs)

    b0, keep0, got0, edges0 = start(rhs, thick_here, even)
    b1, keep1, got1, edges1 = start(cotangent, even, 1.0 / thick_here)
    edges = jnp.concatenate([edges0, edges1]).reshape(4, 2, ky, total).transpose(2, 0, 1, 3)
    edges = jnp.pad(edges, ((0, padded), (0, 0), (0, 0), (0, 0)))
    edges = everywhere(edges.reshape(devices, share, 8, total))
    inverse = [inverse_sums(thickness, face, my_shifts[a] + across_k, size // LANES) for a in range(share)]
    mine0, theirs0 = middle(keep0, got0)
    mine1, theirs1 = middle(keep1, got1)
    values = [interface(edges[:, a].reshape(devices * 8, total), inverse[a], waves, count, size) for a in range(share)]
    values = jnp.stack(values, 0).reshape(1, share, waves, 8, total).transpose(0, 2, 1, 3, 4)
    values = jnp.broadcast_to(values, (count, waves, share, 8, total)).reshape(devices, share, 8, total)
    values = everywhere(values).reshape(devices * share, 2, 4, total)[:ky]
    values = values.transpose(2, 0, 1, 3).reshape(4, ky, 2 * total)
    tables = (sines, t, r, m, end)
    pressure = backward(place, thickness, even, b0, values[:2], mine0, theirs0, *tables)
    adjoint = backward(place, thickness, thick_here, b1, values[2:], mine1, theirs1, *tables)
    return pressure, adjoint


def solution(mesh):
    spec = P(None, "depth", None, "wave")
    return jax.shard_map(shards, mesh=mesh, in_specs=(spec, spec, P(), P()), out_specs=(spec, spec), check_vma=False)
```

time: 140 us -> 175 us (1.25)
  local copies, waits for them, and re-layouts: 14.2 us -> 54.7 us
  waiting for transfers between devices: 39.3 us -> 0.03 us
  Pallas kernels: 53.2 us -> 86.3 us
  starting transfers between devices: 28.9 us -> 21.6 us
  other arithmetic: 2.61 us -> 9.22 us
    pallas_call x5 -> x7, Pallas kernels: 42.3 us -> 79.9 us  [the longest x2 26.8 us: backward(): pl.pallas_call(functools.partial(backward_kernel, total), grid=(2,), in_s...]
    ppermute x12 -> x0, waiting for transfers between devices: 37.6 us -> none  [exchange(): lax.ppermute(blocks[s], 'wave', turns[s])]
    unnamed x52 -> x98, local copies, waits for them, and re-layouts: 7.85 us -> 41.4 us
    ppermute x12 -> x0, starting transfers between devices: 18 us -> none  [exchange(): lax.ppermute(blocks[s], 'wave', turns[s])]
    all_to_all x0 -> x2, starting transfers between devices: none -> 8.93 us  [everywhere(): return lax.all_to_all(a, everyone, split_axis=0, concat_axis=0, tiled=True)]
    slice x0 -> x5, local copies, waits for them, and re-layouts: none -> 5.94 us  [the longest x2 3.07 us: shards(): values[:2]]
    all_to_all x0 -> x2, other arithmetic: none -> 4.37 us  [everywhere(): return lax.all_to_all(a, everyone, split_axis=0, concat_axis=0, tiled=True)]
    dynamic_slice x3 -> x1, local copies, waits for them, and re-layouts: 4.29 us -> 1.24 us  [shards(): lax.dynamic_slice_in_dim(jnp.pad(ky_shift, (0, padded), constant_values=1...]
  transfers between devices with their start and end apart: 22 -> 12, of which waited for: 5 -> 0; matrix products, arithmetic and copies ran while one was open for 4% -> 15% of each run, Pallas kernels for 38% -> 32%
where the time goes in v3:
time: 175 us; the launch traced here: 173 us
  Pallas kernels  86.3 us (49%)
  local copies, waits for them, and re-layouts  54.7 us (31%)
  starting transfers between devices  21.6 us (12%)
  other arithmetic  9.22 us (5%)
    unnamed x98, local copies, waits for them, and re-layouts  41.4 us
    pallas_call x2, Pallas kernels, backward(): pl.pallas_call(functools.partial(backward_kernel, total), grid=(2,), in_s...  26.8 us
    pallas_call x2, Pallas kernels, forward(): pl.pallas_call(functools.partial(forward_kernel, total), grid=(2,), in_sp...  25.1 us
    pallas_call x1, Pallas kernels, inverse_sums(): pl.pallas_call(functools.partial(inverse_kernel, per), in_specs=[in_smem,...  23 us
    ppermute x6, starting transfers between devices, along(): lax.ppermute(a, 'depth', [(d, (d + 2 * apart) % count) for d in range(cou...  11.6 us
    all_to_all x2, starting transfers between devices, everywhere(): return lax.all_to_all(a, everyone, split_axis=0, concat_axis=0, tiled=True)  8.93 us
    pallas_call x1, Pallas kernels, coefficients(): pl.pallas_call(functools.partial(coefficient_kernel, levels, total), grid...  4.41 us
    all_to_all x2, other arithmetic, everywhere(): return lax.all_to_all(a, everyone, split_axis=0, concat_axis=0, tiled=True)  4.37 us
  transfers between devices with their start and end apart: 12, of which 0 were waited for; matrix products, arithmetic and copies ran while one was open for 15% of the time, Pallas kernels for 32%

profile of v3, /device:TPU:0, one launch (start us, length us, event | category | flops | bytes accessed | tf_op | source)
XLA Modules:
  0.0 173.3 jit_solution(5741052589646539593)
XLA Ops:
  0.7 0.8 add_divide_fusion
  1.5 1.2 broadcast_divide_fusion
  4.2 0.7 broadcast_add_fusion.lam
  5.7 4.4 %coefficients.1 = (f32[65,32,1024]{2,1,0:T(8,128)S(1)}, f32[8,32,1024]{2,1,0:T(8,128)S(1)}, f32[8,32,1024]{2,1,0:T(8,128)S(1)}, f32[3,32,1024]{2,1,0:T(8,128)S(1...) custom-call(s32[1]{0:T(128)} %bitcast.place, f32[64]{0:T(128)S(1)} %copy-done.39, ...), custom_call_target="tpu_custom_call" | custom-call | tf_op jit(solution)/shard_map/coefficients/pallas_call | solution.py:169
  10.1 3.4 %copy-done = f32[65,32,1024]{2,1,0:T(8,128)} copy-done((f32[65,32,1024]{2,1,0:T(8,128)}, f32[65,32,1024]{2,1,0:T(8,128)S(1)}, u32[]{:S(2)}) %copy-start) | copy-done | bytes 8519704
  13.4 0.8 copy-done.18
  14.2 2.1 %copy-done.1 = bf16[1024,1024]{1,0:T(8,128)(2,1)S(1)} copy-done((bf16[1024,1024]{1,0:T(8,128)(2,1)S(1)}, bf16[1024,1024]{1,0:T(8,128)(2,1)}, u32[]{:S(2)}) %copy-start.1) | copy-done | bytes 2097176
  16.4 1.6 copy-done.3
  18.0 1.6 copy-done.16
  19.5 0.8 copy-done.27
  20.3 0.7 copy-done.41
  21.7 12.3 %forward.3 = (f32[2,8,32,1024]{3,2,1,0:T(8,128)S(1)}, f32[2,2,16,1024]{3,2,1,0:T(8,128)S(1)}, f32[2,2,16,1024]{3,2,1,0:T(8,128)S(1)}, f32[2,2,2048]{2,1,0:T(2,128)S(1)}) custom-call(s32[1]{0:T(128)} %bitcast.place, f32[8]{0:T(128)S(1)} %broadcast_1_share_before_after.2.share.before.after, f32[8]{0:T(128)S(1)} %copy-done.44, ...), custom_call_target="tpu_custom_call" | custom-call | tf_op jit(solution)/shard_map/forward/pallas_call | solution.py:248
  33.9 1.3 copy-done.14
  35.7 12.8 %forward.2 = (f32[2,8,32,1024]{3,2,1,0:T(8,128)S(1)}, f32[2,2,16,1024]{3,2,1,0:T(8,128)S(1)}, f32[2,2,16,1024]{3,2,1,0:T(8,128)}, f32[2,2,2048]{2,1,0:T(2,128)S(1)}) custom-call(s32[1]{0:T(128)} %bitcast.place, f32[8]{0:T(128)S(1)} %get-tuple-element.51.before.after, f32[8]{0:T(128)S(1)} %broadcast_1_share_before_after.2.share.before.after, ...), custom_call_target="tpu_custom_call" | custom-call | tf_op jit(solution)/shard_map/forward/pallas_call | solution.py:248
  48.5 1.3 copy-done.12
  49.9 0.8 chip_sums.3
  50.7 3.1 %collective-permute-start.6 = (f32[2,16,1024]{2,1,0:T(8,128)}, f32[2,16,1024]{2,1,0:T(8,128)}, u32[]{:S(2)}, u32[]{:S(2)}) collective-permute-start(f32[2,16,1024]{2,1,0:T(8,128)} %get-tuple-element.45), channel_id=1, source_target_pairs={{0,8},{4,12},{8,16},{12,20},{16,24},{20,28},{24,0},{28,4},{1,9},{5... | collective-permute-start | bytes 393224 | tf_op jit(solution)/shard_map/ppermute | solution.py:535
  54.5 1.6 reshape.30
  56.1 1.7 copy.27
  57.8 1.6 reshape.33
  59.4 5.0 %all-to-all-start = ((f32[32,1,512]{2,1,0:T(1,128)}), f32[32,1,512]{2,1,0:T(1,128)}, u32[]{:S(2)}, u32[]{:S(2)}) async-start(f32[32,1,512]{2,1,0:T(1,128)} %reshape.33), calls=%async_computation | async-start | bytes 131072 | tf_op jit(solution)/shard_map/all_to_all | solution.py:538
  64.5 1.2 dynamic_slice.7
  65.7 2.6 %collective-permute-start.7 = (f32[2,16,1024]{2,1,0:T(8,128)}, f32[2,16,1024]{2,1,0:T(8,128)}, u32[]{:S(2)}, u32[]{:S(2)}) collective-permute-start(f32[2,16,1024]{2,1,0:T(8,128)} %copy-done.46), channel_id=1, source_target_pairs={{0,16},{4,20},{8,24},{12,28},{16,0},{20,4},{24,8},{28,12},{1,17},{... | collective-permute-start | bytes 393224 | tf_op jit(solution)/shard_map/ppermute | solution.py:535
  68.3 1.5 collective-permute-start.8
  69.8 1.0 copy-done.10
  70.8 0.9 copy-done.21
  71.8 1.7 %chip_sums.2 = (f32[2,16,1024]{2,1,0:T(8,128)}, f32[2,16,1024]{2,1,0:T(8,128)}, f32[2,16,1024]{2,1,0:T(8,128)}) custom-call(s32[1]{0:T(128)} %bitcast.place, f32[2,2,16,1024]{3,2,1,0:T(8,128)S(1)} %copy-done.21, f32[2,2,16,1024]{3,2,1,0:T(8,128)} %collective-permute-done.got, f32[4,32,1024]{2,1,0:T(8,128)S(1)} %copy-done.10), custom_call_target="tpu_custom_call" | custom-call | tf_op jit(solution)/shard_map/chip_sums/pallas_call | solution.py:283
  74.1 0.9 collective-permute-start.2
  75.0 2.9 %collective-permute-start.3 = (f32[2,16,1024]{2,1,0:T(8,128)}, f32[2,16,1024]{2,1,0:T(8,128)}, u32[]{:S(2)}, u32[]{:S(2)}) collective-permute-start(f32[2,16,1024]{2,1,0:T(8,128)} %get-tuple-element.39), channel_id=1, source_target_pairs={{0,24},{4,28},{8,0},{12,4},{16,8},{20,12},{24,16},{28,20},{1,25},{... | collective-permute-start | bytes 393224 | tf_op jit(solution)/shard_map/ppermute | solution.py:535
  78.0 1.3 broadcast_add_fusion.1.lam
  79.2 23.0 %inverse_sums.1.inverse = f32[3,64,128]{2,1,0:T(8,128)S(1)} custom-call(f32[64]{0:T(128)S(1)} %copy-done.40, f32[65]{0:T(128)S(1)} %copy-done.43, f32[24,128]{1,0:T(8,128)S(1)} %broadcast_add_fusion.1.lam), custom_call_target="tpu_custom_call" | custom-call | tf_op jit(solution)/shard_map/inverse_sums/pallas_call | solution.py:410
  103.4 2.2 %reduce = f32[32,512]{1,0:T(8,128)} reduce(f32[32,1,512]{2,1,0:T(1,128)} %all-to-all-done, f32[]{:T(128)} %broadcast.11), dimensions={1}, to_apply=%all_to_all.6.reduce_sub_computation | reduce | bytes 131076 | tf_op jit(solution)/shard_map/all_to_all | solution.py:538
  105.6 1.6 reshape.34
  107.1 0.9 copy-done.29
  108.0 0.9 copy-done.31
  108.9 0.9 copy-done.38
  109.8 0.7 interface.1
  111.2 1.7 reshape.35
  112.8 3.9 %all-to-all-start.1 = ((f32[32,1,512]{2,1,0:T(1,128)}), f32[32,1,512]{2,1,0:T(1,128)}, u32[]{:S(2)}, u32[]{:S(2)}) async-start(f32[32,1,512]{2,1,0:T(1,128)} %reshape.35), calls=%async_computation.1 | async-start | bytes 131072 | tf_op jit(solution)/shard_map/all_to_all | solution.py:538
  116.8 1.0 copy-done.11
  117.8 1.0 copy-done.19
  118.8 0.9 copy-done.24
  119.7 0.9 copy-done.26
  120.7 1.9 %join.3 = (f32[2,2,16,1024]{3,2,1,0:T(8,128)S(1)}, f32[2,2,16,1024]{3,2,1,0:T(8,128)}) custom-call(s32[1]{0:T(128)} %bitcast.place, f32[2,2,16,1024]{3,2,1,0:T(8,128)S(1)} %copy-done.24, f32[2,2,16,1024]{3,2,1,0:T(8,128)S(1)} %copy-done.26, f32[4,32,1024]{2,1,0:T(8,128)S(1)} %copy-done.11, f32[3,32,1024]{2,1,0:T(8,128)S(1)} %copy-done.19, ...), custom_call_target="tpu_custom_call" | custom-call | tf_op jit(solution)/shard_map/join/pallas_call | solution.py:322
  122.6 0.7 copy-done.32
  123.3 0.9 copy-done.22
  124.2 1.9 %join.2 = (f32[2,2,16,1024]{3,2,1,0:T(8,128)S(1)}, f32[2,2,16,1024]{3,2,1,0:T(8,128)}) custom-call(s32[1]{0:T(128)} %bitcast.place, f32[2,2,16,1024]{3,2,1,0:T(8,128)S(1)} %copy-done.22, f32[2,2,16,1024]{3,2,1,0:T(8,128)} %collective-permute-done.got, f32[4,32,1024]{2,1,0:T(8,128)S(1)} %copy-done.11, f32[3,32,1024]{2,1,0:T(8,128)S(1)} %copy-done.19, ...), custom_call_target="tpu_custom_call" | custom-call | tf_op jit(solution)/shard_map/join/pallas_call | solution.py:322
  126.2 0.7 copy-done.34
  127.4 2.2 %reduce.1 = f32[32,512]{1,0:T(8,128)} reduce(f32[32,1,512]{2,1,0:T(1,128)} %all-to-all-done.1, f32[]{:T(128)} %broadcast.11), dimensions={1}, to_apply=%all_to_all.7.reduce_sub_computation | reduce | bytes 131076 | tf_op jit(solution)/shard_map/all_to_all | solution.py:538
  129.6 1.6 reshape.36
  131.1 0.9 copy.28
  132.7 0.7 copy.30
  133.4 1.5 slice.27.edges
  134.9 1.5 copy.29
  136.5 1.6 slice.25.edges
  138.0 1.6 copy-done.5
  139.6 1.2 copy-done.7
  140.8 1.6 copy-done.8
  142.4 1.6 copy-done.15
  144.0 0.8 copy-done.28
  144.8 0.9 copy-done.33
  145.7 0.8 copy-done.37
  146.5 13.5 %backward.3 = f32[2,8,32,1024]{3,2,1,0:T(8,128)} custom-call(s32[1]{0:T(128)} %bitcast.place, f32[64]{0:T(128)S(1)} %copy-done.40, f32[8]{0:T(128)S(1)} %get-tuple-element.51.before.after, f32[2,8,32,1024]{3,2,1,0:T(8,128)S(1)} %copy-done.15, f32[2,32,128]{2,1,0:T(8,128)S(1)} %copy-done.37, bf16[128,8192]{1,0:T(8,128)(2,1)S(1)} %copy-done.8, ...), custom_call_target="tpu_custom_call" | custom-call | tf_op jit(solution)/shard_map/backward/pallas_call | solution.py:501
  160.0 13.3 %backward.2 = f32[2,8,32,1024]{3,2,1,0:T(8,128)} custom-call(s32[1]{0:T(128)} %bitcast.place, f32[64]{0:T(128)S(1)} %copy-done.40, f32[8]{0:T(128)S(1)} %broadcast_1_share_before_after.2.share.before.after, f32[2,8,32,1024]{3,2,1,0:T(8,128)S(1)} %copy-done.13, f32[2,32,128]{2,1,0:T(8,128)S(1)} %copy-done.36, bf16[128,8192]{1,0:T(8,128)(2,1)S(1)} %copy-done.8, ...), custom_call_target="tpu_custom_call" | custom-call | tf_op jit(solution)/shard_map/backward/pallas_call | solution.py:501
  (92 shorter events, 7.0 us)
Async XLA Ops:
  5.0 9.2 %copy-start.42 = (f32[65]{0:T(128)}, f32[65]{0:T(128)S(1)}, u32[]{:S(2)}) copy-start(f32[65]{0:T(128)S(1)} %pad_maximum_fusion.1.face) | copy-start | bytes 784
  5.0 0.7 copy-start.39
  10.1 3.4 %copy-start = (f32[65,32,1024]{2,1,0:T(8,128)}, f32[65,32,1024]{2,1,0:T(8,128)S(1)}, u32[]{:S(2)}) copy-start(f32[65,32,1024]{2,1,0:T(8,128)S(1)} %get-tuple-element.26.t) | copy-start | bytes 25559044
  13.4 0.8 copy-start.18
  14.2 21.5 %copy-start.6 = (f32[8,32,1024]{2,1,0:T(8,128)}, f32[8,32,1024]{2,1,0:T(8,128)S(1)}, u32[]{:S(2)}) copy-start(f32[8,32,1024]{2,1,0:T(8,128)S(1)} %get-tuple-element.28.m) | copy-start | bytes 3145732
  14.2 35.7 %copy-start.9 = (f32[4,32,1024]{2,1,0:T(8,128)}, f32[4,32,1024]{2,1,0:T(8,128)S(1)}, u32[]{:S(2)}) copy-start(f32[4,32,1024]{2,1,0:T(8,128)S(1)} %get-tuple-element.35.pair) | copy-start | bytes 1572868
  14.2 2.2 %copy-start.1 = (bf16[1024,1024]{1,0:T(8,128)(2,1)S(1)}, bf16[1024,1024]{1,0:T(8,128)(2,1)}, u32[]{:S(2)}) copy-start(bf16[1024,1024]{1,0:T(8,128)(2,1)} %constant.60.clone.rest) | copy-start | bytes 6291460
  16.4 1.6 copy-start.3
  18.0 1.6 copy-start.16
  19.5 0.8 copy-start.27
  20.3 0.7 copy-start.41
  21.0 0.7 copy-start.44
  21.6 14.1 %copy-start.2 = (bf16[1024,1024]{1,0:T(8,128)(2,1)S(1)}, bf16[1024,1024]{1,0:T(8,128)(2,1)}, u32[]{:S(2)}) copy-start(bf16[1024,1024]{1,0:T(8,128)(2,1)} %constant.60.clone.rest) | copy-start | bytes 6291460
  21.6 14.1 %copy-start.4 = (bf16[1024,1024]{1,0:T(8,128)(2,1)S(1)}, bf16[1024,1024]{1,0:T(8,128)(2,1)}, u32[]{:S(2)}) copy-start(bf16[1024,1024]{1,0:T(8,128)(2,1)} %constant.59.clone.top) | copy-start | bytes 6291460
  21.7 14.1 %copy-start.17 = (f32[2,8,32,1024]{3,2,1,0:T(8,128)S(1)}, f32[2,8,32,1024]{3,2,1,0:T(8,128)}, u32[]{:S(2)}) copy-start(f32[2,8,32,1024]{3,2,1,0:T(8,128)} %x.2) | copy-start | bytes 6291460
  33.9 1.3 copy-start.14
  35.3 14.7 %copy-start.23 = (f32[2,2,16,1024]{3,2,1,0:T(8,128)}, f32[2,2,16,1024]{3,2,1,0:T(8,128)S(1)}, u32[]{:S(2)}) copy-start(f32[2,2,16,1024]{3,2,1,0:T(8,128)S(1)} %get-tuple-element.43.keep) | copy-start | bytes 786436
  35.3 14.7 %collective-permute-start.5 = (f32[2,2,16,1024]{3,2,1,0:T(8,128)S(1)}, f32[2,2,16,1024]{3,2,1,0:T(8,128)S(1)}, u32[]{:S(2)}, u32[]{:S(2)}) collective-permute-start(f32[2,2,16,1024]{3,2,1,0:T(8,128)S(1)} %get-tuple-element.44), channel_id=1, source_target_pairs={{0,4},{4,0},{8,12},{12,8},{16,20},{20,16},{24,28},{28,24},{1,5},{5... | collective-permute-start | bytes 786440 | tf_op jit(solution)/shard_map/ppermute | solution.py:532
  48.5 1.3 copy-start.12
  49.8 0.9 copy-start.20
  49.9 29.4 %copy-start.40 = (f32[64]{0:T(128)S(1)}, f32[64]{0:T(128)}, u32[]{:S(2)}) copy-start(f32[64]{0:T(128)} %thick.7) | copy-start | bytes 772
  49.9 29.4 %copy-start.43 = (f32[65]{0:T(128)S(1)}, f32[65]{0:T(128)}, u32[]{:S(2)}) copy-start(f32[65]{0:T(128)} %copy-done.42) | copy-start | bytes 784
  49.9 19.9 %collective-permute-start = (f32[2,2,16,1024]{3,2,1,0:T(8,128)}, f32[2,2,16,1024]{3,2,1,0:T(8,128)}, u32[]{:S(2)}, u32[]{:S(2)}) collective-permute-start(f32[2,2,16,1024]{3,2,1,0:T(8,128)} %get-tuple-element.34), channel_id=1, source_target_pairs={{0,4},{4,0},{8,12},{12,8},{16,20},{20,16},{24,28},{28,24},{1,5},{5... | collective-permute-start | bytes 786440 | tf_op jit(solution)/shard_map/ppermute | solution.py:532
  49.9 0.8 copy-start.25
  50.7 3.1 %copy-start.45 = (f32[2,16,1024]{2,1,0:T(8,128)}, f32[2,16,1024]{2,1,0:T(8,128)S(1)}, u32[]{:S(2)}) copy-start(f32[2,16,1024]{2,1,0:T(8,128)S(1)} %get-tuple-element.47) | copy-start | bytes 393220
  50.7 3.1 %copy-start.46 = (f32[2,16,1024]{2,1,0:T(8,128)}, f32[2,16,1024]{2,1,0:T(8,128)S(1)}, u32[]{:S(2)}) copy-start(f32[2,16,1024]{2,1,0:T(8,128)S(1)} %get-tuple-element.46) | copy-start | bytes 393220
  50.7 24.3 %collective-permute-start.6 = (f32[2,16,1024]{2,1,0:T(8,128)}, f32[2,16,1024]{2,1,0:T(8,128)}, u32[]{:S(2)}, u32[]{:S(2)}) collective-permute-start(f32[2,16,1024]{2,1,0:T(8,128)} %get-tuple-element.45), channel_id=1, source_target_pairs={{0,8},{4,12},{8,16},{12,20},{16,24},{20,28},{24,0},{28,4},{1,9},{5... | collective-permute-start | bytes 393224 | tf_op jit(solution)/shard_map/ppermute | solution.py:535
  59.4 43.4 %all-to-all-start = ((f32[32,1,512]{2,1,0:T(1,128)}), f32[32,1,512]{2,1,0:T(1,128)}, u32[]{:S(2)}, u32[]{:S(2)}) async-start(f32[32,1,512]{2,1,0:T(1,128)} %reshape.33), calls=%async_computation | async-start | bytes 131072 | tf_op jit(solution)/shard_map/all_to_all | solution.py:538
  65.7 51.0 %collective-permute-start.7 = (f32[2,16,1024]{2,1,0:T(8,128)}, f32[2,16,1024]{2,1,0:T(8,128)}, u32[]{:S(2)}, u32[]{:S(2)}) collective-permute-start(f32[2,16,1024]{2,1,0:T(8,128)} %copy-done.46), channel_id=1, source_target_pairs={{0,16},{4,20},{8,24},{12,28},{16,0},{20,4},{24,8},{28,12},{1,17},{... | collective-permute-start | bytes 393224 | tf_op jit(solution)/shard_map/ppermute | solution.py:535
  68.3 48.4 %collective-permute-start.8 = (f32[2,16,1024]{2,1,0:T(8,128)}, f32[2,16,1024]{2,1,0:T(8,128)}, u32[]{:S(2)}, u32[]{:S(2)}) collective-permute-start(f32[2,16,1024]{2,1,0:T(8,128)} %copy-done.45), channel_id=1, source_target_pairs={{0,24},{4,28},{8,0},{12,4},{16,8},{20,12},{24,16},{28,20},{1,25},{... | collective-permute-start | bytes 393224 | tf_op jit(solution)/shard_map/ppermute | solution.py:535
  69.8 1.0 copy-start.10
  70.8 0.9 copy-start.21
  73.5 49.8 %collective-permute-start.1 = (f32[2,16,1024]{2,1,0:T(8,128)}, f32[2,16,1024]{2,1,0:T(8,128)}, u32[]{:S(2)}, u32[]{:S(2)}) collective-permute-start(f32[2,16,1024]{2,1,0:T(8,128)} %get-tuple-element.37), channel_id=1, source_target_pairs={{0,8},{4,12},{8,16},{12,20},{16,24},{20,28},{24,0},{28,4},{1,9},{5... | collective-permute-start | bytes 393224 | tf_op jit(solution)/shard_map/ppermute | solution.py:535
  74.1 49.2 %collective-permute-start.2 = (f32[2,16,1024]{2,1,0:T(8,128)}, f32[2,16,1024]{2,1,0:T(8,128)}, u32[]{:S(2)}, u32[]{:S(2)}) collective-permute-start(f32[2,16,1024]{2,1,0:T(8,128)} %get-tuple-element.38), channel_id=1, source_target_pairs={{0,16},{4,20},{8,24},{12,28},{16,0},{20,4},{24,8},{28,12},{1,17},{... | collective-permute-start | bytes 393224 | tf_op jit(solution)/shard_map/ppermute | solution.py:535
  75.0 48.2 %collective-permute-start.3 = (f32[2,16,1024]{2,1,0:T(8,128)}, f32[2,16,1024]{2,1,0:T(8,128)}, u32[]{:S(2)}, u32[]{:S(2)}) collective-permute-start(f32[2,16,1024]{2,1,0:T(8,128)} %get-tuple-element.39), channel_id=1, source_target_pairs={{0,24},{4,28},{8,0},{12,4},{16,8},{20,12},{24,16},{28,20},{1,25},{... | collective-permute-start | bytes 393224 | tf_op jit(solution)/shard_map/ppermute | solution.py:535
  102.2 0.6 copy-start.30
  107.1 0.9 copy-start.29
  108.0 0.9 copy-start.31
  108.9 0.9 copy-start.38
  112.8 14.6 %all-to-all-start.1 = ((f32[32,1,512]{2,1,0:T(1,128)}), f32[32,1,512]{2,1,0:T(1,128)}, u32[]{:S(2)}, u32[]{:S(2)}) async-start(f32[32,1,512]{2,1,0:T(1,128)} %reshape.35), calls=%async_computation.1 | async-start | bytes 131072 | tf_op jit(solution)/shard_map/all_to_all | solution.py:538
  116.7 1.0 copy-start.11
  117.8 1.0 copy-start.19
  118.8 0.9 copy-start.24
  119.7 0.9 copy-start.26
  122.6 0.7 copy-start.32
  123.3 14.8 %collective-permute-start.9 = (f32[2,2,16,1024]{3,2,1,0:T(8,128)}, f32[2,2,16,1024]{3,2,1,0:T(8,128)}, u32[]{:S(2)}, u32[]{:S(2)}) collective-permute-start(f32[2,2,16,1024]{3,2,1,0:T(8,128)} %get-tuple-element.49), channel_id=1, source_target_pairs={{0,4},{4,0},{8,12},{12,8},{16,20},{20,16},{24,28},{28,24},{1,5},{5... | collective-permute-start | bytes 786440 | tf_op jit(solution)/shard_map/ppermute | solution.py:532
  123.3 1.0 copy-start.22
  126.2 0.7 copy-start.34
  126.9 33.1 %collective-permute-start.4 = (f32[2,2,16,1024]{3,2,1,0:T(8,128)}, f32[2,2,16,1024]{3,2,1,0:T(8,128)}, u32[]{:S(2)}, u32[]{:S(2)}) collective-permute-start(f32[2,2,16,1024]{3,2,1,0:T(8,128)} %get-tuple-element.41), channel_id=1, source_target_pairs={{0,4},{4,0},{8,12},{12,8},{16,20},{20,16},{24,28},{28,24},{1,5},{5... | collective-permute-start | bytes 786440 | tf_op jit(solution)/shard_map/ppermute | solution.py:532
  138.0 1.6 copy-start.5
  139.6 1.2 copy-start.7
  140.8 1.6 copy-start.8
  142.4 1.6 copy-start.15
  144.0 0.8 copy-start.28
  144.8 0.9 copy-start.33
  145.7 0.8 copy-start.37
  146.5 13.5 %copy-start.13 = (f32[2,8,32,1024]{3,2,1,0:T(8,128)S(1)}, f32[2,8,32,1024]{3,2,1,0:T(8,128)}, u32[]{:S(2)}) copy-start(f32[2,8,32,1024]{3,2,1,0:T(8,128)} %copy-done.12) | copy-start | bytes 6291460
  146.5 13.5 %copy-start.35 = (f32[2,2,16,1024]{3,2,1,0:T(8,128)S(1)}, f32[2,2,16,1024]{3,2,1,0:T(8,128)}, u32[]{:S(2)}) copy-start(f32[2,2,16,1024]{3,2,1,0:T(8,128)} %copy-done.34) | copy-start | bytes 786436
  146.5 13.5 %copy-start.36 = (f32[2,32,128]{2,1,0:T(8,128)S(1)}, f32[2,32,128]{2,1,0:T(8,128)}, u32[]{:S(2)}) copy-start(f32[2,32,128]{2,1,0:T(8,128)} %slice.25.edges) | copy-start | bytes 98308

commit v4 on v3

v4 whole, which is shorter than its diff:
```python
import functools
import math

import jax
import jax.numpy as jnp
import numpy as np
from jax import lax
from jax.experimental import pallas as pl
from jax.experimental.pallas import tpu as pltpu
from jax.sharding import PartitionSpec as P

aspect_ratio = 1.0
LANES = 128
ROWS = 8
VMEM_BYTES = 24 * 1024 * 1024
real_dot = functools.partial(jnp.dot, preferred_element_type=jnp.float32)
exact_dot = functools.partial(lax.dot_general, precision=lax.Precision.HIGHEST, preferred_element_type=jnp.float32)
NN = (((1,), (0,)), ((), ()))
NT = (((1,), (1,)), ((), ()))
in_smem = pl.BlockSpec(memory_space=pltpu.SMEM)
in_vmem = pl.BlockSpec(memory_space=pltpu.VMEM)
params = pltpu.CompilerParams(vmem_limit_bytes=VMEM_BYTES)


def wave_order(size):
    return np.concatenate([np.arange(1, size, 2), np.arange(0, size, 2)])


def half_sines(size, back=False):
    half = size // 2
    place = np.arange(half)
    place[0] = half
    parts = []
    for waves in (np.arange(1, size, 2), np.arange(0, size, 2)):
        matrix = np.sin(np.pi * (np.outer(place, waves) % (2 * size)) / size)
        if waves[0] == 0:
            matrix[0] = 0.0
            matrix[:, 0] = 0.0
        matrix = (matrix.T if back else matrix).astype(np.float32)
        top = matrix.astype(jnp.bfloat16)
        parts += [top, (matrix - top.astype(np.float32)).astype(jnp.bfloat16)]
    return parts


def edge_signs(size):
    signs = np.zeros((2 * ROWS, LANES), np.float32)
    signs[0] = 2.0 / size
    signs[1] = np.where(np.arange(LANES) < LANES // 2, 2.0 / size, -2.0 / size)
    return signs.astype(jnp.bfloat16)


def interface_matrices(waves, size):
    classes = waves // 2 + 1
    matrix = np.zeros((2, classes, 2, waves, 4, waves, 4))
    for c in range(classes):
        weight = (1.0 if c in (0, waves // 2) else 2.0) / (size * waves)
        for w in range(waves):
            for e in range(2):
                for v in range(waves):
                    for g in range(2):
                        value = weight * math.cos(2.0 * math.pi * (c * (w + e - v - g) % waves) / waves)
                        for f in range(4):
                            matrix[g, c, e, w, f, v, f] = value
    return matrix.reshape(2, classes * 2 * waves * 4, waves * 4).astype(np.float32)


def split(values):
    high = values.astype(jnp.bfloat16)
    return high, (values - high.astype(jnp.float32)).astype(jnp.bfloat16)


def product(values, top, rest):
    high, low = split(values)
    return real_dot(high, top[...]) + (real_dot(low, top[...]) + real_dot(high, rest[...]))


def mirror(values):
    rows = values.shape[0]
    lane = lax.broadcasted_iota(jnp.int32, (rows, LANES), 1)
    back = (LANES - lane) % LANES
    tiles = [values[:, a * LANES:(a + 1) * LANES] for a in range(values.shape[1] // LANES)]
    many = len(tiles)
    out = []
    for a in range(many):
        turned = jnp.take_along_axis(tiles[many - 1 - a], back, axis=1)
        out.append(jnp.where(lane == 0, tiles[(many - a) % many], turned))
    return jnp.concatenate(out, 1) if many > 1 else out[0]


def to_waves(values, odd_top, odd_rest, even_top, even_rest):
    half = values.shape[1] // 2
    low, high = values[:, :half], mirror(values[:, half:])
    lane = lax.broadcasted_iota(jnp.int32, low.shape, 1)
    low = jnp.where(lane == 0, 0.0, low)
    return product(low + high, odd_top, odd_rest), product(low - high, even_top, even_rest)


def to_cells(odd, even, odd_top, odd_rest, even_top, even_rest):
    p, m = product(odd, odd_top, odd_rest), product(even, even_top, even_rest)
    return p + m, mirror(p - m)


def coefficient_kernel(levels, total, group, place, thick, face, shifts, across, t_out, r_out, m_out, end_out, pair_out, far_out, lam, m_chip, r_chip, f_chip, n_chip, u_chip, down_all, up_all):
    ky = t_out.shape[1]
    span = 2 * levels
    chips = total // span
    chip = place[0] // 2
    start = chip * span
    upper = place[0] % 2 == 0
    own = (place[0] % 2) * levels
    for row in range(ky):
        lam[row:row + 1, :] = across[...] + shifts[row]

    def down_step(shift, j, f, r):
        m = face[j] * r
        f = shift * thick[j] + m * f
        return m, f, 1.0 / (face[j + 1] + f)

    def up_step(shift, j, phi, s):
        n = face[j + 1] * s
        u = n * phi
        phi = shift * thick[j] + u
        return n, u, phi, 1.0 / (face[j] + phi)

    def part(g, _):
        here = pl.ds(pl.multiple_of(g * group, group), group)
        shift = lam[here]
        one = jnp.ones_like(shift)
        zero = jnp.zeros_like(shift)

        def down_chip(c, state):
            f, r = state
            product = one
            for i in range(span):
                m, f, r = down_step(shift, c * span + i, f, r)
                t_out[c * span + i, here] = m
                product = product * m
            down_all[c] = product
            return f, r

        def up_chip(back, state):
            phi, s = state
            c = chips - 1 - back
            product = one
            for i in range(span - 1, -1, -1):
                n, _, phi, s = up_step(shift, c * span + i, phi, s)
                t_out[c * span + i + 1, here] = n
                product = product * n
            up_all[c] = product
            return phi, s

        f, r = lax.fori_loop(0, chip, down_chip, (one, one))
        for i in range(span):
            m, f, r = down_step(shift, start + i, f, r)
            m_chip[i], f_chip[i], r_chip[i] = m, f, r
        phi, s = lax.fori_loop(0, chips - 1 - chip, up_chip, (zero, zero))
        for i in range(span - 1, -1, -1):
            n, u, phi, s = up_step(shift, start + i, phi, s)
            n_chip[i], u_chip[i] = n, u

        for i in range(levels):
            t_out[start + i, here] = m_chip[i]
            t_out[start + levels + 1 + i, here] = n_chip[levels + i]
        t_out[start + levels, here] = jnp.where(upper, n_chip[levels - 1], m_chip[levels])
        for i in range(levels):
            r_out[i, here] = r_chip[own + i]
            m_out[i, here] = m_chip[own + i]
        last = own + levels - 1
        end_out[0, here] = n_chip[last]
        end_out[1, here] = 1.0 / (f_chip[last] + u_chip[last])
        end_out[2, here] = f_chip[own] + u_chip[own]
        for core in range(2):
            down, up = m_chip[core * levels], n_chip[core * levels]
            for i in range(1, levels):
                down = down * m_chip[core * levels + i]
                up = up * n_chip[core * levels + i]
            pair_out[core, here] = down
            pair_out[2 + core, here] = up
        above, below = [one], [one]
        for apart in range(1, chips - 1):
            above.append(above[-1] * jnp.where(chip >= apart, down_all[jnp.maximum(chip - apart, 0)], one))
            below.append(below[-1] * jnp.where(chip + apart < chips, up_all[jnp.minimum(chip + apart, chips - 1)], one))
        for apart in range(1, chips):
            far_out[apart - 1, here] = jnp.where(chip >= apart, above[apart - 1], below[chips - apart - 1])
        return 0

    lax.fori_loop(0, ky // group, part, 0)


def coefficients(place, thick, face, shifts, across, levels):
    ky, size = shifts.shape[0], across.shape[1]
    total = thick.shape[0]
    chips = total // (2 * levels)
    group = min(2 * ROWS, ky)
    sizes = (total + 1, levels, levels, 3, 4, chips - 1)
    scratch = lambda n: pltpu.VMEM((n, group, size), jnp.float32)
    return pl.pallas_call(
        functools.partial(coefficient_kernel, levels, total, group),
        in_specs=[in_smem] * 4 + [in_vmem],
        out_specs=[in_vmem] * 6,
        out_shape=[jax.ShapeDtypeStruct((n, ky, size), jnp.float32) for n in sizes],
        scratch_shapes=[pltpu.VMEM((ky, size), jnp.float32)] + [scratch(2 * levels)] * 5 + [scratch(chips)] * 2,
        compiler_params=params,
        name="coefficients",
    )(place, thick, face, shifts, across)


def lane_sum(values):
    tiles = [values[:, t * LANES:(t + 1) * LANES] for t in range(values.shape[1] // LANES)]
    while len(tiles) > 1:
        tiles = [a + b for a, b in zip(tiles[0::2], tiles[1::2])] + tiles[len(tiles) // 2 * 2:]
    return tiles[0]


def two_sums(values):
    half = values.shape[1] // 2
    odd, even = lane_sum(values[:, :half]), lane_sum(values[:, half:])
    odd = odd + pltpu.roll(odd, LANES // 2, 1)
    even = even + pltpu.roll(even, LANES // 2, 1)
    return jnp.where(lax.broadcasted_iota(jnp.int32, odd.shape, 1) < LANES // 2, odd, even)


def forward_kernel(total, scaled, part, place, thick, x, odd_top, odd_rest, even_top, even_rest, sines, signs, t, r, m, end, *refs):
    b_out, keep_out, give_out, edge_out, c_all, z_all, sums = refs[-7:]
    _, levels, ky, size = x.shape
    first = place[0] * levels
    half = size // 2
    lane = lax.broadcasted_iota(jnp.int32, (ROWS, LANES), 1)
    spot = jnp.where((lane == 0) | (lane == LANES // 2), size / 4.0, 0.0)
    edge_out[...] = refs[0][...] if part else jnp.zeros_like(edge_out)
    odd, even = to_waves(x[...].reshape(2 * levels * ky, size), odd_top, odd_rest, even_top, even_rest)
    for ri in range(2):
        for j in range(levels):
            rows = slice((ri * levels + j) * ky, (ri * levels + j + 1) * ky)
            scale = thick[first + j] if scaled else 1.0
            b_out[ri, j, :, :half] = odd[rows] * scale
            b_out[ri, j, :, half:] = even[rows] * scale

    for ri in range(2):
        def tile(g, _):
            here = pl.ds(pl.multiple_of(g * ROWS, ROWS), ROWS)
            wave = sines[...]
            y = b_out[ri, 0, here]
            ys = [y]
            for j in range(1, levels):
                y = b_out[ri, j, here] + m[j, here] * y
                ys.append(y)
            c_all[0, here] = y
            value = y * end[1, here]
            z_all[1, here] = value * wave
            for j in range(levels - 1, -1, -1):
                if j < levels - 1:
                    value = r[j, here] * ys[j] + m[j + 1, here] * value
                height = thick[first + j]
                own = jnp.broadcast_to(x[ri, j, here, 0:1], (ROWS, LANES)) * (spot * height if scaled else spot)
                sums[pl.ds(g * ROWS * total + first + j, ROWS, stride=total), :] = two_sums(value * wave) * height + own
            z_all[0, here] = value * wave
            c_all[1, here] = value * end[2, here]
            return 0

        lax.fori_loop(0, ky // ROWS, tile, 0)

        def reach_up(back, z):
            j = first - 1 - back
            z = t[j + 1] * z
            sums[pl.ds(j, ky, stride=total), :] = two_sums(z) * thick[j]
            return z

        def reach_down(ahead, z):
            j = first + levels + ahead
            z = t[j] * z
            sums[pl.ds(j, ky, stride=total), :] = two_sums(z) * thick[j]
            return z

        lax.fori_loop(0, first, reach_up, z_all[0])
        lax.fori_loop(0, total - levels - first, reach_down, z_all[1])
        high, low = split(sums[...])
        edges = lax.dot_general(signs[...], high, NT, preferred_element_type=jnp.float32)
        edges = edges + lax.dot_general(signs[...], low, NT, preferred_element_type=jnp.float32)
        row = part * 2 + ri
        for i in range(ky):
            edge_out[i, row:row + 1, :total] = edges[0:1, i * total:(i + 1) * total]
            edge_out[i, row:row + 1, total:] = edges[1:2, i * total:(i + 1) * total]
        core = place[0] % 2
        keep_out[:, ri] = c_all[:, pl.ds(pl.multiple_of(core * (ky // 2), ROWS), ky // 2)]
        give_out[:, ri] = c_all[:, pl.ds(pl.multiple_of((1 - core) * (ky // 2), ROWS), ky // 2)]


def forward(place, thick, x, scaled, sines, t, r, m, end, devices, edges=None):
    _, levels, ky, size = x.shape
    total = t.shape[0] - 1
    part = 0 if edges is None else 1
    half = (2, 2, ky // 2, size)
    old = [] if edges is None else [edges]
    return pl.pallas_call(
        functools.partial(forward_kernel, total, scaled, part),
        in_specs=[in_smem, in_smem] + [in_vmem] * (11 + part),
        out_specs=[in_vmem] * 4,
        out_shape=[
            jax.ShapeDtypeStruct(x.shape, jnp.float32),
            jax.ShapeDtypeStruct(half, jnp.float32),
            jax.ShapeDtypeStruct(half, jnp.float32),
            jax.ShapeDtypeStruct((devices, 4, 2 * total), jnp.float32),
        ],
        scratch_shapes=[
            pltpu.VMEM((2, ky, size), jnp.float32),
            pltpu.VMEM((2, ky, size), jnp.float32),
            pltpu.VMEM((ky * total, LANES), jnp.float32),
        ],
        compiler_params=params,
        name="forward",
    )(place, thick, x, *half_sines(size), sines, edge_signs(size), t, r, m, end, *old)


def chip_kernel(chips, place, keep, got, pair, *outs):
    chip = place[0] // 2
    upper = place[0] % 2 == 0
    half = keep.shape[2]
    here = pl.ds(pl.multiple_of((place[0] % 2) * half, ROWS), half)
    first, second = jnp.where(upper, keep[...], got[...]), jnp.where(upper, got[...], keep[...])
    down = second[0] + pair[1, here] * first[0]
    up = first[1] + pair[2, here] * second[1]
    for apart in range(1, chips):
        outs[apart - 1][...] = jnp.where(chip + apart < chips, down, up)


def chip_sums(place, keep, got, pair, chips):
    return pl.pallas_call(
        functools.partial(chip_kernel, chips),
        in_specs=[in_smem] + [in_vmem] * 3,
        out_specs=[in_vmem] * (chips - 1),
        out_shape=[jax.ShapeDtypeStruct(keep.shape[1:], jnp.float32)] * (chips - 1),
        compiler_params=params,
        name="chip_sums",
    )(place, keep, got, pair)


def join_kernel(chips, place, keep, got, pair, far, *refs):
    news = refs[:chips - 1]
    mine, theirs = refs[chips - 1:]
    chip = place[0] // 2
    upper = place[0] % 2 == 0
    half = keep.shape[2]
    here = pl.ds(pl.multiple_of((place[0] % 2) * half, ROWS), half)
    first, second = jnp.where(upper, keep[...], got[...]), jnp.where(upper, got[...], keep[...])
    down = jnp.zeros(first.shape[1:], jnp.float32)
    up = down
    for apart in range(1, chips):
        term = far[apart - 1, here] * news[apart - 1][...]
        down = down + jnp.where(chip >= apart, term, 0.0)
        up = up + jnp.where(chip >= apart, 0.0, term)
    inner_up = second[1] + pair[3, here] * up
    inner_down = first[0] + pair[0, here] * down
    mine[0] = jnp.where(upper, down, inner_down)
    mine[1] = jnp.where(upper, inner_up, up)
    theirs[0] = jnp.where(upper, inner_down, down)
    theirs[1] = jnp.where(upper, up, inner_up)


def join(place, keep, got, pair, far, news):
    chips = len(news) + 1
    return pl.pallas_call(
        functools.partial(join_kernel, chips),
        in_specs=[in_smem] + [in_vmem] * (3 + chips),
        out_specs=[in_vmem] * 2,
        out_shape=[jax.ShapeDtypeStruct(keep.shape, jnp.float32)] * 2,
        compiler_params=params,
        name="join",
    )(place, keep, got, pair, far, *news)


def inverse_kernel(per, thick, face, lam, out, m_all, f_all, g_all):
    total = f_all.shape[0]
    rows = lam.shape[0]
    classes = out.shape[0]
    shift = lam[...]
    one = jnp.ones_like(shift)
    zero = jnp.zeros_like(shift)

    def step(j, state):
        f, r, phi, s = state
        m = face[j] * r
        f = shift * thick[j] + m * f
        r = 1.0 / (face[j + 1] + f)
        m_all[j] = m
        f_all[j] = f
        i = total - 1 - j
        u = face[i + 1] * s * phi
        phi = shift * thick[i] + u
        s = 1.0 / (face[i] + phi)
        g_all[i] = u
        return f, r, phi, s

    lax.fori_loop(0, total, step, (one, one, zero, zero))

    def centre(j, _):
        g_all[j] = 1.0 / (f_all[j] + g_all[j])
        return 0

    lax.fori_loop(0, total, centre, 0)
    wide = out.shape[2]
    sub = lax.broadcasted_iota(jnp.int32, (ROWS, LANES), 0)
    lane = lax.broadcasted_iota(jnp.int32, (ROWS, wide), 1)
    row = lax.broadcasted_iota(jnp.int32, (ROWS, wide), 0)
    line = lambda ref, j, t: jnp.broadcast_to(ref[j, t:t + 1, :], (ROWS, LANES))

    def put(j, z, sums):
        new = []
        for c in range(classes):
            tiles = z[c * per:(c + 1) * per]
            total_tile = tiles[0]
            for tile in tiles[1:]:
                total_tile = total_tile + tile
            value = jnp.sum(total_tile, axis=1, keepdims=True)
            new.append(jnp.where(lane == j, value, sums[c]))
        return new

    for base in range(0, total, ROWS):
        z = [jnp.zeros((ROWS, LANES), jnp.float32)] * (classes * per)
        sums = [jnp.zeros((ROWS, wide), jnp.float32)] * classes
        for i in range(ROWS - 1, -1, -1):
            j = base + i
            for t in range(classes * per):
                moved = z[t] * line(m_all, j + 1, t) if i < ROWS - 1 else z[t]
                z[t] = jnp.where(sub == i, line(g_all, j, t), moved)
            sums = put(j, z, sums)

        def above(back, state):
            z, sums = state
            for i in range(ROWS):
                j = base - 1 - back * ROWS - i
                z = [z[t] * line(m_all, j + 1, t) for t in range(classes * per)]
                sums = put(j, z, sums)
            return z, sums

        if base:
            z, sums = lax.fori_loop(0, base // ROWS, above, (z, sums))
        for c in range(classes):
            out[c, base:base + ROWS, :] = sums[c] * jnp.where(lane == base + row, 0.5, 1.0)


def inverse_sums(thick, face, lam, per):
    total = thick.shape[0]
    classes = lam.shape[0] // per
    wide = -(-total // LANES) * LANES
    spare = -lam.shape[0] % ROWS
    lam = jnp.pad(lam, ((0, spare), (0, 0)), constant_values=1.0) if spare else lam
    return pl.pallas_call(
        functools.partial(inverse_kernel, per),
        in_specs=[in_smem, in_smem, in_vmem],
        out_shape=jax.ShapeDtypeStruct((classes, total, wide), jnp.float32),
        scratch_shapes=[pltpu.VMEM((total,) + lam.shape, jnp.float32)] * 3,
        compiler_params=params,
        name="inverse_sums",
    )(thick, face, lam)


def interface_kernel(waves, matrices, edges, inverse, out):
    devices, _, wide = edges.shape
    total = wide // 2
    rows = 4 * waves
    lines = []
    for w in range(waves):
        line = edges[w]
        for d in range(1, devices // waves):
            line = line + edges[d * waves + w]
        lines.append(line)
    lines = jnp.concatenate(lines, 0)
    near, far = exact_dot(matrices[0], lines, NN), exact_dot(matrices[1], lines, NN)
    mixed = near[:, :total] + far[:, total:]
    result = jnp.zeros((2 * rows, total), jnp.float32)
    for c in range(inverse.shape[0]):
        part = mixed[c * 2 * rows:(c + 1) * 2 * rows]
        square = inverse[c][:, :total]
        result = result + (exact_dot(part, square, NN) + exact_dot(part, square, NT))
    result = jnp.concatenate([result[:rows], result[rows:]], 1)
    for w in range(waves):
        line = result[4 * w:4 * w + 4]
        for d in range(devices // waves):
            out[d * waves + w] = line


def interface(edges, inverse, waves, size):
    return pl.pallas_call(
        functools.partial(interface_kernel, waves),
        in_specs=[in_vmem] * 3,
        out_specs=in_vmem,
        out_shape=jax.ShapeDtypeStruct(edges.shape, jnp.float32),
        compiler_params=params,
        name="interface",
    )(interface_matrices(waves, size), edges, inverse)


def backward_kernel(total, scaled, part, place, thick, b, edges, mine, theirs, odd_top, odd_rest, even_top, even_rest, sines, t, r, m, end, out, ends, u_all, q_all):
    ri = pl.program_id(0)
    _, levels, ky, size = b.shape
    first = place[0] * levels
    half = size // 2
    many = half // LANES
    core = place[0] % 2
    ends[:, pl.ds(pl.multiple_of(core * (ky // 2), ROWS), ky // 2)] = mine[:, ri]
    ends[:, pl.ds(pl.multiple_of((1 - core) * (ky // 2), ROWS), ky // 2)] = theirs[:, ri]
    values = jnp.where(ri == 0, edges[:ky, 2 * part, :], edges[:ky, 2 * part + 1, :])
    near, far = values[:, :total], values[:, total:]
    plus, minus = near + far, near - far
    for j in range(total):
        u_all[0, j] = jnp.broadcast_to(plus[:, j:j + 1], (ky, LANES))
        u_all[1, j] = jnp.broadcast_to(minus[:, j:j + 1], (ky, LANES))

    def source(j, here=slice(None)):
        return jnp.concatenate([u_all[0, j, here] * thick[j]] * many + [u_all[1, j, here] * thick[j]] * many, 1)

    def from_above(j, y):
        return t[j] * y + source(j)

    def from_below(back, y):
        j = total - 1 - back
        return t[j + 1] * y + source(j)

    zero = jnp.zeros((ky, size), jnp.float32)
    ends[0] += sines[...][:1] * lax.fori_loop(0, first, from_above, zero)
    ends[1] += sines[...][:1] * lax.fori_loop(0, total - levels - first, from_below, zero)

    def tile(g, _):
        here = pl.ds(pl.multiple_of(g * ROWS, ROWS), ROWS)
        wave = sines[...]
        y = ends[0, here]
        ys = []
        for j in range(levels):
            y = b[ri, j, here] + wave * source(first + j, here) + m[j, here] * y
            ys.append(y)
        value = (y + end[0, here] * ends[1, here]) * end[1, here]
        q_all[levels - 1, here] = value
        for j in range(levels - 2, -1, -1):
            value = r[j, here] * ys[j] + m[j + 1, here] * value
            q_all[j, here] = value
        return 0

    lax.fori_loop(0, ky // ROWS, tile, 0)
    rows = levels * ky
    low, high = to_cells(
        q_all[:, :, :half].reshape(rows, half), q_all[:, :, half:].reshape(rows, half), odd_top, odd_rest, even_top, even_rest
    )
    lane = lax.broadcasted_iota(jnp.int32, (ky, LANES), 1)
    for j in range(levels):
        height = thick[first + j] if scaled else 1.0
        scale = (2.0 / size) * height
        here = slice(j * ky, (j + 1) * ky)
        u = (u_all[0, first + j] + u_all[1, first + j]) * (0.5 * height)
        if many > 1:
            out[0, j, :, LANES:half] = low[here, LANES:] * scale
        out[0, j, :, :LANES] = jnp.where(lane == 0, u, low[here, :LANES] * scale)
        out[0, j, :, half:] = high[here] * scale


def backward(place, thick, b, edges, mine, theirs, scaled, part, sines, t, r, m, end):
    _, levels, ky, size = b.shape
    total = t.shape[0] - 1
    return pl.pallas_call(
        functools.partial(backward_kernel, total, scaled, part),
        grid=(2,),
        in_specs=[in_smem, in_smem] + [in_vmem] * 13,
        out_specs=pl.BlockSpec((1, levels, ky, size), lambda i: (i, 0, 0, 0)),
        out_shape=jax.ShapeDtypeStruct(b.shape, jnp.float32),
        scratch_shapes=[
            pltpu.VMEM((2, ky, size), jnp.float32),
            pltpu.VMEM((2, total, ky, LANES), jnp.float32),
            pltpu.VMEM((levels, ky, size), jnp.float32),
        ],
        compiler_params=params,
        name="backward",
    )(place, thick, b, edges, mine, theirs, *half_sines(size, True), sines, t, r, m, end)


def shards(rhs, cotangent, thickness, ky_shift):
    waves = lax.axis_size("wave")
    count = lax.axis_size("depth")
    depth_pos = lax.axis_index("depth")
    wave_pos = lax.axis_index("wave")
    _, levels, ky, size = rhs.shape
    full = waves * size
    devices = waves * count
    chips = count // 2
    place = depth_pos.astype(jnp.int32).reshape(1)

    def across(a):
        return lax.ppermute(a, "depth", [(d, d ^ 1) for d in range(count)])

    def along(a, apart):
        return lax.ppermute(a, "depth", [(d, (d + 2 * apart) % count) for d in range(count)])

    def everywhere(a):
        return lax.all_to_all(a, ("depth", "wave"), split_axis=0, concat_axis=0, tiled=True)

    def horizontal(wavenumber, length):
        return (aspect_ratio * 4.0 * np.sin(math.pi * wavenumber / length) ** 2).astype(np.float32)

    inner_face = 2.0 / (thickness[:-1] + thickness[1:])
    face = jnp.concatenate([2.0 / thickness[:1], inner_face, jnp.zeros((1,), jnp.float32)])
    order = wave_order(size)
    t, r, m, end, pair, far = coefficients(place, thickness, face, ky_shift, horizontal(order, 2 * size)[None, :], levels)
    sines = jnp.asarray(np.broadcast_to(np.sin(np.pi * order / size)[None, :], (ROWS, size)), jnp.float32)
    tables = (sines, t, r, m, end)

    classes = waves // 2 + 1
    wavenumber = (np.arange(classes)[:, None] + waves * np.arange(size)[None, :]).reshape(-1, LANES)
    shifts = jnp.pad(ky_shift, (0, devices - ky), constant_values=1.0) if devices > ky else ky_shift
    my_shift = lax.dynamic_slice_in_dim(shifts, depth_pos * waves + wave_pos, 1)

    def middle(keep, give):
        got = across(give)
        sums = chip_sums(place, keep, got, pair, chips)
        news = [along(sums[apart - 1], apart) for apart in range(1, chips)]
        mine, theirs = join(place, keep, got, pair, far, news)
        return mine, across(theirs)

    b0, keep0, give0, edges = forward(place, thickness, rhs, True, *tables, devices)
    b1, keep1, give1, edges = forward(place, thickness, cotangent, False, *tables, devices, edges)
    edges = everywhere(edges)
    inverse = inverse_sums(thickness, face, my_shift + horizontal(wavenumber, full), size // LANES)
    mine0, theirs0 = middle(keep0, give0)
    mine1, theirs1 = middle(keep1, give1)
    values = everywhere(interface(edges, inverse, waves, size))
    pressure = backward(place, thickness, b0, values, mine0, theirs0, False, 0, *tables)
    adjoint = backward(place, thickness, b1, values, mine1, theirs1, True, 1, *tables)
    return pressure, adjoint


def solution(mesh):
    spec = P(None, "depth", None, "wave")
    return jax.shard_map(shards, mesh=mesh, in_specs=(spec, spec, P(), P()), out_specs=(spec, spec), check_vma=False)
```

time: 175 us -> 155 us (0.89)
  local copies, waits for them, and re-layouts: 54.7 us -> 36.6 us
  blocking collectives: 0 us -> 13.8 us
  other arithmetic: 9.22 us -> 2.27 us
  Pallas kernels: 86.3 us -> 80.5 us
  starting transfers between devices: 21.6 us -> 18.8 us
    pallas_call x1, Pallas kernels: 23 us -> 6.86 us  [inverse_sums(): pl.pallas_call(functools.partial(inverse_kernel, per), in_specs=[in_smem,...]
    all_to_all x0 -> x1, blocking collectives: none -> 13.8 us  [everywhere(): lax.all_to_all(a, ('depth', 'wave'), split_axis=0, concat_axis=0, tiled=T...]
    pallas_call x10, Pallas kernels: 63.3 us -> 73.7 us  [the longest x2 33.1 us: backward(): pl.pallas_call(functools.partial(backward_kernel, total, scaled, part), g...]
    slice x5 -> x0, local copies, waits for them, and re-layouts: 5.94 us -> none  [the longest x2 3.07 us: shards(): values[:2]]
    unnamed x98 -> x100, local copies, waits for them, and re-layouts: 41.4 us -> 35.9 us
    all_to_all x2 -> x0, other arithmetic: 4.37 us -> none  [everywhere(): return lax.all_to_all(a, everyone, split_axis=0, concat_axis=0, tiled=True)]
    all_to_all x2 -> x1, starting transfers between devices: 8.93 us -> 6.82 us  [everywhere(): lax.all_to_all(a, ('depth', 'wave'), split_axis=0, concat_axis=0, tiled=T...]
  transfers between devices with their start and end apart: 12 -> 11, of which waited for: 0 -> 0; matrix products, arithmetic and copies ran while one was open for 15% -> 1% of each run, Pallas kernels for 32% -> 30%
where the time goes in v4:
time: 155 us; the launch traced here: 153 us
  Pallas kernels  80.5 us (52%)
  local copies, waits for them, and re-layouts  36.6 us (24%)
  starting transfers between devices  18.8 us (12%)
  blocking collectives  13.8 us (9%)
  other arithmetic  2.27 us (1%)
    unnamed x100, local copies, waits for them, and re-layouts  35.9 us
    pallas_call x2, Pallas kernels, backward(): pl.pallas_call(functools.partial(backward_kernel, total, scaled, part), g...  33.1 us
    pallas_call x2, Pallas kernels, forward(): pl.pallas_call(functools.partial(forward_kernel, total, scaled, part), in...  30.1 us
    all_to_all x1, blocking collectives, everywhere(): lax.all_to_all(a, ('depth', 'wave'), split_axis=0, concat_axis=0, tiled=T...  13.8 us
    ppermute x6, starting transfers between devices, along(): lax.ppermute(a, 'depth', [(d, (d + 2 * apart) % count) for d in range(cou...  10.9 us
    pallas_call x1, Pallas kernels, inverse_sums(): pl.pallas_call(functools.partial(inverse_kernel, per), in_specs=[in_smem,...  6.86 us
    all_to_all x1, starting transfers between devices, everywhere(): lax.all_to_all(a, ('depth', 'wave'), split_axis=0, concat_axis=0, tiled=T...  6.82 us
    pallas_call x2, Pallas kernels, join(): pl.pallas_call(functools.partial(join_kernel, chips), in_specs=[in_smem]...  3.7 us
  transfers between devices with their start and end apart: 11, of which 0 were waited for; matrix products, arithmetic and copies ran while one was open for 1% of the time, Pallas kernels for 30%

profile of v4, /device:TPU:0, one launch (start us, length us, event | category | flops | bytes accessed | tf_op | source)
XLA Modules:
  0.0 153.4 jit_solution(17225782902484393812)
XLA Ops:
  0.6 0.8 add_divide_fusion
  2.1 0.1 pad_maximum_fusion.face
  2.2 0.7 copy-done.42
  2.9 0.7 copy-done.47
  3.6 0.7 copy-done.48
  4.2 3.6 %coefficients.1 = (f32[65,32,1024]{2,1,0:T(8,128)S(1)}, f32[8,32,1024]{2,1,0:T(8,128)S(1)}, f32[8,32,1024]{2,1,0:T(8,128)S(1)}, f32[3,32,1024]{2,1,0:T(8,128)S(1...) custom-call(s32[1]{0:T(128)} %bitcast.place, f32[64]{0:T(128)S(1)} %copy-done.42, f32[65]{0:T(128)S(1)} %pad_maximum_fusion.face, ...), custom_call_target="tpu_custom_call" | custom-call | tf_op jit(solution)/shard_map/coefficients/pallas_call | solution.py:197
  7.8 0.7 copy-done.20
  8.5 1.4 copy-done.2
  9.9 1.4 copy-done.4
  11.4 1.4 copy-done.14
  12.8 1.0 copy-done.16
  13.8 1.6 %copy-done.18 = f32[2,8,32,1024]{3,2,1,0:T(8,128)S(1)} copy-done((f32[2,8,32,1024]{3,2,1,0:T(8,128)S(1)}, f32[2,8,32,1024]{3,2,1,0:T(8,128)}, u32[]{:S(2)}) %copy-start.18) | copy-done | bytes 2097176
  15.4 0.8 copy-done.30
  16.2 0.7 copy-done.43
  16.8 0.7 copy-done.45
  17.6 0.0 copy-start.46
  17.6 15.1 %forward.2 = (f32[2,8,32,1024]{3,2,1,0:T(8,128)S(1)}, f32[2,2,16,1024]{3,2,1,0:T(8,128)S(1)}, f32[2,2,16,1024]{3,2,1,0:T(8,128)S(1)}, f32[32,4,128]{2,1,0:T(4,128)S(1)}) custom-call(s32[1]{0:T(128)} %bitcast.place, f32[64]{0:T(128)S(1)} %copy-done.43, f32[2,8,32,1024]{3,2,1,0:T(8,128)S(1)} %copy-done.18, bf16[512,512]{1,0:T(8,128)(2,1)S(1)} %copy-done.16, ...), custom_call_target="tpu_custom_call" | custom-call | tf_op jit(solution)/shard_map/forward/pallas_call | solution.py:295
  32.6 1.3 copy-done.10
  34.0 0.5 collective-permute-start
  34.5 15.1 %forward.3 = (f32[2,8,32,1024]{3,2,1,0:T(8,128)S(1)}, f32[2,2,16,1024]{3,2,1,0:T(8,128)S(1)}, f32[2,2,16,1024]{3,2,1,0:T(8,128)S(1)}, f32[32,4,128]{2,1,0:T(4,128)S(1)}) custom-call(s32[1]{0:T(128)} %bitcast.place, f32[64]{0:T(128)S(1)} %copy-done.44, f32[2,8,32,1024]{3,2,1,0:T(8,128)S(1)} %copy-done.19, bf16[512,512]{1,0:T(8,128)(2,1)S(1)} %copy-done.17, ...), custom_call_target="tpu_custom_call" | custom-call | tf_op jit(solution)/shard_map/forward/pallas_call | solution.py:295
  49.6 0.6 copy-done.41
  50.2 0.1 collective-permute-start.5
  50.3 0.8 chip_sums.2
  51.1 0.7 copy-done.28
  51.8 3.1 %collective-permute-start.1 = (f32[2,16,1024]{2,1,0:T(8,128)S(1)}, f32[2,16,1024]{2,1,0:T(8,128)S(1)}, u32[]{:S(2)}, u32[]{:S(2)}) collective-permute-start(f32[2,16,1024]{2,1,0:T(8,128)S(1)} %get-tuple-element.37), channel_id=1, source_target_pairs={{0,8},{4,12},{8,16},{12,20},{16,24},{20,28},{24,0},{28,4},{1,9},{5... | collective-permute-start | bytes 393224 | tf_op jit(solution)/shard_map/ppermute | solution.py:590
  54.9 2.6 %collective-permute-start.2 = (f32[2,16,1024]{2,1,0:T(8,128)}, f32[2,16,1024]{2,1,0:T(8,128)}, u32[]{:S(2)}, u32[]{:S(2)}) collective-permute-start(f32[2,16,1024]{2,1,0:T(8,128)} %get-tuple-element.38), channel_id=1, source_target_pairs={{0,16},{4,20},{8,24},{12,28},{16,0},{20,4},{24,8},{28,12},{1,17},{... | collective-permute-start | bytes 393224 | tf_op jit(solution)/shard_map/ppermute | solution.py:590
  57.5 1.4 collective-permute-start.3
  58.9 0.8 chip_sums.3
  59.7 0.7 copy-done.22
  60.4 0.7 copy-done.24
  61.1 0.7 collective-permute-start.6
  61.8 0.3 collective-permute-start.7
  62.1 0.7 copy-done.38
  62.8 2.9 %collective-permute-start.8 = (f32[2,16,1024]{2,1,0:T(8,128)}, f32[2,16,1024]{2,1,0:T(8,128)}, u32[]{:S(2)}, u32[]{:S(2)}) collective-permute-start(f32[2,16,1024]{2,1,0:T(8,128)} %get-tuple-element.47), channel_id=1, source_target_pairs={{0,24},{4,28},{8,0},{12,4},{16,8},{20,12},{24,16},{28,20},{1,25},{... | collective-permute-start | bytes 393224 | tf_op jit(solution)/shard_map/ppermute | solution.py:590
  65.6 6.8 %all-to-all-start = ((f32[32,4,128]{2,1,0:T(4,128)}), f32[32,4,128]{2,1,0:T(4,128)}, u32[]{:S(2)}, u32[]{:S(2)}) async-start(f32[32,4,128]{2,1,0:T(4,128)} %copy-done.41), calls=%async_computation | async-start | bytes 131072 | tf_op jit(solution)/shard_map/all_to_all | solution.py:593
  72.5 0.7 dynamic_slice.3
  73.2 1.0 copy-done.7
  74.2 1.0 copy-done.21
  75.2 0.9 copy-done.27
  76.1 0.9 copy-done.29
  77.1 0.9 copy-done.39
  78.0 1.8 %join.2 = (f32[2,2,16,1024]{3,2,1,0:T(8,128)S(1)}, f32[2,2,16,1024]{3,2,1,0:T(8,128)}) custom-call(s32[1]{0:T(128)} %bitcast.place, f32[2,2,16,1024]{3,2,1,0:T(8,128)S(1)} %copy-done.27, f32[2,2,16,1024]{3,2,1,0:T(8,128)S(1)} %copy-done.29, f32[4,32,1024]{2,1,0:T(8,128)S(1)} %copy-done.7, f32[3,32,1024]{2,1,0:T(8,128)S(1)} %copy-done.21, ...), custom_call_target="tpu_custom_call" | custom-call | tf_op jit(solution)/shard_map/join/pallas_call | solution.py:362
  79.8 0.7 copy-done.34
  80.5 0.2 collective-permute-start.4
  80.7 0.9 copy-done.23
  81.7 0.9 copy-done.25
  82.6 1.9 %join.3 = (f32[2,2,16,1024]{3,2,1,0:T(8,128)S(1)}, f32[2,2,16,1024]{3,2,1,0:T(8,128)}) custom-call(s32[1]{0:T(128)} %bitcast.place, f32[2,2,16,1024]{3,2,1,0:T(8,128)S(1)} %copy-done.23, f32[2,2,16,1024]{3,2,1,0:T(8,128)S(1)} %copy-done.25, f32[4,32,1024]{2,1,0:T(8,128)S(1)} %copy-done.7, f32[3,32,1024]{2,1,0:T(8,128)S(1)} %copy-done.21, ...), custom_call_target="tpu_custom_call" | custom-call | tf_op jit(solution)/shard_map/join/pallas_call | solution.py:362
  84.5 0.7 copy-done.36
  85.2 0.3 collective-permute-start.9
  85.5 1.4 broadcast_add_fusion.lam
  86.9 6.9 %inverse_sums.1.inverse = f32[3,64,128]{2,1,0:T(8,128)S(1)} custom-call(f32[64]{0:T(128)S(1)} %copy-done.44, f32[65]{0:T(128)S(1)} %pad_maximum_fusion.face, f32[24,128]{1,0:T(8,128)S(1)} %broadcast_add_fusion.lam), custom_call_target="tpu_custom_call" | custom-call | tf_op jit(solution)/shard_map/inverse_sums/pallas_call | solution.py:448
  93.8 0.6 copy-done.32
  94.4 0.9 copy-done.33
  95.3 0.9 copy-done.40
  96.2 1.5 interface.1
  97.8 13.8 %all_to_all.10.edges = f32[32,4,128]{2,1,0:T(4,128)S(1)} all-to-all(f32[32,4,128]{2,1,0:T(4,128)S(1)} %interface.1), channel_id=1, replica_groups=mesh['depth'=8,'wave'=4] {'depth','wave'}, dimensions={0} | all-to-all | bytes 131072 | tf_op jit(solution)/shard_map/all_to_all | solution.py:593
  111.5 3.4 %copy-done.1 = f32[65,32,1024]{2,1,0:T(8,128)S(1)} copy-done((f32[65,32,1024]{2,1,0:T(8,128)S(1)}, f32[65,32,1024]{2,1,0:T(8,128)}, u32[]{:S(2)}) %copy-start.1) | copy-done | bytes 8519704
  115.0 1.6 %copy-done.11 = f32[2,8,32,1024]{3,2,1,0:T(8,128)S(1)} copy-done((f32[2,8,32,1024]{3,2,1,0:T(8,128)S(1)}, f32[2,8,32,1024]{3,2,1,0:T(8,128)}, u32[]{:S(2)}) %copy-start.11) | copy-done | bytes 2097176
  116.6 1.0 copy-done.12
  117.6 1.0 copy-done.13
  118.6 0.8 copy-done.31
  119.4 0.9 copy-done.35
  120.4 16.6 %backward.2 = f32[2,8,32,1024]{3,2,1,0:T(8,128)} custom-call(s32[1]{0:T(128)} %bitcast.place, f32[64]{0:T(128)S(1)} %copy-done.44, f32[2,8,32,1024]{3,2,1,0:T(8,128)S(1)} %copy-done.11, f32[32,4,128]{2,1,0:T(4,128)S(1)} %all_to_all.10.edges, f32[2,2,16,1024]{3,2,1,0:T(8,128)S(1)} %copy-done.35, f32[2,2,16,1024]{3,2,1,0:T(8,128)} %collective-permute-done.4.theirs, ...), custom_call_target="tpu_custom_call" | custom-call | tf_op jit(solution)/shard_map/backward/pallas_call | solution.py:559
  137.0 16.5 %backward.3 = f32[2,8,32,1024]{3,2,1,0:T(8,128)} custom-call(s32[1]{0:T(128)} %bitcast.place, f32[64]{0:T(128)S(1)} %copy-done.44, f32[2,8,32,1024]{3,2,1,0:T(8,128)S(1)} %copy-done.9, f32[32,4,128]{2,1,0:T(4,128)S(1)} %all_to_all.10.edges, f32[2,2,16,1024]{3,2,1,0:T(8,128)S(1)} %copy-done.37, f32[2,2,16,1024]{3,2,1,0:T(8,128)} %collective-permute-done.9.theirs, ...), custom_call_target="tpu_custom_call" | custom-call | tf_op jit(solution)/shard_map/backward/pallas_call | solution.py:559
  (74 shorter events, 0.1 us)
Async XLA Ops:
  2.2 0.7 copy-start.42
  2.9 0.7 copy-start.47
  3.6 0.7 copy-start.48
  7.8 0.7 copy-start.20
  8.5 25.9 %copy-start = (f32[65,32,1024]{2,1,0:T(8,128)}, f32[65,32,1024]{2,1,0:T(8,128)S(1)}, u32[]{:S(2)}) copy-start(f32[65,32,1024]{2,1,0:T(8,128)S(1)} %get-tuple-element.26.t) | copy-start | bytes 25559044
  8.5 50.4 %copy-start.6 = (f32[4,32,1024]{2,1,0:T(8,128)}, f32[4,32,1024]{2,1,0:T(8,128)S(1)}, u32[]{:S(2)}) copy-start(f32[4,32,1024]{2,1,0:T(8,128)S(1)} %get-tuple-element.35.pair) | copy-start | bytes 1572868
  8.5 1.4 copy-start.2
  9.9 1.4 copy-start.4
  11.4 1.4 copy-start.14
  12.8 1.0 copy-start.16
  13.8 1.6 %copy-start.18 = (f32[2,8,32,1024]{3,2,1,0:T(8,128)S(1)}, f32[2,8,32,1024]{3,2,1,0:T(8,128)}, u32[]{:S(2)}) copy-start(f32[2,8,32,1024]{3,2,1,0:T(8,128)} %x.2) | copy-start | bytes 6291460
  15.4 0.8 copy-start.30
  16.2 0.7 copy-start.43
  16.8 0.7 copy-start.45
  17.5 16.9 %copy-start.3 = (bf16[512,512]{1,0:T(8,128)(2,1)S(1)}, bf16[512,512]{1,0:T(8,128)(2,1)}, u32[]{:S(2)}) copy-start(bf16[512,512]{1,0:T(8,128)(2,1)} %constant.48.clone.even_rest) | copy-start | bytes 1572868
  17.5 16.9 %copy-start.5 = (bf16[512,512]{1,0:T(8,128)(2,1)S(1)}, bf16[512,512]{1,0:T(8,128)(2,1)}, u32[]{:S(2)}) copy-start(bf16[512,512]{1,0:T(8,128)(2,1)} %constant.47.clone.even_top) | copy-start | bytes 1572868
  17.5 16.9 %copy-start.15 = (bf16[512,512]{1,0:T(8,128)(2,1)S(1)}, bf16[512,512]{1,0:T(8,128)(2,1)}, u32[]{:S(2)}) copy-start(bf16[512,512]{1,0:T(8,128)(2,1)} %constant.46.clone.odd_rest) | copy-start | bytes 1572868
  17.5 16.9 %copy-start.17 = (bf16[512,512]{1,0:T(8,128)(2,1)S(1)}, bf16[512,512]{1,0:T(8,128)(2,1)}, u32[]{:S(2)}) copy-start(bf16[512,512]{1,0:T(8,128)(2,1)} %constant.45.clone.odd_top) | copy-start | bytes 1572868
  17.5 16.9 %copy-start.19 = (f32[2,8,32,1024]{3,2,1,0:T(8,128)S(1)}, f32[2,8,32,1024]{3,2,1,0:T(8,128)}, u32[]{:S(2)}) copy-start(f32[2,8,32,1024]{3,2,1,0:T(8,128)} %x.3) | copy-start | bytes 6291460
  17.5 16.9 %copy-start.44 = (f32[64]{0:T(128)S(1)}, f32[64]{0:T(128)}, u32[]{:S(2)}) copy-start(f32[64]{0:T(128)} %thick.11) | copy-start | bytes 772
  17.6 16.9 %copy-start.46 = (bf16[16,128]{1,0:T(8,128)(2,1)S(1)}, bf16[16,128]{1,0:T(8,128)(2,1)}, u32[]{:S(2)}) copy-start(bf16[16,128]{1,0:T(8,128)(2,1)} %constant.49.clone.signs) | copy-start | bytes 12292
  32.6 1.3 copy-start.10
  34.0 16.3 %copy-start.26 = (f32[2,2,16,1024]{3,2,1,0:T(8,128)}, f32[2,2,16,1024]{3,2,1,0:T(8,128)S(1)}, u32[]{:S(2)}) copy-start(f32[2,2,16,1024]{3,2,1,0:T(8,128)S(1)} %get-tuple-element.33.keep) | copy-start | bytes 786436
  34.0 16.3 %collective-permute-start = (f32[2,2,16,1024]{3,2,1,0:T(8,128)S(1)}, f32[2,2,16,1024]{3,2,1,0:T(8,128)S(1)}, u32[]{:S(2)}, u32[]{:S(2)}) collective-permute-start(f32[2,2,16,1024]{3,2,1,0:T(8,128)S(1)} %get-tuple-element.34), channel_id=1, source_target_pairs={{0,4},{4,0},{8,12},{12,8},{16,20},{20,16},{24,28},{28,24},{1,5},{5... | collective-permute-start | bytes 786440 | tf_op jit(solution)/shard_map/ppermute | solution.py:587
  49.6 0.6 copy-start.41
  50.2 9.5 %copy-start.8 = (f32[2,8,32,1024]{3,2,1,0:T(8,128)}, f32[2,8,32,1024]{3,2,1,0:T(8,128)S(1)}, u32[]{:S(2)}) copy-start(f32[2,8,32,1024]{3,2,1,0:T(8,128)S(1)} %get-tuple-element.42.b) | copy-start | bytes 6291460
  50.2 22.3 %copy-start.49 = (f32[32]{0:T(128)S(1)}, f32[32]{0:T(128)}, u32[]{:S(2)}) copy-start(f32[32]{0:T(128)} %shifts.1) | copy-start | bytes 388
  50.2 8.7 %collective-permute-start.5 = (f32[2,2,16,1024]{3,2,1,0:T(8,128)S(1)}, f32[2,2,16,1024]{3,2,1,0:T(8,128)S(1)}, u32[]{:S(2)}, u32[]{:S(2)}) collective-permute-start(f32[2,2,16,1024]{3,2,1,0:T(8,128)S(1)} %get-tuple-element.44), channel_id=1, source_target_pairs={{0,4},{4,0},{8,12},{12,8},{16,20},{20,16},{24,28},{28,24},{1,5},{5... | collective-permute-start | bytes 786440 | tf_op jit(solution)/shard_map/ppermute | solution.py:587
  51.1 0.7 copy-start.28
  51.8 10.3 %collective-permute-start.1 = (f32[2,16,1024]{2,1,0:T(8,128)S(1)}, f32[2,16,1024]{2,1,0:T(8,128)S(1)}, u32[]{:S(2)}, u32[]{:S(2)}) collective-permute-start(f32[2,16,1024]{2,1,0:T(8,128)S(1)} %get-tuple-element.37), channel_id=1, source_target_pairs={{0,8},{4,12},{8,16},{12,20},{16,24},{20,28},{24,0},{28,4},{1,9},{5... | collective-permute-start | bytes 393224 | tf_op jit(solution)/shard_map/ppermute | solution.py:590
  54.9 18.2 %collective-permute-start.2 = (f32[2,16,1024]{2,1,0:T(8,128)}, f32[2,16,1024]{2,1,0:T(8,128)}, u32[]{:S(2)}, u32[]{:S(2)}) collective-permute-start(f32[2,16,1024]{2,1,0:T(8,128)} %get-tuple-element.38), channel_id=1, source_target_pairs={{0,16},{4,20},{8,24},{12,28},{16,0},{20,4},{24,8},{28,12},{1,17},{... | collective-permute-start | bytes 393224 | tf_op jit(solution)/shard_map/ppermute | solution.py:590
  57.5 15.6 %collective-permute-start.3 = (f32[2,16,1024]{2,1,0:T(8,128)}, f32[2,16,1024]{2,1,0:T(8,128)}, u32[]{:S(2)}, u32[]{:S(2)}) collective-permute-start(f32[2,16,1024]{2,1,0:T(8,128)} %get-tuple-element.39), channel_id=1, source_target_pairs={{0,24},{4,28},{8,0},{12,4},{16,8},{20,12},{24,16},{28,20},{1,25},{... | collective-permute-start | bytes 393224 | tf_op jit(solution)/shard_map/ppermute | solution.py:590
  59.7 0.7 copy-start.22
  60.4 0.7 copy-start.24
  61.1 19.6 %collective-permute-start.6 = (f32[2,16,1024]{2,1,0:T(8,128)}, f32[2,16,1024]{2,1,0:T(8,128)}, u32[]{:S(2)}, u32[]{:S(2)}) collective-permute-start(f32[2,16,1024]{2,1,0:T(8,128)} %get-tuple-element.45), channel_id=1, source_target_pairs={{0,8},{4,12},{8,16},{12,20},{16,24},{20,28},{24,0},{28,4},{1,9},{5... | collective-permute-start | bytes 393224 | tf_op jit(solution)/shard_map/ppermute | solution.py:590
  61.8 18.9 %collective-permute-start.7 = (f32[2,16,1024]{2,1,0:T(8,128)}, f32[2,16,1024]{2,1,0:T(8,128)}, u32[]{:S(2)}, u32[]{:S(2)}) collective-permute-start(f32[2,16,1024]{2,1,0:T(8,128)} %get-tuple-element.46), channel_id=1, source_target_pairs={{0,16},{4,20},{8,24},{12,28},{16,0},{20,4},{24,8},{28,12},{1,17},{... | collective-permute-start | bytes 393224 | tf_op jit(solution)/shard_map/ppermute | solution.py:590
  62.1 0.7 copy-start.38
  62.8 17.9 %collective-permute-start.8 = (f32[2,16,1024]{2,1,0:T(8,128)}, f32[2,16,1024]{2,1,0:T(8,128)}, u32[]{:S(2)}, u32[]{:S(2)}) collective-permute-start(f32[2,16,1024]{2,1,0:T(8,128)} %get-tuple-element.47), channel_id=1, source_target_pairs={{0,24},{4,28},{8,0},{12,4},{16,8},{20,12},{24,16},{28,20},{1,25},{... | collective-permute-start | bytes 393224 | tf_op jit(solution)/shard_map/ppermute | solution.py:590
  65.6 28.8 %all-to-all-start = ((f32[32,4,128]{2,1,0:T(4,128)}), f32[32,4,128]{2,1,0:T(4,128)}, u32[]{:S(2)}, u32[]{:S(2)}) async-start(f32[32,4,128]{2,1,0:T(4,128)} %copy-done.41), calls=%async_computation | async-start | bytes 131072 | tf_op jit(solution)/shard_map/all_to_all | solution.py:593
  73.1 1.0 copy-start.7
  74.2 1.0 copy-start.21
  75.2 0.9 copy-start.27
  76.1 0.9 copy-start.29
  77.1 0.9 copy-start.39
  79.8 0.7 copy-start.34
  80.5 31.0 %collective-permute-start.4 = (f32[2,2,16,1024]{3,2,1,0:T(8,128)}, f32[2,2,16,1024]{3,2,1,0:T(8,128)}, u32[]{:S(2)}, u32[]{:S(2)}) collective-permute-start(f32[2,2,16,1024]{3,2,1,0:T(8,128)} %get-tuple-element.41), channel_id=1, source_target_pairs={{0,4},{4,0},{8,12},{12,8},{16,20},{20,16},{24,28},{28,24},{1,5},{5... | collective-permute-start | bytes 786440 | tf_op jit(solution)/shard_map/ppermute | solution.py:587
  80.7 1.0 copy-start.23
  81.7 0.9 copy-start.25
  84.5 0.7 copy-start.36
  85.2 51.7 %collective-permute-start.9 = (f32[2,2,16,1024]{3,2,1,0:T(8,128)}, f32[2,2,16,1024]{3,2,1,0:T(8,128)}, u32[]{:S(2)}, u32[]{:S(2)}) collective-permute-start(f32[2,2,16,1024]{3,2,1,0:T(8,128)} %get-tuple-element.49), channel_id=1, source_target_pairs={{0,4},{4,0},{8,12},{12,8},{16,20},{20,16},{24,28},{28,24},{1,5},{5... | collective-permute-start | bytes 786440 | tf_op jit(solution)/shard_map/ppermute | solution.py:587
  93.8 0.7 copy-start.32
  94.4 0.9 copy-start.33
  95.3 0.9 copy-start.40
  111.5 3.4 %copy-start.1 = (f32[65,32,1024]{2,1,0:T(8,128)S(1)}, f32[65,32,1024]{2,1,0:T(8,128)}, u32[]{:S(2)}) copy-start(f32[65,32,1024]{2,1,0:T(8,128)} %copy-done) | copy-start | bytes 25559044
  115.0 1.6 %copy-start.11 = (f32[2,8,32,1024]{3,2,1,0:T(8,128)S(1)}, f32[2,8,32,1024]{3,2,1,0:T(8,128)}, u32[]{:S(2)}) copy-start(f32[2,8,32,1024]{3,2,1,0:T(8,128)} %copy-done.10) | copy-start | bytes 6291460
  116.6 1.0 copy-start.12
  117.6 1.0 copy-start.13
  118.6 0.8 copy-start.31
  119.4 0.9 copy-start.35
  120.3 16.6 %copy-start.9 = (f32[2,8,32,1024]{3,2,1,0:T(8,128)S(1)}, f32[2,8,32,1024]{3,2,1,0:T(8,128)}, u32[]{:S(2)}) copy-start(f32[2,8,32,1024]{3,2,1,0:T(8,128)} %copy-done.8) | copy-start | bytes 6291460
  120.4 16.6 %copy-start.37 = (f32[2,2,16,1024]{3,2,1,0:T(8,128)S(1)}, f32[2,2,16,1024]{3,2,1,0:T(8,128)}, u32[]{:S(2)}) copy-start(f32[2,2,16,1024]{3,2,1,0:T(8,128)} %copy-done.36) | copy-start | bytes 786436

commit v5 on v4

v5 whole, which is shorter than its diff:
```python
import functools
import math

import jax
import jax.numpy as jnp
import numpy as np
from jax import lax
from jax.experimental import pallas as pl
from jax.experimental.pallas import tpu as pltpu
from jax.sharding import PartitionSpec as P

aspect_ratio = 1.0
LANES = 128
ROWS = 8
VMEM_BYTES = 60 * 1024 * 1024
real_dot = functools.partial(jnp.dot, preferred_element_type=jnp.float32)
exact_dot = functools.partial(lax.dot_general, precision=lax.Precision.HIGHEST, preferred_element_type=jnp.float32)
NN = (((1,), (0,)), ((), ()))
NT = (((1,), (1,)), ((), ()))
in_smem = pl.BlockSpec(memory_space=pltpu.SMEM)
in_hbm = pl.BlockSpec(memory_space=pl.ANY)
in_vmem = pl.BlockSpec(memory_space=pltpu.VMEM)
params = pltpu.CompilerParams(vmem_limit_bytes=VMEM_BYTES)


def wave_order(size):
    return np.concatenate([np.arange(1, size, 2), np.arange(0, size, 2)])


def half_sines(size, back=False):
    half = size // 2
    place = np.arange(half)
    place[0] = half
    parts = []
    for waves in (np.arange(1, size, 2), np.arange(0, size, 2)):
        matrix = np.sin(np.pi * (np.outer(place, waves) % (2 * size)) / size)
        if waves[0] == 0:
            matrix[0] = 0.0
            matrix[:, 0] = 0.0
        matrix = (matrix.T if back else matrix).astype(np.float32)
        top = matrix.astype(jnp.bfloat16)
        parts += [top, (matrix - top.astype(np.float32)).astype(jnp.bfloat16)]
    return parts


def edge_matrix(size, total):
    matrix = np.full((2 * LANES, 2 * total), 2.0 / size, np.float32)
    matrix[LANES:, total:] = -2.0 / size
    return matrix.astype(jnp.bfloat16)


def spread_matrix(total):
    matrix = np.ones((2 * total, 2 * LANES), np.float32)
    matrix[total:, LANES:] = -1.0
    return matrix.astype(jnp.bfloat16)


def interface_matrices(waves, size):
    classes = waves // 2 + 1
    matrix = np.zeros((2, classes, 2, waves, 4, waves, 4))
    for c in range(classes):
        weight = (1.0 if c in (0, waves // 2) else 2.0) / (size * waves)
        for w in range(waves):
            for e in range(2):
                for v in range(waves):
                    for g in range(2):
                        value = weight * math.cos(2.0 * math.pi * (c * (w + e - v - g) % waves) / waves)
                        for f in range(4):
                            matrix[g, c, e, w, f, v, f] = value
    return matrix.reshape(2, classes * 2 * waves * 4, waves * 4).astype(np.float32)


def split(values):
    high = values.astype(jnp.bfloat16)
    return high, (values - high.astype(jnp.float32)).astype(jnp.bfloat16)


def product(values, top, rest):
    high, low = split(values)
    return real_dot(high, top[...]) + (real_dot(low, top[...]) + real_dot(high, rest[...]))


def mirror(values):
    rows = values.shape[0]
    lane = lax.broadcasted_iota(jnp.int32, (rows, LANES), 1)
    back = (LANES - lane) % LANES
    tiles = [values[:, a * LANES:(a + 1) * LANES] for a in range(values.shape[1] // LANES)]
    many = len(tiles)
    out = []
    for a in range(many):
        turned = jnp.take_along_axis(tiles[many - 1 - a], back, axis=1)
        out.append(jnp.where(lane == 0, tiles[(many - a) % many], turned))
    return jnp.concatenate(out, 1) if many > 1 else out[0]


def to_waves(values, odd_top, odd_rest, even_top, even_rest):
    half = values.shape[1] // 2
    low, high = values[:, :half], mirror(values[:, half:])
    lane = lax.broadcasted_iota(jnp.int32, low.shape, 1)
    low = jnp.where(lane == 0, 0.0, low)
    return product(low + high, odd_top, odd_rest), product(low - high, even_top, even_rest)


def to_cells(odd, even, odd_top, odd_rest, even_top, even_rest):
    p, m = product(odd, odd_top, odd_rest), product(even, even_top, even_rest)
    return p + m, mirror(p - m)


class Copies:
    def __init__(self, sems):
        self.sems, self.used = sems, 0

    def start(self, source, target):
        copy = pltpu.make_async_copy(source, target, self.sems.at[self.used])
        self.used += 1
        copy.start()
        return copy


def coefficients(levels, total, group, place, thick, face, shifts, across, t_out, r_out, m_out, end_out, pair_out, far_out, lam, m_chip, r_chip, f_chip, n_chip, u_chip, down_all, up_all):
    ky = lam.shape[0]
    span = 2 * levels
    chips = total // span
    chip = place[0] // 2
    start = chip * span
    upper = place[0] % 2 == 0
    own = (place[0] % 2) * levels
    for row in range(ky):
        lam[row:row + 1, :] = across[...] + shifts[row]

    def down_step(shift, j, f, r):
        m = face[j] * r
        f = shift * thick[j] + m * f
        return m, f, 1.0 / (face[j + 1] + f)

    def up_step(shift, j, phi, s):
        n = face[j + 1] * s
        u = n * phi
        phi = shift * thick[j] + u
        return n, u, phi, 1.0 / (face[j] + phi)

    def part(g, _):
        here = pl.ds(pl.multiple_of(g * group, group), group)
        shift = lam[here]
        one = jnp.ones_like(shift)
        zero = jnp.zeros_like(shift)

        def down_chip(c, state):
            f, r = state
            product = one
            for i in range(span):
                m, f, r = down_step(shift, c * span + i, f, r)
                t_out[c * span + i, here] = m
                product = product * m
            down_all[c] = product
            return f, r

        def up_chip(back, state):
            phi, s = state
            c = chips - 1 - back
            product = one
            for i in range(span - 1, -1, -1):
                n, _, phi, s = up_step(shift, c * span + i, phi, s)
                t_out[c * span + i + 1, here] = n
                product = product * n
            up_all[c] = product
            return phi, s

        f, r = lax.fori_loop(0, chip, down_chip, (one, one))
        for i in range(span):
            m, f, r = down_step(shift, start + i, f, r)
            m_chip[i], f_chip[i], r_chip[i] = m, f, r
        phi, s = lax.fori_loop(0, chips - 1 - chip, up_chip, (zero, zero))
        for i in range(span - 1, -1, -1):
            n, u, phi, s = up_step(shift, start + i, phi, s)
            n_chip[i], u_chip[i] = n, u

        for i in range(levels):
            t_out[start + i, here] = m_chip[i]
            t_out[start + levels + 1 + i, here] = n_chip[levels + i]
        t_out[start + levels, here] = jnp.where(upper, n_chip[levels - 1], m_chip[levels])
        for i in range(levels):
            r_out[i, here] = r_chip[own + i]
            m_out[i, here] = m_chip[own + i]
        last = own + levels - 1
        end_out[0, here] = n_chip[last]
        end_out[1, here] = 1.0 / (f_chip[last] + u_chip[last])
        end_out[2, here] = f_chip[own] + u_chip[own]
        for core in range(2):
            down, up = m_chip[core * levels], n_chip[core * levels]
            for i in range(1, levels):
                down = down * m_chip[core * levels + i]
                up = up * n_chip[core * levels + i]
            pair_out[core, here] = down
            pair_out[2 + core, here] = up
        above, below = [one], [one]
        for apart in range(1, chips - 1):
            above.append(above[-1] * jnp.where(chip >= apart, down_all[jnp.maximum(chip - apart, 0)], one))
            below.append(below[-1] * jnp.where(chip + apart < chips, up_all[jnp.minimum(chip + apart, chips - 1)], one))
        for apart in range(1, chips):
            far_out[apart - 1, here] = jnp.where(chip >= apart, above[apart - 1], below[chips - apart - 1])
        return 0

    lax.fori_loop(0, ky // group, part, 0)


def lane_sum(values):
    tiles = [values[:, t * LANES:(t + 1) * LANES] for t in range(values.shape[1] // LANES)]
    while len(tiles) > 1:
        tiles = [a + b for a, b in zip(tiles[0::2], tiles[1::2])] + tiles[len(tiles) // 2 * 2:]
    return tiles[0]


def front_kernel(levels, total, group, place, thick, face, shifts, across, sines, edge_mix, x0, x1, odd_top, odd_rest, even_top, even_rest, t_out, r_out, m_out, end_out, pair_out, far_out, b_out, keep_out, give_out, edge_out, sems, *scratch):
    across_v, sines_v, mix_v, x, ot, orest, et, er, t, r, m, end, pair, far, b, c_all, z_all, sums, edges, lam, *work = scratch
    _, _, _, ky, size = x.shape
    first = place[0] * levels
    half = size // 2
    copies = Copies(sems)
    early = [copies.start(across, across_v)]
    fields = [copies.start(x0, x.at[0])]
    mats = [copies.start(source, target) for source, target in ((odd_top, ot), (odd_rest, orest), (even_top, et), (even_rest, er))]
    mats += [copies.start(sines, sines_v)]
    fields += [copies.start(x1, x.at[1])]
    late = [copies.start(edge_mix, mix_v)]
    for copy in early:
        copy.wait()
    coefficients(levels, total, group, place, thick, face, shifts, across_v, t, r, m, end, pair, far, lam, *work)
    outs = [copies.start(source, target) for source, target in ((pair, pair_out), (far, far_out))]
    outs += [copies.start(source, target) for source, target in ((t, t_out), (r, r_out), (m, m_out), (end, end_out))]
    for copy in mats:
        copy.wait()
    lane = lax.broadcasted_iota(jnp.int32, (ROWS, LANES), 1)
    spot = jnp.where(lane == 0, size / 4.0, 0.0)
    core = place[0] % 2

    def put(f, rows, values, height, own=None):
        odd, even = lane_sum(values[:, :half]) * height, lane_sum(values[:, half:]) * height
        if own is not None:
            odd, even = odd + own, even + own
        sums[f, 0, rows, :] = odd
        sums[f, 1, rows, :] = even

    for a in range(2):
        fields[a].wait()
        odd, even = to_waves(x[a].reshape(2 * levels * ky, size), ot, orest, et, er)
        for ri in range(2):
            for j in range(levels):
                rows = slice((ri * levels + j) * ky, (ri * levels + j + 1) * ky)
                scale = thick[first + j] if a == 0 else 1.0
                b[a, ri, j, :, :half] = odd[rows] * scale
                b[a, ri, j, :, half:] = even[rows] * scale
        outs.append(copies.start(b.at[a], b_out.at[a]))
        for ri in range(2):
            f = 2 * a + ri

            def tile(g, _):
                here = pl.ds(pl.multiple_of(g * ROWS, ROWS), ROWS)
                wave = sines_v[...]
                y = b[a, ri, 0, here]
                ys = [y]
                for j in range(1, levels):
                    y = b[a, ri, j, here] + m[j, here] * y
                    ys.append(y)
                c_all[a, 0, ri, here] = y
                value = y * end[1, here]
                z_all[1, f, here] = value * wave
                for j in range(levels - 1, -1, -1):
                    if j < levels - 1:
                        value = r[j, here] * ys[j] + m[j + 1, here] * value
                    height = thick[first + j]
                    own = jnp.broadcast_to(x[a, ri, j, here, 0:1], (ROWS, LANES)) * (spot * height if a == 0 else spot)
                    put(f, pl.ds(g * ROWS * total + first + j, ROWS, stride=total), value * wave, height, own)
                z_all[0, f, here] = value * wave
                c_all[a, 1, ri, here] = value * end[2, here]
                return 0

            lax.fori_loop(0, ky // ROWS, tile, 0)
        for start, out in ((core, keep_out), (1 - core, give_out)):
            here = pl.ds(pl.multiple_of(start * (ky // 2), ROWS), ky // 2)
            outs.append(copies.start(c_all.at[a, :, :, here], out.at[a]))

    def reach(g, _):
        here = pl.ds(pl.multiple_of(g * ROWS, ROWS), ROWS)

        def up(block, z):
            for i in range(levels):
                j = first - 1 - block * levels - i
                step = t[j + 1, here]
                z = [step * one for one in z]
                for f in range(4):
                    put(f, pl.ds(g * ROWS * total + j, ROWS, stride=total), z[f], thick[j])
            return z

        def down(block, z):
            for i in range(levels):
                j = first + levels + block * levels + i
                step = t[j, here]
                z = [step * one for one in z]
                for f in range(4):
                    put(f, pl.ds(g * ROWS * total + j, ROWS, stride=total), z[f], thick[j])
            return z

        lax.fori_loop(0, place[0], up, [z_all[0, f, here] for f in range(4)])
        lax.fori_loop(0, total // levels - 1 - place[0], down, [z_all[1, f, here] for f in range(4)])
        return 0

    lax.fori_loop(0, ky // ROWS, reach, 0)
    for copy in late:
        copy.wait()
    if edges.shape[0] > ky:
        edges[...] = jnp.zeros_like(edges)
    wide = 2 * total
    row = lax.broadcasted_iota(jnp.int32, (ky, total, wide), 1)
    column = lax.broadcasted_iota(jnp.int32, (ky, total, wide), 2)
    diagonal = (row == column) | (row + total == column)
    for f in range(4):
        high, low = split(jnp.concatenate([sums[f, 0], sums[f, 1]], 1))
        spread = (real_dot(high, mix_v[...]) + real_dot(low, mix_v[...])).reshape(ky, total, wide)
        edges[:ky, f, :] = jnp.sum(jnp.where(diagonal, spread, 0.0), axis=1)
    outs.append(copies.start(edges, edge_out))
    for copy in outs:
        copy.wait()


def front(place, thick, face, shifts, across, sines, rhs, cotangent, devices):
    _, levels, ky, size = rhs.shape
    total = thick.shape[0]
    chips = total // (2 * levels)
    group = min(2 * ROWS, ky)
    half = size // 2
    wide = 2 * total
    single = lambda *shape: pltpu.VMEM(shape, jnp.float32)
    tables = [(n, ky, size) for n in (total + 1, levels, levels, 3, 4, chips - 1)]
    shapes = tables + [(2, 2, levels, ky, size), (2, 2, 2, ky // 2, size), (2, 2, 2, ky // 2, size), (devices, 4, wide)]
    return pl.pallas_call(
        functools.partial(front_kernel, levels, total, group),
        in_specs=[in_smem] * 4 + [in_hbm] * 9,
        out_specs=[in_hbm] * len(shapes),
        out_shape=[jax.ShapeDtypeStruct(shape, jnp.float32) for shape in shapes],
        scratch_shapes=[
            pltpu.SemaphoreType.DMA((22,)),
            single(1, size),
            single(ROWS, size),
            pltpu.VMEM((2 * LANES, wide), jnp.bfloat16),
            single(2, 2, levels, ky, size),
            *[pltpu.VMEM((half, half), jnp.bfloat16)] * 4,
            *[single(*shape) for shape in tables],
            single(2, 2, levels, ky, size),
            single(2, 2, 2, ky, size),
            single(2, 4, ky, size),
            single(4, 2, ky * total, LANES),
            single(devices, 4, wide),
            single(ky, size),
            *[single(2 * levels, group, size)] * 5,
            *[single(chips, group, size)] * 2,
        ],
        compiler_params=params,
        name="front",
    )(place, thick, face, shifts, across, sines, edge_matrix(size, total), rhs, cotangent, *half_sines(size))


def chip_kernel(chips, place, keep, got, pair, *refs):
    outs = refs[:chips - 1]
    sems, keep_v, got_v, pair_v, down_v, up_v = refs[chips - 1:]
    copies = Copies(sems)
    chip = place[0] // 2
    upper = place[0] % 2 == 0
    half = keep_v.shape[3]
    here = pl.ds(pl.multiple_of((place[0] % 2) * half, ROWS), half)
    for copy in [copies.start(keep, keep_v), copies.start(got, got_v), copies.start(pair.at[:, here], pair_v)]:
        copy.wait()
    for a in range(2):
        first, second = jnp.where(upper, keep_v[a], got_v[a]), jnp.where(upper, got_v[a], keep_v[a])
        down_v[a] = second[0] + pair_v[1] * first[0]
        up_v[a] = first[1] + pair_v[2] * second[1]
    for apart in range(1, chips):
        goes_down = chip + apart < chips
        sem = sems.at[2 + apart]

        @pl.when(goes_down)
        def _():
            pltpu.make_async_copy(down_v, outs[apart - 1], sem).start()

        @pl.when(jnp.logical_not(goes_down))
        def _():
            pltpu.make_async_copy(up_v, outs[apart - 1], sem).start()

    for apart in range(1, chips):
        pltpu.make_async_copy(down_v, outs[apart - 1], sems.at[2 + apart]).wait()


def chip_sums(place, keep, got, pair, chips):
    _, _, _, half, size = keep.shape
    single = lambda *shape: pltpu.VMEM(shape, jnp.float32)
    shape = (2, 2, half, size)
    return pl.pallas_call(
        functools.partial(chip_kernel, chips),
        in_specs=[in_smem] + [in_hbm] * 3,
        out_specs=[in_hbm] * (chips - 1),
        out_shape=[jax.ShapeDtypeStruct(shape, jnp.float32)] * (chips - 1),
        scratch_shapes=[
            pltpu.SemaphoreType.DMA((2 + chips,)),
            single(*keep.shape),
            single(*keep.shape),
            single(4, half, size),
            single(*shape),
            single(*shape),
        ],
        compiler_params=params,
        name="chip_sums",
    )(place, keep, got, pair)


def join_kernel(chips, place, keep, got, pair, far, *refs):
    news = refs[:chips - 1]
    mine, theirs, sems, keep_v, got_v, pair_v, far_v, news_v, mine_v, theirs_v = refs[chips - 1:]
    copies = Copies(sems)
    chip = place[0] // 2
    upper = place[0] % 2 == 0
    half = keep_v.shape[3]
    here = pl.ds(pl.multiple_of((place[0] % 2) * half, ROWS), half)
    ready = [copies.start(keep, keep_v), copies.start(got, got_v), copies.start(pair.at[:, here], pair_v), copies.start(far.at[:, here], far_v)]
    ready += [copies.start(news[i], news_v.at[i]) for i in range(chips - 1)]
    for copy in ready:
        copy.wait()
    for a in range(2):
        for ri in range(2):
            first, second = (keep_v, got_v), (got_v, keep_v)
            pick = lambda refs, way: jnp.where(upper, refs[0][a, way, ri], refs[1][a, way, ri])
            down = jnp.zeros((half, keep_v.shape[4]), jnp.float32)
            up = down
            for apart in range(1, chips):
                term = far_v[apart - 1] * news_v[apart - 1, a, ri]
                down = down + jnp.where(chip >= apart, term, 0.0)
                up = up + jnp.where(chip >= apart, 0.0, term)
            inner_up = pick(second, 1) + pair_v[3] * up
            inner_down = pick(first, 0) + pair_v[0] * down
            mine_v[a, 0, ri] = jnp.where(upper, down, inner_down)
            mine_v[a, 1, ri] = jnp.where(upper, inner_up, up)
            theirs_v[a, 0, ri] = jnp.where(upper, inner_down, down)
            theirs_v[a, 1, ri] = jnp.where(upper, up, inner_up)
    for copy in [copies.start(theirs_v, theirs), copies.start(mine_v, mine)]:
        copy.wait()


def join(place, keep, got, pair, far, news):
    chips = len(news) + 1
    _, _, _, half, size = keep.shape
    single = lambda *shape: pltpu.VMEM(shape, jnp.float32)
    return pl.pallas_call(
        functools.partial(join_kernel, chips),
        in_specs=[in_smem] + [in_hbm] * (3 + chips),
        out_specs=[in_hbm] * 2,
        out_shape=[jax.ShapeDtypeStruct(keep.shape, jnp.float32)] * 2,
        scratch_shapes=[
            pltpu.SemaphoreType.DMA((5 + chips,)),
            single(*keep.shape),
            single(*keep.shape),
            single(4, half, size),
            single(chips - 1, half, size),
            single(chips - 1, 2, 2, half, size),
            single(*keep.shape),
            single(*keep.shape),
        ],
        compiler_params=params,
        name="join",
    )(place, keep, got, pair, far, *news)


def inverse_kernel(per, thick, face, lam, out, m_all, f_all, g_all):
    total = f_all.shape[0]
    rows = lam.shape[0]
    classes = out.shape[0]
    shift = lam[...]
    one = jnp.ones_like(shift)
    zero = jnp.zeros_like(shift)

    def step(j, state):
        f, r, phi, s = state
        m = face[j] * r
        f = shift * thick[j] + m * f
        r = 1.0 / (face[j + 1] + f)
        m_all[j] = m
        f_all[j] = f
        i = total - 1 - j
        u = face[i + 1] * s * phi
        phi = shift * thick[i] + u
        s = 1.0 / (face[i] + phi)
        g_all[i] = u
        return f, r, phi, s

    lax.fori_loop(0, total, step, (one, one, zero, zero))

    def centre(j, _):
        g_all[j] = 1.0 / (f_all[j] + g_all[j])
        return 0

    lax.fori_loop(0, total, centre, 0)
    wide = out.shape[2]
    sub = lax.broadcasted_iota(jnp.int32, (ROWS, LANES), 0)
    lane = lax.broadcasted_iota(jnp.int32, (ROWS, wide), 1)
    row = lax.broadcasted_iota(jnp.int32, (ROWS, wide), 0)
    line = lambda ref, j, t: jnp.broadcast_to(ref[j, t:t + 1, :], (ROWS, LANES))

    def put(j, z, sums):
        new = []
        for c in range(classes):
            tiles = z[c * per:(c + 1) * per]
            total_tile = tiles[0]
            for tile in tiles[1:]:
                total_tile = total_tile + tile
            value = jnp.sum(total_tile, axis=1, keepdims=True)
            new.append(jnp.where(lane == j, value, sums[c]))
        return new

    for base in range(0, total, ROWS):
        z = [jnp.zeros((ROWS, LANES), jnp.float32)] * (classes * per)
        sums = [jnp.zeros((ROWS, wide), jnp.float32)] * classes
        for i in range(ROWS - 1, -1, -1):
            j = base + i
            for t in range(classes * per):
                moved = z[t] * line(m_all, j + 1, t) if i < ROWS - 1 else z[t]
                z[t] = jnp.where(sub == i, line(g_all, j, t), moved)
            sums = put(j, z, sums)

        def above(back, state):
            z, sums = state
            for i in range(ROWS):
                j = base - 1 - back * ROWS - i
                z = [z[t] * line(m_all, j + 1, t) for t in range(classes * per)]
                sums = put(j, z, sums)
            return z, sums

        if base:
            z, sums = lax.fori_loop(0, base // ROWS, above, (z, sums))
        for c in range(classes):
            out[c, base:base + ROWS, :] = sums[c] * jnp.where(lane == base + row, 0.5, 1.0)


def inverse_sums(thick, face, lam, per):
    total = thick.shape[0]
    classes = lam.shape[0] // per
    wide = -(-total // LANES) * LANES
    spare = -lam.shape[0] % ROWS
    lam = jnp.pad(lam, ((0, spare), (0, 0)), constant_values=1.0) if spare else lam
    return pl.pallas_call(
        functools.partial(inverse_kernel, per),
        in_specs=[in_smem, in_smem, in_vmem],
        out_shape=jax.ShapeDtypeStruct((classes, total, wide), jnp.float32),
        scratch_shapes=[pltpu.VMEM((total,) + lam.shape, jnp.float32)] * 3,
        compiler_params=params,
        name="inverse_sums",
    )(thick, face, lam)


def interface_kernel(waves, matrices, edges, inverse, out):
    devices, _, wide = edges.shape
    total = wide // 2
    rows = 4 * waves
    lines = []
    for w in range(waves):
        line = edges[w]
        for d in range(1, devices // waves):
            line = line + edges[d * waves + w]
        lines.append(line)
    lines = jnp.concatenate(lines, 0)
    near, far = exact_dot(matrices[0], lines, NN), exact_dot(matrices[1], lines, NN)
    mixed = near[:, :total] + far[:, total:]
    result = jnp.zeros((2 * rows, total), jnp.float32)
    for c in range(inverse.shape[0]):
        part = mixed[c * 2 * rows:(c + 1) * 2 * rows]
        square = inverse[c][:, :total]
        result = result + (exact_dot(part, square, NN) + exact_dot(part, square, NT))
    result = jnp.concatenate([result[:rows], result[rows:]], 1)
    for w in range(waves):
        line = result[4 * w:4 * w + 4]
        for d in range(devices // waves):
            out[d * waves + w] = line


def interface(edges, inverse, waves, size):
    return pl.pallas_call(
        functools.partial(interface_kernel, waves),
        in_specs=[in_vmem] * 3,
        out_specs=in_vmem,
        out_shape=jax.ShapeDtypeStruct(edges.shape, jnp.float32),
        compiler_params=params,
        name="interface",
    )(interface_matrices(waves, size), edges, inverse)


def back_kernel(levels, total, place, thick, values, spread, t, mine, theirs, sines, b, r, m, end, odd_top, odd_rest, even_top, even_rest, out0, out1, sems, values_v, spread_v, t_v, ends, sines_v, b_v, r_v, m_v, end_v, ot, orest, et, er, picked, u_all, q_all, out_v):
    _, _, _, ky, size = b_v.shape
    first = place[0] * levels
    half = size // 2
    many = half // LANES
    core = place[0] % 2
    copies = Copies(sems)
    early = [copies.start(values.at[pl.ds(0, ky)], values_v), copies.start(spread, spread_v)]
    table = copies.start(t, t_v)
    both = []
    for source, start in ((mine, core), (theirs, 1 - core)):
        here = pl.ds(pl.multiple_of(start * (ky // 2), ROWS), ky // 2)
        both.append(copies.start(source, ends.at[:, :, :, here]))
    both.append(copies.start(sines, sines_v))
    rest = [copies.start(source, target) for source, target in ((r, r_v), (m, m_v), (end, end_v), (b, b_v), (odd_top, ot), (odd_rest, orest), (even_top, et), (even_rest, er))]
    for copy in early:
        copy.wait()
    lane = lax.broadcasted_iota(jnp.int32, (ky, 2 * total), 1)
    for f in range(4):
        parts = [part.astype(jnp.float32) for part in split(values_v[:, f, :])]
        for j in range(total):
            spot = (lane == j) | (lane == total + j)
            for p in range(2):
                picked[p, j * ky:(j + 1) * ky, :] = jnp.where(spot, parts[p], 0.0).astype(jnp.bfloat16)
        u_all[f] = (real_dot(picked[0], spread_v[...]) + real_dot(picked[1], spread_v[...])).reshape(total, ky, 2 * LANES)
    table.wait()
    for copy in both:
        copy.wait()

    def source(f, j, here):
        pair = u_all[f, j, here] * thick[j]
        return jnp.concatenate([pair[:, :LANES]] * many + [pair[:, LANES:]] * many, 1)

    def sweep(g, _):
        here = pl.ds(pl.multiple_of(g * ROWS, ROWS), ROWS)

        def from_above(block, y):
            for i in range(levels):
                j = block * levels + i
                step = t_v[j, here]
                y = [step * y[f] + source(f, j, here) for f in range(4)]
            return y

        def from_below(block, y):
            for i in range(levels):
                j = total - 1 - block * levels - i
                step = t_v[j + 1, here]
                y = [step * y[f] + source(f, j, here) for f in range(4)]
            return y

        zero = [jnp.zeros((ROWS, size), jnp.float32)] * 4
        wave = sines_v[...]
        for way, y in (
            (0, lax.fori_loop(0, place[0], from_above, zero)),
            (1, lax.fori_loop(0, total // levels - 1 - place[0], from_below, zero)),
        ):
            for f in range(4):
                ends[f // 2, way, f % 2, here] += wave * y[f]
        return 0

    lax.fori_loop(0, ky // ROWS, sweep, 0)
    for copy in rest:
        copy.wait()
    rows = levels * ky
    lane = lax.broadcasted_iota(jnp.int32, (ky, LANES), 1)
    outs = []
    for f in range(4):
        a, ri = f // 2, f % 2

        def tile(g, _):
            here = pl.ds(pl.multiple_of(g * ROWS, ROWS), ROWS)
            wave = sines_v[...]
            y = ends[a, 0, ri, here]
            ys = []
            for j in range(levels):
                y = b_v[a, ri, j, here] + wave * source(f, first + j, here) + m_v[j, here] * y
                ys.append(y)
            value = (y + end_v[0, here] * ends[a, 1, ri, here]) * end_v[1, here]
            q_all[levels - 1, here] = value
            for j in range(levels - 2, -1, -1):
                value = r_v[j, here] * ys[j] + m_v[j + 1, here] * value
                q_all[j, here] = value
            return 0

        lax.fori_loop(0, ky // ROWS, tile, 0)
        low, high = to_cells(
            q_all[:, :, :half].reshape(rows, half), q_all[:, :, half:].reshape(rows, half), ot, orest, et, er
        )
        for j in range(levels):
            height = thick[first + j] if a else 1.0
            scale = (2.0 / size) * height
            here = slice(j * ky, (j + 1) * ky)
            u = (u_all[f, first + j, :, :LANES] + u_all[f, first + j, :, LANES:]) * (0.5 * height)
            if many > 1:
                out_v[f, j, :, LANES:half] = low[here, LANES:] * scale
            out_v[f, j, :, :LANES] = jnp.where(lane == 0, u, low[here, :LANES] * scale)
            out_v[f, j, :, half:] = high[here] * scale
        outs.append(copies.start(out_v.at[f], (out0, out1)[a].at[ri]))
    for copy in outs:
        copy.wait()


def back(place, thick, values, sines, t, r, m, end, b, mine, theirs):
    _, _, levels, ky, size = b.shape
    total = t.shape[0] - 1
    half = size // 2
    single = lambda *shape: pltpu.VMEM(shape, jnp.float32)
    return pl.pallas_call(
        functools.partial(back_kernel, levels, total),
        in_specs=[in_smem] * 2 + [in_hbm] * 14,
        out_specs=[in_hbm] * 2,
        out_shape=[jax.ShapeDtypeStruct((2, levels, ky, size), jnp.float32)] * 2,
        scratch_shapes=[
            pltpu.SemaphoreType.DMA((18,)),
            single(ky, 4, 2 * total),
            pltpu.VMEM((2 * total, 2 * LANES), jnp.bfloat16),
            single(*t.shape),
            single(2, 2, 2, ky, size),
            single(ROWS, size),
            single(*b.shape),
            single(*r.shape),
            single(*m.shape),
            single(*end.shape),
            *[pltpu.VMEM((half, half), jnp.bfloat16)] * 4,
            pltpu.VMEM((2, total * ky, 2 * total), jnp.bfloat16),
            single(4, total, ky, 2 * LANES),
            single(levels, ky, size),
            single(4, levels, ky, size),
        ],
        compiler_params=params,
        name="back",
    )(place, thick, values, spread_matrix(total), t, mine, theirs, sines, b, r, m, end, *half_sines(size, True))


def shards(rhs, cotangent, thickness, ky_shift):
    waves = lax.axis_size("wave")
    count = lax.axis_size("depth")
    depth_pos = lax.axis_index("depth")
    wave_pos = lax.axis_index("wave")
    _, levels, ky, size = rhs.shape
    full = waves * size
    devices = waves * count
    chips = count // 2
    place = depth_pos.astype(jnp.int32).reshape(1)

    def across(a):
        return lax.ppermute(a, "depth", [(d, d ^ 1) for d in range(count)])

    def along(a, apart):
        return lax.ppermute(a, "depth", [(d, (d + 2 * apart) % count) for d in range(count)])

    def everywhere(a):
        return lax.all_to_all(a, ("depth", "wave"), split_axis=0, concat_axis=0, tiled=True)

    def horizontal(wavenumber, length):
        return (aspect_ratio * 4.0 * np.sin(math.pi * wavenumber / length) ** 2).astype(np.float32)

    inner_face = 2.0 / (thickness[:-1] + thickness[1:])
    face = jnp.concatenate([2.0 / thickness[:1], inner_face, jnp.zeros((1,), jnp.float32)])
    order = wave_order(size)
    sines = np.broadcast_to(np.sin(np.pi * order / size)[None, :], (ROWS, size)).astype(np.float32)
    across_k = horizontal(order, 2 * size)[None, :]
    t, r, m, end, pair, far, b, keep, give, edges = front(
        place, thickness, face, ky_shift, across_k, sines, rhs, cotangent, devices
    )

    classes = waves // 2 + 1
    wavenumber = (np.arange(classes)[:, None] + waves * np.arange(size)[None, :]).reshape(-1, LANES)
    shifts = jnp.pad(ky_shift, (0, devices - ky), constant_values=1.0) if devices > ky else ky_shift
    my_shift = lax.dynamic_slice_in_dim(shifts, depth_pos * waves + wave_pos, 1)

    got = across(give)
    edges = everywhere(edges)
    sums = chip_sums(place, keep, got, pair, chips)
    news = [along(sums[apart - 1], apart) for apart in range(1, chips)]
    inverse = inverse_sums(thickness, face, my_shift + horizontal(wavenumber, full), size // LANES)
    values = everywhere(interface(edges, inverse, waves, size))
    mine, theirs = join(place, keep, got, pair, far, news)
    return back(place, thickness, values, sines, t, r, m, end, b, mine, across(theirs))


def solution(mesh):
    spec = P(None, "depth", None, "wave")
    return jax.shard_map(shards, mesh=mesh, in_specs=(spec, spec, P(), P()), out_specs=(spec, spec), check_vma=False)
```

time: 155 us -> 107 us (0.69)
  local copies, waits for them, and re-layouts: 36.6 us -> 3.64 us
  Pallas kernels: 80.5 us -> 50 us
  waiting for transfers between devices: 0.03 us -> 18.4 us
    unnamed x100 -> x16, local copies, waits for them, and re-layouts: 35.9 us -> 3.05 us
    pallas_call x5 -> x2, Pallas kernels: 66.8 us -> 35 us  [the longest x1 21.1 us: front(): pl.pallas_call(functools.partial(front_kernel, levels, total, group), in_...]
    ppermute x6 -> x3, waiting for transfers between devices: 0.02 us -> 16.6 us  [along(): lax.ppermute(a, 'depth', [(d, (d + 2 * apart) % count) for d in range(cou...]
    ppermute x6 -> x3, starting transfers between devices: 10.9 us -> 7.44 us  [along(): lax.ppermute(a, 'depth', [(d, (d + 2 * apart) % count) for d in range(cou...]
    all_to_all x1, starting transfers between devices: 6.82 us -> 9.12 us  [everywhere(): lax.all_to_all(a, ('depth', 'wave'), split_axis=0, concat_axis=0, tiled=T...]
    ppermute x4 -> x2, waiting for transfers between devices: 0.01 us -> 1.75 us  [across(): return lax.ppermute(a, 'depth', [(d, d ^ 1) for d in range(count)])]
    pallas_call x2 -> x1, Pallas kernels: 3.7 us -> 2.77 us  [join(): pl.pallas_call(functools.partial(join_kernel, chips), in_specs=[in_smem]...]
  transfers between devices with their start and end apart: 11 -> 6, of which waited for: 0 -> 3; matrix products, arithmetic and copies ran while one was open for 1% -> 2% of each run, Pallas kernels for 30% -> 9%
where the time goes in v5:
time: 107 us
  Pallas kernels  50 us (47%)
  waiting for transfers between devices  18.4 us (17%)
  starting transfers between devices  17.3 us (16%)
  blocking collectives  13.4 us (13%)
  local copies, waits for them, and re-layouts  3.64 us (3%)
  other arithmetic  2.65 us (2%)
  between operations  1.57 us (1%)
    pallas_call x1, Pallas kernels, front(): pl.pallas_call(functools.partial(front_kernel, levels, total, group), in_...  21.1 us
    ppermute x3, waiting for transfers between devices, along(): lax.ppermute(a, 'depth', [(d, (d + 2 * apart) % count) for d in range(cou...  16.6 us
    pallas_call x1, Pallas kernels, back(): pl.pallas_call(functools.partial(back_kernel, levels, total), in_specs=[i...  13.9 us
    all_to_all x1, blocking collectives, everywhere(): lax.all_to_all(a, ('depth', 'wave'), split_axis=0, concat_axis=0, tiled=T...  13.4 us
    all_to_all x1, starting transfers between devices, everywhere(): lax.all_to_all(a, ('depth', 'wave'), split_axis=0, concat_axis=0, tiled=T...  9.12 us
    pallas_call x1, Pallas kernels, inverse_sums(): pl.pallas_call(functools.partial(inverse_kernel, per), in_specs=[in_smem,...  7.68 us
    ppermute x3, starting transfers between devices, along(): lax.ppermute(a, 'depth', [(d, (d + 2 * apart) % count) for d in range(cou...  7.44 us
    unnamed x16, local copies, waits for them, and re-layouts  3.05 us
  transfers between devices with their start and end apart: 6, of which 3 were waited for; matrix products, arithmetic and copies ran while one was open for 2% of the time, Pallas kernels for 9%

profile of v5, /device:TPU:0, one launch (start us, length us, event | category | flops | bytes accessed | tf_op | source)
XLA Modules:
  0.0 106.9 jit_solution(15594714025424590860)
XLA Ops:
  0.6 0.8 add_divide_fusion
  2.1 0.6 pad_maximum_fusion.face
  2.7 21.1 %front.1 = (f32[65,32,1024]{2,1,0:T(8,128)}, f32[8,32,1024]{2,1,0:T(8,128)}, f32[8,32,1024]{2,1,0:T(8,128)}, f32[3,32,1024]{2,1,0:T(8,128)}, f32[4,32,1024]{2,1,...) custom-call(s32[1]{0:T(128)} %bitcast.place, ...), custom_call_target="tpu_custom_call" | custom-call | tf_op jit(solution)/shard_map/front/pallas_call | solution.py:336
  23.8 0.7 collective-permute-start
  24.5 1.7 %collective-permute-done.got = f32[2,2,2,16,1024]{4,3,2,1,0:T(8,128)S(1)} collective-permute-done((f32[2,2,2,16,1024]{4,3,2,1,0:T(8,128)}, f32[2,2,2,16,1024]{4,3,2,1,0:T(8,128)S(1)}, u32[]{:S(2)}, u32[]{:S(2)}) %collective-permute-start) | collective-permute-done | bytes 524320 | tf_op jit(solution)/shard_map/ppermute | solution.py:739
  26.2 0.0 copy-start
  26.2 0.8 copy-done
  27.1 0.0 copy-start.7
  27.1 0.0 copy-start.6
  27.1 2.2 %chip_sums.1 = (f32[2,2,16,1024]{3,2,1,0:T(8,128)}, f32[2,2,16,1024]{3,2,1,0:T(8,128)}, f32[2,2,16,1024]{3,2,1,0:T(8,128)}) custom-call(s32[1]{0:T(128)} %bitcast.place, f32[2,2,2,16,1024]{4,3,2,1,0:T(8,128)} %get-tuple-element.19.keep, f32[2,2,2,16,1024]{4,3,2,1,0:T(8,128)} %copy-done, f32[4,32,1024]{2,1,0:T(8,128)} %get-tuple-element.21.pair), custom_call_target="tpu_custom_call" | custom-call | tf_op jit(solution)/shard_map/chip_sums/pallas_call | solution.py:397
  29.3 3.2 %collective-permute-start.1 = (f32[2,2,16,1024]{3,2,1,0:T(8,128)}, f32[2,2,16,1024]{3,2,1,0:T(8,128)S(1)}, u32[]{:S(2)}, u32[]{:S(2)}) collective-permute-start(f32[2,2,16,1024]{3,2,1,0:T(8,128)} %get-tuple-element.23), channel_id=1, source_target_pairs={{0,8},{4,12},{8,16},{12,20},{16,24},{20,28},{24,0},{28,4},{1,9},{5... | collective-permute-start | bytes 786440 | tf_op jit(solution)/shard_map/ppermute | solution.py:742
  32.5 3.3 %collective-permute-start.2 = (f32[2,2,16,1024]{3,2,1,0:T(8,128)}, f32[2,2,16,1024]{3,2,1,0:T(8,128)S(1)}, u32[]{:S(2)}, u32[]{:S(2)}) collective-permute-start(f32[2,2,16,1024]{3,2,1,0:T(8,128)} %get-tuple-element.24), channel_id=1, source_target_pairs={{0,16},{4,20},{8,24},{12,28},{16,0},{20,4},{24,8},{28,12},{1,17},{... | collective-permute-start | bytes 786440 | tf_op jit(solution)/shard_map/ppermute | solution.py:742
  35.8 1.0 collective-permute-start.3
  36.7 5.9 %collective-permute-done.1.refs_0_ = f32[2,2,16,1024]{3,2,1,0:T(8,128)S(1)} collective-permute-done((f32[2,2,16,1024]{3,2,1,0:T(8,128)}, f32[2,2,16,1024]{3,2,1,0:T(8,128)S(1)}, u32[]{:S(2)}, u32[]{:S(2)}) %collective-permute-start.1) | collective-permute-done | bytes 262176 | tf_op jit(solution)/shard_map/ppermute | solution.py:742
  42.6 0.0 copy-start.2
  42.6 10.7 %collective-permute-done.2.refs_1_ = f32[2,2,16,1024]{3,2,1,0:T(8,128)S(1)} collective-permute-done((f32[2,2,16,1024]{3,2,1,0:T(8,128)}, f32[2,2,16,1024]{3,2,1,0:T(8,128)S(1)}, u32[]{:S(2)}, u32[]{:S(2)}) %collective-permute-start.2) | collective-permute-done | bytes 262176 | tf_op jit(solution)/shard_map/ppermute | solution.py:742
  53.4 0.0 copy-start.3
  53.4 0.0 collective-permute-done.3.refs_2_
  53.4 0.0 copy-start.4
  53.4 0.0 copy-done.2
  53.4 0.7 copy-done.3
  54.1 0.1 copy-done.4
  54.2 2.8 %join.1 = (f32[2,2,2,16,1024]{4,3,2,1,0:T(8,128)}, f32[2,2,2,16,1024]{4,3,2,1,0:T(8,128)}) custom-call(s32[1]{0:T(128)} %bitcast.place, f32[2,2,2,16,1024]{4,3,2,1,0:T(8,128)} %get-tuple-element.19.keep, f32[2,2,2,16,1024]{4,3,2,1,0:T(8,128)} %copy-done, f32[4,32,1024]{2,1,0:T(8,128)} %get-tuple-element.21.pair, f32[3,32,1024]{2,1,0:T(8,128)} %get-tuple-element.22.far, ...), custom_call_target="tpu_custom_call" | custom-call | tf_op jit(solution)/shard_map/join/pallas_call | solution.py:451
  57.0 0.1 collective-permute-start.4
  57.0 9.1 %all-to-all-start = ((f32[32,4,128]{2,1,0:T(4,128)}), f32[32,4,128]{2,1,0:T(4,128)S(1)}, u32[]{:S(2)}, u32[]{:S(2)}) async-start(f32[32,4,128]{2,1,0:T(4,128)} %get-tuple-element.17), calls=%async_computation | async-start | bytes 131072 | tf_op jit(solution)/shard_map/all_to_all | solution.py:745
  66.2 0.0 copy-done.7
  66.2 0.6 dynamic_slice.3
  66.8 0.0 copy-done.6
  66.8 1.2 %broadcast_add_fusion.lam = f32[24,128]{1,0:T(8,128)} fusion(f32[24,128]{1,0:T(8,128)S(1)} %copy-done.6, f32[]{:T(128)} %bitcast.1), kind=kLoop, calls=%fused_computation | loop fusion | flops 3072 | bytes 24580 | tf_op jit(solution)/shard_map/add | solution.py:768
  68.0 7.7 %inverse_sums.1.inverse = f32[3,64,128]{2,1,0:T(8,128)} custom-call(f32[64]{0:T(128)} %thick.5, f32[65]{0:T(128)} %pad_maximum_fusion.face, f32[24,128]{1,0:T(8,128)} %broadcast_add_fusion.lam), custom_call_target="tpu_custom_call" | custom-call | tf_op jit(solution)/shard_map/inverse_sums/pallas_call | solution.py:547
  75.7 0.0 all-to-all-done.edges
  75.7 0.0 copy-start.5
  75.7 0.6 copy-done.5
  76.3 2.3 %interface.1 = f32[32,4,128]{2,1,0:T(4,128)} custom-call(f32[2,96,16]{2,1,0:T(8,128)} %constant.53.clone.matrices, f32[32,4,128]{2,1,0:T(4,128)} %copy-done.5, f32[3,64,128]{2,1,0:T(8,128)} %inverse_sums.1.inverse), custom_call_target="tpu_custom_call" | custom-call | tf_op jit(solution)/shard_map/interface/pallas_call | solution.py:583
  78.6 13.4 %all_to_all.10.values = f32[32,4,128]{2,1,0:T(4,128)} all-to-all(f32[32,4,128]{2,1,0:T(4,128)} %interface.1), channel_id=1, replica_groups=mesh['depth'=8,'wave'=4] {'depth','wave'}, dimensions={0} | all-to-all | bytes 131072 | tf_op jit(solution)/shard_map/all_to_all | solution.py:745
  92.0 0.0 collective-permute-done.4.theirs
  92.0 0.0 copy-start.1
  92.1 0.8 copy-done.1
  92.9 13.9 %back.1 = (f32[2,8,32,1024]{3,2,1,0:T(8,128)}, f32[2,8,32,1024]{3,2,1,0:T(8,128)}) custom-call(s32[1]{0:T(128)} %bitcast.place, f32[64]{0:T(128)} %thick.5, f32[32,4,128]{2,1,0:T(4,128)} %all_to_all.10.values, bf16[128,256]{1,0:T(8,128)(2,1)} %constant.54.clone.spread, f32[65,32,1024]{2,1,0:T(8,128)} %get-tuple-element.18.t, ...), custom_call_target="tpu_custom_call" | custom-call | tf_op jit(solution)/shard_map/back/pallas_call | solution.py:700
Async XLA Ops:
  23.8 2.4 %collective-permute-start = (f32[2,2,2,16,1024]{4,3,2,1,0:T(8,128)}, f32[2,2,2,16,1024]{4,3,2,1,0:T(8,128)S(1)}, u32[]{:S(2)}, u32[]{:S(2)}) collective-permute-start(f32[2,2,2,16,1024]{4,3,2,1,0:T(8,128)} %get-tuple-element.20), channel_id=1, source_target_pairs={{0,4},{4,0},{8,12},{12,8},{16,20},{20,16},{24,28},{28,24},{1,5},{5... | collective-permute-start | bytes 1572872 | tf_op jit(solution)/shard_map/ppermute | solution.py:739
  26.2 0.8 copy-start
  27.1 39.1 %copy-start.7 = (f32[32]{0:T(128)S(1)}, f32[32]{0:T(128)}, u32[]{:S(2)}) copy-start(f32[32]{0:T(128)} %shifts.1) | copy-start | bytes 388
  27.1 39.7 %copy-start.6 = (f32[24,128]{1,0:T(8,128)S(1)}, f32[24,128]{1,0:T(8,128)}, u32[]{:S(2)}) copy-start(f32[24,128]{1,0:T(8,128)} %constant.52.clone) | copy-start | bytes 36868
  29.3 13.3 %collective-permute-start.1 = (f32[2,2,16,1024]{3,2,1,0:T(8,128)}, f32[2,2,16,1024]{3,2,1,0:T(8,128)S(1)}, u32[]{:S(2)}, u32[]{:S(2)}) collective-permute-start(f32[2,2,16,1024]{3,2,1,0:T(8,128)} %get-tuple-element.23), channel_id=1, source_target_pairs={{0,8},{4,12},{8,16},{12,20},{16,24},{20,28},{24,0},{28,4},{1,9},{5... | collective-permute-start | bytes 786440 | tf_op jit(solution)/shard_map/ppermute | solution.py:742
  32.5 20.9 %collective-permute-start.2 = (f32[2,2,16,1024]{3,2,1,0:T(8,128)}, f32[2,2,16,1024]{3,2,1,0:T(8,128)S(1)}, u32[]{:S(2)}, u32[]{:S(2)}) collective-permute-start(f32[2,2,16,1024]{3,2,1,0:T(8,128)} %get-tuple-element.24), channel_id=1, source_target_pairs={{0,16},{4,20},{8,24},{12,28},{16,0},{20,4},{24,8},{28,12},{1,17},{... | collective-permute-start | bytes 786440 | tf_op jit(solution)/shard_map/ppermute | solution.py:742
  35.8 17.6 %collective-permute-start.3 = (f32[2,2,16,1024]{3,2,1,0:T(8,128)}, f32[2,2,16,1024]{3,2,1,0:T(8,128)S(1)}, u32[]{:S(2)}, u32[]{:S(2)}) collective-permute-start(f32[2,2,16,1024]{3,2,1,0:T(8,128)} %get-tuple-element.25), channel_id=1, source_target_pairs={{0,24},{4,28},{8,0},{12,4},{16,8},{20,12},{24,16},{28,20},{1,25},{... | collective-permute-start | bytes 786440 | tf_op jit(solution)/shard_map/ppermute | solution.py:742
  42.6 10.7 %copy-start.2 = (f32[2,2,16,1024]{3,2,1,0:T(8,128)}, f32[2,2,16,1024]{3,2,1,0:T(8,128)S(1)}, u32[]{:S(2)}) copy-start(f32[2,2,16,1024]{3,2,1,0:T(8,128)S(1)} %collective-permute-done.1.refs_0_) | copy-start | bytes 786436
  53.4 0.7 copy-start.3
  53.4 0.8 copy-start.4
  57.0 35.1 %collective-permute-start.4 = (f32[2,2,2,16,1024]{4,3,2,1,0:T(8,128)}, f32[2,2,2,16,1024]{4,3,2,1,0:T(8,128)S(1)}, u32[]{:S(2)}, u32[]{:S(2)}) collective-permute-start(f32[2,2,2,16,1024]{4,3,2,1,0:T(8,128)} %get-tuple-element.27), channel_id=1, source_target_pairs={{0,4},{4,0},{8,12},{12,8},{16,20},{20,16},{24,28},{28,24},{1,5},{5... | collective-permute-start | bytes 1572872 | tf_op jit(solution)/shard_map/ppermute | solution.py:739
  57.0 18.7 %all-to-all-start = ((f32[32,4,128]{2,1,0:T(4,128)}), f32[32,4,128]{2,1,0:T(4,128)S(1)}, u32[]{:S(2)}, u32[]{:S(2)}) async-start(f32[32,4,128]{2,1,0:T(4,128)} %get-tuple-element.17), calls=%async_computation | async-start | bytes 131072 | tf_op jit(solution)/shard_map/all_to_all | solution.py:745
  75.7 0.6 copy-start.5
  92.0 0.8 copy-start.1

commit v6 on v5

--- a/solution.py
+++ b/solution.py
@@ -766,7 +766,9 @@
     sums = chip_sums(place, keep, got, pair, chips)
     news = [along(sums[apart - 1], apart) for apart in range(1, chips)]
     inverse = inverse_sums(thickness, face, my_shift + horizontal(wavenumber, full), size // LANES)
-    values = everywhere(interface(edges, inverse, waves, size))
+    values = interface(edges, inverse, waves, size)
+    news, values = lax.optimization_barrier((news, values))
+    values = everywhere(values)
     mine, theirs = join(place, keep, got, pair, far, news)
     return back(place, thickness, values, sines, t, r, m, end, b, mine, across(theirs))
 

time: 107 us -> 94.3 us (0.88)
  starting transfers between devices: 17.3 us -> 11.5 us
  waiting for transfers between devices: 18.4 us -> 14.4 us
  blocking collectives: 13.4 us -> 9.89 us
    ppermute x3, waiting for transfers between devices: 16.6 us -> 0.01 us  [along(): lax.ppermute(a, 'depth', [(d, (d + 2 * apart) % count) for d in range(cou...]
    all_to_all x1, waiting for transfers between devices: 0.01 us -> 12.6 us  [everywhere(): lax.all_to_all(a, ('depth', 'wave'), split_axis=0, concat_axis=0, tiled=T...]
    all_to_all x1, starting transfers between devices: 9.12 us -> 3.29 us  [everywhere(): lax.all_to_all(a, ('depth', 'wave'), split_axis=0, concat_axis=0, tiled=T...]
    all_to_all x1, blocking collectives: 13.4 us -> 9.89 us  [everywhere(): lax.all_to_all(a, ('depth', 'wave'), split_axis=0, concat_axis=0, tiled=T...]
    unnamed x16 -> x18, local copies, waits for them, and re-layouts: 3.05 us -> 3.09 us
  transfers between devices with their start and end apart: 6 -> 6, of which waited for: 3 -> 2; matrix products, arithmetic and copies ran while one was open for 2% -> 2% of each run, Pallas kernels for 9% -> 11%
where the time goes in v6:
time: 94.3 us; the launch traced here: 93.9 us
  Pallas kernels  50.2 us (53%)
  waiting for transfers between devices  14.4 us (15%)
  starting transfers between devices  11.5 us (12%)
  blocking collectives  9.89 us (10%)
  local copies, waits for them, and re-layouts  3.71 us (4%)
  other arithmetic  2.66 us (3%)
  between operations  1.6 us (2%)
    pallas_call x1, Pallas kernels, front(): pl.pallas_call(functools.partial(front_kernel, levels, total, group), in_...  21.2 us
    pallas_call x1, Pallas kernels, back(): pl.pallas_call(functools.partial(back_kernel, levels, total), in_specs=[i...  13.9 us
    all_to_all x1, waiting for transfers between devices, everywhere(): lax.all_to_all(a, ('depth', 'wave'), split_axis=0, concat_axis=0, tiled=T...  12.6 us
    all_to_all x1, blocking collectives, everywhere(): lax.all_to_all(a, ('depth', 'wave'), split_axis=0, concat_axis=0, tiled=T...  9.89 us
    pallas_call x1, Pallas kernels, inverse_sums(): pl.pallas_call(functools.partial(inverse_kernel, per), in_specs=[in_smem,...  7.68 us
    ppermute x3, starting transfers between devices, along(): lax.ppermute(a, 'depth', [(d, (d + 2 * apart) % count) for d in range(cou...  7.45 us
    all_to_all x1, starting transfers between devices, everywhere(): lax.all_to_all(a, ('depth', 'wave'), split_axis=0, concat_axis=0, tiled=T...  3.29 us
    unnamed x18, local copies, waits for them, and re-layouts  3.09 us
  transfers between devices with their start and end apart: 6, of which 2 were waited for; matrix products, arithmetic and copies ran while one was open for 2% of the time, Pallas kernels for 11%

profile of v6, /device:TPU:0, one launch (start us, length us, event | category | flops | bytes accessed | tf_op | source)
XLA Modules:
  0.0 93.9 jit_solution(5248322581348511155)
XLA Ops:
  0.6 0.8 add_divide_fusion
  2.1 0.7 pad_maximum_fusion.face
  2.8 0.0 copy-start.8
  2.8 0.0 copy-start.7
  2.8 21.2 %front.1 = (f32[65,32,1024]{2,1,0:T(8,128)}, f32[8,32,1024]{2,1,0:T(8,128)}, f32[8,32,1024]{2,1,0:T(8,128)}, f32[3,32,1024]{2,1,0:T(8,128)}, f32[4,32,1024]{2,1,...) custom-call(s32[1]{0:T(128)} %bitcast.place, ...), custom_call_target="tpu_custom_call" | custom-call | tf_op jit(solution)/shard_map/front/pallas_call | solution.py:336
  24.0 0.7 collective-permute-start
  24.7 1.7 %collective-permute-done.got = f32[2,2,2,16,1024]{4,3,2,1,0:T(8,128)S(1)} collective-permute-done((f32[2,2,2,16,1024]{4,3,2,1,0:T(8,128)}, f32[2,2,2,16,1024]{4,3,2,1,0:T(8,128)S(1)}, u32[]{:S(2)}, u32[]{:S(2)}) %collective-permute-start) | collective-permute-done | bytes 524320 | tf_op jit(solution)/shard_map/ppermute | solution.py:739
  26.4 0.0 copy-start
  26.4 0.8 copy-done
  27.2 2.3 %chip_sums.1 = (f32[2,2,16,1024]{3,2,1,0:T(8,128)}, f32[2,2,16,1024]{3,2,1,0:T(8,128)}, f32[2,2,16,1024]{3,2,1,0:T(8,128)}) custom-call(s32[1]{0:T(128)} %bitcast.place, f32[2,2,2,16,1024]{4,3,2,1,0:T(8,128)} %get-tuple-element.21.keep, f32[2,2,2,16,1024]{4,3,2,1,0:T(8,128)} %copy-done, f32[4,32,1024]{2,1,0:T(8,128)} %get-tuple-element.23.pair), custom_call_target="tpu_custom_call" | custom-call | tf_op jit(solution)/shard_map/chip_sums/pallas_call | solution.py:397
  29.5 3.2 %collective-permute-start.1 = (f32[2,2,16,1024]{3,2,1,0:T(8,128)}, f32[2,2,16,1024]{3,2,1,0:T(8,128)S(1)}, u32[]{:S(2)}, u32[]{:S(2)}) collective-permute-start(f32[2,2,16,1024]{3,2,1,0:T(8,128)} %get-tuple-element.24), channel_id=1, source_target_pairs={{0,8},{4,12},{8,16},{12,20},{16,24},{20,28},{24,0},{28,4},{1,9},{5... | collective-permute-start | bytes 786440 | tf_op jit(solution)/shard_map/ppermute | solution.py:742
  32.7 3.3 %collective-permute-start.2 = (f32[2,2,16,1024]{3,2,1,0:T(8,128)}, f32[2,2,16,1024]{3,2,1,0:T(8,128)S(1)}, u32[]{:S(2)}, u32[]{:S(2)}) collective-permute-start(f32[2,2,16,1024]{3,2,1,0:T(8,128)} %get-tuple-element.25), channel_id=1, source_target_pairs={{0,16},{4,20},{8,24},{12,28},{16,0},{20,4},{24,8},{28,12},{1,17},{... | collective-permute-start | bytes 786440 | tf_op jit(solution)/shard_map/ppermute | solution.py:742
  36.0 1.0 %collective-permute-start.3 = (f32[2,2,16,1024]{3,2,1,0:T(8,128)}, f32[2,2,16,1024]{3,2,1,0:T(8,128)S(1)}, u32[]{:S(2)}, u32[]{:S(2)}) collective-permute-start(f32[2,2,16,1024]{3,2,1,0:T(8,128)} %get-tuple-element.26), channel_id=1, source_target_pairs={{0,24},{4,28},{8,0},{12,4},{16,8},{20,12},{24,16},{28,20},{1,25},{... | collective-permute-start | bytes 786440 | tf_op jit(solution)/shard_map/ppermute | solution.py:742
  37.0 3.3 %all-to-all-start = ((f32[32,4,128]{2,1,0:T(4,128)}), f32[32,4,128]{2,1,0:T(4,128)S(1)}, u32[]{:S(2)}, u32[]{:S(2)}) async-start(f32[32,4,128]{2,1,0:T(4,128)} %get-tuple-element.27), calls=%async_computation | async-start | bytes 131072 | tf_op jit(solution)/shard_map/all_to_all | solution.py:745
  40.3 0.0 copy-done.8
  40.3 0.6 dynamic_slice.3
  40.9 0.0 copy-done.7
  40.9 1.2 %broadcast_add_fusion.lam = f32[24,128]{1,0:T(8,128)} fusion(f32[24,128]{1,0:T(8,128)S(1)} %copy-done.7, f32[]{:T(128)} %bitcast.1), kind=kLoop, calls=%fused_computation | loop fusion | flops 3072 | bytes 24580 | tf_op jit(solution)/shard_map/add | solution.py:768
  42.1 7.7 %inverse_sums.1.inverse = f32[3,64,128]{2,1,0:T(8,128)} custom-call(f32[64]{0:T(128)} %thick.5, f32[65]{0:T(128)} %pad_maximum_fusion.face, f32[24,128]{1,0:T(8,128)} %broadcast_add_fusion.lam), custom_call_target="tpu_custom_call" | custom-call | tf_op jit(solution)/shard_map/inverse_sums/pallas_call | solution.py:547
  49.8 12.6 %all-to-all-done.edges = f32[32,4,128]{2,1,0:T(4,128)S(1)} async-done(((f32[32,4,128]{2,1,0:T(4,128)}), f32[32,4,128]{2,1,0:T(4,128)S(1)}, u32[]{:S(2)}, u32[]{:S(2)}) %all-to-all-start) | async-done | bytes 65568 | tf_op jit(solution)/shard_map/all_to_all | solution.py:745
  62.4 0.0 copy-start.5
  62.4 0.6 copy-done.5
  63.0 2.3 %interface.1 = f32[32,4,128]{2,1,0:T(4,128)} custom-call(f32[2,96,16]{2,1,0:T(8,128)} %constant.53.clone.matrices, f32[32,4,128]{2,1,0:T(4,128)} %copy-done.5, f32[3,64,128]{2,1,0:T(8,128)} %inverse_sums.1.inverse), custom_call_target="tpu_custom_call" | custom-call | tf_op jit(solution)/shard_map/interface/pallas_call | solution.py:583
  65.3 0.0 copy-start.6
  65.3 0.0 collective-permute-done.1.refs_0_
  65.3 0.0 copy-start.2
  65.3 0.0 collective-permute-done.2.refs_1_
  65.3 0.0 copy-start.3
  65.3 0.0 collective-permute-done.3.refs_2_
  65.3 0.0 copy-start.4
  65.4 0.6 copy-done.2
  66.0 0.1 copy-done.3
  66.1 0.1 copy-done.4
  66.2 2.8 %join.1 = (f32[2,2,2,16,1024]{4,3,2,1,0:T(8,128)}, f32[2,2,2,16,1024]{4,3,2,1,0:T(8,128)}) custom-call(s32[1]{0:T(128)} %bitcast.place, f32[2,2,2,16,1024]{4,3,2,1,0:T(8,128)} %get-tuple-element.21.keep, f32[2,2,2,16,1024]{4,3,2,1,0:T(8,128)} %copy-done, f32[4,32,1024]{2,1,0:T(8,128)} %get-tuple-element.23.pair, f32[3,32,1024]{2,1,0:T(8,128)} %get-tuple-element.30.far, ...), custom_call_target="tpu_custom_call" | custom-call | tf_op jit(solution)/shard_map/join/pallas_call | solution.py:451
  69.1 0.1 collective-permute-start.4
  69.1 0.0 copy-done.6
  69.2 9.9 %all_to_all.10.values = f32[32,4,128]{2,1,0:T(4,128)} all-to-all(f32[32,4,128]{2,1,0:T(4,128)S(1)} %copy-done.6), channel_id=1, replica_groups=mesh['depth'=8,'wave'=4] {'depth','wave'}, dimensions={0} | all-to-all | bytes 131072 | tf_op jit(solution)/shard_map/all_to_all | solution.py:745
  79.0 0.0 collective-permute-done.4.theirs
  79.0 0.0 copy-start.1
  79.1 0.8 copy-done.1
  79.9 13.9 %back.1 = (f32[2,8,32,1024]{3,2,1,0:T(8,128)}, f32[2,8,32,1024]{3,2,1,0:T(8,128)}) custom-call(s32[1]{0:T(128)} %bitcast.place, f32[64]{0:T(128)} %thick.5, f32[32,4,128]{2,1,0:T(4,128)} %all_to_all.10.values, bf16[128,256]{1,0:T(8,128)(2,1)} %constant.54.clone.spread, f32[65,32,1024]{2,1,0:T(8,128)} %get-tuple-element.29.t, ...), custom_call_target="tpu_custom_call" | custom-call | tf_op jit(solution)/shard_map/back/pallas_call | solution.py:700
Async XLA Ops:
  2.8 37.5 %copy-start.8 = (f32[32]{0:T(128)S(1)}, f32[32]{0:T(128)}, u32[]{:S(2)}) copy-start(f32[32]{0:T(128)} %shifts.1) | copy-start | bytes 388
  2.8 38.1 %copy-start.7 = (f32[24,128]{1,0:T(8,128)S(1)}, f32[24,128]{1,0:T(8,128)}, u32[]{:S(2)}) copy-start(f32[24,128]{1,0:T(8,128)} %constant.52.clone) | copy-start | bytes 36868
  24.0 2.4 %collective-permute-start = (f32[2,2,2,16,1024]{4,3,2,1,0:T(8,128)}, f32[2,2,2,16,1024]{4,3,2,1,0:T(8,128)S(1)}, u32[]{:S(2)}, u32[]{:S(2)}) collective-permute-start(f32[2,2,2,16,1024]{4,3,2,1,0:T(8,128)} %get-tuple-element.22), channel_id=1, source_target_pairs={{0,4},{4,0},{8,12},{12,8},{16,20},{20,16},{24,28},{28,24},{1,5},{5... | collective-permute-start | bytes 1572872 | tf_op jit(solution)/shard_map/ppermute | solution.py:739
  26.4 0.8 copy-start
  29.5 35.8 %collective-permute-start.1 = (f32[2,2,16,1024]{3,2,1,0:T(8,128)}, f32[2,2,16,1024]{3,2,1,0:T(8,128)S(1)}, u32[]{:S(2)}, u32[]{:S(2)}) collective-permute-start(f32[2,2,16,1024]{3,2,1,0:T(8,128)} %get-tuple-element.24), channel_id=1, source_target_pairs={{0,8},{4,12},{8,16},{12,20},{16,24},{20,28},{24,0},{28,4},{1,9},{5... | collective-permute-start | bytes 786440 | tf_op jit(solution)/shard_map/ppermute | solution.py:742
  32.7 32.6 %collective-permute-start.2 = (f32[2,2,16,1024]{3,2,1,0:T(8,128)}, f32[2,2,16,1024]{3,2,1,0:T(8,128)S(1)}, u32[]{:S(2)}, u32[]{:S(2)}) collective-permute-start(f32[2,2,16,1024]{3,2,1,0:T(8,128)} %get-tuple-element.25), channel_id=1, source_target_pairs={{0,16},{4,20},{8,24},{12,28},{16,0},{20,4},{24,8},{28,12},{1,17},{... | collective-permute-start | bytes 786440 | tf_op jit(solution)/shard_map/ppermute | solution.py:742
  36.0 29.4 %collective-permute-start.3 = (f32[2,2,16,1024]{3,2,1,0:T(8,128)}, f32[2,2,16,1024]{3,2,1,0:T(8,128)S(1)}, u32[]{:S(2)}, u32[]{:S(2)}) collective-permute-start(f32[2,2,16,1024]{3,2,1,0:T(8,128)} %get-tuple-element.26), channel_id=1, source_target_pairs={{0,24},{4,28},{8,0},{12,4},{16,8},{20,12},{24,16},{28,20},{1,25},{... | collective-permute-start | bytes 786440 | tf_op jit(solution)/shard_map/ppermute | solution.py:742
  37.0 25.4 %all-to-all-start = ((f32[32,4,128]{2,1,0:T(4,128)}), f32[32,4,128]{2,1,0:T(4,128)S(1)}, u32[]{:S(2)}, u32[]{:S(2)}) async-start(f32[32,4,128]{2,1,0:T(4,128)} %get-tuple-element.27), calls=%async_computation | async-start | bytes 131072 | tf_op jit(solution)/shard_map/all_to_all | solution.py:745
  62.4 0.6 copy-start.5
  65.3 3.8 %copy-start.6 = (f32[32,4,128]{2,1,0:T(4,128)S(1)}, f32[32,4,128]{2,1,0:T(4,128)}, u32[]{:S(2)}) copy-start(f32[32,4,128]{2,1,0:T(4,128)} %interface.1) | copy-start | bytes 196612
  65.3 0.7 copy-start.2
  65.3 0.8 copy-start.3
  65.3 0.9 copy-start.4
  69.1 10.0 %collective-permute-start.4 = (f32[2,2,2,16,1024]{4,3,2,1,0:T(8,128)}, f32[2,2,2,16,1024]{4,3,2,1,0:T(8,128)S(1)}, u32[]{:S(2)}, u32[]{:S(2)}) collective-permute-start(f32[2,2,2,16,1024]{4,3,2,1,0:T(8,128)} %get-tuple-element.35), channel_id=1, source_target_pairs={{0,4},{4,0},{8,12},{12,8},{16,20},{20,16},{24,28},{28,24},{1,5},{5... | collective-permute-start | bytes 1572872 | tf_op jit(solution)/shard_map/ppermute | solution.py:739
  79.0 0.8 copy-start.1

commit v7 on v6

--- a/solution.py
+++ b/solution.py
@@ -21,6 +21,8 @@
 in_hbm = pl.BlockSpec(memory_space=pl.ANY)
 in_vmem = pl.BlockSpec(memory_space=pltpu.VMEM)
 params = pltpu.CompilerParams(vmem_limit_bytes=VMEM_BYTES)
+brief = pl.CostEstimate(flops=1, bytes_accessed=1, transcendentals=0)
+lengthy = pl.CostEstimate(flops=20_000_000_000, bytes_accessed=40_000_000, transcendentals=0)
 
 
 def wave_order(size):
@@ -408,6 +410,7 @@
             single(*shape),
         ],
         compiler_params=params,
+        cost_estimate=brief,
         name="chip_sums",
     )(place, keep, got, pair)
 
@@ -464,6 +467,7 @@
             single(*keep.shape),
         ],
         compiler_params=params,
+        cost_estimate=lengthy,
         name="join",
     )(place, keep, got, pair, far, *news)
 
@@ -550,6 +554,7 @@
         out_shape=jax.ShapeDtypeStruct((classes, total, wide), jnp.float32),
         scratch_shapes=[pltpu.VMEM((total,) + lam.shape, jnp.float32)] * 3,
         compiler_params=params,
+        cost_estimate=lengthy,
         name="inverse_sums",
     )(thick, face, lam)
 
@@ -767,8 +772,8 @@
     news = [along(sums[apart - 1], apart) for apart in range(1, chips)]
     inverse = inverse_sums(thickness, face, my_shift + horizontal(wavenumber, full), size // LANES)
     values = interface(edges, inverse, waves, size)
-    news, values = lax.optimization_barrier((news, values))
     values = everywhere(values)
+    news, _ = lax.optimization_barrier((news, values))
     mine, theirs = join(place, keep, got, pair, far, news)
     return back(place, thickness, values, sines, t, r, m, end, b, mine, across(theirs))
 

time: 94.3 us -> 89.5 us (0.949)
  waiting for transfers between devices: 14.4 us -> 2.12 us
  blocking collectives: 9.89 us -> 14.6 us
  starting transfers between devices: 11.5 us -> 14.2 us
    all_to_all x1, waiting for transfers between devices: 12.6 us -> 0.01 us  [everywhere(): lax.all_to_all(a, ('depth', 'wave'), split_axis=0, concat_axis=0, tiled=T...]
    all_to_all x1, blocking collectives: 9.89 us -> 14.6 us  [everywhere(): lax.all_to_all(a, ('depth', 'wave'), split_axis=0, concat_axis=0, tiled=T...]
    all_to_all x1, starting transfers between devices: 3.29 us -> 7.79 us  [everywhere(): lax.all_to_all(a, ('depth', 'wave'), split_axis=0, concat_axis=0, tiled=T...]
    ppermute x3, starting transfers between devices: 7.45 us -> 5.65 us  [along(): lax.ppermute(a, 'depth', [(d, (d + 2 * apart) % count) for d in range(cou...]
    unnamed x18 -> x16, local copies, waits for them, and re-layouts: 3.09 us -> 3.06 us
  transfers between devices with their start and end apart: 6 -> 6, of which waited for: 2 -> 1; matrix products, arithmetic and copies ran while one was open for 2% -> 2% of each run, Pallas kernels for 11% -> 14%
where the time goes in v7:
time: 89.5 us; the launch traced here: 89.1 us
  Pallas kernels  50.2 us (56%)
  blocking collectives  14.6 us (16%)
  starting transfers between devices  14.2 us (16%)
  local copies, waits for them, and re-layouts  3.71 us (4%)
  other arithmetic  2.65 us (3%)
  waiting for transfers between devices  2.12 us (2%)
  between operations  1.59 us (2%)
    pallas_call x1, Pallas kernels, front(): pl.pallas_call(functools.partial(front_kernel, levels, total, group), in_...  21.2 us
    all_to_all x1, blocking collectives, everywhere(): lax.all_to_all(a, ('depth', 'wave'), split_axis=0, concat_axis=0, tiled=T...  14.6 us
    pallas_call x1, Pallas kernels, back(): pl.pallas_call(functools.partial(back_kernel, levels, total), in_specs=[i...  13.9 us
    all_to_all x1, starting transfers between devices, everywhere(): lax.all_to_all(a, ('depth', 'wave'), split_axis=0, concat_axis=0, tiled=T...  7.79 us
    pallas_call x1, Pallas kernels, inverse_sums(): pl.pallas_call(functools.partial(inverse_kernel, per), in_specs=[in_smem,...  7.67 us
    ppermute x3, starting transfers between devices, along(): lax.ppermute(a, 'depth', [(d, (d + 2 * apart) % count) for d in range(cou...  5.65 us
    unnamed x16, local copies, waits for them, and re-layouts  3.06 us
    pallas_call x1, Pallas kernels, join(): pl.pallas_call(functools.partial(join_kernel, chips), in_specs=[in_smem]...  2.83 us
  transfers between devices with their start and end apart: 6, of which 1 were waited for; matrix products, arithmetic and copies ran while one was open for 2% of the time, Pallas kernels for 14%

profile of v7, /device:TPU:0, one launch (start us, length us, event | category | flops | bytes accessed | tf_op | source)
XLA Modules:
  0.0 89.1 jit_solution(10999758840777173512)
XLA Ops:
  0.6 0.8 add_divide_fusion
  2.1 0.6 pad_maximum_fusion.face
  2.8 0.0 copy-start.4
  2.8 0.0 copy-start.3
  2.8 21.2 %front.1 = (f32[65,32,1024]{2,1,0:T(8,128)}, f32[8,32,1024]{2,1,0:T(8,128)}, f32[8,32,1024]{2,1,0:T(8,128)}, f32[3,32,1024]{2,1,0:T(8,128)}, f32[4,32,1024]{2,1,...) custom-call(s32[1]{0:T(128)} %bitcast.place, ...), custom_call_target="tpu_custom_call" | custom-call | tf_op jit(solution)/shard_map/front/pallas_call | solution.py:338
  24.0 0.7 collective-permute-start
  24.6 7.8 %all-to-all-start = ((f32[32,4,128]{2,1,0:T(4,128)}), f32[32,4,128]{2,1,0:T(4,128)S(1)}, u32[]{:S(2)}, u32[]{:S(2)}) async-start(f32[32,4,128]{2,1,0:T(4,128)} %get-tuple-element.20), calls=%async_computation | async-start | bytes 131072 | tf_op jit(solution)/shard_map/all_to_all | solution.py:750
  32.5 0.0 copy-done.4
  32.5 0.7 dynamic_slice.3
  33.1 0.0 copy-done.3
  33.1 1.2 %broadcast_add_fusion.lam = f32[24,128]{1,0:T(8,128)} fusion(f32[24,128]{1,0:T(8,128)S(1)} %copy-done.3, f32[]{:T(128)} %bitcast.1), kind=kLoop, calls=%fused_computation | loop fusion | flops 3072 | bytes 24580 | tf_op jit(solution)/shard_map/add | solution.py:773
  34.3 0.0 collective-permute-done.got
  34.4 0.0 copy-start.1
  34.4 0.8 copy-done.1
  35.1 2.3 %chip_sums.1 = (f32[2,2,16,1024]{3,2,1,0:T(8,128)}, f32[2,2,16,1024]{3,2,1,0:T(8,128)}, f32[2,2,16,1024]{3,2,1,0:T(8,128)}) custom-call(s32[1]{0:T(128)} %bitcast.place, f32[2,2,2,16,1024]{4,3,2,1,0:T(8,128)} %get-tuple-element.22.keep, f32[2,2,2,16,1024]{4,3,2,1,0:T(8,128)} %copy-done.1, f32[4,32,1024]{2,1,0:T(8,128)} %get-tuple-element.24.pair), custom_call_target="tpu_custom_call" | custom-call | flops 1 | bytes 1 | tf_op jit(solution)/shard_map/chip_sums/pallas_call | solution.py:399
  37.4 1.8 %collective-permute-start.1 = (f32[2,2,16,1024]{3,2,1,0:T(8,128)}, f32[2,2,16,1024]{3,2,1,0:T(8,128)S(1)}, u32[]{:S(2)}, u32[]{:S(2)}) collective-permute-start(f32[2,2,16,1024]{3,2,1,0:T(8,128)} %get-tuple-element.26), channel_id=1, source_target_pairs={{0,8},{4,12},{8,16},{12,20},{16,24},{20,28},{24,0},{28,4},{1,9},{5... | collective-permute-start | bytes 786440 | tf_op jit(solution)/shard_map/ppermute | solution.py:747
  39.2 2.4 %collective-permute-start.2 = (f32[2,2,16,1024]{3,2,1,0:T(8,128)}, f32[2,2,16,1024]{3,2,1,0:T(8,128)S(1)}, u32[]{:S(2)}, u32[]{:S(2)}) collective-permute-start(f32[2,2,16,1024]{3,2,1,0:T(8,128)} %get-tuple-element.27), channel_id=1, source_target_pairs={{0,16},{4,20},{8,24},{12,28},{16,0},{20,4},{24,8},{28,12},{1,17},{... | collective-permute-start | bytes 786440 | tf_op jit(solution)/shard_map/ppermute | solution.py:747
  41.7 1.4 %collective-permute-start.3 = (f32[2,2,16,1024]{3,2,1,0:T(8,128)}, f32[2,2,16,1024]{3,2,1,0:T(8,128)S(1)}, u32[]{:S(2)}, u32[]{:S(2)}) collective-permute-start(f32[2,2,16,1024]{3,2,1,0:T(8,128)} %get-tuple-element.28), channel_id=1, source_target_pairs={{0,24},{4,28},{8,0},{12,4},{16,8},{20,12},{24,16},{28,20},{1,25},{... | collective-permute-start | bytes 786440 | tf_op jit(solution)/shard_map/ppermute | solution.py:747
  43.1 7.7 %inverse_sums.1.inverse = f32[3,64,128]{2,1,0:T(8,128)} custom-call(f32[64]{0:T(128)} %thick.5, f32[65]{0:T(128)} %pad_maximum_fusion.face, f32[24,128]{1,0:T(8,128)} %broadcast_add_fusion.lam), custom_call_target="tpu_custom_call" | custom-call | flops 20000000000 | bytes 40000000 | tf_op jit(solution)/shard_map/inverse_sums/pallas_call | solution.py:551
  50.7 0.0 all-to-all-done.edges
  50.7 0.0 copy-start.2
  50.7 0.6 copy-done.2
  51.4 2.3 %interface.1 = f32[32,4,128]{2,1,0:T(4,128)} custom-call(f32[2,96,16]{2,1,0:T(8,128)} %constant.53.clone.matrices, f32[32,4,128]{2,1,0:T(4,128)} %copy-done.2, f32[3,64,128]{2,1,0:T(8,128)} %inverse_sums.1.inverse), custom_call_target="tpu_custom_call" | custom-call | tf_op jit(solution)/shard_map/interface/pallas_call | solution.py:588
  53.6 14.6 %all_to_all.10.values = f32[32,4,128]{2,1,0:T(4,128)} all-to-all(f32[32,4,128]{2,1,0:T(4,128)} %interface.1), channel_id=1, replica_groups=mesh['depth'=8,'wave'=4] {'depth','wave'}, dimensions={0} | all-to-all | bytes 131072 | tf_op jit(solution)/shard_map/all_to_all | solution.py:750
  68.3 0.0 collective-permute-done.1.refs_0_
  68.3 0.0 copy-start.5
  68.3 0.0 collective-permute-done.2.refs_1_
  68.3 0.0 copy-start.6
  68.3 0.0 collective-permute-done.3.refs_2_
  68.3 0.0 copy-start.7
  68.3 0.7 copy-done.5
  69.0 0.1 copy-done.6
  69.1 0.1 copy-done.7
  69.2 2.8 %join.1 = (f32[2,2,2,16,1024]{4,3,2,1,0:T(8,128)}, f32[2,2,2,16,1024]{4,3,2,1,0:T(8,128)}) custom-call(s32[1]{0:T(128)} %bitcast.place, f32[2,2,2,16,1024]{4,3,2,1,0:T(8,128)} %get-tuple-element.22.keep, f32[2,2,2,16,1024]{4,3,2,1,0:T(8,128)} %copy-done.1, f32[4,32,1024]{2,1,0:T(8,128)} %get-tuple-element.24.pair, f32[3,32,1024]{2,1,0:T(8,128)} %get-tuple-element.25.far, ...), custom_call_target="tpu_custom_call" | custom-call | flops 20000000000 | bytes 40000000 | tf_op jit(solution)/shard_map/join/pallas_call | solution.py:454
  72.0 0.1 collective-permute-start.4
  72.1 2.1 %collective-permute-done.4.theirs = f32[2,2,2,16,1024]{4,3,2,1,0:T(8,128)S(1)} collective-permute-done((f32[2,2,2,16,1024]{4,3,2,1,0:T(8,128)}, f32[2,2,2,16,1024]{4,3,2,1,0:T(8,128)S(1)}, u32[]{:S(2)}, u32[]{:S(2)}) %collective-permute-start.4) | collective-permute-done | bytes 524320 | tf_op jit(solution)/shard_map/ppermute | solution.py:744
  74.2 0.0 copy-start
  74.2 0.8 copy-done
  75.0 13.9 %back.1 = (f32[2,8,32,1024]{3,2,1,0:T(8,128)}, f32[2,8,32,1024]{3,2,1,0:T(8,128)}) custom-call(s32[1]{0:T(128)} %bitcast.place, f32[64]{0:T(128)} %thick.5, f32[32,4,128]{2,1,0:T(4,128)} %all_to_all.10.values, bf16[128,256]{1,0:T(8,128)(2,1)} %constant.54.clone.spread, f32[65,32,1024]{2,1,0:T(8,128)} %get-tuple-element.21.t, ...), custom_call_target="tpu_custom_call" | custom-call | tf_op jit(solution)/shard_map/back/pallas_call | solution.py:705
Async XLA Ops:
  2.8 29.7 %copy-start.4 = (f32[32]{0:T(128)S(1)}, f32[32]{0:T(128)}, u32[]{:S(2)}) copy-start(f32[32]{0:T(128)} %shifts.1) | copy-start | bytes 388
  2.8 30.4 %copy-start.3 = (f32[24,128]{1,0:T(8,128)S(1)}, f32[24,128]{1,0:T(8,128)}, u32[]{:S(2)}) copy-start(f32[24,128]{1,0:T(8,128)} %constant.52.clone) | copy-start | bytes 36868
  24.0 10.4 %collective-permute-start = (f32[2,2,2,16,1024]{4,3,2,1,0:T(8,128)}, f32[2,2,2,16,1024]{4,3,2,1,0:T(8,128)S(1)}, u32[]{:S(2)}, u32[]{:S(2)}) collective-permute-start(f32[2,2,2,16,1024]{4,3,2,1,0:T(8,128)} %get-tuple-element.23), channel_id=1, source_target_pairs={{0,4},{4,0},{8,12},{12,8},{16,20},{20,16},{24,28},{28,24},{1,5},{5... | collective-permute-start | bytes 1572872 | tf_op jit(solution)/shard_map/ppermute | solution.py:744
  24.6 26.1 %all-to-all-start = ((f32[32,4,128]{2,1,0:T(4,128)}), f32[32,4,128]{2,1,0:T(4,128)S(1)}, u32[]{:S(2)}, u32[]{:S(2)}) async-start(f32[32,4,128]{2,1,0:T(4,128)} %get-tuple-element.20), calls=%async_computation | async-start | bytes 131072 | tf_op jit(solution)/shard_map/all_to_all | solution.py:750
  34.4 0.8 copy-start.1
  37.4 30.9 %collective-permute-start.1 = (f32[2,2,16,1024]{3,2,1,0:T(8,128)}, f32[2,2,16,1024]{3,2,1,0:T(8,128)S(1)}, u32[]{:S(2)}, u32[]{:S(2)}) collective-permute-start(f32[2,2,16,1024]{3,2,1,0:T(8,128)} %get-tuple-element.26), channel_id=1, source_target_pairs={{0,8},{4,12},{8,16},{12,20},{16,24},{20,28},{24,0},{28,4},{1,9},{5... | collective-permute-start | bytes 786440 | tf_op jit(solution)/shard_map/ppermute | solution.py:747
  39.2 29.1 %collective-permute-start.2 = (f32[2,2,16,1024]{3,2,1,0:T(8,128)}, f32[2,2,16,1024]{3,2,1,0:T(8,128)S(1)}, u32[]{:S(2)}, u32[]{:S(2)}) collective-permute-start(f32[2,2,16,1024]{3,2,1,0:T(8,128)} %get-tuple-element.27), channel_id=1, source_target_pairs={{0,16},{4,20},{8,24},{12,28},{16,0},{20,4},{24,8},{28,12},{1,17},{... | collective-permute-start | bytes 786440 | tf_op jit(solution)/shard_map/ppermute | solution.py:747
  41.7 26.6 %collective-permute-start.3 = (f32[2,2,16,1024]{3,2,1,0:T(8,128)}, f32[2,2,16,1024]{3,2,1,0:T(8,128)S(1)}, u32[]{:S(2)}, u32[]{:S(2)}) collective-permute-start(f32[2,2,16,1024]{3,2,1,0:T(8,128)} %get-tuple-element.28), channel_id=1, source_target_pairs={{0,24},{4,28},{8,0},{12,4},{16,8},{20,12},{24,16},{28,20},{1,25},{... | collective-permute-start | bytes 786440 | tf_op jit(solution)/shard_map/ppermute | solution.py:747
  50.7 0.6 copy-start.2
  68.3 0.7 copy-start.5
  68.3 0.8 copy-start.6
  68.3 0.9 copy-start.7
  72.0 2.2 %collective-permute-start.4 = (f32[2,2,2,16,1024]{4,3,2,1,0:T(8,128)}, f32[2,2,2,16,1024]{4,3,2,1,0:T(8,128)S(1)}, u32[]{:S(2)}, u32[]{:S(2)}) collective-permute-start(f32[2,2,2,16,1024]{4,3,2,1,0:T(8,128)} %get-tuple-element.33), channel_id=1, source_target_pairs={{0,4},{4,0},{8,12},{12,8},{16,20},{20,16},{24,28},{28,24},{1,5},{5... | collective-permute-start | bytes 1572872 | tf_op jit(solution)/shard_map/ppermute | solution.py:744
  74.2 0.8 copy-start

commit v8 on v7

--- a/solution.py
+++ b/solution.py
@@ -108,6 +108,29 @@
     return p + m, mirror(p - m)
 
 
+def horizontal(wavenumber, length):
+    return (aspect_ratio * 4.0 * np.sin(math.pi * wavenumber / length) ** 2).astype(np.float32)
+
+
+def set_faces(thick, faces):
+    total = faces.shape[0] - 1
+    two = jnp.full((ROWS, LANES), 2.0, jnp.float32)
+    faces[0] = two / (two * 0.0 + thick[0])
+    faces[total] = two * 0.0
+
+    def one(j, _):
+        faces[j] = two / (two * 0.0 + (thick[j - 1] + thick[j]))
+        return 0
+
+    lax.fori_loop(1, total, one, 0, unroll=3)
+
+
+def spread_face(tile, like):
+    rows, lanes = like.shape
+    wide = jnp.concatenate([tile] * (lanes // LANES), 1) if lanes > LANES else tile
+    return jnp.concatenate([wide] * (rows // ROWS), 0) if rows > ROWS else wide
+
+
 class Copies:
     def __init__(self, sems):
         self.sems, self.used = sems, 0
@@ -119,7 +142,7 @@
         return copy
 
 
-def coefficients(levels, total, group, place, thick, face, shifts, across, t_out, r_out, m_out, end_out, pair_out, far_out, lam, m_chip, r_chip, f_chip, n_chip, u_chip, down_all, up_all):
+def coefficients(levels, total, group, place, thick, faces, shifts, across, t_out, m_out, end_out, pair_out, far_out, lam, m_chip, f_chip, n_chip, u_chip, down_all, up_all):
     ky = lam.shape[0]
     span = 2 * levels
     chips = total // span
@@ -131,15 +154,15 @@
         lam[row:row + 1, :] = across[...] + shifts[row]
 
     def down_step(shift, j, f, r):
-        m = face[j] * r
+        m = spread_face(faces[j], r) * r
         f = shift * thick[j] + m * f
-        return m, f, 1.0 / (face[j + 1] + f)
+        return m, f, 1.0 / (spread_face(faces[j + 1], f) + f)
 
     def up_step(shift, j, phi, s):
-        n = face[j + 1] * s
+        n = spread_face(faces[j + 1], s) * s
         u = n * phi
         phi = shift * thick[j] + u
-        return n, u, phi, 1.0 / (face[j] + phi)
+        return n, u, phi, 1.0 / (spread_face(faces[j], phi) + phi)
 
     def part(g, _):
         here = pl.ds(pl.multiple_of(g * group, group), group)
@@ -171,7 +194,7 @@
         f, r = lax.fori_loop(0, chip, down_chip, (one, one))
         for i in range(span):
             m, f, r = down_step(shift, start + i, f, r)
-            m_chip[i], f_chip[i], r_chip[i] = m, f, r
+            m_chip[i], f_chip[i] = m, f
         phi, s = lax.fori_loop(0, chips - 1 - chip, up_chip, (zero, zero))
         for i in range(span - 1, -1, -1):
             n, u, phi, s = up_step(shift, start + i, phi, s)
@@ -182,7 +205,6 @@
             t_out[start + levels + 1 + i, here] = n_chip[levels + i]
         t_out[start + levels, here] = jnp.where(upper, n_chip[levels - 1], m_chip[levels])
         for i in range(levels):
-            r_out[i, here] = r_chip[own + i]
             m_out[i, here] = m_chip[own + i]
         last = own + levels - 1
         end_out[0, here] = n_chip[last]
@@ -213,8 +235,8 @@
     return tiles[0]
 
 
-def front_kernel(levels, total, group, place, thick, face, shifts, across, sines, edge_mix, x0, x1, odd_top, odd_rest, even_top, even_rest, t_out, r_out, m_out, end_out, pair_out, far_out, b_out, keep_out, give_out, edge_out, sems, *scratch):
-    across_v, sines_v, mix_v, x, ot, orest, et, er, t, r, m, end, pair, far, b, c_all, z_all, sums, edges, lam, *work = scratch
+def front_kernel(levels, total, group, place, thick, shifts, across, sines, edge_mix, x0, x1, odd_top, odd_rest, even_top, even_rest, t_out, m_out, end_out, pair_out, far_out, b_out, keep_out, give_out, edge_out, sems, *scratch):
+    across_v, sines_v, mix_v, x, ot, orest, et, er, t, m, end, pair, far, b, c_all, z_all, sums, edges, faces, lam, *work = scratch
     _, _, _, ky, size = x.shape
     first = place[0] * levels
     half = size // 2
@@ -225,23 +247,24 @@
     mats += [copies.start(sines, sines_v)]
     fields += [copies.start(x1, x.at[1])]
     late = [copies.start(edge_mix, mix_v)]
+    set_faces(thick, faces)
     for copy in early:
         copy.wait()
-    coefficients(levels, total, group, place, thick, face, shifts, across_v, t, r, m, end, pair, far, lam, *work)
+    coefficients(levels, total, group, place, thick, faces, shifts, across_v, t, m, end, pair, far, lam, *work)
     outs = [copies.start(source, target) for source, target in ((pair, pair_out), (far, far_out))]
-    outs += [copies.start(source, target) for source, target in ((t, t_out), (r, r_out), (m, m_out), (end, end_out))]
+    outs += [copies.start(source, target) for source, target in ((t, t_out), (m, m_out), (end, end_out))]
     for copy in mats:
         copy.wait()
     lane = lax.broadcasted_iota(jnp.int32, (ROWS, LANES), 1)
     spot = jnp.where(lane == 0, size / 4.0, 0.0)
     core = place[0] % 2
 
-    def put(f, rows, values, height, own=None):
+    def put(f, j, here, values, height, own=None):
         odd, even = lane_sum(values[:, :half]) * height, lane_sum(values[:, half:]) * height
         if own is not None:
             odd, even = odd + own, even + own
-        sums[f, 0, rows, :] = odd
-        sums[f, 1, rows, :] = even
+        sums[f, 0, j, here] = odd
+        sums[f, 1, j, here] = even
 
     for a in range(2):
         fields[a].wait()
@@ -269,10 +292,10 @@
                 z_all[1, f, here] = value * wave
                 for j in range(levels - 1, -1, -1):
                     if j < levels - 1:
-                        value = r[j, here] * ys[j] + m[j + 1, here] * value
+                        value = m[j + 1, here] * (ys[j] * (0.5 * (thick[first + j] + thick[first + j + 1])) + value)
                     height = thick[first + j]
                     own = jnp.broadcast_to(x[a, ri, j, here, 0:1], (ROWS, LANES)) * (spot * height if a == 0 else spot)
-                    put(f, pl.ds(g * ROWS * total + first + j, ROWS, stride=total), value * wave, height, own)
+                    put(f, first + j, here, value * wave, height, own)
                 z_all[0, f, here] = value * wave
                 c_all[a, 1, ri, here] = value * end[2, here]
                 return 0
@@ -291,7 +314,7 @@
                 step = t[j + 1, here]
                 z = [step * one for one in z]
                 for f in range(4):
-                    put(f, pl.ds(g * ROWS * total + j, ROWS, stride=total), z[f], thick[j])
+                    put(f, j, here, z[f], thick[j])
             return z
 
         def down(block, z):
@@ -300,7 +323,7 @@
                 step = t[j, here]
                 z = [step * one for one in z]
                 for f in range(4):
-                    put(f, pl.ds(g * ROWS * total + j, ROWS, stride=total), z[f], thick[j])
+                    put(f, j, here, z[f], thick[j])
             return z
 
         lax.fori_loop(0, place[0], up, [z_all[0, f, here] for f in range(4)])
@@ -313,19 +336,21 @@
     if edges.shape[0] > ky:
         edges[...] = jnp.zeros_like(edges)
     wide = 2 * total
-    row = lax.broadcasted_iota(jnp.int32, (ky, total, wide), 1)
-    column = lax.broadcasted_iota(jnp.int32, (ky, total, wide), 2)
-    diagonal = (row == column) | (row + total == column)
+    lane = lax.broadcasted_iota(jnp.int32, (ky, wide), 1) % total
     for f in range(4):
-        high, low = split(jnp.concatenate([sums[f, 0], sums[f, 1]], 1))
-        spread = (real_dot(high, mix_v[...]) + real_dot(low, mix_v[...])).reshape(ky, total, wide)
-        edges[:ky, f, :] = jnp.sum(jnp.where(diagonal, spread, 0.0), axis=1)
+        both = [sums[f, way].reshape(total * ky, LANES) for way in range(2)]
+        high, low = split(jnp.concatenate(both, 1))
+        spread = (real_dot(high, mix_v[...]) + real_dot(low, mix_v[...])).reshape(total, ky, wide)
+        line = spread[0]
+        for j in range(1, total):
+            line = jnp.where(lane == j, spread[j], line)
+        edges[:ky, f, :] = line
     outs.append(copies.start(edges, edge_out))
     for copy in outs:
         copy.wait()
 
 
-def front(place, thick, face, shifts, across, sines, rhs, cotangent, devices):
+def front(place, thick, shifts, across, sines, rhs, cotangent, devices):
     _, levels, ky, size = rhs.shape
     total = thick.shape[0]
     chips = total // (2 * levels)
@@ -333,11 +358,11 @@
     half = size // 2
     wide = 2 * total
     single = lambda *shape: pltpu.VMEM(shape, jnp.float32)
-    tables = [(n, ky, size) for n in (total + 1, levels, levels, 3, 4, chips - 1)]
+    tables = [(n, ky, size) for n in (total + 1, levels, 3, 4, chips - 1)]
     shapes = tables + [(2, 2, levels, ky, size), (2, 2, 2, ky // 2, size), (2, 2, 2, ky // 2, size), (devices, 4, wide)]
     return pl.pallas_call(
         functools.partial(front_kernel, levels, total, group),
-        in_specs=[in_smem] * 4 + [in_hbm] * 9,
+        in_specs=[in_smem] * 3 + [in_hbm] * 9,
         out_specs=[in_hbm] * len(shapes),
         out_shape=[jax.ShapeDtypeStruct(shape, jnp.float32) for shape in shapes],
         scratch_shapes=[
@@ -351,15 +376,16 @@
             single(2, 2, levels, ky, size),
             single(2, 2, 2, ky, size),
             single(2, 4, ky, size),
-            single(4, 2, ky * total, LANES),
+            single(4, 2, total, ky, LANES),
             single(devices, 4, wide),
+            single(total + 1, ROWS, LANES),
             single(ky, size),
-            *[single(2 * levels, group, size)] * 5,
+            *[single(2 * levels, group, size)] * 4,
             *[single(chips, group, size)] * 2,
         ],
         compiler_params=params,
         name="front",
-    )(place, thick, face, shifts, across, sines, edge_matrix(size, total), rhs, cotangent, *half_sines(size))
+    )(place, thick, shifts, across, sines, edge_matrix(size, total), rhs, cotangent, *half_sines(size))
 
 
 def chip_kernel(chips, place, keep, got, pair, *refs):
@@ -472,35 +498,38 @@
     )(place, keep, got, pair, far, *news)
 
 
-def inverse_kernel(per, thick, face, lam, out, m_all, f_all, g_all):
+def inverse_kernel(counts, my, thick, shifts, across, weights, out, faces, m_all, f_all, g_all):
     total = f_all.shape[0]
-    rows = lam.shape[0]
     classes = out.shape[0]
-    shift = lam[...]
+    ky = shifts.shape[0]
+    starts = [sum(counts[:c]) for c in range(classes + 1)]
+    set_faces(thick, faces)
+    shift = across[...] + jnp.where(my[0] < ky, shifts[jnp.minimum(my[0], ky - 1)], 1.0)
     one = jnp.ones_like(shift)
     zero = jnp.zeros_like(shift)
 
     def step(j, state):
         f, r, phi, s = state
-        m = face[j] * r
+        m = spread_face(faces[j], r) * r
         f = shift * thick[j] + m * f
-        r = 1.0 / (face[j + 1] + f)
+        r = 1.0 / (spread_face(faces[j + 1], f) + f)
         m_all[j] = m
         f_all[j] = f
         i = total - 1 - j
-        u = face[i + 1] * s * phi
+        u = spread_face(faces[i + 1], s) * s * phi
         phi = shift * thick[i] + u
-        s = 1.0 / (face[i] + phi)
+        s = 1.0 / (spread_face(faces[i], phi) + phi)
         g_all[i] = u
         return f, r, phi, s
 
-    lax.fori_loop(0, total, step, (one, one, zero, zero))
+    lax.fori_loop(0, total, step, (one, one, zero, zero), unroll=4)
+    weight = weights[...]
 
     def centre(j, _):
-        g_all[j] = 1.0 / (f_all[j] + g_all[j])
+        g_all[j] = weight / (f_all[j] + g_all[j])
         return 0
 
-    lax.fori_loop(0, total, centre, 0)
+    lax.fori_loop(0, total, centre, 0, unroll=8)
     wide = out.shape[2]
     sub = lax.broadcasted_iota(jnp.int32, (ROWS, LANES), 0)
     lane = lax.broadcasted_iota(jnp.int32, (ROWS, wide), 1)
@@ -510,7 +539,7 @@
     def put(j, z, sums):
         new = []
         for c in range(classes):
-            tiles = z[c * per:(c + 1) * per]
+            tiles = z[starts[c]:starts[c + 1]]
             total_tile = tiles[0]
             for tile in tiles[1:]:
                 total_tile = total_tile + tile
@@ -519,11 +548,11 @@
         return new
 
     for base in range(0, total, ROWS):
-        z = [jnp.zeros((ROWS, LANES), jnp.float32)] * (classes * per)
+        z = [jnp.zeros((ROWS, LANES), jnp.float32)] * (starts[-1])
         sums = [jnp.zeros((ROWS, wide), jnp.float32)] * classes
         for i in range(ROWS - 1, -1, -1):
             j = base + i
-            for t in range(classes * per):
+            for t in range(starts[-1]):
                 moved = z[t] * line(m_all, j + 1, t) if i < ROWS - 1 else z[t]
                 z[t] = jnp.where(sub == i, line(g_all, j, t), moved)
             sums = put(j, z, sums)
@@ -532,7 +561,7 @@
             z, sums = state
             for i in range(ROWS):
                 j = base - 1 - back * ROWS - i
-                z = [z[t] * line(m_all, j + 1, t) for t in range(classes * per)]
+                z = [z[t] * line(m_all, j + 1, t) for t in range(starts[-1])]
                 sums = put(j, z, sums)
             return z, sums
 
@@ -542,21 +571,35 @@
             out[c, base:base + ROWS, :] = sums[c] * jnp.where(lane == base + row, 0.5, 1.0)
 
 
-def inverse_sums(thick, face, lam, per):
+def inverse_sums(my, thick, shifts, waves, size):
     total = thick.shape[0]
-    classes = lam.shape[0] // per
+    classes = waves // 2 + 1
+    lines, weights, counts = [], [], []
+    for c in range(classes):
+        k = c + waves * np.arange(size)
+        weight = np.ones(size)
+        if c in (0, waves // 2):
+            partner = (waves * size - k) % (waves * size)
+            weight = np.where(k < partner, 2.0, 1.0)[k <= partner]
+            k = k[k <= partner]
+        spare = -len(k) % LANES
+        counts.append((len(k) + spare) // LANES)
+        lines.append(np.pad(k, (0, spare)))
+        weights.append(np.pad(weight, (0, spare)))
+    spare = -sum(counts) % ROWS * LANES
+    k = np.pad(np.concatenate(lines), (0, spare)).reshape(-1, LANES)
+    weight = np.pad(np.concatenate(weights), (0, spare)).reshape(-1, LANES).astype(np.float32)
+    across = horizontal(k, waves * size)
     wide = -(-total // LANES) * LANES
-    spare = -lam.shape[0] % ROWS
-    lam = jnp.pad(lam, ((0, spare), (0, 0)), constant_values=1.0) if spare else lam
     return pl.pallas_call(
-        functools.partial(inverse_kernel, per),
-        in_specs=[in_smem, in_smem, in_vmem],
+        functools.partial(inverse_kernel, counts),
+        in_specs=[in_smem] * 3 + [in_vmem] * 2,
         out_shape=jax.ShapeDtypeStruct((classes, total, wide), jnp.float32),
-        scratch_shapes=[pltpu.VMEM((total,) + lam.shape, jnp.float32)] * 3,
+        scratch_shapes=[pltpu.VMEM((total + 1, ROWS, LANES), jnp.float32)] + [pltpu.VMEM((total,) + across.shape, jnp.float32)] * 3,
         compiler_params=params,
         cost_estimate=lengthy,
         name="inverse_sums",
-    )(thick, face, lam)
+    )(my, thick, shifts, across, weight)
 
 
 def interface_kernel(waves, matrices, edges, inverse, out):
@@ -595,7 +638,7 @@
     )(interface_matrices(waves, size), edges, inverse)
 
 
-def back_kernel(levels, total, place, thick, values, spread, t, mine, theirs, sines, b, r, m, end, odd_top, odd_rest, even_top, even_rest, out0, out1, sems, values_v, spread_v, t_v, ends, sines_v, b_v, r_v, m_v, end_v, ot, orest, et, er, picked, u_all, q_all, out_v):
+def back_kernel(levels, total, place, thick, values, spread, t, mine, theirs, sines, b, m, end, odd_top, odd_rest, even_top, even_rest, out0, out1, sems, values_v, spread_v, t_v, ends, sines_v, b_v, m_v, end_v, ot, orest, et, er, picked, u_all, q_all, out_v):
     _, _, _, ky, size = b_v.shape
     first = place[0] * levels
     half = size // 2
@@ -609,7 +652,8 @@
         here = pl.ds(pl.multiple_of(start * (ky // 2), ROWS), ky // 2)
         both.append(copies.start(source, ends.at[:, :, :, here]))
     both.append(copies.start(sines, sines_v))
-    rest = [copies.start(source, target) for source, target in ((r, r_v), (m, m_v), (end, end_v), (b, b_v), (odd_top, ot), (odd_rest, orest), (even_top, et), (even_rest, er))]
+    rest = [copies.start(source, target) for source, target in ((m, m_v), (end, end_v), (odd_top, ot), (odd_rest, orest), (even_top, et), (even_rest, er))]
+    fields = [copies.start(b.at[f // 2, f % 2], b_v.at[f // 2, f % 2]) for f in range(4)]
     for copy in early:
         copy.wait()
     lane = lax.broadcasted_iota(jnp.int32, (ky, 2 * total), 1)
@@ -663,6 +707,7 @@
     outs = []
     for f in range(4):
         a, ri = f // 2, f % 2
+        fields[f].wait()
 
         def tile(g, _):
             here = pl.ds(pl.multiple_of(g * ROWS, ROWS), ROWS)
@@ -675,7 +720,7 @@
             value = (y + end_v[0, here] * ends[a, 1, ri, here]) * end_v[1, here]
             q_all[levels - 1, here] = value
             for j in range(levels - 2, -1, -1):
-                value = r_v[j, here] * ys[j] + m_v[j + 1, here] * value
+                value = m_v[j + 1, here] * (ys[j] * (0.5 * (thick[first + j] + thick[first + j + 1])) + value)
                 q_all[j, here] = value
             return 0
 
@@ -697,25 +742,24 @@
         copy.wait()
 
 
-def back(place, thick, values, sines, t, r, m, end, b, mine, theirs):
+def back(place, thick, values, sines, t, m, end, b, mine, theirs):
     _, _, levels, ky, size = b.shape
     total = t.shape[0] - 1
     half = size // 2
     single = lambda *shape: pltpu.VMEM(shape, jnp.float32)
     return pl.pallas_call(
         functools.partial(back_kernel, levels, total),
-        in_specs=[in_smem] * 2 + [in_hbm] * 14,
+        in_specs=[in_smem] * 2 + [in_hbm] * 13,
         out_specs=[in_hbm] * 2,
         out_shape=[jax.ShapeDtypeStruct((2, levels, ky, size), jnp.float32)] * 2,
         scratch_shapes=[
-            pltpu.SemaphoreType.DMA((18,)),
+            pltpu.SemaphoreType.DMA((20,)),
             single(ky, 4, 2 * total),
             pltpu.VMEM((2 * total, 2 * LANES), jnp.bfloat16),
             single(*t.shape),
             single(2, 2, 2, ky, size),
             single(ROWS, size),
             single(*b.shape),
-            single(*r.shape),
             single(*m.shape),
             single(*end.shape),
             *[pltpu.VMEM((half, half), jnp.bfloat16)] * 4,
@@ -726,7 +770,7 @@
         ],
         compiler_params=params,
         name="back",
-    )(place, thick, values, spread_matrix(total), t, mine, theirs, sines, b, r, m, end, *half_sines(size, True))
+    )(place, thick, values, spread_matrix(total), t, mine, theirs, sines, b, m, end, *half_sines(size, True))
 
 
 def shards(rhs, cotangent, thickness, ky_shift):
@@ -735,7 +779,6 @@
     depth_pos = lax.axis_index("depth")
     wave_pos = lax.axis_index("wave")
     _, levels, ky, size = rhs.shape
-    full = waves * size
     devices = waves * count
     chips = count // 2
     place = depth_pos.astype(jnp.int32).reshape(1)
@@ -749,33 +792,24 @@
     def everywhere(a):
         return lax.all_to_all(a, ("depth", "wave"), split_axis=0, concat_axis=0, tiled=True)
 
-    def horizontal(wavenumber, length):
-        return (aspect_ratio * 4.0 * np.sin(math.pi * wavenumber / length) ** 2).astype(np.float32)
-
-    inner_face = 2.0 / (thickness[:-1] + thickness[1:])
-    face = jnp.concatenate([2.0 / thickness[:1], inner_face, jnp.zeros((1,), jnp.float32)])
     order = wave_order(size)
     sines = np.broadcast_to(np.sin(np.pi * order / size)[None, :], (ROWS, size)).astype(np.float32)
     across_k = horizontal(order, 2 * size)[None, :]
-    t, r, m, end, pair, far, b, keep, give, edges = front(
-        place, thickness, face, ky_shift, across_k, sines, rhs, cotangent, devices
+    t, m, end, pair, far, b, keep, give, edges = front(
+        place, thickness, ky_shift, across_k, sines, rhs, cotangent, devices
     )
 
-    classes = waves // 2 + 1
-    wavenumber = (np.arange(classes)[:, None] + waves * np.arange(size)[None, :]).reshape(-1, LANES)
-    shifts = jnp.pad(ky_shift, (0, devices - ky), constant_values=1.0) if devices > ky else ky_shift
-    my_shift = lax.dynamic_slice_in_dim(shifts, depth_pos * waves + wave_pos, 1)
-
+    my = (depth_pos * waves + wave_pos).astype(jnp.int32).reshape(1)
     got = across(give)
     edges = everywhere(edges)
     sums = chip_sums(place, keep, got, pair, chips)
     news = [along(sums[apart - 1], apart) for apart in range(1, chips)]
-    inverse = inverse_sums(thickness, face, my_shift + horizontal(wavenumber, full), size // LANES)
+    inverse = inverse_sums(my, thickness, ky_shift, waves, size)
     values = interface(edges, inverse, waves, size)
     values = everywhere(values)
     news, _ = lax.optimization_barrier((news, values))
     mine, theirs = join(place, keep, got, pair, far, news)
-    return back(place, thickness, values, sines, t, r, m, end, b, mine, across(theirs))
+    return back(place, thickness, values, sines, t, m, end, b, mine, across(theirs))
 
 
 def solution(mesh):

time: 89.5 us -> 78.8 us (0.88)
  Pallas kernels: 50.2 us -> 42.8 us
  other arithmetic: 2.65 us -> 0 us
  blocking collectives: 14.6 us -> 15.6 us
    pallas_call x1, Pallas kernels: 21.2 us -> 14.8 us  [front(): pl.pallas_call(functools.partial(front_kernel, levels, total, group), in_...]
    add x1 -> x0, other arithmetic: 1.23 us -> none  [shards(): my_shift + horizontal(wavenumber, full)]
    pallas_call x1, Pallas kernels: 7.67 us -> 6.67 us  [inverse_sums(): pl.pallas_call(functools.partial(inverse_kernel, counts), in_specs=[in_sm...]
    all_to_all x1, blocking collectives: 14.6 us -> 15.6 us  [everywhere(): lax.all_to_all(a, ('depth', 'wave'), split_axis=0, concat_axis=0, tiled=T...]
    unnamed x16 -> x12, local copies, waits for them, and re-layouts: 3.06 us -> 3.08 us
  transfers between devices with their start and end apart: 6 -> 6, of which waited for: 1 -> 1; matrix products, arithmetic and copies ran while one was open for 2% -> 0% of each run, Pallas kernels for 14% -> 14%
where the time goes in v8:
time: 78.8 us; the launch traced here: 78.4 us
  Pallas kernels  42.8 us (54%)
  blocking collectives  15.6 us (20%)
  starting transfers between devices  13.9 us (18%)
  local copies, waits for them, and re-layouts  3.08 us (4%)
  waiting for transfers between devices  2.12 us (3%)
  between operations  0.9 us (1%)
    all_to_all x1, blocking collectives, everywhere(): lax.all_to_all(a, ('depth', 'wave'), split_axis=0, concat_axis=0, tiled=T...  15.6 us
    pallas_call x1, Pallas kernels, front(): pl.pallas_call(functools.partial(front_kernel, levels, total, group), in_...  14.8 us
    pallas_call x1, Pallas kernels, back(): pl.pallas_call(functools.partial(back_kernel, levels, total), in_specs=[i...  13.9 us
    all_to_all x1, starting transfers between devices, everywhere(): lax.all_to_all(a, ('depth', 'wave'), split_axis=0, concat_axis=0, tiled=T...  7.59 us
    pallas_call x1, Pallas kernels, inverse_sums(): pl.pallas_call(functools.partial(inverse_kernel, counts), in_specs=[in_sm...  6.67 us
    ppermute x3, starting transfers between devices, along(): lax.ppermute(a, 'depth', [(d, (d + 2 * apart) % count) for d in range(cou...  5.65 us
    unnamed x12, local copies, waits for them, and re-layouts  3.08 us
    pallas_call x1, Pallas kernels, join(): pl.pallas_call(functools.partial(join_kernel, chips), in_specs=[in_smem]...  2.81 us
  transfers between devices with their start and end apart: 6, of which 1 were waited for; matrix products, arithmetic and copies ran while one was open for 0% of the time, Pallas kernels for 14%

profile of v8, /device:TPU:0, one launch (start us, length us, event | category | flops | bytes accessed | tf_op | source)
XLA Modules:
  0.0 78.4 jit_solution(513189387885073059)
XLA Ops:
  0.6 14.8 %front.1 = (f32[65,32,1024]{2,1,0:T(8,128)}, f32[8,32,1024]{2,1,0:T(8,128)}, f32[3,32,1024]{2,1,0:T(8,128)}, f32[4,32,1024]{2,1,0:T(8,128)}, f32[3,32,1024]{2,1,...) custom-call(s32[1]{0:T(128)} %bitcast.place, ...), custom_call_target="tpu_custom_call" | custom-call | tf_op jit(solution)/shard_map/front/pallas_call | solution.py:363
  15.4 0.6 collective-permute-start
  16.0 7.6 %all-to-all-start = ((f32[32,4,128]{2,1,0:T(4,128)}), f32[32,4,128]{2,1,0:T(4,128)S(1)}, u32[]{:S(2)}, u32[]{:S(2)}) async-start(f32[32,4,128]{2,1,0:T(4,128)} %get-tuple-element.19), calls=%async_computation | async-start | bytes 131072 | tf_op jit(solution)/shard_map/all_to_all | solution.py:793
  23.7 0.0 collective-permute-done.got
  23.7 0.0 copy-start.1
  23.7 0.8 %copy-done.1 = f32[2,2,2,16,1024]{4,3,2,1,0:T(8,128)} copy-done((f32[2,2,2,16,1024]{4,3,2,1,0:T(8,128)}, f32[2,2,2,16,1024]{4,3,2,1,0:T(8,128)S(1)}, u32[]{:S(2)}) %copy-start.1) | copy-done | bytes 524312
  24.5 2.3 %chip_sums.1 = (f32[2,2,16,1024]{3,2,1,0:T(8,128)}, f32[2,2,16,1024]{3,2,1,0:T(8,128)}, f32[2,2,16,1024]{3,2,1,0:T(8,128)}) custom-call(s32[1]{0:T(128)} %bitcast.place, f32[2,2,2,16,1024]{4,3,2,1,0:T(8,128)} %get-tuple-element.21.keep, f32[2,2,2,16,1024]{4,3,2,1,0:T(8,128)} %copy-done.1, f32[4,32,1024]{2,1,0:T(8,128)} %get-tuple-element.23.pair), custom_call_target="tpu_custom_call" | custom-call | flops 1 | bytes 1 | tf_op jit(solution)/shard_map/chip_sums/pallas_call | solution.py:425
  26.7 1.8 %collective-permute-start.1 = (f32[2,2,16,1024]{3,2,1,0:T(8,128)}, f32[2,2,16,1024]{3,2,1,0:T(8,128)S(1)}, u32[]{:S(2)}, u32[]{:S(2)}) collective-permute-start(f32[2,2,16,1024]{3,2,1,0:T(8,128)} %get-tuple-element.25), channel_id=1, source_target_pairs={{0,8},{4,12},{8,16},{12,20},{16,24},{20,28},{24,0},{28,4},{1,9},{5... | collective-permute-start | bytes 786440 | tf_op jit(solution)/shard_map/ppermute | solution.py:790
  28.6 2.4 %collective-permute-start.2 = (f32[2,2,16,1024]{3,2,1,0:T(8,128)}, f32[2,2,16,1024]{3,2,1,0:T(8,128)S(1)}, u32[]{:S(2)}, u32[]{:S(2)}) collective-permute-start(f32[2,2,16,1024]{3,2,1,0:T(8,128)} %get-tuple-element.26), channel_id=1, source_target_pairs={{0,16},{4,20},{8,24},{12,28},{16,0},{20,4},{24,8},{28,12},{1,17},{... | collective-permute-start | bytes 786440 | tf_op jit(solution)/shard_map/ppermute | solution.py:790
  31.0 1.4 %collective-permute-start.3 = (f32[2,2,16,1024]{3,2,1,0:T(8,128)}, f32[2,2,16,1024]{3,2,1,0:T(8,128)S(1)}, u32[]{:S(2)}, u32[]{:S(2)}) collective-permute-start(f32[2,2,16,1024]{3,2,1,0:T(8,128)} %get-tuple-element.27), channel_id=1, source_target_pairs={{0,24},{4,28},{8,0},{12,4},{16,8},{20,12},{24,16},{28,20},{1,25},{... | collective-permute-start | bytes 786440 | tf_op jit(solution)/shard_map/ppermute | solution.py:790
  32.4 6.7 %inverse_sums.1.inverse = f32[3,64,128]{2,1,0:T(8,128)} custom-call(s32[1]{0:T(128)} %bitcast.1.my, f32[64]{0:T(128)} %thick.5, f32[32]{0:T(128)} %shifts.3, f32[24,128]{1,0:T(8,128)} %constant.44.clone.across, f32[24,128]{1,0:T(8,128)} %constant.45.clone.weights), custom_call_target="tpu_custom_call" | custom-call | flops 20000000000 | bytes 40000000 | tf_op jit(solution)/shard_map/inverse_sums/pallas_call | solution.py:594
  39.1 0.0 all-to-all-done.edges
  39.1 0.0 copy-start.2
  39.1 0.6 copy-done.2
  39.7 2.3 %interface.1 = f32[32,4,128]{2,1,0:T(4,128)} custom-call(f32[2,96,16]{2,1,0:T(8,128)} %constant.46.clone.matrices, f32[32,4,128]{2,1,0:T(4,128)} %copy-done.2, f32[3,64,128]{2,1,0:T(8,128)} %inverse_sums.1.inverse), custom_call_target="tpu_custom_call" | custom-call | tf_op jit(solution)/shard_map/interface/pallas_call | solution.py:631
  42.0 15.6 %all_to_all.10.values = f32[32,4,128]{2,1,0:T(4,128)} all-to-all(f32[32,4,128]{2,1,0:T(4,128)} %interface.1), channel_id=1, replica_groups=mesh['depth'=8,'wave'=4] {'depth','wave'}, dimensions={0} | all-to-all | bytes 131072 | tf_op jit(solution)/shard_map/all_to_all | solution.py:793
  57.6 0.0 collective-permute-done.1.refs_0_
  57.6 0.0 copy-start.3
  57.6 0.0 collective-permute-done.2.refs_1_
  57.6 0.0 copy-start.4
  57.6 0.0 collective-permute-done.3.refs_2_
  57.6 0.0 copy-start.5
  57.7 0.7 copy-done.3
  58.3 0.1 copy-done.4
  58.4 0.1 copy-done.5
  58.5 2.8 %join.1 = (f32[2,2,2,16,1024]{4,3,2,1,0:T(8,128)}, f32[2,2,2,16,1024]{4,3,2,1,0:T(8,128)}) custom-call(s32[1]{0:T(128)} %bitcast.place, f32[2,2,2,16,1024]{4,3,2,1,0:T(8,128)} %get-tuple-element.21.keep, f32[2,2,2,16,1024]{4,3,2,1,0:T(8,128)} %copy-done.1, f32[4,32,1024]{2,1,0:T(8,128)} %get-tuple-element.23.pair, f32[3,32,1024]{2,1,0:T(8,128)} %get-tuple-element.24.far, ...), custom_call_target="tpu_custom_call" | custom-call | flops 20000000000 | bytes 40000000 | tf_op jit(solution)/shard_map/join/pallas_call | solution.py:480
  61.3 0.1 collective-permute-start.4
  61.4 2.1 %collective-permute-done.4.theirs = f32[2,2,2,16,1024]{4,3,2,1,0:T(8,128)S(1)} collective-permute-done((f32[2,2,2,16,1024]{4,3,2,1,0:T(8,128)}, f32[2,2,2,16,1024]{4,3,2,1,0:T(8,128)S(1)}, u32[]{:S(2)}, u32[]{:S(2)}) %collective-permute-start.4) | collective-permute-done | bytes 524320 | tf_op jit(solution)/shard_map/ppermute | solution.py:787
  63.5 0.0 copy-start
  63.5 0.8 %copy-done = f32[2,2,2,16,1024]{4,3,2,1,0:T(8,128)} copy-done((f32[2,2,2,16,1024]{4,3,2,1,0:T(8,128)}, f32[2,2,2,16,1024]{4,3,2,1,0:T(8,128)S(1)}, u32[]{:S(2)}) %copy-start) | copy-done | bytes 524312
  64.3 13.9 %back.1 = (f32[2,8,32,1024]{3,2,1,0:T(8,128)}, f32[2,8,32,1024]{3,2,1,0:T(8,128)}) custom-call(s32[1]{0:T(128)} %bitcast.place, f32[64]{0:T(128)} %thick.5, f32[32,4,128]{2,1,0:T(4,128)} %all_to_all.10.values, bf16[128,256]{1,0:T(8,128)(2,1)} %constant.47.clone.spread, f32[65,32,1024]{2,1,0:T(8,128)} %get-tuple-element.20.t, ...), custom_call_target="tpu_custom_call" | custom-call | tf_op jit(solution)/shard_map/back/pallas_call | solution.py:750
Async XLA Ops:
  15.4 8.2 %collective-permute-start = (f32[2,2,2,16,1024]{4,3,2,1,0:T(8,128)}, f32[2,2,2,16,1024]{4,3,2,1,0:T(8,128)S(1)}, u32[]{:S(2)}, u32[]{:S(2)}) collective-permute-start(f32[2,2,2,16,1024]{4,3,2,1,0:T(8,128)} %get-tuple-element.22), channel_id=1, source_target_pairs={{0,4},{4,0},{8,12},{12,8},{16,20},{20,16},{24,28},{28,24},{1,5},{5... | collective-permute-start | bytes 1572872 | tf_op jit(solution)/shard_map/ppermute | solution.py:787
  16.0 23.0 %all-to-all-start = ((f32[32,4,128]{2,1,0:T(4,128)}), f32[32,4,128]{2,1,0:T(4,128)S(1)}, u32[]{:S(2)}, u32[]{:S(2)}) async-start(f32[32,4,128]{2,1,0:T(4,128)} %get-tuple-element.19), calls=%async_computation | async-start | bytes 131072 | tf_op jit(solution)/shard_map/all_to_all | solution.py:793
  23.7 0.8 %copy-start.1 = (f32[2,2,2,16,1024]{4,3,2,1,0:T(8,128)}, f32[2,2,2,16,1024]{4,3,2,1,0:T(8,128)S(1)}, u32[]{:S(2)}) copy-start(f32[2,2,2,16,1024]{4,3,2,1,0:T(8,128)S(1)} %collective-permute-done.got) | copy-start | bytes 1572868
  26.7 30.9 %collective-permute-start.1 = (f32[2,2,16,1024]{3,2,1,0:T(8,128)}, f32[2,2,16,1024]{3,2,1,0:T(8,128)S(1)}, u32[]{:S(2)}, u32[]{:S(2)}) collective-permute-start(f32[2,2,16,1024]{3,2,1,0:T(8,128)} %get-tuple-element.25), channel_id=1, source_target_pairs={{0,8},{4,12},{8,16},{12,20},{16,24},{20,28},{24,0},{28,4},{1,9},{5... | collective-permute-start | bytes 786440 | tf_op jit(solution)/shard_map/ppermute | solution.py:790
  28.6 29.1 %collective-permute-start.2 = (f32[2,2,16,1024]{3,2,1,0:T(8,128)}, f32[2,2,16,1024]{3,2,1,0:T(8,128)S(1)}, u32[]{:S(2)}, u32[]{:S(2)}) collective-permute-start(f32[2,2,16,1024]{3,2,1,0:T(8,128)} %get-tuple-element.26), channel_id=1, source_target_pairs={{0,16},{4,20},{8,24},{12,28},{16,0},{20,4},{24,8},{28,12},{1,17},{... | collective-permute-start | bytes 786440 | tf_op jit(solution)/shard_map/ppermute | solution.py:790
  31.0 26.6 %collective-permute-start.3 = (f32[2,2,16,1024]{3,2,1,0:T(8,128)}, f32[2,2,16,1024]{3,2,1,0:T(8,128)S(1)}, u32[]{:S(2)}, u32[]{:S(2)}) collective-permute-start(f32[2,2,16,1024]{3,2,1,0:T(8,128)} %get-tuple-element.27), channel_id=1, source_target_pairs={{0,24},{4,28},{8,0},{12,4},{16,8},{20,12},{24,16},{28,20},{1,25},{... | collective-permute-start | bytes 786440 | tf_op jit(solution)/shard_map/ppermute | solution.py:790
  39.1 0.6 copy-start.2
  57.6 0.7 copy-start.3
  57.6 0.8 %copy-start.4 = (f32[2,2,16,1024]{3,2,1,0:T(8,128)}, f32[2,2,16,1024]{3,2,1,0:T(8,128)S(1)}, u32[]{:S(2)}) copy-start(f32[2,2,16,1024]{3,2,1,0:T(8,128)S(1)} %collective-permute-done.2.refs_1_) | copy-start | bytes 786436
  57.6 0.9 %copy-start.5 = (f32[2,2,16,1024]{3,2,1,0:T(8,128)}, f32[2,2,16,1024]{3,2,1,0:T(8,128)S(1)}, u32[]{:S(2)}) copy-start(f32[2,2,16,1024]{3,2,1,0:T(8,128)S(1)} %collective-permute-done.3.refs_2_) | copy-start | bytes 786436
  61.3 2.2 %collective-permute-start.4 = (f32[2,2,2,16,1024]{4,3,2,1,0:T(8,128)}, f32[2,2,2,16,1024]{4,3,2,1,0:T(8,128)S(1)}, u32[]{:S(2)}, u32[]{:S(2)}) collective-permute-start(f32[2,2,2,16,1024]{4,3,2,1,0:T(8,128)} %get-tuple-element.32), channel_id=1, source_target_pairs={{0,4},{4,0},{8,12},{12,8},{16,20},{20,16},{24,28},{28,24},{1,5},{5... | collective-permute-start | bytes 1572872 | tf_op jit(solution)/shard_map/ppermute | solution.py:787
  63.5 0.8 %copy-start = (f32[2,2,2,16,1024]{4,3,2,1,0:T(8,128)}, f32[2,2,2,16,1024]{4,3,2,1,0:T(8,128)S(1)}, u32[]{:S(2)}) copy-start(f32[2,2,2,16,1024]{4,3,2,1,0:T(8,128)S(1)} %collective-permute-done.4.theirs) | copy-start | bytes 1572868

commit v9 on v8

--- a/solution.py
+++ b/solution.py
@@ -12,7 +12,7 @@
 aspect_ratio = 1.0
 LANES = 128
 ROWS = 8
-VMEM_BYTES = 60 * 1024 * 1024
+VMEM_BYTES = 56 * 1024 * 1024
 real_dot = functools.partial(jnp.dot, preferred_element_type=jnp.float32)
 exact_dot = functools.partial(lax.dot_general, precision=lax.Precision.HIGHEST, preferred_element_type=jnp.float32)
 NN = (((1,), (0,)), ((), ()))
@@ -21,6 +21,8 @@
 in_hbm = pl.BlockSpec(memory_space=pl.ANY)
 in_vmem = pl.BlockSpec(memory_space=pltpu.VMEM)
 params = pltpu.CompilerParams(vmem_limit_bytes=VMEM_BYTES)
+small = pltpu.CompilerParams(vmem_limit_bytes=12 * 1024 * 1024)
+medium = pltpu.CompilerParams(vmem_limit_bytes=30 * 1024 * 1024)
 brief = pl.CostEstimate(flops=1, bytes_accessed=1, transcendentals=0)
 lengthy = pl.CostEstimate(flops=20_000_000_000, bytes_accessed=40_000_000, transcendentals=0)
 
@@ -29,7 +31,7 @@
     return np.concatenate([np.arange(1, size, 2), np.arange(0, size, 2)])
 
 
-def half_sines(size, back=False):
+def half_sines(size, back=False, scale=1.0):
     half = size // 2
     place = np.arange(half)
     place[0] = half
@@ -39,7 +41,7 @@
         if waves[0] == 0:
             matrix[0] = 0.0
             matrix[:, 0] = 0.0
-        matrix = (matrix.T if back else matrix).astype(np.float32)
+        matrix = (matrix.T if back else matrix).astype(np.float32) * np.float32(scale)
         top = matrix.astype(jnp.bfloat16)
         parts += [top, (matrix - top.astype(np.float32)).astype(jnp.bfloat16)]
     return parts
@@ -69,7 +71,8 @@
                         value = weight * math.cos(2.0 * math.pi * (c * (w + e - v - g) % waves) / waves)
                         for f in range(4):
                             matrix[g, c, e, w, f, v, f] = value
-    return matrix.reshape(2, classes * 2 * waves * 4, waves * 4).astype(np.float32)
+    matrix = matrix.reshape(2, classes * 2 * waves * 4, waves * 4)
+    return np.concatenate([matrix[0], matrix[1]], 1).astype(np.float32)
 
 
 def split(values):
@@ -388,15 +391,15 @@
     )(place, thick, shifts, across, sines, edge_matrix(size, total), rhs, cotangent, *half_sines(size))
 
 
-def chip_kernel(chips, place, keep, got, pair, *refs):
+def chip_kernel(chips, place, keep, got_v, pair, *refs):
     outs = refs[:chips - 1]
-    sems, keep_v, got_v, pair_v, down_v, up_v = refs[chips - 1:]
+    sems, keep_v, pair_v, down_v, up_v = refs[chips - 1:]
     copies = Copies(sems)
     chip = place[0] // 2
     upper = place[0] % 2 == 0
     half = keep_v.shape[3]
     here = pl.ds(pl.multiple_of((place[0] % 2) * half, ROWS), half)
-    for copy in [copies.start(keep, keep_v), copies.start(got, got_v), copies.start(pair.at[:, here], pair_v)]:
+    for copy in [copies.start(keep, keep_v), copies.start(pair.at[:, here], pair_v)]:
         copy.wait()
     for a in range(2):
         first, second = jnp.where(upper, keep_v[a], got_v[a]), jnp.where(upper, got_v[a], keep_v[a])
@@ -404,7 +407,7 @@
         up_v[a] = first[1] + pair_v[2] * second[1]
     for apart in range(1, chips):
         goes_down = chip + apart < chips
-        sem = sems.at[2 + apart]
+        sem = sems.at[1 + apart]
 
         @pl.when(goes_down)
         def _():
@@ -415,7 +418,7 @@
             pltpu.make_async_copy(up_v, outs[apart - 1], sem).start()
 
     for apart in range(1, chips):
-        pltpu.make_async_copy(down_v, outs[apart - 1], sems.at[2 + apart]).wait()
+        pltpu.make_async_copy(down_v, outs[apart - 1], sems.at[1 + apart]).wait()
 
 
 def chip_sums(place, keep, got, pair, chips):
@@ -424,18 +427,17 @@
     shape = (2, 2, half, size)
     return pl.pallas_call(
         functools.partial(chip_kernel, chips),
-        in_specs=[in_smem] + [in_hbm] * 3,
+        in_specs=[in_smem, in_hbm, in_vmem, in_hbm],
         out_specs=[in_hbm] * (chips - 1),
         out_shape=[jax.ShapeDtypeStruct(shape, jnp.float32)] * (chips - 1),
         scratch_shapes=[
-            pltpu.SemaphoreType.DMA((2 + chips,)),
-            single(*keep.shape),
+            pltpu.SemaphoreType.DMA((1 + chips,)),
             single(*keep.shape),
             single(4, half, size),
             single(*shape),
             single(*shape),
         ],
-        compiler_params=params,
+        compiler_params=small,
         cost_estimate=brief,
         name="chip_sums",
     )(place, keep, got, pair)
@@ -443,14 +445,13 @@
 
 def join_kernel(chips, place, keep, got, pair, far, *refs):
     news = refs[:chips - 1]
-    mine, theirs, sems, keep_v, got_v, pair_v, far_v, news_v, mine_v, theirs_v = refs[chips - 1:]
+    mine, theirs, sems, keep_v, got_v, pair_v, far_v, mine_v, theirs_v = refs[chips - 1:]
     copies = Copies(sems)
     chip = place[0] // 2
     upper = place[0] % 2 == 0
     half = keep_v.shape[3]
     here = pl.ds(pl.multiple_of((place[0] % 2) * half, ROWS), half)
     ready = [copies.start(keep, keep_v), copies.start(got, got_v), copies.start(pair.at[:, here], pair_v), copies.start(far.at[:, here], far_v)]
-    ready += [copies.start(news[i], news_v.at[i]) for i in range(chips - 1)]
     for copy in ready:
         copy.wait()
     for a in range(2):
@@ -460,7 +461,7 @@
             down = jnp.zeros((half, keep_v.shape[4]), jnp.float32)
             up = down
             for apart in range(1, chips):
-                term = far_v[apart - 1] * news_v[apart - 1, a, ri]
+                term = far_v[apart - 1] * news[apart - 1][a, ri]
                 down = down + jnp.where(chip >= apart, term, 0.0)
                 up = up + jnp.where(chip >= apart, 0.0, term)
             inner_up = pick(second, 1) + pair_v[3] * up
@@ -479,20 +480,19 @@
     single = lambda *shape: pltpu.VMEM(shape, jnp.float32)
     return pl.pallas_call(
         functools.partial(join_kernel, chips),
-        in_specs=[in_smem] + [in_hbm] * (3 + chips),
+        in_specs=[in_smem] + [in_hbm] * 4 + [in_vmem] * (chips - 1),
         out_specs=[in_hbm] * 2,
         out_shape=[jax.ShapeDtypeStruct(keep.shape, jnp.float32)] * 2,
         scratch_shapes=[
-            pltpu.SemaphoreType.DMA((5 + chips,)),
+            pltpu.SemaphoreType.DMA((6,)),
             single(*keep.shape),
             single(*keep.shape),
             single(4, half, size),
             single(chips - 1, half, size),
-            single(chips - 1, 2, 2, half, size),
             single(*keep.shape),
             single(*keep.shape),
         ],
-        compiler_params=params,
+        compiler_params=small,
         cost_estimate=lengthy,
         name="join",
     )(place, keep, got, pair, far, *news)
@@ -596,7 +596,7 @@
         in_specs=[in_smem] * 3 + [in_vmem] * 2,
         out_shape=jax.ShapeDtypeStruct((classes, total, wide), jnp.float32),
         scratch_shapes=[pltpu.VMEM((total + 1, ROWS, LANES), jnp.float32)] + [pltpu.VMEM((total,) + across.shape, jnp.float32)] * 3,
-        compiler_params=params,
+        compiler_params=small,
         cost_estimate=lengthy,
         name="inverse_sums",
     )(my, thick, shifts, across, weight)
@@ -613,13 +613,12 @@
             line = line + edges[d * waves + w]
         lines.append(line)
     lines = jnp.concatenate(lines, 0)
-    near, far = exact_dot(matrices[0], lines, NN), exact_dot(matrices[1], lines, NN)
-    mixed = near[:, :total] + far[:, total:]
-    result = jnp.zeros((2 * rows, total), jnp.float32)
-    for c in range(inverse.shape[0]):
-        part = mixed[c * 2 * rows:(c + 1) * 2 * rows]
-        square = inverse[c][:, :total]
-        result = result + (exact_dot(part, square, NN) + exact_dot(part, square, NT))
+    lines = jnp.concatenate([lines[:, :total], lines[:, total:]], 0)
+    mixed = exact_dot(matrices[...], lines, NN)
+    classes = inverse.shape[0]
+    parts = jnp.concatenate([mixed[c * 2 * rows:(c + 1) * 2 * rows] for c in range(classes)], 1)
+    squares = [inverse[c][:, :total] for c in range(classes)]
+    result = exact_dot(parts, jnp.concatenate(squares, 0), NN) + exact_dot(parts, jnp.concatenate(squares, 1), NT)
     result = jnp.concatenate([result[:rows], result[rows:]], 1)
     for w in range(waves):
         line = result[4 * w:4 * w + 4]
@@ -633,40 +632,29 @@
         in_specs=[in_vmem] * 3,
         out_specs=in_vmem,
         out_shape=jax.ShapeDtypeStruct(edges.shape, jnp.float32),
-        compiler_params=params,
+        compiler_params=small,
         name="interface",
     )(interface_matrices(waves, size), edges, inverse)
 
 
-def back_kernel(levels, total, place, thick, values, spread, t, mine, theirs, sines, b, m, end, odd_top, odd_rest, even_top, even_rest, out0, out1, sems, values_v, spread_v, t_v, ends, sines_v, b_v, m_v, end_v, ot, orest, et, er, picked, u_all, q_all, out_v):
+def back_kernel(levels, total, place, thick, values_v, spread_v, t_v, mine, theirs, sines_v, b_v, m_v, end_v, ot, orest, et, er, out0, out1, sems, ends, picked, u_all, q_all, out_v):
     _, _, _, ky, size = b_v.shape
     first = place[0] * levels
     half = size // 2
     many = half // LANES
     core = place[0] % 2
     copies = Copies(sems)
-    early = [copies.start(values.at[pl.ds(0, ky)], values_v), copies.start(spread, spread_v)]
-    table = copies.start(t, t_v)
-    both = []
-    for source, start in ((mine, core), (theirs, 1 - core)):
-        here = pl.ds(pl.multiple_of(start * (ky // 2), ROWS), ky // 2)
-        both.append(copies.start(source, ends.at[:, :, :, here]))
-    both.append(copies.start(sines, sines_v))
-    rest = [copies.start(source, target) for source, target in ((m, m_v), (end, end_v), (odd_top, ot), (odd_rest, orest), (even_top, et), (even_rest, er))]
-    fields = [copies.start(b.at[f // 2, f % 2], b_v.at[f // 2, f % 2]) for f in range(4)]
-    for copy in early:
-        copy.wait()
+    here, there = (pl.ds(pl.multiple_of(start * (ky // 2), ROWS), ky // 2) for start in (core, 1 - core))
     lane = lax.broadcasted_iota(jnp.int32, (ky, 2 * total), 1)
     for f in range(4):
-        parts = [part.astype(jnp.float32) for part in split(values_v[:, f, :])]
+        parts = [part.astype(jnp.float32) for part in split(values_v[:ky, f, :])]
         for j in range(total):
             spot = (lane == j) | (lane == total + j)
             for p in range(2):
                 picked[p, j * ky:(j + 1) * ky, :] = jnp.where(spot, parts[p], 0.0).astype(jnp.bfloat16)
         u_all[f] = (real_dot(picked[0], spread_v[...]) + real_dot(picked[1], spread_v[...])).reshape(total, ky, 2 * LANES)
-    table.wait()
-    for copy in both:
-        copy.wait()
+    ends[:, :, :, here] = mine[...]
+    ends[:, :, :, there] = theirs[...]
 
     def source(f, j, here):
         pair = u_all[f, j, here] * thick[j]
@@ -700,44 +688,41 @@
         return 0
 
     lax.fori_loop(0, ky // ROWS, sweep, 0)
-    for copy in rest:
-        copy.wait()
-    rows = levels * ky
+    rows = 2 * levels * ky
     lane = lax.broadcasted_iota(jnp.int32, (ky, LANES), 1)
     outs = []
-    for f in range(4):
-        a, ri = f // 2, f % 2
-        fields[f].wait()
-
+    for a in range(2):
         def tile(g, _):
             here = pl.ds(pl.multiple_of(g * ROWS, ROWS), ROWS)
             wave = sines_v[...]
-            y = ends[a, 0, ri, here]
-            ys = []
-            for j in range(levels):
-                y = b_v[a, ri, j, here] + wave * source(f, first + j, here) + m_v[j, here] * y
-                ys.append(y)
-            value = (y + end_v[0, here] * ends[a, 1, ri, here]) * end_v[1, here]
-            q_all[levels - 1, here] = value
-            for j in range(levels - 2, -1, -1):
-                value = m_v[j + 1, here] * (ys[j] * (0.5 * (thick[first + j] + thick[first + j + 1])) + value)
-                q_all[j, here] = value
+            for ri in range(2):
+                y = ends[a, 0, ri, here]
+                ys = []
+                for j in range(levels):
+                    y = b_v[a, ri, j, here] + wave * source(2 * a + ri, first + j, here) + m_v[j, here] * y
+                    ys.append(y)
+                value = (y + end_v[0, here] * ends[a, 1, ri, here]) * end_v[1, here]
+                q_all[ri, levels - 1, here] = value
+                for j in range(levels - 2, -1, -1):
+                    value = m_v[j + 1, here] * (ys[j] * (0.5 * (thick[first + j] + thick[first + j + 1])) + value)
+                    q_all[ri, j, here] = value
             return 0
 
         lax.fori_loop(0, ky // ROWS, tile, 0)
         low, high = to_cells(
-            q_all[:, :, :half].reshape(rows, half), q_all[:, :, half:].reshape(rows, half), ot, orest, et, er
+            q_all[:, :, :, :half].reshape(rows, half), q_all[:, :, :, half:].reshape(rows, half), ot, orest, et, er
         )
-        for j in range(levels):
-            height = thick[first + j] if a else 1.0
-            scale = (2.0 / size) * height
-            here = slice(j * ky, (j + 1) * ky)
-            u = (u_all[f, first + j, :, :LANES] + u_all[f, first + j, :, LANES:]) * (0.5 * height)
-            if many > 1:
-                out_v[f, j, :, LANES:half] = low[here, LANES:] * scale
-            out_v[f, j, :, :LANES] = jnp.where(lane == 0, u, low[here, :LANES] * scale)
-            out_v[f, j, :, half:] = high[here] * scale
-        outs.append(copies.start(out_v.at[f], (out0, out1)[a].at[ri]))
+        for ri in range(2):
+            for j in range(levels):
+                height = thick[first + j] if a else 1.0
+                here = slice((ri * levels + j) * ky, (ri * levels + j + 1) * ky)
+                u = u_all[2 * a + ri, first + j]
+                u = (u[:, :LANES] + u[:, LANES:]) * (0.5 * height)
+                if many > 1:
+                    out_v[a, ri, j, :, LANES:half] = low[here, LANES:] * height
+                out_v[a, ri, j, :, :LANES] = jnp.where(lane == 0, u, low[here, :LANES] * height)
+                out_v[a, ri, j, :, half:] = high[here] * height
+            outs.append(copies.start(out_v.at[a, ri], (out0, out1)[a].at[ri]))
     for copy in outs:
         copy.wait()
 
@@ -749,28 +734,20 @@
     single = lambda *shape: pltpu.VMEM(shape, jnp.float32)
     return pl.pallas_call(
         functools.partial(back_kernel, levels, total),
-        in_specs=[in_smem] * 2 + [in_hbm] * 13,
+        in_specs=[in_smem] * 2 + [in_vmem] * 13,
         out_specs=[in_hbm] * 2,
         out_shape=[jax.ShapeDtypeStruct((2, levels, ky, size), jnp.float32)] * 2,
         scratch_shapes=[
-            pltpu.SemaphoreType.DMA((20,)),
-            single(ky, 4, 2 * total),
-            pltpu.VMEM((2 * total, 2 * LANES), jnp.bfloat16),
-            single(*t.shape),
+            pltpu.SemaphoreType.DMA((4,)),
             single(2, 2, 2, ky, size),
-            single(ROWS, size),
-            single(*b.shape),
-            single(*m.shape),
-            single(*end.shape),
-            *[pltpu.VMEM((half, half), jnp.bfloat16)] * 4,
             pltpu.VMEM((2, total * ky, 2 * total), jnp.bfloat16),
             single(4, total, ky, 2 * LANES),
-            single(levels, ky, size),
-            single(4, levels, ky, size),
+            single(2, levels, ky, size),
+            single(2, 2, levels, ky, size),
         ],
-        compiler_params=params,
+        compiler_params=medium,
         name="back",
-    )(place, thick, values, spread_matrix(total), t, mine, theirs, sines, b, m, end, *half_sines(size, True))
+    )(place, thick, values, spread_matrix(total), t, mine, theirs, sines, b, m, end, *half_sines(size, True, 2.0 / size))
 
 
 def shards(rhs, cotangent, thickness, ky_shift):

time: 78.8 us -> 76.4 us (0.970)
  Pallas kernels: 42.8 us -> 35.6 us
  blocking collectives: 15.6 us -> 18.6 us
  local copies, waits for them, and re-layouts: 3.08 us -> 5.07 us
    all_to_all x1, blocking collectives: 15.6 us -> 18.6 us  [everywhere(): lax.all_to_all(a, ('depth', 'wave'), split_axis=0, concat_axis=0, tiled=T...]
    pallas_call x1, Pallas kernels: 2.81 us -> 0.54 us  [join(): pl.pallas_call(functools.partial(join_kernel, chips), in_specs=[in_smem]...]
    unnamed x12 -> x44, local copies, waits for them, and re-layouts: 3.08 us -> 5.07 us
    pallas_call x1, Pallas kernels: 2.3 us -> 0.66 us  [interface(): pl.pallas_call(functools.partial(interface_kernel, waves), in_specs=[in_v...]
    pallas_call x1, Pallas kernels: 2.26 us -> 0.88 us  [chip_sums(): pl.pallas_call(functools.partial(chip_kernel, chips), in_specs=[in_smem,...]
    pallas_call x1, Pallas kernels: 13.9 us -> 12.7 us  [back(): pl.pallas_call(functools.partial(back_kernel, levels, total), in_specs=[i...]
    pallas_call x1, Pallas kernels: 6.67 us -> 5.86 us  [inverse_sums(): pl.pallas_call(functools.partial(inverse_kernel, counts), in_specs=[in_sm...]
  transfers between devices with their start and end apart: 6 -> 6, of which waited for: 1 -> 1; matrix products, arithmetic and copies ran while one was open for 0% -> 0% of each run, Pallas kernels for 14% -> 10%
where the time goes in v9:
time: 76.4 us; the launch traced here: 76.1 us
  Pallas kernels  35.6 us (47%)
  blocking collectives  18.6 us (24%)
  starting transfers between devices  13.9 us (18%)
  local copies, waits for them, and re-layouts  5.07 us (7%)
  waiting for transfers between devices  1.91 us (2%)
  between operations  1.08 us (1%)
    all_to_all x1, blocking collectives, everywhere(): lax.all_to_all(a, ('depth', 'wave'), split_axis=0, concat_axis=0, tiled=T...  18.6 us
    pallas_call x1, Pallas kernels, front(): pl.pallas_call(functools.partial(front_kernel, levels, total, group), in_...  14.9 us
    pallas_call x1, Pallas kernels, back(): pl.pallas_call(functools.partial(back_kernel, levels, total), in_specs=[i...  12.7 us
    all_to_all x1, starting transfers between devices, everywhere(): lax.all_to_all(a, ('depth', 'wave'), split_axis=0, concat_axis=0, tiled=T...  7.6 us
    pallas_call x1, Pallas kernels, inverse_sums(): pl.pallas_call(functools.partial(inverse_kernel, counts), in_specs=[in_sm...  5.86 us
    ppermute x3, starting transfers between devices, along(): lax.ppermute(a, 'depth', [(d, (d + 2 * apart) % count) for d in range(cou...  5.65 us
    unnamed x44, local copies, waits for them, and re-layouts  5.07 us
    ppermute x2, waiting for transfers between devices, across(): return lax.ppermute(a, 'depth', [(d, d ^ 1) for d in range(count)])  1.9 us
  transfers between devices with their start and end apart: 6, of which 1 were waited for; matrix products, arithmetic and copies ran while one was open for 0% of the time, Pallas kernels for 10%

profile of v9, /device:TPU:0, one launch (start us, length us, event | category | flops | bytes accessed | tf_op | source)
XLA Modules:
  0.0 76.1 jit_solution(4338930285869225700)
XLA Ops:
  0.6 0.0 copy-start.14
  0.6 0.0 copy-start.15
  0.7 0.0 copy-start.17
  0.7 0.0 copy-start.18
  0.7 14.9 %front.1 = (f32[65,32,1024]{2,1,0:T(8,128)}, f32[8,32,1024]{2,1,0:T(8,128)}, f32[3,32,1024]{2,1,0:T(8,128)}, f32[4,32,1024]{2,1,0:T(8,128)}, f32[3,32,1024]{2,1,...) custom-call(s32[1]{0:T(128)} %bitcast.place, ...), custom_call_target="tpu_custom_call" | custom-call | tf_op jit(solution)/shard_map/front/pallas_call | solution.py:366
  15.6 0.6 collective-permute-start
  16.2 7.6 %all-to-all-start = ((f32[32,4,128]{2,1,0:T(4,128)}), f32[32,4,128]{2,1,0:T(4,128)S(1)}, u32[]{:S(2)}, u32[]{:S(2)}) async-start(f32[32,4,128]{2,1,0:T(4,128)} %get-tuple-element.19), calls=%async_computation | async-start | bytes 131072 | tf_op jit(solution)/shard_map/all_to_all | solution.py:770
  23.9 0.0 collective-permute-done.got_v.got
  23.9 0.0 copy-start.6
  23.9 1.0 %copy-done.6 = f32[4,32,1024]{2,1,0:T(8,128)S(1)} copy-done((f32[4,32,1024]{2,1,0:T(8,128)S(1)}, f32[4,32,1024]{2,1,0:T(8,128)}, u32[]{:S(2)}) %copy-start.6) | copy-done | bytes 524312
  24.9 0.0 copy-start.8
  24.9 1.0 %copy-done.8 = f32[2,2,2,16,1024]{4,3,2,1,0:T(8,128)S(1)} copy-done((f32[2,2,2,16,1024]{4,3,2,1,0:T(8,128)S(1)}, f32[2,2,2,16,1024]{4,3,2,1,0:T(8,128)}, u32[]{:S(2)}) %copy-start.8) | copy-done | bytes 524312
  26.0 0.9 %chip_sums.1 = (f32[2,2,16,1024]{3,2,1,0:T(8,128)}, f32[2,2,16,1024]{3,2,1,0:T(8,128)S(1)}, f32[2,2,16,1024]{3,2,1,0:T(8,128)S(1)}) custom-call(s32[1]{0:T(128)} %bitcast.place, f32[2,2,2,16,1024]{4,3,2,1,0:T(8,128)S(1)} %copy-done.8, f32[2,2,2,16,1024]{4,3,2,1,0:T(8,128)S(1)} %collective-permute-done.got_v.got, f32[4,32,1024]{2,1,0:T(8,128)S(1)} %copy-done.6), custom_call_target="tpu_custom_call" | custom-call | flops 1 | bytes 1 | tf_op jit(solution)/shard_map/chip_sums/pallas_call | solution.py:428
  26.8 1.8 %collective-permute-start.1 = (f32[2,2,16,1024]{3,2,1,0:T(8,128)}, f32[2,2,16,1024]{3,2,1,0:T(8,128)S(1)}, u32[]{:S(2)}, u32[]{:S(2)}) collective-permute-start(f32[2,2,16,1024]{3,2,1,0:T(8,128)} %get-tuple-element.25), channel_id=1, source_target_pairs={{0,8},{4,12},{8,16},{12,20},{16,24},{20,28},{24,0},{28,4},{1,9},{5... | collective-permute-start | bytes 786440 | tf_op jit(solution)/shard_map/ppermute | solution.py:767
  28.7 2.5 %collective-permute-start.2 = (f32[2,2,16,1024]{3,2,1,0:T(8,128)S(1)}, f32[2,2,16,1024]{3,2,1,0:T(8,128)S(1)}, u32[]{:S(2)}, u32[]{:S(2)}) collective-permute-start(f32[2,2,16,1024]{3,2,1,0:T(8,128)S(1)} %get-tuple-element.26), channel_id=1, source_target_pairs={{0,16},{4,20},{8,24},{12,28},{16,0},{20,4},{24,8},{28,12},{1,17},{... | collective-permute-start | bytes 786440 | tf_op jit(solution)/shard_map/ppermute | solution.py:767
  31.1 1.4 %collective-permute-start.3 = (f32[2,2,16,1024]{3,2,1,0:T(8,128)S(1)}, f32[2,2,16,1024]{3,2,1,0:T(8,128)S(1)}, u32[]{:S(2)}, u32[]{:S(2)}) collective-permute-start(f32[2,2,16,1024]{3,2,1,0:T(8,128)S(1)} %get-tuple-element.27), channel_id=1, source_target_pairs={{0,24},{4,28},{8,0},{12,4},{16,8},{20,12},{24,16},{28,20},{1,25},{... | collective-permute-start | bytes 786440 | tf_op jit(solution)/shard_map/ppermute | solution.py:767
  32.5 0.0 copy-done.14
  32.5 0.0 copy-done.15
  32.5 0.0 copy-done.17
  32.5 0.0 copy-done.18
  32.5 0.0 copy-start.13
  32.5 0.0 copy-start.7
  32.5 0.0 copy-start.9
  32.5 0.0 copy-start.16
  32.6 5.9 %inverse_sums.1.inverse = f32[3,64,128]{2,1,0:T(8,128)S(1)} custom-call(s32[1]{0:T(128)} %bitcast.1.my, f32[64]{0:T(128)S(1)} %copy-done.14, f32[32]{0:T(128)S(1)} %copy-done.15, f32[24,128]{1,0:T(8,128)S(1)} %copy-done.18, f32[24,128]{1,0:T(8,128)S(1)} %copy-done.17), custom_call_target="tpu_custom_call" | custom-call | flops 20000000000 | bytes 40000000 | tf_op jit(solution)/shard_map/inverse_sums/pallas_call | solution.py:594
  38.4 0.0 all-to-all-done.edges
  38.4 0.0 copy-done.13
  38.4 0.7 interface.1
  39.1 18.6 %all_to_all.10.values_v = f32[32,4,128]{2,1,0:T(4,128)S(1)} all-to-all(f32[32,4,128]{2,1,0:T(4,128)S(1)} %interface.1), channel_id=1, replica_groups=mesh['depth'=8,'wave'=4] {'depth','wave'}, dimensions={0} | all-to-all | bytes 131072 | tf_op jit(solution)/shard_map/all_to_all | solution.py:770
  57.6 0.0 collective-permute-done.1.refs_0_
  57.6 0.0 collective-permute-done.2.refs_1_
  57.7 0.0 collective-permute-done.3.refs_2_
  57.7 0.0 slice-start
  57.7 0.0 copy-done.7
  57.7 0.0 copy-done.9
  57.7 0.0 copy-done.16
  57.7 0.0 slice-start.1
  57.7 0.0 slice-start.2
  57.7 0.0 copy-start
  57.7 0.0 copy-start.1
  57.7 0.0 copy-start.2
  57.8 0.0 copy-start.3
  57.8 0.0 copy-start.4
  57.8 0.0 copy-start.5
  57.8 0.0 copy-start.10
  57.8 0.0 copy-start.11
  57.8 0.0 copy-start.12
  57.8 0.5 join.1
  58.4 0.1 collective-permute-start.4
  58.5 1.9 %collective-permute-done.4.theirs = f32[2,2,2,16,1024]{4,3,2,1,0:T(8,128)S(1)} collective-permute-done((f32[2,2,2,16,1024]{4,3,2,1,0:T(8,128)S(1)}, f32[2,2,2,16,1024]{4,3,2,1,0:T(8,128)S(1)}, u32[]{:S(2)}, u32[]{:S(2)}) %collective-permute-start.4) | collective-permute-done | bytes 524320 | tf_op jit(solution)/shard_map/ppermute | solution.py:764
  60.4 0.0 slice-done
  60.4 0.8 %slice-done.1 = s8[4194304]{0:T(1024)(128)(4,1)S(1)} async-done(((s8[8519680]{0:T(1024)(128)(4,1)}), s8[4194304]{0:T(1024)(128)(4,1)S(1)}, s32[]{:S(2)}) %slice-start.1) | async-done | bytes 4194328
  61.1 0.0 slice-done.2
  61.1 1.2 %copy-done = f32[2,2,8,32,1024]{4,3,2,1,0:T(8,128)S(1)} copy-done((f32[2,2,8,32,1024]{4,3,2,1,0:T(8,128)S(1)}, f32[2,2,8,32,1024]{4,3,2,1,0:T(8,128)}, u32[]{:S(2)}) %copy-start) | copy-done | bytes 4194328
  62.4 0.2 copy-done.1
  62.6 0.1 copy-done.2
  62.7 0.2 copy-done.3
  62.8 0.2 copy-done.4
  63.0 0.2 copy-done.5
  63.2 0.1 copy-done.10
  63.3 0.0 copy-done.11
  63.3 0.0 copy-done.12
  63.3 12.7 %back.1 = (f32[2,8,32,1024]{3,2,1,0:T(8,128)}, f32[2,8,32,1024]{3,2,1,0:T(8,128)}) custom-call(s32[1]{0:T(128)} %bitcast.place, f32[64]{0:T(128)S(1)} %copy-done.14, f32[32,4,128]{2,1,0:T(4,128)S(1)} %all_to_all.10.values_v, bf16[128,256]{1,0:T(8,128)(2,1)S(1)} %copy-done.12, f32[65,32,1024]{2,1,0:T(8,128)S(1)} %bitcast.3, ...), custom_call_target="tpu_custom_call" | custom-call | tf_op jit(solution)/shard_map/back/pallas_call | solution.py:735
  (1 shorter events, 0.0 us)
Async XLA Ops:
  0.6 31.9 %copy-start.14 = (f32[64]{0:T(128)S(1)}, f32[64]{0:T(128)}, u32[]{:S(2)}) copy-start(f32[64]{0:T(128)} %thick.5) | copy-start | bytes 772
  0.6 31.9 %copy-start.15 = (f32[32]{0:T(128)S(1)}, f32[32]{0:T(128)}, u32[]{:S(2)}) copy-start(f32[32]{0:T(128)} %shifts.3) | copy-start | bytes 388
  0.7 31.8 %copy-start.17 = (f32[24,128]{1,0:T(8,128)S(1)}, f32[24,128]{1,0:T(8,128)}, u32[]{:S(2)}) copy-start(f32[24,128]{1,0:T(8,128)} %constant.49.clone.weights) | copy-start | bytes 36868
  0.7 31.8 %copy-start.18 = (f32[24,128]{1,0:T(8,128)S(1)}, f32[24,128]{1,0:T(8,128)}, u32[]{:S(2)}) copy-start(f32[24,128]{1,0:T(8,128)} %constant.48.clone.across) | copy-start | bytes 36868
  15.6 8.2 %collective-permute-start = (f32[2,2,2,16,1024]{4,3,2,1,0:T(8,128)}, f32[2,2,2,16,1024]{4,3,2,1,0:T(8,128)S(1)}, u32[]{:S(2)}, u32[]{:S(2)}) collective-permute-start(f32[2,2,2,16,1024]{4,3,2,1,0:T(8,128)} %get-tuple-element.22), channel_id=1, source_target_pairs={{0,4},{4,0},{8,12},{12,8},{16,20},{20,16},{24,28},{28,24},{1,5},{5... | collective-permute-start | bytes 1572872 | tf_op jit(solution)/shard_map/ppermute | solution.py:764
  16.2 22.2 %all-to-all-start = ((f32[32,4,128]{2,1,0:T(4,128)}), f32[32,4,128]{2,1,0:T(4,128)S(1)}, u32[]{:S(2)}, u32[]{:S(2)}) async-start(f32[32,4,128]{2,1,0:T(4,128)} %get-tuple-element.19), calls=%async_computation | async-start | bytes 131072 | tf_op jit(solution)/shard_map/all_to_all | solution.py:770
  23.9 1.0 %copy-start.6 = (f32[4,32,1024]{2,1,0:T(8,128)S(1)}, f32[4,32,1024]{2,1,0:T(8,128)}, u32[]{:S(2)}) copy-start(f32[4,32,1024]{2,1,0:T(8,128)} %get-tuple-element.23.pair) | copy-start | bytes 1572868
  24.9 1.0 %copy-start.8 = (f32[2,2,2,16,1024]{4,3,2,1,0:T(8,128)S(1)}, f32[2,2,2,16,1024]{4,3,2,1,0:T(8,128)}, u32[]{:S(2)}) copy-start(f32[2,2,2,16,1024]{4,3,2,1,0:T(8,128)} %get-tuple-element.21.keep) | copy-start | bytes 1572868
  26.8 30.8 %collective-permute-start.1 = (f32[2,2,16,1024]{3,2,1,0:T(8,128)}, f32[2,2,16,1024]{3,2,1,0:T(8,128)S(1)}, u32[]{:S(2)}, u32[]{:S(2)}) collective-permute-start(f32[2,2,16,1024]{3,2,1,0:T(8,128)} %get-tuple-element.25), channel_id=1, source_target_pairs={{0,8},{4,12},{8,16},{12,20},{16,24},{20,28},{24,0},{28,4},{1,9},{5... | collective-permute-start | bytes 786440 | tf_op jit(solution)/shard_map/ppermute | solution.py:767
  28.7 29.0 %collective-permute-start.2 = (f32[2,2,16,1024]{3,2,1,0:T(8,128)S(1)}, f32[2,2,16,1024]{3,2,1,0:T(8,128)S(1)}, u32[]{:S(2)}, u32[]{:S(2)}) collective-permute-start(f32[2,2,16,1024]{3,2,1,0:T(8,128)S(1)} %get-tuple-element.26), channel_id=1, source_target_pairs={{0,16},{4,20},{8,24},{12,28},{16,0},{20,4},{24,8},{28,12},{1,17},{... | collective-permute-start | bytes 786440 | tf_op jit(solution)/shard_map/ppermute | solution.py:767
  31.1 26.5 %collective-permute-start.3 = (f32[2,2,16,1024]{3,2,1,0:T(8,128)S(1)}, f32[2,2,16,1024]{3,2,1,0:T(8,128)S(1)}, u32[]{:S(2)}, u32[]{:S(2)}) collective-permute-start(f32[2,2,16,1024]{3,2,1,0:T(8,128)S(1)} %get-tuple-element.27), channel_id=1, source_target_pairs={{0,24},{4,28},{8,0},{12,4},{16,8},{20,12},{24,16},{28,20},{1,25},{... | collective-permute-start | bytes 786440 | tf_op jit(solution)/shard_map/ppermute | solution.py:767
  32.5 5.9 %copy-start.13 = (f32[96,32]{1,0:T(8,128)S(1)}, f32[96,32]{1,0:T(8,128)}, u32[]{:S(2)}) copy-start(f32[96,32]{1,0:T(8,128)} %constant.50.clone.matrices) | copy-start | bytes 36868
  32.5 25.2 %copy-start.7 = (f32[4,32,1024]{2,1,0:T(8,128)S(1)}, f32[4,32,1024]{2,1,0:T(8,128)}, u32[]{:S(2)}) copy-start(f32[4,32,1024]{2,1,0:T(8,128)} %get-tuple-element.23.pair) | copy-start | bytes 1572868
  32.5 25.1 %copy-start.9 = (f32[2,2,2,16,1024]{4,3,2,1,0:T(8,128)S(1)}, f32[2,2,2,16,1024]{4,3,2,1,0:T(8,128)}, u32[]{:S(2)}) copy-start(f32[2,2,2,16,1024]{4,3,2,1,0:T(8,128)} %get-tuple-element.21.keep) | copy-start | bytes 1572868
  32.5 25.1 %copy-start.16 = (f32[3,32,1024]{2,1,0:T(8,128)S(1)}, f32[3,32,1024]{2,1,0:T(8,128)}, u32[]{:S(2)}) copy-start(f32[3,32,1024]{2,1,0:T(8,128)} %get-tuple-element.24.far) | copy-start | bytes 1179652
  57.7 2.7 %slice-start = ((s8[8519680]{0:T(1024)(128)(4,1)}), s8[4194304]{0:T(1024)(128)(4,1)S(1)}, s32[]{:S(2)}) async-start(s8[8519680]{0:T(1024)(128)(4,1)} %bitcast.2), calls=%async_computation.2 | async-start | bytes 8388608
  57.7 3.4 %slice-start.1 = ((s8[8519680]{0:T(1024)(128)(4,1)}), s8[4194304]{0:T(1024)(128)(4,1)S(1)}, s32[]{:S(2)}) async-start(s8[8519680]{0:T(1024)(128)(4,1)} %bitcast.2), calls=%async_computation.3 | async-start | bytes 8388608
  57.7 3.4 %slice-start.2 = ((s8[8519680]{0:T(1024)(128)(4,1)}), s8[131072]{0:T(1024)(128)(4,1)S(1)}, s32[]{:S(2)}) async-start(s8[8519680]{0:T(1024)(128)(4,1)} %bitcast.2), calls=%async_computation.4 | async-start | bytes 262144
  57.7 4.7 %copy-start = (f32[2,2,8,32,1024]{4,3,2,1,0:T(8,128)S(1)}, f32[2,2,8,32,1024]{4,3,2,1,0:T(8,128)}, u32[]{:S(2)}) copy-start(f32[2,2,8,32,1024]{4,3,2,1,0:T(8,128)} %get-tuple-element.33.b_v) | copy-start | bytes 12582916
  57.7 4.9 %copy-start.1 = (f32[8,32,1024]{2,1,0:T(8,128)S(1)}, f32[8,32,1024]{2,1,0:T(8,128)}, u32[]{:S(2)}) copy-start(f32[8,32,1024]{2,1,0:T(8,128)} %get-tuple-element.34.m_v) | copy-start | bytes 3145732
  57.7 5.0 %copy-start.2 = (bf16[512,512]{1,0:T(8,128)(2,1)S(1)}, bf16[512,512]{1,0:T(8,128)(2,1)}, u32[]{:S(2)}) copy-start(bf16[512,512]{1,0:T(8,128)(2,1)} %constant.55.clone.er) | copy-start | bytes 1572868
  57.8 5.1 %copy-start.3 = (bf16[512,512]{1,0:T(8,128)(2,1)S(1)}, bf16[512,512]{1,0:T(8,128)(2,1)}, u32[]{:S(2)}) copy-start(bf16[512,512]{1,0:T(8,128)(2,1)} %constant.54.clone.et) | copy-start | bytes 1572868
  57.8 5.2 %copy-start.4 = (bf16[512,512]{1,0:T(8,128)(2,1)S(1)}, bf16[512,512]{1,0:T(8,128)(2,1)}, u32[]{:S(2)}) copy-start(bf16[512,512]{1,0:T(8,128)(2,1)} %constant.53.clone.orest) | copy-start | bytes 1572868
  57.8 5.4 %copy-start.5 = (bf16[512,512]{1,0:T(8,128)(2,1)S(1)}, bf16[512,512]{1,0:T(8,128)(2,1)}, u32[]{:S(2)}) copy-start(bf16[512,512]{1,0:T(8,128)(2,1)} %constant.52.clone.ot) | copy-start | bytes 1572868
  57.8 5.5 %copy-start.10 = (f32[3,32,1024]{2,1,0:T(8,128)S(1)}, f32[3,32,1024]{2,1,0:T(8,128)}, u32[]{:S(2)}) copy-start(f32[3,32,1024]{2,1,0:T(8,128)} %get-tuple-element.35.end_v) | copy-start | bytes 1179652
  57.8 5.5 %copy-start.11 = (f32[8,1024]{1,0:T(8,128)S(1)}, f32[8,1024]{1,0:T(8,128)}, u32[]{:S(2)}) copy-start(f32[8,1024]{1,0:T(8,128)} %constant.42.clone.sines.sines_v) | copy-start | bytes 98308
  57.8 5.4 %copy-start.12 = (bf16[128,256]{1,0:T(8,128)(2,1)S(1)}, bf16[128,256]{1,0:T(8,128)(2,1)}, u32[]{:S(2)}) copy-start(bf16[128,256]{1,0:T(8,128)(2,1)} %constant.51.clone.spread_v) | copy-start | bytes 196612
  58.4 2.0 %collective-permute-start.4 = (f32[2,2,2,16,1024]{4,3,2,1,0:T(8,128)S(1)}, f32[2,2,2,16,1024]{4,3,2,1,0:T(8,128)S(1)}, u32[]{:S(2)}, u32[]{:S(2)}) collective-permute-start(f32[2,2,2,16,1024]{4,3,2,1,0:T(8,128)S(1)} %get-tuple-element.32), channel_id=1, source_target_pairs={{0,4},{4,0},{8,12},{12,8},{16,20},{20,16},{24,28},{28,24},{1,5},{5... | collective-permute-start | bytes 1572872 | tf_op jit(solution)/shard_map/ppermute | solution.py:764

commit v10 on v9

--- a/solution.py
+++ b/solution.py
@@ -22,7 +22,7 @@
 in_vmem = pl.BlockSpec(memory_space=pltpu.VMEM)
 params = pltpu.CompilerParams(vmem_limit_bytes=VMEM_BYTES)
 small = pltpu.CompilerParams(vmem_limit_bytes=12 * 1024 * 1024)
-medium = pltpu.CompilerParams(vmem_limit_bytes=30 * 1024 * 1024)
+medium = pltpu.CompilerParams(vmem_limit_bytes=46 * 1024 * 1024)
 brief = pl.CostEstimate(flops=1, bytes_accessed=1, transcendentals=0)
 lengthy = pl.CostEstimate(flops=20_000_000_000, bytes_accessed=40_000_000, transcendentals=0)
 
@@ -238,7 +238,7 @@
     return tiles[0]
 
 
-def front_kernel(levels, total, group, place, thick, shifts, across, sines, edge_mix, x0, x1, odd_top, odd_rest, even_top, even_rest, t_out, m_out, end_out, pair_out, far_out, b_out, keep_out, give_out, edge_out, sems, *scratch):
+def front_kernel(levels, total, group, place, thick, shifts, across, sines, edge_mix, x0, x1, odd_top, odd_rest, even_top, even_rest, t_out, m_out, end_out, b_out, local_out, give_out, edge_out, sems, *scratch):
     across_v, sines_v, mix_v, x, ot, orest, et, er, t, m, end, pair, far, b, c_all, z_all, sums, edges, faces, lam, *work = scratch
     _, _, _, ky, size = x.shape
     first = place[0] * levels
@@ -254,13 +254,15 @@
     for copy in early:
         copy.wait()
     coefficients(levels, total, group, place, thick, faces, shifts, across_v, t, m, end, pair, far, lam, *work)
-    outs = [copies.start(source, target) for source, target in ((pair, pair_out), (far, far_out))]
-    outs += [copies.start(source, target) for source, target in ((t, t_out), (m, m_out), (end, end_out))]
+    outs = [copies.start(source, target) for source, target in ((t, t_out), (m, m_out), (end, end_out))]
     for copy in mats:
         copy.wait()
     lane = lax.broadcasted_iota(jnp.int32, (ROWS, LANES), 1)
     spot = jnp.where(lane == 0, size / 4.0, 0.0)
     core = place[0] % 2
+    mine, other = (pl.ds(pl.multiple_of(start * (ky // 2), ROWS), ky // 2) for start in (core, 1 - core))
+    outs.append(copies.start(pair.at[:, mine], local_out.at[pl.ds(8, 4)]))
+    outs.append(copies.start(far.at[:, mine], local_out.at[pl.ds(12, far.shape[0])]))
 
     def put(f, j, here, values, height, own=None):
         odd, even = lane_sum(values[:, :half]) * height, lane_sum(values[:, half:]) * height
@@ -290,7 +292,7 @@
                 for j in range(1, levels):
                     y = b[a, ri, j, here] + m[j, here] * y
                     ys.append(y)
-                c_all[a, 0, ri, here] = y
+                c_all[a, ri, here] = y
                 value = y * end[1, here]
                 z_all[1, f, here] = value * wave
                 for j in range(levels - 1, -1, -1):
@@ -300,13 +302,12 @@
                     own = jnp.broadcast_to(x[a, ri, j, here, 0:1], (ROWS, LANES)) * (spot * height if a == 0 else spot)
                     put(f, first + j, here, value * wave, height, own)
                 z_all[0, f, here] = value * wave
-                c_all[a, 1, ri, here] = value * end[2, here]
+                c_all[a, 2 + ri, here] = value * end[2, here]
                 return 0
 
             lax.fori_loop(0, ky // ROWS, tile, 0)
-        for start, out in ((core, keep_out), (1 - core, give_out)):
-            here = pl.ds(pl.multiple_of(start * (ky // 2), ROWS), ky // 2)
-            outs.append(copies.start(c_all.at[a, :, :, here], out.at[a]))
+        outs.append(copies.start(c_all.at[a, :, mine], local_out.at[pl.ds(4 * a, 4)]))
+        outs.append(copies.start(c_all.at[a, :, other], give_out.at[a]))
 
     def reach(g, _):
         here = pl.ds(pl.multiple_of(g * ROWS, ROWS), ROWS)
@@ -362,7 +363,7 @@
     wide = 2 * total
     single = lambda *shape: pltpu.VMEM(shape, jnp.float32)
     tables = [(n, ky, size) for n in (total + 1, levels, 3, 4, chips - 1)]
-    shapes = tables + [(2, 2, levels, ky, size), (2, 2, 2, ky // 2, size), (2, 2, 2, ky // 2, size), (devices, 4, wide)]
+    shapes = tables[:3] + [(2, 2, levels, ky, size), (11 + chips, ky // 2, size), (2, 4, ky // 2, size), (devices, 4, wide)]
     return pl.pallas_call(
         functools.partial(front_kernel, levels, total, group),
         in_specs=[in_smem] * 3 + [in_hbm] * 9,
@@ -377,7 +378,7 @@
             *[pltpu.VMEM((half, half), jnp.bfloat16)] * 4,
             *[single(*shape) for shape in tables],
             single(2, 2, levels, ky, size),
-            single(2, 2, 2, ky, size),
+            single(2, 4, ky, size),
             single(2, 4, ky, size),
             single(4, 2, total, ky, LANES),
             single(devices, 4, wide),
@@ -391,23 +392,20 @@
     )(place, thick, shifts, across, sines, edge_matrix(size, total), rhs, cotangent, *half_sines(size))
 
 
-def chip_kernel(chips, place, keep, got_v, pair, *refs):
+def chip_kernel(chips, place, local, got, *refs):
     outs = refs[:chips - 1]
-    sems, keep_v, pair_v, down_v, up_v = refs[chips - 1:]
-    copies = Copies(sems)
+    sems, down_v, up_v = refs[chips - 1:]
     chip = place[0] // 2
     upper = place[0] % 2 == 0
-    half = keep_v.shape[3]
-    here = pl.ds(pl.multiple_of((place[0] % 2) * half, ROWS), half)
-    for copy in [copies.start(keep, keep_v), copies.start(pair.at[:, here], pair_v)]:
-        copy.wait()
     for a in range(2):
-        first, second = jnp.where(upper, keep_v[a], got_v[a]), jnp.where(upper, got_v[a], keep_v[a])
-        down_v[a] = second[0] + pair_v[1] * first[0]
-        up_v[a] = first[1] + pair_v[2] * second[1]
+        for ri in range(2):
+            sums = [(local[4 * a + 2 * way + ri], got[a, 2 * way + ri]) for way in range(2)]
+            first, second = ([jnp.where(upper, *one[::turn]) for one in sums] for turn in (1, -1))
+            down_v[2 * a + ri] = second[0] + local[9] * first[0]
+            up_v[2 * a + ri] = first[1] + local[10] * second[1]
     for apart in range(1, chips):
         goes_down = chip + apart < chips
-        sem = sems.at[1 + apart]
+        sem = sems.at[apart - 1]
 
         @pl.when(goes_down)
         def _():
@@ -418,84 +416,63 @@
             pltpu.make_async_copy(up_v, outs[apart - 1], sem).start()
 
     for apart in range(1, chips):
-        pltpu.make_async_copy(down_v, outs[apart - 1], sems.at[1 + apart]).wait()
-
-
-def chip_sums(place, keep, got, pair, chips):
-    _, _, _, half, size = keep.shape
-    single = lambda *shape: pltpu.VMEM(shape, jnp.float32)
-    shape = (2, 2, half, size)
+        pltpu.make_async_copy(down_v, outs[apart - 1], sems.at[apart - 1]).wait()
+
+
+def chip_sums(place, local, got, chips):
+    _, half, size = local.shape
+    shape = (4, half, size)
     return pl.pallas_call(
         functools.partial(chip_kernel, chips),
-        in_specs=[in_smem, in_hbm, in_vmem, in_hbm],
+        in_specs=[in_smem] + [in_vmem] * 2,
         out_specs=[in_hbm] * (chips - 1),
         out_shape=[jax.ShapeDtypeStruct(shape, jnp.float32)] * (chips - 1),
         scratch_shapes=[
-            pltpu.SemaphoreType.DMA((1 + chips,)),
-            single(*keep.shape),
-            single(4, half, size),
-            single(*shape),
-            single(*shape),
+            pltpu.SemaphoreType.DMA((chips - 1,)),
+            pltpu.VMEM(shape, jnp.float32),
+            pltpu.VMEM(shape, jnp.float32),
         ],
         compiler_params=small,
         cost_estimate=brief,
         name="chip_sums",
-    )(place, keep, got, pair)
-
-
-def join_kernel(chips, place, keep, got, pair, far, *refs):
+    )(place, local, got)
+
+
+def join_kernel(chips, place, local, got, *refs):
     news = refs[:chips - 1]
-    mine, theirs, sems, keep_v, got_v, pair_v, far_v, mine_v, theirs_v = refs[chips - 1:]
-    copies = Copies(sems)
+    mine, theirs = refs[chips - 1:]
     chip = place[0] // 2
     upper = place[0] % 2 == 0
-    half = keep_v.shape[3]
-    here = pl.ds(pl.multiple_of((place[0] % 2) * half, ROWS), half)
-    ready = [copies.start(keep, keep_v), copies.start(got, got_v), copies.start(pair.at[:, here], pair_v), copies.start(far.at[:, here], far_v)]
-    for copy in ready:
-        copy.wait()
     for a in range(2):
         for ri in range(2):
-            first, second = (keep_v, got_v), (got_v, keep_v)
-            pick = lambda refs, way: jnp.where(upper, refs[0][a, way, ri], refs[1][a, way, ri])
-            down = jnp.zeros((half, keep_v.shape[4]), jnp.float32)
+            sums = [(local[4 * a + 2 * way + ri], got[a, 2 * way + ri]) for way in range(2)]
+            first, second = ([jnp.where(upper, *one[::turn]) for one in sums] for turn in (1, -1))
+            down = jnp.zeros(local.shape[1:], jnp.float32)
             up = down
             for apart in range(1, chips):
-                term = far_v[apart - 1] * news[apart - 1][a, ri]
+                term = local[11 + apart] * news[apart - 1][2 * a + ri]
                 down = down + jnp.where(chip >= apart, term, 0.0)
                 up = up + jnp.where(chip >= apart, 0.0, term)
-            inner_up = pick(second, 1) + pair_v[3] * up
-            inner_down = pick(first, 0) + pair_v[0] * down
-            mine_v[a, 0, ri] = jnp.where(upper, down, inner_down)
-            mine_v[a, 1, ri] = jnp.where(upper, inner_up, up)
-            theirs_v[a, 0, ri] = jnp.where(upper, inner_down, down)
-            theirs_v[a, 1, ri] = jnp.where(upper, up, inner_up)
-    for copy in [copies.start(theirs_v, theirs), copies.start(mine_v, mine)]:
-        copy.wait()
-
-
-def join(place, keep, got, pair, far, news):
+            inner_up = second[1] + local[11] * up
+            inner_down = first[0] + local[8] * down
+            mine[a, 0, ri] = jnp.where(upper, down, inner_down)
+            mine[a, 1, ri] = jnp.where(upper, inner_up, up)
+            theirs[a, 0, ri] = jnp.where(upper, inner_down, down)
+            theirs[a, 1, ri] = jnp.where(upper, up, inner_up)
+
+
+def join(place, local, got, news):
     chips = len(news) + 1
-    _, _, _, half, size = keep.shape
-    single = lambda *shape: pltpu.VMEM(shape, jnp.float32)
+    _, half, size = local.shape
     return pl.pallas_call(
         functools.partial(join_kernel, chips),
-        in_specs=[in_smem] + [in_hbm] * 4 + [in_vmem] * (chips - 1),
-        out_specs=[in_hbm] * 2,
-        out_shape=[jax.ShapeDtypeStruct(keep.shape, jnp.float32)] * 2,
-        scratch_shapes=[
-            pltpu.SemaphoreType.DMA((6,)),
-            single(*keep.shape),
-            single(*keep.shape),
-            single(4, half, size),
-            single(chips - 1, half, size),
-            single(*keep.shape),
-            single(*keep.shape),
-        ],
+        in_specs=[in_smem] + [in_vmem] * (1 + chips),
+        out_specs=[in_vmem] * 2,
+        out_shape=[jax.ShapeDtypeStruct((2, 2, 2, half, size), jnp.float32)] * 2,
         compiler_params=small,
         cost_estimate=lengthy,
         name="join",
-    )(place, keep, got, pair, far, *news)
+    )(place, local, got, *news)
 
 
 def inverse_kernel(counts, my, thick, shifts, across, weights, out, faces, m_all, f_all, g_all):
@@ -637,13 +614,15 @@
     )(interface_matrices(waves, size), edges, inverse)
 
 
-def back_kernel(levels, total, place, thick, values_v, spread_v, t_v, mine, theirs, sines_v, b_v, m_v, end_v, ot, orest, et, er, out0, out1, sems, ends, picked, u_all, q_all, out_v):
+def back_kernel(levels, total, place, thick, values_v, spread_v, t, mine, theirs, sines_v, b, m_v, end_v, ot, orest, et, er, out0, out1, sems, t_v, b_v, ends, picked, u_all, q_all, out_v):
     _, _, _, ky, size = b_v.shape
     first = place[0] * levels
     half = size // 2
     many = half // LANES
     core = place[0] % 2
     copies = Copies(sems)
+    table = copies.start(t, t_v)
+    fields = [copies.start(b.at[a], b_v.at[a]) for a in range(2)]
     here, there = (pl.ds(pl.multiple_of(start * (ky // 2), ROWS), ky // 2) for start in (core, 1 - core))
     lane = lax.broadcasted_iota(jnp.int32, (ky, 2 * total), 1)
     for f in range(4):
@@ -653,6 +632,7 @@
             for p in range(2):
                 picked[p, j * ky:(j + 1) * ky, :] = jnp.where(spot, parts[p], 0.0).astype(jnp.bfloat16)
         u_all[f] = (real_dot(picked[0], spread_v[...]) + real_dot(picked[1], spread_v[...])).reshape(total, ky, 2 * LANES)
+    table.wait()
     ends[:, :, :, here] = mine[...]
     ends[:, :, :, there] = theirs[...]
 
@@ -692,6 +672,8 @@
     lane = lax.broadcasted_iota(jnp.int32, (ky, LANES), 1)
     outs = []
     for a in range(2):
+        fields[a].wait()
+
         def tile(g, _):
             here = pl.ds(pl.multiple_of(g * ROWS, ROWS), ROWS)
             wave = sines_v[...]
@@ -734,11 +716,13 @@
     single = lambda *shape: pltpu.VMEM(shape, jnp.float32)
     return pl.pallas_call(
         functools.partial(back_kernel, levels, total),
-        in_specs=[in_smem] * 2 + [in_vmem] * 13,
+        in_specs=[in_smem] * 2 + [in_vmem] * 2 + [in_hbm] + [in_vmem] * 3 + [in_hbm] + [in_vmem] * 6,
         out_specs=[in_hbm] * 2,
         out_shape=[jax.ShapeDtypeStruct((2, levels, ky, size), jnp.float32)] * 2,
         scratch_shapes=[
-            pltpu.SemaphoreType.DMA((4,)),
+            pltpu.SemaphoreType.DMA((7,)),
+            single(*t.shape),
+            single(*b.shape),
             single(2, 2, 2, ky, size),
             pltpu.VMEM((2, total * ky, 2 * total), jnp.bfloat16),
             single(4, total, ky, 2 * LANES),
@@ -772,20 +756,20 @@
     order = wave_order(size)
     sines = np.broadcast_to(np.sin(np.pi * order / size)[None, :], (ROWS, size)).astype(np.float32)
     across_k = horizontal(order, 2 * size)[None, :]
-    t, m, end, pair, far, b, keep, give, edges = front(
+    t, m, end, b, local, give, edges = front(
         place, thickness, ky_shift, across_k, sines, rhs, cotangent, devices
     )
 
     my = (depth_pos * waves + wave_pos).astype(jnp.int32).reshape(1)
     got = across(give)
     edges = everywhere(edges)
-    sums = chip_sums(place, keep, got, pair, chips)
+    sums = chip_sums(place, local, got, chips)
     news = [along(sums[apart - 1], apart) for apart in range(1, chips)]
     inverse = inverse_sums(my, thickness, ky_shift, waves, size)
     values = interface(edges, inverse, waves, size)
     values = everywhere(values)
     news, _ = lax.optimization_barrier((news, values))
-    mine, theirs = join(place, keep, got, pair, far, news)
+    mine, theirs = join(place, local, got, news)
     return back(place, thickness, values, sines, t, m, end, b, mine, across(theirs))
 
 

time: 76.4 us -> 72 us (0.942)
  local copies, waits for them, and re-layouts: 5.07 us -> 1.27 us
    unnamed x44 -> x30, local copies, waits for them, and re-layouts: 5.07 us -> 1.27 us
  transfers between devices with their start and end apart: 6 -> 6, of which waited for: 1 -> 1; matrix products, arithmetic and copies ran while one was open for 0% -> 0% of each run, Pallas kernels for 10% -> 9%
where the time goes in v10:
time: 72 us; the launch traced here: 71.8 us
  Pallas kernels  35.2 us (49%)
  blocking collectives  18.4 us (26%)
  starting transfers between devices  13.9 us (19%)
  waiting for transfers between devices  1.91 us (3%)
  local copies, waits for them, and re-layouts  1.27 us (2%)
  between operations  1.04 us (1%)
    all_to_all x1, blocking collectives, everywhere(): lax.all_to_all(a, ('depth', 'wave'), split_axis=0, concat_axis=0, tiled=T...  18.4 us
    pallas_call x1, Pallas kernels, front(): pl.pallas_call(functools.partial(front_kernel, levels, total, group), in_...  14.9 us
    pallas_call x1, Pallas kernels, back(): pl.pallas_call(functools.partial(back_kernel, levels, total), in_specs=[i...  13.4 us
    all_to_all x1, starting transfers between devices, everywhere(): lax.all_to_all(a, ('depth', 'wave'), split_axis=0, concat_axis=0, tiled=T...  7.6 us
    pallas_call x1, Pallas kernels, inverse_sums(): pl.pallas_call(functools.partial(inverse_kernel, counts), in_specs=[in_sm...  5.86 us
    ppermute x3, starting transfers between devices, along(): lax.ppermute(a, 'depth', [(d, (d + 2 * apart) % count) for d in range(cou...  5.65 us
    ppermute x2, waiting for transfers between devices, across(): return lax.ppermute(a, 'depth', [(d, d ^ 1) for d in range(count)])  1.9 us
  transfers between devices with their start and end apart: 6, of which 1 were waited for; matrix products, arithmetic and copies ran while one was open for 0% of the time, Pallas kernels for 9%

profile of v10, /device:TPU:0, one launch (start us, length us, event | category | flops | bytes accessed | tf_op | source)
XLA Modules:
  0.0 71.8 jit_solution(15099291402643738143)
XLA Ops:
  0.6 0.0 copy-start.11
  0.6 0.0 copy-start.12
  0.7 0.0 copy-start.13
  0.7 0.0 copy-start.14
  0.7 14.9 %front.1 = (f32[65,32,1024]{2,1,0:T(8,128)}, f32[8,32,1024]{2,1,0:T(8,128)}, f32[3,32,1024]{2,1,0:T(8,128)}, f32[2,2,8,32,1024]{4,3,2,1,0:T(8,128)}, f32[15,16,1...) custom-call(s32[1]{0:T(128)} %bitcast.place, f32[64]{0:T(128)} %thick.5, f32[32]{0:T(128)} %shifts.3, ...), custom_call_target="tpu_custom_call" | custom-call | tf_op jit(solution)/shard_map/front/pallas_call | solution.py:367
  15.6 0.6 collective-permute-start
  16.2 7.6 %all-to-all-start = ((f32[32,4,128]{2,1,0:T(4,128)}), f32[32,4,128]{2,1,0:T(4,128)S(1)}, u32[]{:S(2)}, u32[]{:S(2)}) async-start(f32[32,4,128]{2,1,0:T(4,128)} %get-tuple-element.17), calls=%async_computation | async-start | bytes 131072 | tf_op jit(solution)/shard_map/all_to_all | solution.py:754
  23.8 0.0 collective-permute-done.got
  23.9 0.0 copy-start.1
  23.9 1.2 %copy-done.1 = f32[15,16,1024]{2,1,0:T(8,128)S(1)} copy-done((f32[15,16,1024]{2,1,0:T(8,128)S(1)}, f32[15,16,1024]{2,1,0:T(8,128)}, u32[]{:S(2)}) %copy-start.1) | copy-done | bytes 983064
  25.1 0.2 chip_sums.1
  25.2 1.8 %collective-permute-start.1 = (f32[4,16,1024]{2,1,0:T(8,128)S(1)}, f32[4,16,1024]{2,1,0:T(8,128)S(1)}, u32[]{:S(2)}, u32[]{:S(2)}) collective-permute-start(f32[4,16,1024]{2,1,0:T(8,128)S(1)} %get-tuple-element.21), channel_id=1, source_target_pairs={{0,8},{4,12},{8,16},{12,20},{16,24},{20,28},{24,0},{28,4},{1,9},{5... | collective-permute-start | bytes 786440 | tf_op jit(solution)/shard_map/ppermute | solution.py:751
  27.1 2.4 %collective-permute-start.2 = (f32[4,16,1024]{2,1,0:T(8,128)S(1)}, f32[4,16,1024]{2,1,0:T(8,128)S(1)}, u32[]{:S(2)}, u32[]{:S(2)}) collective-permute-start(f32[4,16,1024]{2,1,0:T(8,128)S(1)} %get-tuple-element.22), channel_id=1, source_target_pairs={{0,16},{4,20},{8,24},{12,28},{16,0},{20,4},{24,8},{28,12},{1,17},{... | collective-permute-start | bytes 786440 | tf_op jit(solution)/shard_map/ppermute | solution.py:751
  29.5 1.4 %collective-permute-start.3 = (f32[4,16,1024]{2,1,0:T(8,128)S(1)}, f32[4,16,1024]{2,1,0:T(8,128)S(1)}, u32[]{:S(2)}, u32[]{:S(2)}) collective-permute-start(f32[4,16,1024]{2,1,0:T(8,128)S(1)} %get-tuple-element.23), channel_id=1, source_target_pairs={{0,24},{4,28},{8,0},{12,4},{16,8},{20,12},{24,16},{28,20},{1,25},{... | collective-permute-start | bytes 786440 | tf_op jit(solution)/shard_map/ppermute | solution.py:751
  30.9 0.0 copy-done.11
  30.9 0.0 copy-done.12
  30.9 0.0 copy-done.13
  30.9 0.0 copy-done.14
  30.9 0.0 copy-start.10
  30.9 0.0 copy-start.2
  30.9 5.9 %inverse_sums.1.inverse = f32[3,64,128]{2,1,0:T(8,128)S(1)} custom-call(s32[1]{0:T(128)} %bitcast.1.my, f32[64]{0:T(128)S(1)} %copy-done.11, f32[32]{0:T(128)S(1)} %copy-done.12, f32[24,128]{1,0:T(8,128)S(1)} %copy-done.14, f32[24,128]{1,0:T(8,128)S(1)} %copy-done.13), custom_call_target="tpu_custom_call" | custom-call | flops 20000000000 | bytes 40000000 | tf_op jit(solution)/shard_map/inverse_sums/pallas_call | solution.py:571
  36.8 0.0 all-to-all-done.edges
  36.8 0.0 copy-done.10
  36.8 0.7 interface.1
  37.5 18.4 %all_to_all.10.values_v = f32[32,4,128]{2,1,0:T(4,128)S(1)} all-to-all(f32[32,4,128]{2,1,0:T(4,128)S(1)} %interface.1), channel_id=1, replica_groups=mesh['depth'=8,'wave'=4] {'depth','wave'}, dimensions={0} | all-to-all | bytes 131072 | tf_op jit(solution)/shard_map/all_to_all | solution.py:754
  55.8 0.0 copy-start
  55.8 0.0 copy-start.3
  55.8 0.0 copy-start.4
  55.8 0.0 copy-start.5
  55.8 0.0 copy-start.6
  55.9 0.0 copy-start.7
  55.9 0.0 copy-start.8
  55.9 0.0 copy-start.9
  55.9 0.0 collective-permute-done.1.refs_0_
  55.9 0.0 collective-permute-done.2.refs_1_
  55.9 0.0 collective-permute-done.3.refs_2_
  55.9 0.0 copy-done.2
  55.9 0.3 join.1
  56.2 0.1 collective-permute-start.4
  56.3 1.9 %collective-permute-done.4.theirs = f32[2,2,2,16,1024]{4,3,2,1,0:T(8,128)S(1)} collective-permute-done((f32[2,2,2,16,1024]{4,3,2,1,0:T(8,128)S(1)}, f32[2,2,2,16,1024]{4,3,2,1,0:T(8,128)S(1)}, u32[]{:S(2)}, u32[]{:S(2)}) %collective-permute-start.4) | collective-permute-done | bytes 524320 | tf_op jit(solution)/shard_map/ppermute | solution.py:748
  58.2 0.0 copy-done
  58.2 0.0 copy-done.3
  58.2 0.0 copy-done.4
  58.2 0.0 copy-done.5
  58.2 0.0 copy-done.6
  58.2 0.0 copy-done.7
  58.2 0.0 copy-done.8
  58.2 0.0 copy-done.9
  58.2 13.4 %back.1 = (f32[2,8,32,1024]{3,2,1,0:T(8,128)}, f32[2,8,32,1024]{3,2,1,0:T(8,128)}) custom-call(s32[1]{0:T(128)} %bitcast.place, f32[64]{0:T(128)S(1)} %copy-done.11, f32[32,4,128]{2,1,0:T(4,128)S(1)} %all_to_all.10.values_v, bf16[128,256]{1,0:T(8,128)(2,1)S(1)} %copy-done.9, f32[65,32,1024]{2,1,0:T(8,128)} %get-tuple-element.18.t, ...), custom_call_target="tpu_custom_call" | custom-call | tf_op jit(solution)/shard_map/back/pallas_call | solution.py:717
Async XLA Ops:
  0.6 30.3 %copy-start.11 = (f32[64]{0:T(128)S(1)}, f32[64]{0:T(128)}, u32[]{:S(2)}) copy-start(f32[64]{0:T(128)} %thick.5) | copy-start | bytes 772
  0.6 30.3 %copy-start.12 = (f32[32]{0:T(128)S(1)}, f32[32]{0:T(128)}, u32[]{:S(2)}) copy-start(f32[32]{0:T(128)} %shifts.3) | copy-start | bytes 388
  0.7 30.2 %copy-start.13 = (f32[24,128]{1,0:T(8,128)S(1)}, f32[24,128]{1,0:T(8,128)}, u32[]{:S(2)}) copy-start(f32[24,128]{1,0:T(8,128)} %constant.49.clone.weights) | copy-start | bytes 36868
  0.7 30.2 %copy-start.14 = (f32[24,128]{1,0:T(8,128)S(1)}, f32[24,128]{1,0:T(8,128)}, u32[]{:S(2)}) copy-start(f32[24,128]{1,0:T(8,128)} %constant.48.clone.across) | copy-start | bytes 36868
  15.6 8.2 %collective-permute-start = (f32[2,4,16,1024]{3,2,1,0:T(8,128)}, f32[2,4,16,1024]{3,2,1,0:T(8,128)S(1)}, u32[]{:S(2)}, u32[]{:S(2)}) collective-permute-start(f32[2,4,16,1024]{3,2,1,0:T(8,128)} %get-tuple-element.20), channel_id=1, source_target_pairs={{0,4},{4,0},{8,12},{12,8},{16,20},{20,16},{24,28},{28,24},{1,5},{5... | collective-permute-start | bytes 1572872 | tf_op jit(solution)/shard_map/ppermute | solution.py:748
  16.2 20.6 %all-to-all-start = ((f32[32,4,128]{2,1,0:T(4,128)}), f32[32,4,128]{2,1,0:T(4,128)S(1)}, u32[]{:S(2)}, u32[]{:S(2)}) async-start(f32[32,4,128]{2,1,0:T(4,128)} %get-tuple-element.17), calls=%async_computation | async-start | bytes 131072 | tf_op jit(solution)/shard_map/all_to_all | solution.py:754
  23.9 1.2 %copy-start.1 = (f32[15,16,1024]{2,1,0:T(8,128)S(1)}, f32[15,16,1024]{2,1,0:T(8,128)}, u32[]{:S(2)}) copy-start(f32[15,16,1024]{2,1,0:T(8,128)} %get-tuple-element.19.local) | copy-start | bytes 2949124
  25.2 30.7 %collective-permute-start.1 = (f32[4,16,1024]{2,1,0:T(8,128)S(1)}, f32[4,16,1024]{2,1,0:T(8,128)S(1)}, u32[]{:S(2)}, u32[]{:S(2)}) collective-permute-start(f32[4,16,1024]{2,1,0:T(8,128)S(1)} %get-tuple-element.21), channel_id=1, source_target_pairs={{0,8},{4,12},{8,16},{12,20},{16,24},{20,28},{24,0},{28,4},{1,9},{5... | collective-permute-start | bytes 786440 | tf_op jit(solution)/shard_map/ppermute | solution.py:751
  27.1 28.8 %collective-permute-start.2 = (f32[4,16,1024]{2,1,0:T(8,128)S(1)}, f32[4,16,1024]{2,1,0:T(8,128)S(1)}, u32[]{:S(2)}, u32[]{:S(2)}) collective-permute-start(f32[4,16,1024]{2,1,0:T(8,128)S(1)} %get-tuple-element.22), channel_id=1, source_target_pairs={{0,16},{4,20},{8,24},{12,28},{16,0},{20,4},{24,8},{28,12},{1,17},{... | collective-permute-start | bytes 786440 | tf_op jit(solution)/shard_map/ppermute | solution.py:751
  29.5 26.4 %collective-permute-start.3 = (f32[4,16,1024]{2,1,0:T(8,128)S(1)}, f32[4,16,1024]{2,1,0:T(8,128)S(1)}, u32[]{:S(2)}, u32[]{:S(2)}) collective-permute-start(f32[4,16,1024]{2,1,0:T(8,128)S(1)} %get-tuple-element.23), channel_id=1, source_target_pairs={{0,24},{4,28},{8,0},{12,4},{16,8},{20,12},{24,16},{28,20},{1,25},{... | collective-permute-start | bytes 786440 | tf_op jit(solution)/shard_map/ppermute | solution.py:751
  30.9 5.9 %copy-start.10 = (f32[96,32]{1,0:T(8,128)S(1)}, f32[96,32]{1,0:T(8,128)}, u32[]{:S(2)}) copy-start(f32[96,32]{1,0:T(8,128)} %constant.50.clone.matrices) | copy-start | bytes 36868
  30.9 25.0 %copy-start.2 = (f32[15,16,1024]{2,1,0:T(8,128)S(1)}, f32[15,16,1024]{2,1,0:T(8,128)}, u32[]{:S(2)}) copy-start(f32[15,16,1024]{2,1,0:T(8,128)} %get-tuple-element.19.local) | copy-start | bytes 2949124
  55.8 2.3 %copy-start = (f32[8,32,1024]{2,1,0:T(8,128)S(1)}, f32[8,32,1024]{2,1,0:T(8,128)}, u32[]{:S(2)}) copy-start(f32[8,32,1024]{2,1,0:T(8,128)} %get-tuple-element.30.m_v) | copy-start | bytes 3145732
  55.8 2.3 %copy-start.3 = (bf16[512,512]{1,0:T(8,128)(2,1)S(1)}, bf16[512,512]{1,0:T(8,128)(2,1)}, u32[]{:S(2)}) copy-start(bf16[512,512]{1,0:T(8,128)(2,1)} %constant.55.clone.er) | copy-start | bytes 1572868
  55.8 2.3 %copy-start.4 = (bf16[512,512]{1,0:T(8,128)(2,1)S(1)}, bf16[512,512]{1,0:T(8,128)(2,1)}, u32[]{:S(2)}) copy-start(bf16[512,512]{1,0:T(8,128)(2,1)} %constant.54.clone.et) | copy-start | bytes 1572868
  55.8 2.3 %copy-start.5 = (bf16[512,512]{1,0:T(8,128)(2,1)S(1)}, bf16[512,512]{1,0:T(8,128)(2,1)}, u32[]{:S(2)}) copy-start(bf16[512,512]{1,0:T(8,128)(2,1)} %constant.53.clone.orest) | copy-start | bytes 1572868
  55.8 2.3 %copy-start.6 = (bf16[512,512]{1,0:T(8,128)(2,1)S(1)}, bf16[512,512]{1,0:T(8,128)(2,1)}, u32[]{:S(2)}) copy-start(bf16[512,512]{1,0:T(8,128)(2,1)} %constant.52.clone.ot) | copy-start | bytes 1572868
  55.9 2.3 %copy-start.7 = (f32[3,32,1024]{2,1,0:T(8,128)S(1)}, f32[3,32,1024]{2,1,0:T(8,128)}, u32[]{:S(2)}) copy-start(f32[3,32,1024]{2,1,0:T(8,128)} %get-tuple-element.31.end_v) | copy-start | bytes 1179652
  55.9 2.3 %copy-start.8 = (f32[8,1024]{1,0:T(8,128)S(1)}, f32[8,1024]{1,0:T(8,128)}, u32[]{:S(2)}) copy-start(f32[8,1024]{1,0:T(8,128)} %constant.42.clone.sines.sines_v) | copy-start | bytes 98308
  55.9 2.3 %copy-start.9 = (bf16[128,256]{1,0:T(8,128)(2,1)S(1)}, bf16[128,256]{1,0:T(8,128)(2,1)}, u32[]{:S(2)}) copy-start(bf16[128,256]{1,0:T(8,128)(2,1)} %constant.51.clone.spread_v) | copy-start | bytes 196612
  56.2 2.0 %collective-permute-start.4 = (f32[2,2,2,16,1024]{4,3,2,1,0:T(8,128)S(1)}, f32[2,2,2,16,1024]{4,3,2,1,0:T(8,128)S(1)}, u32[]{:S(2)}, u32[]{:S(2)}) collective-permute-start(f32[2,2,2,16,1024]{4,3,2,1,0:T(8,128)S(1)} %get-tuple-element.28), channel_id=1, source_target_pairs={{0,4},{4,0},{8,12},{12,8},{16,20},{20,16},{24,28},{28,24},{1,5},{5... | collective-permute-start | bytes 1572872 | tf_op jit(solution)/shard_map/ppermute | solution.py:748

commit v11 on v10

--- a/solution.py
+++ b/solution.py
@@ -438,6 +438,51 @@
     )(place, local, got)
 
 
+def pair_kernel(place, local, got, first_out, second_out):
+    even = (place[0] // 2) % 2 == 0
+    upper = place[0] % 2 == 0
+    for a in range(2):
+        for ri in range(2):
+            sums = [(local[4 * a + 2 * way + ri], got[a, 2 * way + ri]) for way in range(2)]
+            first, second = ([jnp.where(upper, *one[::turn]) for one in sums] for turn in (1, -1))
+            down = second[0] + local[9] * first[0]
+            up = first[1] + local[10] * second[1]
+            first_out[2 * a + ri] = jnp.where(even, down, up)
+            second_out[2 * a + ri] = jnp.where(even, up, down)
+
+
+def pair_sums(place, local, got):
+    shape = jax.ShapeDtypeStruct((4,) + local.shape[1:], jnp.float32)
+    return pl.pallas_call(
+        pair_kernel,
+        in_specs=[in_smem] + [in_vmem] * 2,
+        out_specs=[in_vmem] * 2,
+        out_shape=[shape] * 2,
+        compiler_params=small,
+        cost_estimate=brief,
+        name="pair_sums",
+    )(place, local, got)
+
+
+def grow_kernel(place, local, second, near, out):
+    even = (place[0] // 2) % 2 == 0
+    factor = jnp.where(even, local[10] * local[11], local[8] * local[9])
+    for i in range(4):
+        out[i] = second[i] + factor * near[i]
+
+
+def grow(place, local, second, near):
+    return pl.pallas_call(
+        grow_kernel,
+        in_specs=[in_smem] + [in_vmem] * 3,
+        out_specs=in_vmem,
+        out_shape=jax.ShapeDtypeStruct(second.shape, jnp.float32),
+        compiler_params=small,
+        cost_estimate=brief,
+        name="grow",
+    )(place, local, second, near)
+
+
 def join_kernel(chips, place, local, got, *refs):
     news = refs[:chips - 1]
     mine, theirs = refs[chips - 1:]
@@ -449,7 +494,12 @@
             first, second = ([jnp.where(upper, *one[::turn]) for one in sums] for turn in (1, -1))
             down = jnp.zeros(local.shape[1:], jnp.float32)
             up = down
-            for apart in range(1, chips):
+            if chips == 4:
+                near, middle, outer = (one[2 * a + ri] for one in news)
+                outer = near + local[13] * outer
+                down = jnp.where(chip == 0, 0.0, jnp.where(chip == 1, near, jnp.where(chip == 2, middle, outer)))
+                up = jnp.where(chip == 3, 0.0, jnp.where(chip == 2, near, jnp.where(chip == 1, middle, outer)))
+            for apart in range(1, chips if chips != 4 else 0):
                 term = local[11 + apart] * news[apart - 1][2 * a + ri]
                 down = down + jnp.where(chip >= apart, term, 0.0)
                 up = up + jnp.where(chip >= apart, 0.0, term)
@@ -475,7 +525,7 @@
     )(place, local, got, *news)
 
 
-def inverse_kernel(counts, my, thick, shifts, across, weights, out, faces, m_all, f_all, g_all):
+def inverse_kernel(counts, my, thick, shifts, across, weights, out, faces, m_all, g_all, d_all, f_all, e_all):
     total = f_all.shape[0]
     classes = out.shape[0]
     ky = shifts.shape[0]
@@ -485,25 +535,31 @@
     one = jnp.ones_like(shift)
     zero = jnp.zeros_like(shift)
 
-    def step(j, state):
-        f, r, phi, s = state
-        m = spread_face(faces[j], r) * r
-        f = shift * thick[j] + m * f
-        r = 1.0 / (spread_face(faces[j + 1], f) + f)
-        m_all[j] = m
-        f_all[j] = f
-        i = total - 1 - j
-        u = spread_face(faces[i + 1], s) * s * phi
-        phi = shift * thick[i] + u
-        s = 1.0 / (spread_face(faces[i], phi) + phi)
-        g_all[i] = u
-        return f, r, phi, s
-
-    lax.fori_loop(0, total, step, (one, one, zero, zero), unroll=4)
+    def steps(block, state):
+        n, d, p, e = state
+        for i in range(ROWS):
+            j = block * ROWS + i
+            q = spread_face(faces[j], n)
+            a = q * d
+            d = a + n
+            n = (shift * thick[j]) * d + q * n
+            m_all[j], d_all[j], f_all[j] = a, d, n
+            j = total - 1 - j
+            q = spread_face(faces[j + 1], p)
+            w = q * p
+            e = q * e + p
+            p = (shift * thick[j]) * e + w
+            g_all[j], e_all[j] = w, e
+        one, two = pl.reciprocal(d, approx=True), pl.reciprocal(e, approx=True)
+        return n * one, d * one, p * two, e * two
+
+    lax.fori_loop(0, total // ROWS, steps, (one, zero, one, zero))
     weight = weights[...]
 
     def centre(j, _):
-        g_all[j] = weight / (f_all[j] + g_all[j])
+        d, e = d_all[j], e_all[j]
+        m_all[j] = m_all[j] / d
+        g_all[j] = weight * (d * e) / (f_all[j] * e + g_all[j] * d)
         return 0
 
     lax.fori_loop(0, total, centre, 0, unroll=8)
@@ -572,7 +628,7 @@
         functools.partial(inverse_kernel, counts),
         in_specs=[in_smem] * 3 + [in_vmem] * 2,
         out_shape=jax.ShapeDtypeStruct((classes, total, wide), jnp.float32),
-        scratch_shapes=[pltpu.VMEM((total + 1, ROWS, LANES), jnp.float32)] + [pltpu.VMEM((total,) + across.shape, jnp.float32)] * 3,
+        scratch_shapes=[pltpu.VMEM((total + 1, ROWS, LANES), jnp.float32)] + [pltpu.VMEM((total,) + across.shape, jnp.float32)] * 5,
         compiler_params=small,
         cost_estimate=lengthy,
         name="inverse_sums",
@@ -763,9 +819,17 @@
     my = (depth_pos * waves + wave_pos).astype(jnp.int32).reshape(1)
     got = across(give)
     edges = everywhere(edges)
-    sums = chip_sums(place, local, got, chips)
-    news = [along(sums[apart - 1], apart) for apart in range(1, chips)]
     inverse = inverse_sums(my, thickness, ky_shift, waves, size)
+    if chips == 4:
+        both = lambda moves: [(2 * a + core, 2 * b + core) for a, b in moves for core in range(2)]
+        first, second = pair_sums(place, local, got)
+        near = lax.ppermute(first, "depth", both(((0, 1), (1, 0), (2, 3), (3, 2))))
+        near, _, _ = lax.optimization_barrier((near, inverse, edges))
+        grown = grow(place, local, second, near)
+        news = [near] + [lax.ppermute(grown, "depth", both(moves)) for moves in (((1, 2), (2, 1)), ((1, 3), (2, 0)))]
+    else:
+        sums = chip_sums(place, local, got, chips)
+        news = [along(sums[apart - 1], apart) for apart in range(1, chips)]
     values = interface(edges, inverse, waves, size)
     values = everywhere(values)
     news, _ = lax.optimization_barrier((news, values))

time: 72 us -> 70 us (0.972)
  starting transfers between devices: 13.9 us -> 12.1 us
  waiting for transfers between devices: 1.91 us -> 3.43 us
  blocking collectives: 18.4 us -> 16.9 us
    ppermute x3, starting transfers between devices: 5.65 us -> 3.81 us  [the longest x2 1.97 us: shards(): lax.ppermute(grown, 'depth', both(moves))]
    ppermute x3, waiting for transfers between devices: 0.01 us -> 1.53 us  [the longest x1 1.52 us: shards(): near = lax.ppermute(first, 'depth', both(((0, 1), (1, 0), (2, 3), (3, 2))))]
    all_to_all x1, blocking collectives: 18.4 us -> 16.9 us  [everywhere(): lax.all_to_all(a, ('depth', 'wave'), split_axis=0, concat_axis=0, tiled=T...]
  transfers between devices with their start and end apart: 6 -> 6, of which waited for: 1 -> 2; matrix products, arithmetic and copies ran while one was open for 0% -> 0% of each run, Pallas kernels for 9% -> 9%
where the time goes in v11:
time: 70 us; the launch traced here: 69.7 us
  Pallas kernels  35 us (50%)
  blocking collectives  16.9 us (24%)
  starting transfers between devices  12.1 us (17%)
  waiting for transfers between devices  3.43 us (5%)
  local copies, waits for them, and re-layouts  1.27 us (2%)
  between operations  1.04 us (1%)
    all_to_all x1, blocking collectives, everywhere(): lax.all_to_all(a, ('depth', 'wave'), split_axis=0, concat_axis=0, tiled=T...  16.9 us
    pallas_call x1, Pallas kernels, front(): pl.pallas_call(functools.partial(front_kernel, levels, total, group), in_...  14.9 us
    pallas_call x1, Pallas kernels, back(): pl.pallas_call(functools.partial(back_kernel, levels, total), in_specs=[i...  13.4 us
    all_to_all x1, starting transfers between devices, everywhere(): lax.all_to_all(a, ('depth', 'wave'), split_axis=0, concat_axis=0, tiled=T...  7.6 us
    pallas_call x1, Pallas kernels, inverse_sums(): pl.pallas_call(functools.partial(inverse_kernel, counts), in_specs=[in_sm...  5.64 us
    ppermute x2, starting transfers between devices, shards(): lax.ppermute(grown, 'depth', both(moves))  1.97 us
    ppermute x2, waiting for transfers between devices, across(): return lax.ppermute(a, 'depth', [(d, d ^ 1) for d in range(count)])  1.9 us
    ppermute x1, starting transfers between devices, shards(): near = lax.ppermute(first, 'depth', both(((0, 1), (1, 0), (2, 3), (3, 2))))  1.84 us
  transfers between devices with their start and end apart: 6, of which 2 were waited for; matrix products, arithmetic and copies ran while one was open for 0% of the time, Pallas kernels for 9%

profile of v11, /device:TPU:0, one launch (start us, length us, event | category | flops | bytes accessed | tf_op | source)
XLA Modules:
  0.0 69.7 jit_solution(14165770694643936577)
XLA Ops:
  0.6 0.0 copy-start.11
  0.6 0.0 copy-start.12
  0.7 0.0 copy-start.13
  0.7 0.0 copy-start.14
  0.7 14.9 %front.1 = (f32[65,32,1024]{2,1,0:T(8,128)}, f32[8,32,1024]{2,1,0:T(8,128)}, f32[3,32,1024]{2,1,0:T(8,128)}, f32[2,2,8,32,1024]{4,3,2,1,0:T(8,128)}, f32[15,16,1...) custom-call(s32[1]{0:T(128)} %bitcast.place, f32[64]{0:T(128)} %thick.5, f32[32]{0:T(128)} %shifts.3, ...), custom_call_target="tpu_custom_call" | custom-call | tf_op jit(solution)/shard_map/front/pallas_call | solution.py:367
  15.6 0.6 collective-permute-start
  16.2 7.6 %all-to-all-start = ((f32[32,4,128]{2,1,0:T(4,128)}), f32[32,4,128]{2,1,0:T(4,128)S(1)}, u32[]{:S(2)}, u32[]{:S(2)}) async-start(f32[32,4,128]{2,1,0:T(4,128)} %get-tuple-element.17), calls=%async_computation | async-start | bytes 131072 | tf_op jit(solution)/shard_map/all_to_all | solution.py:810
  23.8 0.0 collective-permute-done.got
  23.9 0.0 copy-start
  23.9 1.2 %copy-done = f32[15,16,1024]{2,1,0:T(8,128)S(1)} copy-done((f32[15,16,1024]{2,1,0:T(8,128)S(1)}, f32[15,16,1024]{2,1,0:T(8,128)}, u32[]{:S(2)}) %copy-start) | copy-done | bytes 983064
  25.1 0.1 pair_sums.1
  25.2 1.8 %collective-permute-start.1 = (f32[4,16,1024]{2,1,0:T(8,128)S(1)}, f32[4,16,1024]{2,1,0:T(8,128)S(1)}, u32[]{:S(2)}, u32[]{:S(2)}) collective-permute-start(f32[4,16,1024]{2,1,0:T(8,128)S(1)} %get-tuple-element.21), channel_id=1, source_target_pairs={{0,8},{4,12},{8,0},{12,4},{16,24},{20,28},{24,16},{28,20},{1,9},{5... | collective-permute-start | bytes 786440 | tf_op jit(solution)/shard_map/ppermute | solution.py:826
  27.0 0.0 copy-done.11
  27.0 0.0 copy-done.12
  27.0 0.0 copy-done.13
  27.0 0.0 copy-done.14
  27.0 0.0 copy-start.1
  27.0 0.0 copy-start.10
  27.1 5.6 %inverse_sums.1.inverse = f32[3,64,128]{2,1,0:T(8,128)S(1)} custom-call(s32[1]{0:T(128)} %bitcast.1.my, f32[64]{0:T(128)S(1)} %copy-done.11, f32[32]{0:T(128)S(1)} %copy-done.12, f32[24,128]{1,0:T(8,128)S(1)} %copy-done.14, f32[24,128]{1,0:T(8,128)S(1)} %copy-done.13), custom_call_target="tpu_custom_call" | custom-call | flops 20000000000 | bytes 40000000 | tf_op jit(solution)/shard_map/inverse_sums/pallas_call | solution.py:627
  32.7 0.0 all-to-all-done.edges
  32.7 1.5 %collective-permute-done.1.near.refs_0_ = f32[4,16,1024]{2,1,0:T(8,128)S(1)} collective-permute-done((f32[4,16,1024]{2,1,0:T(8,128)S(1)}, f32[4,16,1024]{2,1,0:T(8,128)S(1)}, u32[]{:S(2)}, u32[]{:S(2)}) %collective-permute-start.1) | collective-permute-done | bytes 262176 | tf_op jit(solution)/shard_map/ppermute | solution.py:826
  34.2 0.0 copy-done.1
  34.3 1.3 %collective-permute-start.3 = (f32[4,16,1024]{2,1,0:T(8,128)S(1)}, f32[4,16,1024]{2,1,0:T(8,128)S(1)}, u32[]{:S(2)}, u32[]{:S(2)}) collective-permute-start(f32[4,16,1024]{2,1,0:T(8,128)S(1)} %grow.1), channel_id=1, source_target_pairs={{8,24},{12,28},{16,0},{20,4},{9,25},{13,29},{17,1},{21,5},{10,26},... | collective-permute-start | bytes 786440 | tf_op jit(solution)/shard_map/ppermute | solution.py:829
  35.6 0.7 collective-permute-start.2
  36.3 0.0 copy-done.10
  36.3 0.7 interface.1
  36.9 16.9 %all_to_all.10.values_v = f32[32,4,128]{2,1,0:T(4,128)S(1)} all-to-all(f32[32,4,128]{2,1,0:T(4,128)S(1)} %interface.1), channel_id=1, replica_groups=mesh['depth'=8,'wave'=4] {'depth','wave'}, dimensions={0} | all-to-all | bytes 131072 | tf_op jit(solution)/shard_map/all_to_all | solution.py:810
  53.8 0.0 copy-start.2
  53.8 0.0 copy-start.3
  53.8 0.0 copy-start.4
  53.8 0.0 copy-start.5
  53.8 0.0 copy-start.6
  53.8 0.0 copy-start.7
  53.8 0.0 copy-start.8
  53.8 0.0 copy-start.9
  53.9 0.0 collective-permute-done.3.refs_2_
  53.9 0.0 collective-permute-done.2.refs_1_
  53.9 0.2 join.1
  54.1 0.1 collective-permute-start.4
  54.2 1.9 %collective-permute-done.4.theirs = f32[2,2,2,16,1024]{4,3,2,1,0:T(8,128)S(1)} collective-permute-done((f32[2,2,2,16,1024]{4,3,2,1,0:T(8,128)S(1)}, f32[2,2,2,16,1024]{4,3,2,1,0:T(8,128)S(1)}, u32[]{:S(2)}, u32[]{:S(2)}) %collective-permute-start.4) | collective-permute-done | bytes 524320 | tf_op jit(solution)/shard_map/ppermute | solution.py:804
  56.1 0.0 copy-done.2
  56.1 0.0 copy-done.3
  56.1 0.0 copy-done.4
  56.1 0.0 copy-done.5
  56.1 0.0 copy-done.6
  56.1 0.0 copy-done.7
  56.1 0.0 copy-done.8
  56.1 0.0 copy-done.9
  56.1 13.4 %back.1 = (f32[2,8,32,1024]{3,2,1,0:T(8,128)}, f32[2,8,32,1024]{3,2,1,0:T(8,128)}) custom-call(s32[1]{0:T(128)} %bitcast.place, f32[64]{0:T(128)S(1)} %copy-done.11, f32[32,4,128]{2,1,0:T(4,128)S(1)} %all_to_all.10.values_v, bf16[128,256]{1,0:T(8,128)(2,1)S(1)} %copy-done.9, f32[65,32,1024]{2,1,0:T(8,128)} %get-tuple-element.18.t, ...), custom_call_target="tpu_custom_call" | custom-call | tf_op jit(solution)/shard_map/back/pallas_call | solution.py:773
  (1 shorter events, 0.0 us)
Async XLA Ops:
  0.6 26.4 %copy-start.11 = (f32[64]{0:T(128)S(1)}, f32[64]{0:T(128)}, u32[]{:S(2)}) copy-start(f32[64]{0:T(128)} %thick.5) | copy-start | bytes 772
  0.6 26.4 %copy-start.12 = (f32[32]{0:T(128)S(1)}, f32[32]{0:T(128)}, u32[]{:S(2)}) copy-start(f32[32]{0:T(128)} %shifts.3) | copy-start | bytes 388
  0.7 26.4 %copy-start.13 = (f32[24,128]{1,0:T(8,128)S(1)}, f32[24,128]{1,0:T(8,128)}, u32[]{:S(2)}) copy-start(f32[24,128]{1,0:T(8,128)} %constant.49.clone.weights) | copy-start | bytes 36868
  0.7 26.4 %copy-start.14 = (f32[24,128]{1,0:T(8,128)S(1)}, f32[24,128]{1,0:T(8,128)}, u32[]{:S(2)}) copy-start(f32[24,128]{1,0:T(8,128)} %constant.48.clone.across) | copy-start | bytes 36868
  15.6 8.2 %collective-permute-start = (f32[2,4,16,1024]{3,2,1,0:T(8,128)}, f32[2,4,16,1024]{3,2,1,0:T(8,128)S(1)}, u32[]{:S(2)}, u32[]{:S(2)}) collective-permute-start(f32[2,4,16,1024]{3,2,1,0:T(8,128)} %get-tuple-element.20), channel_id=1, source_target_pairs={{0,4},{4,0},{8,12},{12,8},{16,20},{20,16},{24,28},{28,24},{1,5},{5... | collective-permute-start | bytes 1572872 | tf_op jit(solution)/shard_map/ppermute | solution.py:804
  16.2 16.5 %all-to-all-start = ((f32[32,4,128]{2,1,0:T(4,128)}), f32[32,4,128]{2,1,0:T(4,128)S(1)}, u32[]{:S(2)}, u32[]{:S(2)}) async-start(f32[32,4,128]{2,1,0:T(4,128)} %get-tuple-element.17), calls=%async_computation | async-start | bytes 131072 | tf_op jit(solution)/shard_map/all_to_all | solution.py:810
  23.9 1.2 %copy-start = (f32[15,16,1024]{2,1,0:T(8,128)S(1)}, f32[15,16,1024]{2,1,0:T(8,128)}, u32[]{:S(2)}) copy-start(f32[15,16,1024]{2,1,0:T(8,128)} %get-tuple-element.19.local) | copy-start | bytes 2949124
  25.2 9.1 %collective-permute-start.1 = (f32[4,16,1024]{2,1,0:T(8,128)S(1)}, f32[4,16,1024]{2,1,0:T(8,128)S(1)}, u32[]{:S(2)}, u32[]{:S(2)}) collective-permute-start(f32[4,16,1024]{2,1,0:T(8,128)S(1)} %get-tuple-element.21), channel_id=1, source_target_pairs={{0,8},{4,12},{8,0},{12,4},{16,24},{20,28},{24,16},{28,20},{1,9},{5... | collective-permute-start | bytes 786440 | tf_op jit(solution)/shard_map/ppermute | solution.py:826
  27.0 7.2 %copy-start.1 = (f32[15,16,1024]{2,1,0:T(8,128)S(1)}, f32[15,16,1024]{2,1,0:T(8,128)}, u32[]{:S(2)}) copy-start(f32[15,16,1024]{2,1,0:T(8,128)} %get-tuple-element.19.local) | copy-start | bytes 2949124
  27.0 9.2 %copy-start.10 = (f32[96,32]{1,0:T(8,128)S(1)}, f32[96,32]{1,0:T(8,128)}, u32[]{:S(2)}) copy-start(f32[96,32]{1,0:T(8,128)} %constant.50.clone.matrices) | copy-start | bytes 36868
  34.3 19.6 %collective-permute-start.3 = (f32[4,16,1024]{2,1,0:T(8,128)S(1)}, f32[4,16,1024]{2,1,0:T(8,128)S(1)}, u32[]{:S(2)}, u32[]{:S(2)}) collective-permute-start(f32[4,16,1024]{2,1,0:T(8,128)S(1)} %grow.1), channel_id=1, source_target_pairs={{8,24},{12,28},{16,0},{20,4},{9,25},{13,29},{17,1},{21,5},{10,26},... | collective-permute-start | bytes 786440 | tf_op jit(solution)/shard_map/ppermute | solution.py:829
  35.6 18.3 %collective-permute-start.2 = (f32[4,16,1024]{2,1,0:T(8,128)S(1)}, f32[4,16,1024]{2,1,0:T(8,128)S(1)}, u32[]{:S(2)}, u32[]{:S(2)}) collective-permute-start(f32[4,16,1024]{2,1,0:T(8,128)S(1)} %grow.1), channel_id=1, source_target_pairs={{8,16},{12,20},{16,8},{20,12},{9,17},{13,21},{17,9},{21,13},{10,18... | collective-permute-start | bytes 786440 | tf_op jit(solution)/shard_map/ppermute | solution.py:829
  53.8 2.3 %copy-start.2 = (f32[8,32,1024]{2,1,0:T(8,128)S(1)}, f32[8,32,1024]{2,1,0:T(8,128)}, u32[]{:S(2)}) copy-start(f32[8,32,1024]{2,1,0:T(8,128)} %get-tuple-element.30.m_v) | copy-start | bytes 3145732
  53.8 2.3 %copy-start.3 = (bf16[512,512]{1,0:T(8,128)(2,1)S(1)}, bf16[512,512]{1,0:T(8,128)(2,1)}, u32[]{:S(2)}) copy-start(bf16[512,512]{1,0:T(8,128)(2,1)} %constant.55.clone.er) | copy-start | bytes 1572868
  53.8 2.3 %copy-start.4 = (bf16[512,512]{1,0:T(8,128)(2,1)S(1)}, bf16[512,512]{1,0:T(8,128)(2,1)}, u32[]{:S(2)}) copy-start(bf16[512,512]{1,0:T(8,128)(2,1)} %constant.54.clone.et) | copy-start | bytes 1572868
  53.8 2.3 %copy-start.5 = (bf16[512,512]{1,0:T(8,128)(2,1)S(1)}, bf16[512,512]{1,0:T(8,128)(2,1)}, u32[]{:S(2)}) copy-start(bf16[512,512]{1,0:T(8,128)(2,1)} %constant.53.clone.orest) | copy-start | bytes 1572868
  53.8 2.3 %copy-start.6 = (bf16[512,512]{1,0:T(8,128)(2,1)S(1)}, bf16[512,512]{1,0:T(8,128)(2,1)}, u32[]{:S(2)}) copy-start(bf16[512,512]{1,0:T(8,128)(2,1)} %constant.52.clone.ot) | copy-start | bytes 1572868
  53.8 2.3 %copy-start.7 = (f32[3,32,1024]{2,1,0:T(8,128)S(1)}, f32[3,32,1024]{2,1,0:T(8,128)}, u32[]{:S(2)}) copy-start(f32[3,32,1024]{2,1,0:T(8,128)} %get-tuple-element.31.end_v) | copy-start | bytes 1179652
  53.8 2.3 %copy-start.8 = (f32[8,1024]{1,0:T(8,128)S(1)}, f32[8,1024]{1,0:T(8,128)}, u32[]{:S(2)}) copy-start(f32[8,1024]{1,0:T(8,128)} %constant.42.clone.sines.sines_v) | copy-start | bytes 98308
  53.8 2.3 %copy-start.9 = (bf16[128,256]{1,0:T(8,128)(2,1)S(1)}, bf16[128,256]{1,0:T(8,128)(2,1)}, u32[]{:S(2)}) copy-start(bf16[128,256]{1,0:T(8,128)(2,1)} %constant.51.clone.spread_v) | copy-start | bytes 196612
  54.1 2.0 %collective-permute-start.4 = (f32[2,2,2,16,1024]{4,3,2,1,0:T(8,128)S(1)}, f32[2,2,2,16,1024]{4,3,2,1,0:T(8,128)S(1)}, u32[]{:S(2)}, u32[]{:S(2)}) collective-permute-start(f32[2,2,2,16,1024]{4,3,2,1,0:T(8,128)S(1)} %get-tuple-element.28), channel_id=1, source_target_pairs={{0,4},{4,0},{8,12},{12,8},{16,20},{20,16},{24,28},{28,24},{1,5},{5... | collective-permute-start | bytes 1572872 | tf_op jit(solution)/shard_map/ppermute | solution.py:804

commit v12 on v11

--- a/solution.py
+++ b/solution.py
@@ -824,13 +824,16 @@
         both = lambda moves: [(2 * a + core, 2 * b + core) for a, b in moves for core in range(2)]
         first, second = pair_sums(place, local, got)
         near = lax.ppermute(first, "depth", both(((0, 1), (1, 0), (2, 3), (3, 2))))
-        near, _, _ = lax.optimization_barrier((near, inverse, edges))
+        values = interface(edges, inverse, waves, size)
+        near, values = lax.optimization_barrier((near, values))
         grown = grow(place, local, second, near)
+        grown, values = lax.optimization_barrier((grown, values))
         news = [near] + [lax.ppermute(grown, "depth", both(moves)) for moves in (((1, 2), (2, 1)), ((1, 3), (2, 0)))]
     else:
         sums = chip_sums(place, local, got, chips)
         news = [along(sums[apart - 1], apart) for apart in range(1, chips)]
-    values = interface(edges, inverse, waves, size)
+    if chips != 4:
+        values = interface(edges, inverse, waves, size)
     values = everywhere(values)
     news, _ = lax.optimization_barrier((news, values))
     mine, theirs = join(place, local, got, news)

time: 70 us -> 70 us (level)
  no operation moved by 1% of the time
where the time goes in v12:
time: 70 us; the launch traced here: 69.7 us
  Pallas kernels  35 us (50%)
  blocking collectives  17.5 us (25%)
  starting transfers between devices  12.1 us (17%)
  waiting for transfers between devices  2.76 us (4%)
  local copies, waits for them, and re-layouts  1.27 us (2%)
  between operations  1.04 us (1%)
    all_to_all x1, blocking collectives, everywhere(): lax.all_to_all(a, ('depth', 'wave'), split_axis=0, concat_axis=0, tiled=T...  17.5 us
    pallas_call x1, Pallas kernels, front(): pl.pallas_call(functools.partial(front_kernel, levels, total, group), in_...  14.9 us
    pallas_call x1, Pallas kernels, back(): pl.pallas_call(functools.partial(back_kernel, levels, total), in_specs=[i...  13.4 us
    all_to_all x1, starting transfers between devices, everywhere(): lax.all_to_all(a, ('depth', 'wave'), split_axis=0, concat_axis=0, tiled=T...  7.6 us
    pallas_call x1, Pallas kernels, inverse_sums(): pl.pallas_call(functools.partial(inverse_kernel, counts), in_specs=[in_sm...  5.64 us
    ppermute x2, starting transfers between devices, shards(): lax.ppermute(grown, 'depth', both(moves))  1.97 us
    ppermute x2, waiting for transfers between devices, across(): return lax.ppermute(a, 'depth', [(d, d ^ 1) for d in range(count)])  1.9 us
    ppermute x1, starting transfers between devices, shards(): near = lax.ppermute(first, 'depth', both(((0, 1), (1, 0), (2, 3), (3, 2))))  1.84 us
  transfers between devices with their start and end apart: 6, of which 2 were waited for; matrix products, arithmetic and copies ran while one was open for 0% of the time, Pallas kernels for 9%

profile of v12, /device:TPU:0, one launch (start us, length us, event | category | flops | bytes accessed | tf_op | source)
XLA Modules:
  0.0 69.7 jit_solution(6685995895477590553)
XLA Ops:
  0.6 0.0 copy-start.11
  0.6 0.0 copy-start.12
  0.7 0.0 copy-start.13
  0.7 0.0 copy-start.14
  0.7 14.9 %front.1 = (f32[65,32,1024]{2,1,0:T(8,128)}, f32[8,32,1024]{2,1,0:T(8,128)}, f32[3,32,1024]{2,1,0:T(8,128)}, f32[2,2,8,32,1024]{4,3,2,1,0:T(8,128)}, f32[15,16,1...) custom-call(s32[1]{0:T(128)} %bitcast.place, f32[64]{0:T(128)} %thick.5, f32[32]{0:T(128)} %shifts.3, ...), custom_call_target="tpu_custom_call" | custom-call | tf_op jit(solution)/shard_map/front/pallas_call | solution.py:367
  15.6 0.6 collective-permute-start
  16.2 7.6 %all-to-all-start = ((f32[32,4,128]{2,1,0:T(4,128)}), f32[32,4,128]{2,1,0:T(4,128)S(1)}, u32[]{:S(2)}, u32[]{:S(2)}) async-start(f32[32,4,128]{2,1,0:T(4,128)} %get-tuple-element.24), calls=%async_computation | async-start | bytes 131072 | tf_op jit(solution)/shard_map/all_to_all | solution.py:810
  23.8 0.0 collective-permute-done.got
  23.9 0.0 copy-start
  23.9 1.2 %copy-done = f32[15,16,1024]{2,1,0:T(8,128)S(1)} copy-done((f32[15,16,1024]{2,1,0:T(8,128)S(1)}, f32[15,16,1024]{2,1,0:T(8,128)}, u32[]{:S(2)}) %copy-start) | copy-done | bytes 983064
  25.1 0.1 pair_sums.1
  25.2 1.8 %collective-permute-start.1 = (f32[4,16,1024]{2,1,0:T(8,128)S(1)}, f32[4,16,1024]{2,1,0:T(8,128)S(1)}, u32[]{:S(2)}, u32[]{:S(2)}) collective-permute-start(f32[4,16,1024]{2,1,0:T(8,128)S(1)} %get-tuple-element.23), channel_id=1, source_target_pairs={{0,8},{4,12},{8,0},{12,4},{16,24},{20,28},{24,16},{28,20},{1,9},{5... | collective-permute-start | bytes 786440 | tf_op jit(solution)/shard_map/ppermute | solution.py:826
  27.0 0.0 copy-done.11
  27.0 0.0 copy-done.12
  27.0 0.0 copy-done.13
  27.0 0.0 copy-done.14
  27.0 0.0 copy-start.10
  27.0 0.0 copy-start.1
  27.1 5.6 %inverse_sums.1.inverse = f32[3,64,128]{2,1,0:T(8,128)S(1)} custom-call(s32[1]{0:T(128)} %bitcast.1.my, f32[64]{0:T(128)S(1)} %copy-done.11, f32[32]{0:T(128)S(1)} %copy-done.12, f32[24,128]{1,0:T(8,128)S(1)} %copy-done.14, f32[24,128]{1,0:T(8,128)S(1)} %copy-done.13), custom_call_target="tpu_custom_call" | custom-call | flops 20000000000 | bytes 40000000 | tf_op jit(solution)/shard_map/inverse_sums/pallas_call | solution.py:627
  32.7 0.0 all-to-all-done.edges
  32.7 0.0 copy-done.10
  32.7 0.7 interface.1
  33.4 0.9 %collective-permute-done.1.near.refs_0_ = f32[4,16,1024]{2,1,0:T(8,128)S(1)} collective-permute-done((f32[4,16,1024]{2,1,0:T(8,128)S(1)}, f32[4,16,1024]{2,1,0:T(8,128)S(1)}, u32[]{:S(2)}, u32[]{:S(2)}) %collective-permute-start.1) | collective-permute-done | bytes 262176 | tf_op jit(solution)/shard_map/ppermute | solution.py:826
  34.2 0.0 copy-done.1
  34.3 1.3 %collective-permute-start.3 = (f32[4,16,1024]{2,1,0:T(8,128)S(1)}, f32[4,16,1024]{2,1,0:T(8,128)S(1)}, u32[]{:S(2)}, u32[]{:S(2)}) collective-permute-start(f32[4,16,1024]{2,1,0:T(8,128)S(1)} %grow.1), channel_id=1, source_target_pairs={{8,24},{12,28},{16,0},{20,4},{9,25},{13,29},{17,1},{21,5},{10,26},... | collective-permute-start | bytes 786440 | tf_op jit(solution)/shard_map/ppermute | solution.py:831
  35.6 0.7 collective-permute-start.2
  36.3 17.5 %all_to_all.10.values_v = f32[32,4,128]{2,1,0:T(4,128)S(1)} all-to-all(f32[32,4,128]{2,1,0:T(4,128)S(1)} %interface.1), channel_id=1, replica_groups=mesh['depth'=8,'wave'=4] {'depth','wave'}, dimensions={0} | all-to-all | bytes 131072 | tf_op jit(solution)/shard_map/all_to_all | solution.py:810
  53.8 0.0 copy-start.2
  53.8 0.0 copy-start.3
  53.8 0.0 copy-start.4
  53.8 0.0 copy-start.5
  53.8 0.0 copy-start.6
  53.8 0.0 copy-start.7
  53.8 0.0 copy-start.8
  53.8 0.0 copy-start.9
  53.9 0.0 collective-permute-done.3.refs_2_
  53.9 0.0 collective-permute-done.2.refs_1_
  53.9 0.2 join.1
  54.1 0.1 collective-permute-start.4
  54.2 1.9 %collective-permute-done.4.theirs = f32[2,2,2,16,1024]{4,3,2,1,0:T(8,128)S(1)} collective-permute-done((f32[2,2,2,16,1024]{4,3,2,1,0:T(8,128)S(1)}, f32[2,2,2,16,1024]{4,3,2,1,0:T(8,128)S(1)}, u32[]{:S(2)}, u32[]{:S(2)}) %collective-permute-start.4) | collective-permute-done | bytes 524320 | tf_op jit(solution)/shard_map/ppermute | solution.py:804
  56.1 0.0 copy-done.2
  56.1 0.0 copy-done.3
  56.1 0.0 copy-done.4
  56.1 0.0 copy-done.5
  56.1 0.0 copy-done.6
  56.1 0.0 copy-done.7
  56.1 0.0 copy-done.8
  56.1 0.0 copy-done.9
  56.2 13.4 %back.1 = (f32[2,8,32,1024]{3,2,1,0:T(8,128)}, f32[2,8,32,1024]{3,2,1,0:T(8,128)}) custom-call(s32[1]{0:T(128)} %bitcast.place, f32[64]{0:T(128)S(1)} %copy-done.11, f32[32,4,128]{2,1,0:T(4,128)S(1)} %all_to_all.10.values_v, bf16[128,256]{1,0:T(8,128)(2,1)S(1)} %copy-done.9, f32[65,32,1024]{2,1,0:T(8,128)} %get-tuple-element.28.t, ...), custom_call_target="tpu_custom_call" | custom-call | tf_op jit(solution)/shard_map/back/pallas_call | solution.py:773
  (1 shorter events, 0.0 us)
Async XLA Ops:
  0.6 26.4 %copy-start.11 = (f32[64]{0:T(128)S(1)}, f32[64]{0:T(128)}, u32[]{:S(2)}) copy-start(f32[64]{0:T(128)} %thick.5) | copy-start | bytes 772
  0.6 26.4 %copy-start.12 = (f32[32]{0:T(128)S(1)}, f32[32]{0:T(128)}, u32[]{:S(2)}) copy-start(f32[32]{0:T(128)} %shifts.3) | copy-start | bytes 388
  0.7 26.4 %copy-start.13 = (f32[24,128]{1,0:T(8,128)S(1)}, f32[24,128]{1,0:T(8,128)}, u32[]{:S(2)}) copy-start(f32[24,128]{1,0:T(8,128)} %constant.49.clone.weights) | copy-start | bytes 36868
  0.7 26.4 %copy-start.14 = (f32[24,128]{1,0:T(8,128)S(1)}, f32[24,128]{1,0:T(8,128)}, u32[]{:S(2)}) copy-start(f32[24,128]{1,0:T(8,128)} %constant.48.clone.across) | copy-start | bytes 36868
  15.6 8.2 %collective-permute-start = (f32[2,4,16,1024]{3,2,1,0:T(8,128)}, f32[2,4,16,1024]{3,2,1,0:T(8,128)S(1)}, u32[]{:S(2)}, u32[]{:S(2)}) collective-permute-start(f32[2,4,16,1024]{3,2,1,0:T(8,128)} %get-tuple-element.21), channel_id=1, source_target_pairs={{0,4},{4,0},{8,12},{12,8},{16,20},{20,16},{24,28},{28,24},{1,5},{5... | collective-permute-start | bytes 1572872 | tf_op jit(solution)/shard_map/ppermute | solution.py:804
  16.2 16.5 %all-to-all-start = ((f32[32,4,128]{2,1,0:T(4,128)}), f32[32,4,128]{2,1,0:T(4,128)S(1)}, u32[]{:S(2)}, u32[]{:S(2)}) async-start(f32[32,4,128]{2,1,0:T(4,128)} %get-tuple-element.24), calls=%async_computation | async-start | bytes 131072 | tf_op jit(solution)/shard_map/all_to_all | solution.py:810
  23.9 1.2 %copy-start = (f32[15,16,1024]{2,1,0:T(8,128)S(1)}, f32[15,16,1024]{2,1,0:T(8,128)}, u32[]{:S(2)}) copy-start(f32[15,16,1024]{2,1,0:T(8,128)} %get-tuple-element.20.local) | copy-start | bytes 2949124
  25.2 9.1 %collective-permute-start.1 = (f32[4,16,1024]{2,1,0:T(8,128)S(1)}, f32[4,16,1024]{2,1,0:T(8,128)S(1)}, u32[]{:S(2)}, u32[]{:S(2)}) collective-permute-start(f32[4,16,1024]{2,1,0:T(8,128)S(1)} %get-tuple-element.23), channel_id=1, source_target_pairs={{0,8},{4,12},{8,0},{12,4},{16,24},{20,28},{24,16},{28,20},{1,9},{5... | collective-permute-start | bytes 786440 | tf_op jit(solution)/shard_map/ppermute | solution.py:826
  27.0 5.7 %copy-start.10 = (f32[96,32]{1,0:T(8,128)S(1)}, f32[96,32]{1,0:T(8,128)}, u32[]{:S(2)}) copy-start(f32[96,32]{1,0:T(8,128)} %constant.50.clone.matrices) | copy-start | bytes 36868
  27.0 7.2 %copy-start.1 = (f32[15,16,1024]{2,1,0:T(8,128)S(1)}, f32[15,16,1024]{2,1,0:T(8,128)}, u32[]{:S(2)}) copy-start(f32[15,16,1024]{2,1,0:T(8,128)} %get-tuple-element.20.local) | copy-start | bytes 2949124
  34.3 19.6 %collective-permute-start.3 = (f32[4,16,1024]{2,1,0:T(8,128)S(1)}, f32[4,16,1024]{2,1,0:T(8,128)S(1)}, u32[]{:S(2)}, u32[]{:S(2)}) collective-permute-start(f32[4,16,1024]{2,1,0:T(8,128)S(1)} %grow.1), channel_id=1, source_target_pairs={{8,24},{12,28},{16,0},{20,4},{9,25},{13,29},{17,1},{21,5},{10,26},... | collective-permute-start | bytes 786440 | tf_op jit(solution)/shard_map/ppermute | solution.py:831
  35.6 18.3 %collective-permute-start.2 = (f32[4,16,1024]{2,1,0:T(8,128)S(1)}, f32[4,16,1024]{2,1,0:T(8,128)S(1)}, u32[]{:S(2)}, u32[]{:S(2)}) collective-permute-start(f32[4,16,1024]{2,1,0:T(8,128)S(1)} %grow.1), channel_id=1, source_target_pairs={{8,16},{12,20},{16,8},{20,12},{9,17},{13,21},{17,9},{21,13},{10,18... | collective-permute-start | bytes 786440 | tf_op jit(solution)/shard_map/ppermute | solution.py:831
  53.8 2.3 %copy-start.2 = (f32[8,32,1024]{2,1,0:T(8,128)S(1)}, f32[8,32,1024]{2,1,0:T(8,128)}, u32[]{:S(2)}) copy-start(f32[8,32,1024]{2,1,0:T(8,128)} %get-tuple-element.36.m_v) | copy-start | bytes 3145732
  53.8 2.3 %copy-start.3 = (bf16[512,512]{1,0:T(8,128)(2,1)S(1)}, bf16[512,512]{1,0:T(8,128)(2,1)}, u32[]{:S(2)}) copy-start(bf16[512,512]{1,0:T(8,128)(2,1)} %constant.55.clone.er) | copy-start | bytes 1572868
  53.8 2.3 %copy-start.4 = (bf16[512,512]{1,0:T(8,128)(2,1)S(1)}, bf16[512,512]{1,0:T(8,128)(2,1)}, u32[]{:S(2)}) copy-start(bf16[512,512]{1,0:T(8,128)(2,1)} %constant.54.clone.et) | copy-start | bytes 1572868
  53.8 2.3 %copy-start.5 = (bf16[512,512]{1,0:T(8,128)(2,1)S(1)}, bf16[512,512]{1,0:T(8,128)(2,1)}, u32[]{:S(2)}) copy-start(bf16[512,512]{1,0:T(8,128)(2,1)} %constant.53.clone.orest) | copy-start | bytes 1572868
  53.8 2.3 %copy-start.6 = (bf16[512,512]{1,0:T(8,128)(2,1)S(1)}, bf16[512,512]{1,0:T(8,128)(2,1)}, u32[]{:S(2)}) copy-start(bf16[512,512]{1,0:T(8,128)(2,1)} %constant.52.clone.ot) | copy-start | bytes 1572868
  53.8 2.3 %copy-start.7 = (f32[3,32,1024]{2,1,0:T(8,128)S(1)}, f32[3,32,1024]{2,1,0:T(8,128)}, u32[]{:S(2)}) copy-start(f32[3,32,1024]{2,1,0:T(8,128)} %get-tuple-element.37.end_v) | copy-start | bytes 1179652
  53.8 2.3 %copy-start.8 = (f32[8,1024]{1,0:T(8,128)S(1)}, f32[8,1024]{1,0:T(8,128)}, u32[]{:S(2)}) copy-start(f32[8,1024]{1,0:T(8,128)} %constant.42.clone.sines.sines_v) | copy-start | bytes 98308
  53.8 2.3 %copy-start.9 = (bf16[128,256]{1,0:T(8,128)(2,1)S(1)}, bf16[128,256]{1,0:T(8,128)(2,1)}, u32[]{:S(2)}) copy-start(bf16[128,256]{1,0:T(8,128)(2,1)} %constant.51.clone.spread_v) | copy-start | bytes 196612
  54.1 2.0 %collective-permute-start.4 = (f32[2,2,2,16,1024]{4,3,2,1,0:T(8,128)S(1)}, f32[2,2,2,16,1024]{4,3,2,1,0:T(8,128)S(1)}, u32[]{:S(2)}, u32[]{:S(2)}) collective-permute-start(f32[2,2,2,16,1024]{4,3,2,1,0:T(8,128)S(1)} %get-tuple-element.34), channel_id=1, source_target_pairs={{0,4},{4,0},{8,12},{12,8},{16,20},{20,16},{24,28},{28,24},{1,5},{5... | collective-permute-start | bytes 1572872 | tf_op jit(solution)/shard_map/ppermute | solution.py:804
